TPU v7x, 32 devices: a whole 2x2x4 slice. The times are simulated.
32 devices in a mesh: parts: 2 (over y), gx: 4 (over x, core), gy: 4 (over z).
Axes of the slice: x: 2, y: 2, z: 4, core: 2. Of those that a mesh axis runs over, the one named last changes fastest.
Arguments:
- adj_fields: float32 [3, 2, 1024, 1024], P(None, None, ('parts', 'gx'), 'gy'), parts along dimension 2, may hold values from -6 to 6
- inv_eps: float32 [2, 1024, 1024], P(None, ('parts', 'gx'), 'gy'), parts along dimension 1, may hold values from 0.0833 to 1
- fwd_diff: float32 [4, 2, 1024, 1024], P(None, None, ('parts', 'gx'), 'gy'), parts along dimension 2, may hold values from -6 to 6
- mon_x: int32 [128], P('parts'), parts along dimension 0, may hold values from 0 to 511
- mon_y: int32 [128], P('parts'), parts along dimension 0, may hold values from 0 to 1023
- mon_amp: float32 [4, 128], P(None, 'parts'), parts along dimension 1, may hold values from -16 to 16
- design_mask: int32 [8, 4, 128], P(('parts', 'gx'), 'gy'), parts along dimension 0, may hold values 0 or 1
- tile_owner: int32 [8, 4, 128, 1], P(('parts', 'gx'), 'gy'), parts along dimension 0, may hold values from 0 to 15; in each aligned block of 128 rows (0 to 127, 128 to 255, ..., all dimensions but the last counted through in order) at most 16 rows name the same one
Outputs:
- adj_final: float32 [3, 2, 1024, 1024], P(None, None, ('parts', 'gx'), 'gy'), parts along dimension 2
- grad_slots: float32 [32, 16, 16, 128], P(('parts', 'gx', 'gy')), parts along dimension 0
There are 2 independent parts, one for each index of `parts`. A program takes and returns all parts, laid end to end along the dimension named above; each array names one. Nothing has to cross between parts.
Inputs may be any that keep to these rules, and one draw needn't show every extreme that they name: `tile_owner`: among the tiles of one device no owner is named more than 16 times, and in every draw some owner is named exactly 16 times there.
All inputs are finite; a program needn't handle non-finite values. No bound on the sum of `design_mask` on one device may be relied on, other than what follows from the above.
Results may differ from a plain program's by a relative error of at most 0.0003.
Values sent between devices are 32-bit elements; how exact they have to be, the bound alone decides.
No kernel may reach another device: no remote copies, remote signals or barrier semaphores. Data moves between devices by JAX's collectives and lax.ppermute only.
A program may use at most 64 MiB of HBM per device.

v0:
```python
import jax
import jax.numpy as jnp
import ml_dtypes
import numpy as np
from jax import lax
from jax.experimental import pallas as pl
from jax.experimental.pallas import tpu as pltpu
from jax.sharding import PartitionSpec as P

STEPS = 4
PIX = 2
TS = 16
RADIUS = 4
COURANT = 0.6
COUPLING = 0.25

LANES = 128
SUB = 8
FAR = STEPS + PIX * (RADIUS - 1)
NEAR = PIX * (RADIUS - 1)
LEFT_OVER = FAR - SUB
PAD = 2 * SUB
HALF = LANES // 2
SIDE = HALF // 2
OUT = SIDE // 2
KEEP = 8
F32 = jnp.float32
BF16 = jnp.bfloat16
WIDTHS = (FAR,) * 4 + (NEAR,) * STEPS
FIRST = tuple(sum(WIDTHS[:k]) for k in range(len(WIDTHS)))
assert sum(WIDTHS) <= HALF and FAR <= OUT and STEPS + KEEP <= OUT


def cone_weights(radius):
    reach_cells = radius - 1
    offsets = np.arange(-reach_cells, reach_cells + 1)
    distance = np.sqrt(offsets[:, None] * offsets[:, None] + offsets[None, :] * offsets[None, :])
    weights = np.maximum(radius - distance, 0.0)
    return weights / weights.sum()


def pool_matrices():
    inner = np.zeros((2, LANES, LANES), np.float32)
    for j in range(2 * LANES):
        if KEEP <= j < 2 * LANES - KEEP:
            inner[j // LANES, j % LANES, j // PIX] = 1.0
    edge = np.zeros((LANES, 4 * LANES), np.float32)
    for lane in range(LANES):
        layer, at = lane // HALF, lane % HALF
        col = at - OUT if at < SIDE else at - SIDE + 2 * LANES - OUT
        pixel = col // PIX
        if 0 <= col < KEEP or 2 * LANES - KEEP <= col < 2 * LANES:
            edge[lane, 2 * layer * LANES + pixel] = 1.0
        elif -NEAR <= col < 0 or 2 * LANES <= col < 2 * LANES + NEAR:
            edge[lane, (2 * layer + 1) * LANES + pixel % LANES] = 1.0
    return inner.astype(ml_dtypes.bfloat16), edge.astype(ml_dtypes.bfloat16)


def split2(value):
    high = value.astype(BF16)
    return high, (value - high.astype(F32)).astype(BF16)


def split3(value):
    high = value.astype(BF16)
    rest = value - high.astype(F32)
    mid = rest.astype(BF16)
    return high, mid, (rest - mid.astype(F32)).astype(BF16)


def dot(a, b):
    return jnp.dot(a, b, preferred_element_type=F32)


def turn(value, shift, axis):
    size = value.shape[axis]
    return pltpu.roll(value, shift % size, axis) if shift % size else value


def lanes():
    return lax.broadcasted_iota(jnp.int32, (SUB, LANES), 1)


def subs():
    return lax.broadcasted_iota(jnp.int32, (SUB, LANES), 0)


def lane_tile(k):
    return pl.ds(k * LANES, LANES)


def is_odd():
    return ((subs() * 0 + lax.axis_index("gx")) & 1) == 1


def rows_kernel(fields, eps, fwd, cross, near, hold, hold_fwd, sems):
    rows, cols = fields.shape[2], fields.shape[3]
    copies = []
    for n, at in enumerate((0, rows - PAD)):
        at_fwd = 0 if n == 0 else rows - SUB
        pairs = (
            (fields.at[:, :, pl.ds(at, PAD), :], hold.at[n, pl.ds(0, 3)]),
            (eps.at[:, pl.ds(at, PAD), :], hold.at[n, 3]),
            (fwd.at[:, :, pl.ds(at_fwd, SUB), :], hold_fwd.at[n]),
        )
        for m, (src, dst) in enumerate(pairs):
            copies.append(pltpu.make_async_copy(src, dst, sems.at[3 * n + m]))
    for copy in copies:
        copy.start()
    for copy in copies:
        copy.wait()
    odd, sub = is_odd(), subs()
    for kind in range(4):
        for layer in range(2):
            plane = 2 * kind + layer
            for k in range(cols // LANES):
                at = lane_tile(k)
                low = hold[0, kind, layer, pl.ds(0, SUB), at]
                high = hold[1, kind, layer, pl.ds(SUB, SUB), at]
                cross[plane, :, at] = jnp.where(odd, high, low)
                near[plane, :, at] = jnp.where(odd, low, high)
                rest_low = turn(hold[0, kind, layer, pl.ds(SUB, SUB), at], -LEFT_OVER, 0)
                rest_high = turn(hold[1, kind, layer, pl.ds(0, SUB), at], LEFT_OVER, 0)
                low = jnp.where(sub >= NEAR, rest_low, hold_fwd[0, kind, layer, :, at])
                high = jnp.where(sub < SUB - NEAR, rest_high, hold_fwd[1, kind, layer, :, at])
                cross[8 + plane, :, at] = jnp.where(odd, high, low)
                near[8 + plane, :, at] = jnp.where(odd, low, high)


def halo_tile(cross, near, odd, tile, kind, layer, at):
    is_above = tile < 2
    outer = tile in (0, 3)
    if outer and kind >= 4:
        return None
    plane = 2 * kind + layer + (8 if outer else 0)
    a, b = near[plane, :, at], cross[plane, :, at]
    value = jnp.where(odd, a, b) if is_above else jnp.where(odd, b, a)
    if outer:
        value = turn(value, -LEFT_OVER if is_above else LEFT_OVER, 0)
    return value


def core_tile(fields, eps, fwd, at, kind, layer, cols):
    if kind < 3:
        return fields[kind, layer, at, cols]
    if kind == 3:
        return eps[layer, at, cols]
    return fwd[kind - 4, layer, at, cols]


def pack_tile(load, lane, right):
    total = jnp.zeros((SUB, LANES), F32)
    for kind, width in enumerate(WIDTHS):
        for layer in range(2):
            value = load(kind, layer)
            if value is None:
                continue
            first = FIRST[kind] + HALF * layer
            value = turn(value, first + width if right else first, 1)
            total = jnp.where((lane >= first) & (lane < first + width), value, total)
    return total


def cols_kernel(fields, eps, fwd, left, right):
    rows, cols = fields.shape[2], fields.shape[3]
    lane = lanes()

    def tile(t, carry):
        at = pl.ds(pl.multiple_of(t * SUB, SUB), SUB)
        out_at = pl.ds(pl.multiple_of(t * SUB + PAD, SUB), SUB)
        for out, lo, is_right in ((left, 0, False), (right, cols - LANES, True)):
            out[out_at, :] = pack_tile(
                lambda kind, layer: core_tile(fields, eps, fwd, at, kind, layer, pl.ds(lo, LANES)),
                lane, is_right,
            )
        return carry

    lax.fori_loop(0, rows // SUB, tile, 0, unroll=4)
    zero = jnp.zeros((PAD, LANES), F32)
    for out in (left, right):
        out[pl.ds(0, PAD), :] = zero
        out[pl.ds(PAD + rows, PAD), :] = zero


def corners_kernel(left_in, right_in, cross, near, left, right):
    rows, cols = left.shape[0] - 2 * PAD, cross.shape[2]
    lane, odd = lanes(), is_odd()
    for out, core, lo, is_right in ((left, left_in, 0, False), (right, right_in, cols - LANES, True)):
        out[pl.ds(PAD, rows), :] = core[pl.ds(PAD, rows), :]
        for tile in range(4):
            base = tile * SUB if tile < 2 else PAD + rows + (tile - 2) * SUB
            out[pl.ds(base, SUB), :] = pack_tile(
                lambda kind, layer: halo_tile(cross, near, odd, tile, kind, layer, pl.ds(lo, LANES)),
                lane, is_right,
            )


def side_kernel(capacity, mon_x, mon_y, amp, mask, owner, src, src_edge, place):
    _, _, ext_rows, cols = src.shape
    rows = ext_rows - 2 * PAD
    channels = mon_x.shape[1]
    row = mon_x[...] - lax.axis_index("gx") * rows + PAD
    col = mon_y[...] - lax.axis_index("gy") * cols
    in_left = (col >= -OUT) & (col < OUT)
    in_right = (col >= cols - OUT) & (col < cols + OUT)
    edge = jnp.where(in_left, col + OUT, jnp.where(in_right, col - cols + OUT + SIDE, -LANES))
    layer = lax.broadcasted_iota(jnp.int32, (1, channels), 1) & 1
    edge = edge + HALF * layer
    inside = jnp.where((col >= 0) & (col < cols), col, -1)
    one_y = lax.broadcasted_iota(jnp.int32, (cols, channels), 0) == inside
    one_e = lax.broadcasted_iota(jnp.int32, (LANES, channels), 0) == edge
    one_y = jnp.where(one_y, 1.0, 0.0).astype(BF16)
    one_e = jnp.where(one_e, 1.0, 0.0).astype(BF16)
    one_y = jnp.concatenate([one_y] * 3, axis=1)
    one_e = jnp.concatenate([one_e] * 3, axis=1)
    one_x = lax.broadcasted_iota(jnp.int32, (ext_rows, channels), 0) == row
    one_x = jnp.where(one_x, 1.0, 0.0).astype(F32)
    nt = (((1,), (1,)), ((), ()))
    for step in range(STEPS):
        parts = [part.astype(F32) for part in split3(amp[pl.ds(step, 1), :])]
        lhs = jnp.concatenate([one_x * part for part in parts], axis=1)
        src_edge[step] = lax.dot_general(lhs.astype(BF16), one_e, nt, preferred_element_type=F32)
        layer_wide = jnp.concatenate([layer] * 3, axis=1)
        for which in range(2):
            some = jnp.where(layer_wide == which, lhs, 0.0).astype(BF16)
            src[step, which] = lax.dot_general(some, one_y, nt, preferred_element_type=F32)
    tiles = owner.shape[1]
    own = owner[...].astype(F32)
    own_wide = jnp.broadcast_to(own, (tiles, tiles))
    earlier = lax.broadcasted_iota(jnp.int32, (tiles, tiles), 0) < lax.broadcasted_iota(
        jnp.int32, (tiles, tiles), 1
    )
    same = (own_wide.T == own_wide) & earlier
    slot = jnp.sum(jnp.where(same, 1.0, 0.0), axis=0, keepdims=True)
    dest = owner[...] * capacity + slot.astype(jnp.int32)
    dest = jnp.where(mask[...] != 0, dest, -1)
    hit = lax.broadcasted_iota(jnp.int32, place.shape, 0) == dest
    place[...] = jnp.where(hit, 1.0, 0.0).astype(BF16)


def yee(bufs, keys, eps_of, change_of, src_of, grad, coef_x, coef_first, next_col, prev_col, other):
    n_tiles = (bufs[0].shape[-2] - 2 * SUB) // SUB
    for step in range(STEPS):
        old, new = ((0, 1), (1, 0), (0, 1), (1, 2))[step]
        old, new = bufs[old], bufs[new]
        low = 0 if step < 2 else 1
        high = n_tiles if step == 0 else n_tiles - 1
        for t in range(low, high):
            at = pl.ds(SUB + t * SUB, SUB)
            under = pl.ds(SUB + t * SUB + 1, SUB)
            over = pl.ds(SUB + t * SUB - 1, SUB)
            coef_y = coef_first if t < PAD // SUB else COURANT
            e = {key: old[(0,) + key + (at, slice(None))] for key in keys}
            e_right = next_col(e)
            hx, hy = {}, {}
            for key in keys:
                hx[key] = old[(1,) + key + (at, slice(None))] + coef_x * (e_right[key] - e[key])
                below = old[(0,) + key + (under, slice(None))]
                hy[key] = old[(2,) + key + (at, slice(None))] - coef_y * (below - e[key])
                new[(1,) + key + (at, slice(None))] = hx[key]
                new[(2,) + key + (at, slice(None))] = hy[key]
            hx_left = prev_col(hx)
            for key in keys:
                hy_above = new[(2,) + key + (over, slice(None))]
                curl = (hy[key] - hy_above) - (hx[key] - hx_left[key])
                curl = curl + COUPLING * (other(e, key) - e[key])
                value = e[key] - eps_of(key, t) * curl + src_of(step, key, t)
                new[(0,) + key + (at, slice(None))] = value
                if 1 <= t < n_tiles - 1:
                    change = value * change_of(step, key, t)
                    where = key + (pl.ds(t * SUB, SUB), slice(None))
                    grad[where] = -change if step == 0 else grad[where] - change


def coef_above():
    return jnp.where((subs() * 0 + lax.axis_index("gx")) > 0, COURANT, 0.0).astype(F32)


def clear_rims(buf):
    size = buf.shape[-2]
    zero = jnp.zeros(buf.shape[:-2] + (SUB, LANES), F32)
    lead = (slice(None),) * (len(buf.shape) - 2)
    buf[lead + (pl.ds(0, SUB), slice(None))] = zero
    buf[lead + (pl.ds(size - SUB, SUB), slice(None))] = zero


def row_pairs(ref, lead, count):
    even = ref[lead + (pl.ds(0, count, stride=PIX), slice(None))]
    return even + ref[lead + (pl.ds(1, count, stride=PIX), slice(None))]


def inner_kernel(fields, eps, fwd, cross, near, src, mats, last, pooled, base, a, b, e, g):
    rows, cols = fields.shape[2], fields.shape[3]
    n_tiles = (rows + 2 * PAD) // SUB
    n_lanes = cols // LANES
    lane, odd = lanes(), is_odd()
    halo_of = {0: 0, 1: 1, n_tiles - 2: 2, n_tiles - 1: 3}

    def load(kind, layer, t, k):
        if t in halo_of:
            return halo_tile(cross, near, odd, halo_of[t], kind, layer, lane_tile(k))
        return core_tile(fields, eps, fwd, pl.ds(t * SUB - PAD, SUB), kind, layer, lane_tile(k))

    for buf in (a, b, last):
        clear_rims(buf)
    for t in range(n_tiles):
        for layer in range(2):
            for k in range(n_lanes):
                for kind in range(3):
                    a[kind, layer, k, pl.ds(SUB + t * SUB, SUB), :] = load(kind, layer, t, k)
                e[layer, k, pl.ds(t * SUB, SUB), :] = COURANT * load(3, layer, t, k)

    at_end, at_start = lane == LANES - 1, lane == 0
    keys = [(layer, k) for layer in range(2) for k in range(n_lanes)]

    def next_col(values):
        moved = {key: turn(value, -1, 1) for key, value in values.items()}
        return {
            (l, k): jnp.where(at_end, moved[l, (k + 1) % n_lanes], moved[l, k]) for l, k in keys
        }

    def prev_col(values):
        moved = {key: turn(value, 1, 1) for key, value in values.items()}
        return {
            (l, k): jnp.where(at_start, moved[l, (k - 1) % n_lanes], moved[l, k]) for l, k in keys
        }

    yee(
        (a, b, last), keys,
        lambda key, t: e[key + (pl.ds(t * SUB, SUB), slice(None))],
        lambda step, key, t: load(4 + step, key[0], t, key[1]),
        lambda step, key, t: src[step, key[0], pl.ds(t * SUB, SUB), lane_tile(key[1])],
        g, COURANT, coef_above(), next_col, prev_col,
        lambda values, key: values[1 - key[0], key[1]],
    )
    for layer in range(2):
        total = None
        for k in range(n_lanes):
            for part in split2(row_pairs(g, (layer, k), n_tiles * SUB // PIX)):
                term = dot(part, mats[k])
                total = term if total is None else total + term
        pooled[layer] = total

    spot = lane & (HALF - 1)
    for t in range(n_tiles):
        for kind in range(4 + STEPS):
            if kind >= 4 and t in (0, n_tiles - 1):
                continue
            total = jnp.zeros((SUB, LANES), F32)
            for layer in range(2):
                mine = (lane >= HALF * layer) & (lane < HALF * (layer + 1))
                low = turn(load(kind, layer, t, 0), HALF * layer + OUT, 1)
                high = turn(load(kind, layer, t, n_lanes - 1), HALF * layer + SIDE + OUT, 1)
                total = jnp.where(mine & (spot < SIDE), low, total)
                total = jnp.where(mine & (spot >= SIDE), high, total)
            base[kind, pl.ds(t * SUB, SUB), :] = total


def edge_kernel(
    last, pooled_in, base, from_left, from_right, src, place, mats, out_fields, out_slots,
    a, b, c, e, d, g, pooled, merged, sem,
):
    rows, cols = merged.shape[2], merged.shape[3]
    n_tiles = (rows + 2 * PAD) // SUB
    n_lanes = cols // LANES
    lane = lanes()
    spot = lane & (HALF - 1)
    is_left, is_right = spot < OUT, spot >= HALF - OUT

    for buf in (a, b, c):
        clear_rims(buf)
    for t in range(n_tiles):
        at = pl.ds(t * SUB, SUB)
        high, low = from_left[at, :], from_right[at, :]
        for kind, width in enumerate(WIDTHS):
            if kind >= 4 and t in (0, n_tiles - 1):
                continue
            value = jnp.where(is_left, turn(high, OUT - width - FIRST[kind], 1), base[kind, at, :])
            value = jnp.where(is_right, turn(low, HALF - OUT - FIRST[kind], 1), value)
            if kind < 3:
                a[kind, pl.ds(SUB + t * SUB, SUB), :] = value
            elif kind == 3:
                e[at, :] = COURANT * value
            else:
                d[kind - 4, at, :] = value

    before = (lax.axis_index("gy") + lane * 0) > 0
    coef_x = jnp.where(before | (spot >= OUT), COURANT, 0.0).astype(F32)
    yee(
        (a, b, c), [()],
        lambda key, t: e[pl.ds(t * SUB, SUB), :],
        lambda step, key, t: d[step, pl.ds(t * SUB, SUB), :],
        lambda step, key, t: src[step, pl.ds(t * SUB, SUB), :],
        g, coef_x, coef_above(),
        lambda values: {(): turn(values[()], -1, 1)},
        lambda values: {(): turn(values[()], 1, 1)},
        lambda values, key: turn(values[()], HALF, 1),
    )

    for t in range(PAD // SUB, n_tiles - PAD // SUB):
        at, out_at = pl.ds(SUB + t * SUB, SUB), pl.ds(t * SUB - PAD, SUB)
        for kind in range(3):
            edge = c[kind, at, :]
            for layer in range(2):
                for k in range(n_lanes):
                    value = last[kind, layer, k, at, :]
                    if k == 0:
                        value = jnp.where(lane < KEEP, turn(edge, -HALF * layer - OUT, 1), value)
                    if k == n_lanes - 1:
                        value = jnp.where(
                            lane >= LANES - KEEP, turn(edge, -HALF * layer - SIDE - OUT, 1), value
                        )
                    merged[kind, layer, out_at, lane_tile(k)] = value
    copy = pltpu.make_async_copy(merged, out_fields, sem)
    copy.start()

    high, low = split2(row_pairs(g, (), n_tiles * SUB // PIX))
    edge = dot(high, mats[...]) + dot(low, mats[...])
    for layer in range(2):
        pooled[layer, 0] = pooled_in[layer] + edge[:, 2 * layer * LANES : (2 * layer + 1) * LANES]
        pooled[layer, 1] = edge[:, (2 * layer + 1) * LANES : (2 * layer + 2) * LANES]

    weights = cone_weights(RADIUS)
    reach = RADIUS - 1
    out_pix = rows // PIX
    first = PAD // PIX
    lane_wide = lax.broadcasted_iota(jnp.int32, (out_pix, LANES), 1)
    blocks = []
    for layer in range(2):
        sums = []
        for part in range(2):
            at = [pooled[layer, part, pl.ds(first + s, out_pix), :] for s in range(-reach, reach + 1)]
            sums.append([at[reach]] + [at[reach + s] + at[reach - s] for s in range(1, reach + 1)])
        total = None
        for shift in range(reach + 1):
            mixed = []
            for part in range(2):
                value = None
                for s in range(reach + 1):
                    weight = float(weights[reach + s, reach + shift])
                    if weight > 0.0:
                        term = weight * sums[part][s]
                        value = term if value is None else value + term
                mixed.append(value)
            if shift == 0:
                total = mixed[0]
            else:
                total = total + turn(jnp.where(lane_wide < shift, mixed[1], mixed[0]), -shift, 1)
                total = total + turn(
                    jnp.where(lane_wide >= LANES - shift, mixed[1], mixed[0]), shift, 1
                )
        blocks.append(total)

    span = TS // PIX
    tile_rows = out_pix // span
    x = jnp.stack([block.reshape(tile_rows, span, LANES) for block in blocks], axis=1)
    x = x.reshape(tile_rows * 2, span, LANES)
    group = lax.broadcasted_iota(jnp.int32, x.shape, 2) // span
    row = lax.broadcasted_iota(jnp.int32, x.shape, 1)
    for bit in (1, 2, 4):
        row_on, lane_on = (row & bit) != 0, (group & bit) != 0
        ahead = turn(turn(x, -bit, 1), bit * span, 2)
        behind = turn(turn(x, bit, 1), -bit * span, 2)
        x = jnp.where(row_on == lane_on, x, jnp.where(lane_on, ahead, behind))
    x = x.reshape(tile_rows, 2, span, LANES)
    even, odd = x[:, 0], x[:, 1]
    upper = lax.broadcasted_iota(jnp.int32, even.shape, 2) >= HALF
    new_even = jnp.where(upper, turn(odd, HALF, 2), even)
    new_odd = jnp.where(upper, odd, turn(even, HALF, 2))
    vals = jnp.stack([new_even, new_odd], axis=1).reshape(tile_rows * 2 * span, LANES)
    high, low = split2(vals)
    out_slots[...] = dot(place[...], high) + dot(place[...], low)
    copy.wait()


def vmem():
    return pl.BlockSpec(memory_space=pltpu.VMEM)


def shape(*dims, dtype=F32):
    return jax.ShapeDtypeStruct(dims, dtype)


def call(kernel, outs, n_in, *, in_space=pltpu.VMEM, out_specs=None, scratch=(), flops=0, size=0):
    return pl.pallas_call(
        kernel,
        out_shape=outs,
        in_specs=[pl.BlockSpec(memory_space=in_space)] * n_in,
        out_specs=out_specs or tuple(vmem() for _ in outs),
        scratch_shapes=list(scratch),
        compiler_params=pltpu.CompilerParams(vmem_limit_bytes=40 * 1024 * 1024),
        cost_estimate=pl.CostEstimate(flops=flops, bytes_accessed=size, transcendentals=0),
    )


def on_device(adj_fields, inv_eps, fwd_diff, mon_x, mon_y, mon_amp, design_mask, tile_owner):
    rows, cols = adj_fields.shape[2], adj_fields.shape[3]
    assert cols == 2 * LANES and rows % TS == 0
    gx_count, gy_count = lax.axis_size("gx"), lax.axis_size("gy")
    owners = gx_count * gy_count
    tiles = (rows // TS) * (cols // TS)
    width = 2 * (TS // PIX) ** 2
    assert width == LANES
    capacity = max(8, 2 * tiles // owners)
    ext_rows = rows + 2 * PAD
    n_lanes = cols // LANES
    cells = rows * cols
    blocks = (adj_fields, inv_eps, fwd_diff)
    inner_mats, edge_mats = pool_matrices()

    strip = shape(16, SUB, cols)
    cross, near = call(
        rows_kernel, (strip, strip), 3, in_space=pltpu.HBM,
        scratch=(
            pltpu.VMEM((2, 4, 2, PAD, cols), F32),
            pltpu.VMEM((2, STEPS, 2, SUB, cols), F32),
            pltpu.SemaphoreType.DMA((6,)),
        ),
        size=2**20,
    )(*blocks)

    def pairs(start):
        some = [(i, i + 1) for i in range(start, gx_count - 1, 2)]
        return some + [(j, i) for i, j in some]

    cross = lax.ppermute(cross, "gx", pairs(1))
    near = lax.ppermute(near, "gx", pairs(0))

    packed = shape(ext_rows, LANES)
    left, right = call(cols_kernel, (packed, packed), 3, flops=16 * cells, size=64 * cells)(*blocks)

    channels = mon_x.shape[0]
    src, src_edge, place = call(
        lambda *refs: side_kernel(capacity, *refs),
        (
            shape(STEPS, 2, ext_rows, cols),
            shape(STEPS, ext_rows, LANES),
            shape(owners * capacity, tiles, dtype=BF16),
        ),
        5,
        flops=16 * ext_rows * (cols + LANES) * 3 * channels,
        size=32 * cells,
    )(
        mon_x.reshape(1, channels),
        mon_y.reshape(1, channels),
        mon_amp,
        design_mask.reshape(1, tiles),
        tile_owner.reshape(1, tiles),
    )

    left, right = call(corners_kernel, (packed, packed), 4, flops=cells, size=8 * ext_rows * LANES)(
        left, right, cross, near
    )
    up = [(i, i + 1) for i in range(gy_count - 1)]
    from_left = lax.ppermute(right, "gy", up)
    from_right = lax.ppermute(left, "gy", [(j, i) for i, j in up])

    state = (3, 2, n_lanes, ext_rows + 2 * SUB, LANES)
    last, pooled, base = call(
        inner_kernel,
        (shape(*state), shape(2, ext_rows // PIX, LANES), shape(4 + STEPS, ext_rows, LANES)),
        7,
        scratch=(
            pltpu.VMEM(state, F32),
            pltpu.VMEM(state, F32),
            pltpu.VMEM((2, n_lanes, ext_rows, LANES), F32),
            pltpu.VMEM((2, n_lanes, ext_rows, LANES), F32),
        ),
        flops=200 * cells,
        size=96 * cells,
    )(*blocks, cross, near, src, inner_mats)

    edge_state = (3, ext_rows + 2 * SUB, LANES)
    fields, outgoing = call(
        edge_kernel,
        (shape(3, 2, rows, cols), shape(owners * capacity, width)),
        8,
        out_specs=(pl.BlockSpec(memory_space=pl.ANY), vmem()),
        scratch=(
            pltpu.VMEM(edge_state, F32),
            pltpu.VMEM(edge_state, F32),
            pltpu.VMEM(edge_state, F32),
            pltpu.VMEM((ext_rows, LANES), F32),
            pltpu.VMEM((STEPS, ext_rows, LANES), F32),
            pltpu.VMEM((ext_rows, LANES), F32),
            pltpu.VMEM((2, 2, ext_rows // PIX, LANES), F32),
            pltpu.VMEM((3, 2, rows, cols), F32),
            pltpu.SemaphoreType.DMA,
        ),
        flops=100 * cells,
        size=32 * cells,
    )(last, pooled, base, from_left, from_right, src_edge, place, edge_mats)

    outgoing = outgoing.reshape(owners, capacity, width)
    incoming = lax.all_to_all(outgoing, ("gx", "gy"), split_axis=0, concat_axis=0, tiled=True)
    return fields, incoming[None]


def solution(mesh):
    placed = (
        P(None, None, ("parts", "gx"), "gy"),
        P(None, ("parts", "gx"), "gy"),
        P(None, None, ("parts", "gx"), "gy"),
        P("parts"),
        P("parts"),
        P(None, "parts"),
        P(("parts", "gx"), "gy", None),
        P(("parts", "gx"), "gy", None, None),
    )
    return jax.shard_map(
        on_device,
        mesh=mesh,
        in_specs=placed,
        out_specs=(
            P(None, None, ("parts", "gx"), "gy"),
            P(("parts", "gx", "gy"), None, None, None),
        ),
        check_vma=False,
    )
```

profile of v0, /device:TPU:0, one launch (start us, length us, event | category | flops | bytes accessed | tf_op | source)
XLA Modules:
  0.0 39.9 jit_solution(7669676884350639583)
XLA Ops:
  0.6 0.0 copy-start
  0.6 1.2 %copy-done = f32[4,2,128,256]{3,2,1,0:T(8,128)S(1)} copy-done((f32[4,2,128,256]{3,2,1,0:T(8,128)S(1)}, f32[4,2,128,256]{3,2,1,0:T(8,128)}, u32[]{:S(2)}) %copy-start) | copy-done | bytes 1048600
  1.9 0.0 copy-start.2
  1.9 1.1 %copy-done.2 = f32[3,2,128,256]{3,2,1,0:T(8,128)S(1)} copy-done((f32[3,2,128,256]{3,2,1,0:T(8,128)S(1)}, f32[3,2,128,256]{3,2,1,0:T(8,128)}, u32[]{:S(2)}) %copy-start.2) | copy-done | bytes 786456
  3.0 0.0 copy-start.4
  3.0 0.9 %copy-done.4 = f32[2,128,256]{2,1,0:T(8,128)S(1)} copy-done((f32[2,128,256]{2,1,0:T(8,128)S(1)}, f32[2,128,256]{2,1,0:T(8,128)}, u32[]{:S(2)}) %copy-start.4) | copy-done | bytes 262168
  3.9 0.2 shard_map.113
  4.1 0.0 copy-start.8
  4.2 0.0 copy-start.9
  4.2 0.0 copy-start.10
  4.2 0.0 copy-start.11
  4.2 0.0 copy-start.12
  4.2 0.8 %collective-permute-start = (f32[16,8,256]{2,1,0:T(8,128)S(1)}, f32[16,8,256]{2,1,0:T(8,128)S(1)}, u32[]{:S(2)}, u32[]{:S(2)}) collective-permute-start(f32[16,8,256]{2,1,0:T(8,128)S(1)} %get-tuple-element.16), channel_id=1, source_target_pairs={{4,8},{8,4},{5,9},{9,5},{6,10},{10,6},{7,11},{11,7},{20,24},{24,20... | collective-permute-start | bytes 393224 | tf_op jit(solution)/shard_map/ppermute | solution.py:526
  5.0 0.0 copy-start.1
  5.0 0.0 copy-start.3
  5.0 0.0 copy-start.5
  5.0 0.0 copy-start.7
  5.1 4.4 %collective-permute-start.1 = (f32[16,8,256]{2,1,0:T(8,128)S(1)}, f32[16,8,256]{2,1,0:T(8,128)S(1)}, u32[]{:S(2)}, u32[]{:S(2)}) collective-permute-start(f32[16,8,256]{2,1,0:T(8,128)S(1)} %get-tuple-element.17), channel_id=1, source_target_pairs={{0,4},{8,12},{4,0},{12,8},{1,5},{9,13},{5,1},{13,9},{2,6},{10,14},... | collective-permute-start | bytes 393224 | tf_op jit(solution)/shard_map/ppermute | solution.py:527
  9.4 0.8 %shard_map.116 = (f32[160,128]{1,0:T(8,128)S(1)}, f32[160,128]{1,0:T(8,128)S(1)}) custom-call(f32[3,2,128,256]{3,2,1,0:T(8,128)S(1)} %copy-done.2, f32[2,128,256]{2,1,0:T(8,128)S(1)} %copy-done.4, f32[4,2,128,256]{3,2,1,0:T(8,128)S(1)} %copy-done), custom_call_target="tpu_custom_call" | custom-call | flops 524288 | bytes 2097152 | tf_op jit(solution)/shard_map/pallas_call | solution.py:530
  10.2 0.0 collective-permute-done.cross
  10.2 0.2 collective-permute-done.1.near
  10.4 0.2 shard_map.117
  10.6 3.5 %collective-permute-start.2 = (f32[160,128]{1,0:T(8,128)S(1)}, f32[160,128]{1,0:T(8,128)S(1)}, u32[]{:S(2)}, u32[]{:S(2)}) collective-permute-start(f32[160,128]{1,0:T(8,128)S(1)} %get-tuple-element.24), channel_id=1, source_target_pairs={{0,1},{1,2},{2,3},{4,5},{5,6},{6,7},{8,9},{9,10},{10,11},{12,13},{... | collective-permute-start | bytes 245768 | tf_op jit(solution)/shard_map/ppermute | solution.py:555
  14.1 1.3 %collective-permute-start.3 = (f32[160,128]{1,0:T(8,128)S(1)}, f32[160,128]{1,0:T(8,128)S(1)}, u32[]{:S(2)}, u32[]{:S(2)}) collective-permute-start(f32[160,128]{1,0:T(8,128)S(1)} %get-tuple-element.25), channel_id=1, source_target_pairs={{1,0},{2,1},{3,2},{5,4},{6,5},{7,6},{9,8},{10,9},{11,10},{13,12},{... | collective-permute-start | bytes 245768 | tf_op jit(solution)/shard_map/ppermute | solution.py:556
  15.4 0.0 copy-done.8
  15.4 0.0 copy-done.9
  15.4 0.0 copy-done.10
  15.4 0.0 copy-done.11
  15.4 0.0 copy-done.12
  15.4 0.6 %shard_map.114 = (f32[4,2,160,256]{3,2,1,0:T(8,128)S(1)}, f32[4,160,128]{2,1,0:T(8,128)S(1)}, bf16[256,128]{1,0:T(8,128)(2,1)S(1)}) custom-call(s32[1,64]{1,0:T(1,128)S(1)} %bitcast.7, s32[1,64]{1,0:T(1,128)S(1)} %bitcast.8, f32[4,64]{1,0:T(4,128)S(1)} %copy-done.8, s32[1,128]{1,0:T(1,128)S(1)} %bitcast.9, s32[1,128]{1,0:T(1,128)S(1)} %bitcast.10), custom_call_target="tpu_custom_call" | custom-call | flops 188743680 | bytes 1048576 | tf_op jit(solution)/shard_map/pallas_call | solution.py:533
  16.1 0.0 copy-done.1
  16.1 0.0 copy-done.3
  16.1 0.0 copy-done.5
  16.1 0.0 copy-done.7
  16.1 0.0 copy-start.6
  16.1 4.7 %shard_map.115 = (f32[3,2,2,176,128]{4,3,2,1,0:T(8,128)S(1)}, f32[2,80,128]{2,1,0:T(8,128)S(1)}, f32[8,160,128]{2,1,0:T(8,128)S(1)}) custom-call(f32[3,2,128,256]{3,2,1,0:T(8,128)S(1)} %copy-done.3, f32[2,128,256]{2,1,0:T(8,128)S(1)} %copy-done.5, f32[4,2,128,256]{3,2,1,0:T(8,128)S(1)} %copy-done.1, f32[16,8,256]{2,1,0:T(8,128)S(1)} %collective-permute-done.cross, ...), custom_call_target="tpu_custom_call" | custom-call | flops 6553600 | bytes 3145728 | tf_op jit(solution)/shard_map/pallas_call | solution.py:559
  20.9 0.0 collective-permute-done.2.from_left
  20.9 0.1 collective-permute-done.3.from_right
  21.0 0.0 copy-done.6
  21.0 2.6 %shard_map.118 = (f32[3,2,128,256]{3,2,1,0:T(8,128)}, f32[256,128]{1,0:T(8,128)S(1)}) custom-call(f32[3,2,2,176,128]{4,3,2,1,0:T(8,128)S(1)} %get-tuple-element.19.last, f32[2,80,128]{2,1,0:T(8,128)S(1)} %get-tuple-element.20.pooled_in, f32[8,160,128]{2,1,0:T(8,128)S(1)} %get-tuple-element.21.base, f32[160,128]{1,0:T(8,128)S(1)} %collective-permute-done.2.from_left, ...), custom_call_target="tpu_custom_call" | custom-call | flops 3276800 | bytes 1048576 | tf_op jit(solution)/shard_map/pallas_call | solution.py:574
  23.6 15.7 %all_to_all.5 = f32[16,16,128]{2,1,0:T(8,128)S(1)} all-to-all(f32[16,16,128]{2,1,0:T(8,128)S(1)} %bitcast.6), channel_id=1, replica_groups=mesh['parts'=2,'gx'=4,'gy'=4] {'gx','gy'}, dimensions={0} | all-to-all | bytes 262144 | tf_op jit(solution)/shard_map/all_to_all | solution.py:595
  39.3 0.7 %copy.13 = f32[1,16,16,128]{3,2,1,0:T(8,128)} copy(f32[1,16,16,128]{3,2,1,0:T(8,128)S(1)} %bitcast.11) | data formatting | bytes 262144
Async XLA Ops:
  0.6 1.2 %copy-start = (f32[4,2,128,256]{3,2,1,0:T(8,128)S(1)}, f32[4,2,128,256]{3,2,1,0:T(8,128)}, u32[]{:S(2)}) copy-start(f32[4,2,128,256]{3,2,1,0:T(8,128)} %fwd.5) | copy-start | bytes 3145732
  1.9 1.1 %copy-start.2 = (f32[3,2,128,256]{3,2,1,0:T(8,128)S(1)}, f32[3,2,128,256]{3,2,1,0:T(8,128)}, u32[]{:S(2)}) copy-start(f32[3,2,128,256]{3,2,1,0:T(8,128)} %fields.5) | copy-start | bytes 2359300
  3.0 0.9 %copy-start.4 = (f32[2,128,256]{2,1,0:T(8,128)S(1)}, f32[2,128,256]{2,1,0:T(8,128)}, u32[]{:S(2)}) copy-start(f32[2,128,256]{2,1,0:T(8,128)} %eps.5) | copy-start | bytes 786436
  4.1 11.2 %copy-start.8 = (f32[4,64]{1,0:T(4,128)S(1)}, f32[4,64]{1,0:T(4,128)}, u32[]{:S(2)}) copy-start(f32[4,64]{1,0:T(4,128)} %refs_2_.1) | copy-start | bytes 3076
  4.2 11.2 %copy-start.9 = (s32[64]{0:T(128)S(1)}, s32[64]{0:T(128)}, u32[]{:S(2)}) copy-start(s32[64]{0:T(128)} %param.13) | copy-start | bytes 772
  4.2 11.2 %copy-start.10 = (s32[64]{0:T(128)S(1)}, s32[64]{0:T(128)}, u32[]{:S(2)}) copy-start(s32[64]{0:T(128)} %param.14) | copy-start | bytes 772
  4.2 11.2 %copy-start.11 = (s32[1,1,128]{2,1,0:T(1,128)S(1)}, s32[1,1,128]{2,1,0:T(1,128)}, u32[]{:S(2)}) copy-start(s32[1,1,128]{2,1,0:T(1,128)} %param.16) | copy-start | bytes 1540
  4.2 11.2 %copy-start.12 = (s32[1,1,128,1]{2,3,1,0:T(1,128)S(1)}, s32[1,1,128,1]{2,3,1,0:T(1,128)}, u32[]{:S(2)}) copy-start(s32[1,1,128,1]{2,3,1,0:T(1,128)} %param.17) | copy-start | bytes 1540
  4.2 6.0 %collective-permute-start = (f32[16,8,256]{2,1,0:T(8,128)S(1)}, f32[16,8,256]{2,1,0:T(8,128)S(1)}, u32[]{:S(2)}, u32[]{:S(2)}) collective-permute-start(f32[16,8,256]{2,1,0:T(8,128)S(1)} %get-tuple-element.16), channel_id=1, source_target_pairs={{4,8},{8,4},{5,9},{9,5},{6,10},{10,6},{7,11},{11,7},{20,24},{24,20... | collective-permute-start | bytes 393224 | tf_op jit(solution)/shard_map/ppermute | solution.py:526
  5.0 11.1 %copy-start.1 = (f32[4,2,128,256]{3,2,1,0:T(8,128)S(1)}, f32[4,2,128,256]{3,2,1,0:T(8,128)}, u32[]{:S(2)}) copy-start(f32[4,2,128,256]{3,2,1,0:T(8,128)} %fwd.5) | copy-start | bytes 3145732
  5.0 11.1 %copy-start.3 = (f32[3,2,128,256]{3,2,1,0:T(8,128)S(1)}, f32[3,2,128,256]{3,2,1,0:T(8,128)}, u32[]{:S(2)}) copy-start(f32[3,2,128,256]{3,2,1,0:T(8,128)} %fields.5) | copy-start | bytes 2359300
  5.0 11.1 %copy-start.5 = (f32[2,128,256]{2,1,0:T(8,128)S(1)}, f32[2,128,256]{2,1,0:T(8,128)}, u32[]{:S(2)}) copy-start(f32[2,128,256]{2,1,0:T(8,128)} %eps.5) | copy-start | bytes 786436
  5.0 11.1 %copy-start.7 = (bf16[2,128,128]{2,1,0:T(8,128)(2,1)S(1)}, bf16[2,128,128]{2,1,0:T(8,128)(2,1)}, u32[]{:S(2)}) copy-start(bf16[2,128,128]{2,1,0:T(8,128)(2,1)} %constant.4.clone.mats) | copy-start | bytes 196612
  5.1 5.3 %collective-permute-start.1 = (f32[16,8,256]{2,1,0:T(8,128)S(1)}, f32[16,8,256]{2,1,0:T(8,128)S(1)}, u32[]{:S(2)}, u32[]{:S(2)}) collective-permute-start(f32[16,8,256]{2,1,0:T(8,128)S(1)} %get-tuple-element.17), channel_id=1, source_target_pairs={{0,4},{8,12},{4,0},{12,8},{1,5},{9,13},{5,1},{13,9},{2,6},{10,14},... | collective-permute-start | bytes 393224 | tf_op jit(solution)/shard_map/ppermute | solution.py:527
  10.6 10.3 %collective-permute-start.2 = (f32[160,128]{1,0:T(8,128)S(1)}, f32[160,128]{1,0:T(8,128)S(1)}, u32[]{:S(2)}, u32[]{:S(2)}) collective-permute-start(f32[160,128]{1,0:T(8,128)S(1)} %get-tuple-element.24), channel_id=1, source_target_pairs={{0,1},{1,2},{2,3},{4,5},{5,6},{6,7},{8,9},{9,10},{10,11},{12,13},{... | collective-permute-start | bytes 245768 | tf_op jit(solution)/shard_map/ppermute | solution.py:555
  14.1 6.9 %collective-permute-start.3 = (f32[160,128]{1,0:T(8,128)S(1)}, f32[160,128]{1,0:T(8,128)S(1)}, u32[]{:S(2)}, u32[]{:S(2)}) collective-permute-start(f32[160,128]{1,0:T(8,128)S(1)} %get-tuple-element.25), channel_id=1, source_target_pairs={{1,0},{2,1},{3,2},{5,4},{6,5},{7,6},{9,8},{10,9},{11,10},{13,12},{... | collective-permute-start | bytes 245768 | tf_op jit(solution)/shard_map/ppermute | solution.py:556
  16.1 4.9 %copy-start.6 = (bf16[128,512]{1,0:T(8,128)(2,1)S(1)}, bf16[128,512]{1,0:T(8,128)(2,1)}, u32[]{:S(2)}) copy-start(bf16[128,512]{1,0:T(8,128)(2,1)} %constant.5.clone.mats) | copy-start | bytes 393220
where the time goes:
time: 40.2 us; the launch traced here: 39.9 us
  blocking collectives  15.7 us (39%)
  starting transfers between devices  9.94 us (25%)
  Pallas kernels  9.08 us (23%)
  local copies, waits for them, and re-layouts  4.02 us (10%)
  between operations  0.86 us (2%)
    all_to_all x1, blocking collectives, on_device(): lax.all_to_all(outgoing, ('gx', 'gy'), split_axis=0, concat_axis=0, tiled...  15.7 us
    pallas_call x1, Pallas kernels, on_device(): call(inner_kernel, (shape(*state), shape(2, ext_rows // PIX, LANES), shap...  4.73 us
    ppermute x1, starting transfers between devices, on_device(): near = lax.ppermute(near, 'gx', pairs(0))  4.36 us
    unnamed x27, local copies, waits for them, and re-layouts  4.02 us
    ppermute x1, starting transfers between devices, on_device(): from_left = lax.ppermute(right, 'gy', up)  3.48 us
    pallas_call x1, Pallas kernels, on_device(): call(edge_kernel, (shape(3, 2, rows, cols), shape(owners * capacity, widt...  2.56 us
    ppermute x1, starting transfers between devices, on_device(): from_right = lax.ppermute(left, 'gy', [(j, i) for i, j in up])  1.29 us
  transfers between devices with their start and end apart: 4, of which 2 were waited for; matrix products, arithmetic and copies ran while one was open for 0% of the time, Pallas kernels for 15%

commit v1 on v0

--- a/solution.py
+++ b/solution.py
@@ -89,8 +89,8 @@
     return pl.ds(k * LANES, LANES)
 
 
-def is_odd():
-    return ((subs() * 0 + lax.axis_index("gx")) & 1) == 1
+def is_odd(axis):
+    return ((subs() * 0 + lax.axis_index(axis)) & 1) == 1
 
 
 def rows_kernel(fields, eps, fwd, cross, near, hold, hold_fwd, sems):
@@ -109,7 +109,7 @@
         copy.start()
     for copy in copies:
         copy.wait()
-    odd, sub = is_odd(), subs()
+    odd, sub = is_odd("gx"), subs()
     for kind in range(4):
         for layer in range(2):
             plane = 2 * kind + layer
@@ -161,38 +161,70 @@
     return total
 
 
-def cols_kernel(fields, eps, fwd, left, right):
+def edge_tile(load, kind, lane, n_lanes):
+    spot = lane & (HALF - 1)
+    total = None
+    for layer in range(2):
+        low = turn(load(kind, layer, 0), HALF * layer + OUT, 1)
+        high = turn(load(kind, layer, n_lanes - 1), HALF * layer + SIDE + OUT, 1)
+        value = jnp.where(spot < SIDE, low, high)
+        total = value if total is None else jnp.where(lane < HALF, total, value)
+    return total
+
+
+def cols_kernel(fields, eps, fwd, cross, near, base):
     rows, cols = fields.shape[2], fields.shape[3]
-    lane = lanes()
+    n_lanes = cols // LANES
+    lane, odd = lanes(), is_odd("gy")
 
     def tile(t, carry):
         at = pl.ds(pl.multiple_of(t * SUB, SUB), SUB)
         out_at = pl.ds(pl.multiple_of(t * SUB + PAD, SUB), SUB)
-        for out, lo, is_right in ((left, 0, False), (right, cols - LANES, True)):
-            out[out_at, :] = pack_tile(
-                lambda kind, layer: core_tile(fields, eps, fwd, at, kind, layer, pl.ds(lo, LANES)),
+
+        def load(kind, layer, k):
+            return core_tile(fields, eps, fwd, at, kind, layer, lane_tile(k))
+
+        left = pack_tile(lambda kind, layer: load(kind, layer, 0), lane, False)
+        right = pack_tile(lambda kind, layer: load(kind, layer, n_lanes - 1), lane, True)
+        cross[out_at, :] = jnp.where(odd, right, left)
+        near[out_at, :] = jnp.where(odd, left, right)
+        for kind in range(4 + STEPS):
+            base[kind, out_at, :] = edge_tile(load, kind, lane, n_lanes)
+        return carry
+
+    lax.fori_loop(0, rows // SUB, tile, 0, unroll=4)
+    zero = jnp.zeros((PAD, LANES), F32)
+    for out in (cross, near) + tuple(base.at[kind] for kind in range(4 + STEPS)):
+        out[pl.ds(0, PAD), :] = zero
+        out[pl.ds(PAD + rows, PAD), :] = zero
+
+
+def corners_kernel(cross_in, near_in, cross_rows, near_rows, cross, near):
+    rows, cols = cross.shape[0] - 2 * PAD, cross_rows.shape[2]
+    lane, odd, odd_col = lanes(), is_odd("gx"), is_odd("gy")
+    core = pl.ds(PAD, rows)
+    cross[core, :] = cross_in[core, :]
+    near[core, :] = near_in[core, :]
+    for tile in range(4):
+        at = pl.ds(tile * SUB if tile < 2 else PAD + rows + (tile - 2) * SUB, SUB)
+        left, right = (
+            pack_tile(
+                lambda kind, layer: halo_tile(
+                    cross_rows, near_rows, odd, tile, kind, layer, pl.ds(lo, LANES)
+                ),
                 lane, is_right,
             )
-        return carry
-
-    lax.fori_loop(0, rows // SUB, tile, 0, unroll=4)
-    zero = jnp.zeros((PAD, LANES), F32)
-    for out in (left, right):
-        out[pl.ds(0, PAD), :] = zero
-        out[pl.ds(PAD + rows, PAD), :] = zero
-
-
-def corners_kernel(left_in, right_in, cross, near, left, right):
-    rows, cols = left.shape[0] - 2 * PAD, cross.shape[2]
-    lane, odd = lanes(), is_odd()
-    for out, core, lo, is_right in ((left, left_in, 0, False), (right, right_in, cols - LANES, True)):
-        out[pl.ds(PAD, rows), :] = core[pl.ds(PAD, rows), :]
-        for tile in range(4):
-            base = tile * SUB if tile < 2 else PAD + rows + (tile - 2) * SUB
-            out[pl.ds(base, SUB), :] = pack_tile(
-                lambda kind, layer: halo_tile(cross, near, odd, tile, kind, layer, pl.ds(lo, LANES)),
-                lane, is_right,
-            )
+            for lo, is_right in ((0, False), (cols - LANES, True))
+        )
+        cross[at, :] = jnp.where(odd_col, right, left)
+        near[at, :] = jnp.where(odd_col, left, right)
+
+
+def prep_kernel(
+    capacity, fields, eps, fwd, mon_x, mon_y, amp, mask, owner, cross, near, base, src, src_edge, place
+):
+    cols_kernel(fields, eps, fwd, cross, near, base)
+    side_kernel(capacity, mon_x, mon_y, amp, mask, owner, src, src_edge, place)
 
 
 def side_kernel(capacity, mon_x, mon_y, amp, mask, owner, src, src_edge, place):
@@ -289,11 +321,11 @@
     return even + ref[lead + (pl.ds(1, count, stride=PIX), slice(None))]
 
 
-def inner_kernel(fields, eps, fwd, cross, near, src, mats, last, pooled, base, a, b, e, g):
+def inner_kernel(fields, eps, fwd, cross, near, src, mats, base_in, last, pooled, base, a, b, e, g):
     rows, cols = fields.shape[2], fields.shape[3]
     n_tiles = (rows + 2 * PAD) // SUB
     n_lanes = cols // LANES
-    lane, odd = lanes(), is_odd()
+    lane, odd = lanes(), is_odd("gx")
     halo_of = {0: 0, 1: 1, n_tiles - 2: 2, n_tiles - 1: 3}
 
     def load(kind, layer, t, k):
@@ -341,29 +373,25 @@
                 total = term if total is None else total + term
         pooled[layer] = total
 
-    spot = lane & (HALF - 1)
     for t in range(n_tiles):
         for kind in range(4 + STEPS):
-            if kind >= 4 and t in (0, n_tiles - 1):
-                continue
-            total = jnp.zeros((SUB, LANES), F32)
-            for layer in range(2):
-                mine = (lane >= HALF * layer) & (lane < HALF * (layer + 1))
-                low = turn(load(kind, layer, t, 0), HALF * layer + OUT, 1)
-                high = turn(load(kind, layer, t, n_lanes - 1), HALF * layer + SIDE + OUT, 1)
-                total = jnp.where(mine & (spot < SIDE), low, total)
-                total = jnp.where(mine & (spot >= SIDE), high, total)
-            base[kind, pl.ds(t * SUB, SUB), :] = total
+            at = pl.ds(t * SUB, SUB)
+            if t not in halo_of:
+                base[kind, at, :] = base_in[kind, at, :]
+            elif kind < 4 or t not in (0, n_tiles - 1):
+                base[kind, at, :] = edge_tile(
+                    lambda kind, layer, k: load(kind, layer, t, k), kind, lane, n_lanes
+                )
 
 
 def edge_kernel(
-    last, pooled_in, base, from_left, from_right, src, place, mats, out_fields, out_slots,
+    last, pooled_in, base, cross, near, src, place, mats, out_fields, out_slots,
     a, b, c, e, d, g, pooled, merged, sem,
 ):
     rows, cols = merged.shape[2], merged.shape[3]
     n_tiles = (rows + 2 * PAD) // SUB
     n_lanes = cols // LANES
-    lane = lanes()
+    lane, odd = lanes(), is_odd("gy")
     spot = lane & (HALF - 1)
     is_left, is_right = spot < OUT, spot >= HALF - OUT
 
@@ -371,7 +399,8 @@
         clear_rims(buf)
     for t in range(n_tiles):
         at = pl.ds(t * SUB, SUB)
-        high, low = from_left[at, :], from_right[at, :]
+        far, close = cross[at, :], near[at, :]
+        high, low = jnp.where(odd, close, far), jnp.where(odd, far, close)
         for kind, width in enumerate(WIDTHS):
             if kind >= 4 and t in (0, n_tiles - 1):
                 continue
@@ -517,49 +546,49 @@
             pltpu.SemaphoreType.DMA((6,)),
         ),
         size=2**20,
-    )(*blocks)
-
-    def pairs(start):
-        some = [(i, i + 1) for i in range(start, gx_count - 1, 2)]
+    )(*(pltpu.with_memory_space_constraint(block, pltpu.HBM) for block in blocks))
+
+    def pairs(count, start):
+        some = [(i, i + 1) for i in range(start, count - 1, 2)]
         return some + [(j, i) for i, j in some]
 
-    cross = lax.ppermute(cross, "gx", pairs(1))
-    near = lax.ppermute(near, "gx", pairs(0))
+    cross = lax.ppermute(cross, "gx", pairs(gx_count, 1))
+    near = lax.ppermute(near, "gx", pairs(gx_count, 0))
 
     packed = shape(ext_rows, LANES)
-    left, right = call(cols_kernel, (packed, packed), 3, flops=16 * cells, size=64 * cells)(*blocks)
-
     channels = mon_x.shape[0]
-    src, src_edge, place = call(
-        lambda *refs: side_kernel(capacity, *refs),
+    cross_cols, near_cols, base, src, src_edge, place = call(
+        lambda *refs: prep_kernel(capacity, *refs),
         (
+            packed,
+            packed,
+            shape(4 + STEPS, ext_rows, LANES),
             shape(STEPS, 2, ext_rows, cols),
             shape(STEPS, ext_rows, LANES),
             shape(owners * capacity, tiles, dtype=BF16),
         ),
-        5,
+        8,
         flops=16 * ext_rows * (cols + LANES) * 3 * channels,
-        size=32 * cells,
+        size=64 * cells,
     )(
+        *blocks,
         mon_x.reshape(1, channels),
         mon_y.reshape(1, channels),
         mon_amp,
         design_mask.reshape(1, tiles),
         tile_owner.reshape(1, tiles),
     )
-
-    left, right = call(corners_kernel, (packed, packed), 4, flops=cells, size=8 * ext_rows * LANES)(
-        left, right, cross, near
-    )
-    up = [(i, i + 1) for i in range(gy_count - 1)]
-    from_left = lax.ppermute(right, "gy", up)
-    from_right = lax.ppermute(left, "gy", [(j, i) for i, j in up])
+    cross_cols, near_cols = call(
+        corners_kernel, (packed, packed), 4, flops=cells, size=8 * ext_rows * LANES
+    )(cross_cols, near_cols, cross, near)
+    cross_cols = lax.ppermute(cross_cols, "gy", pairs(gy_count, 1))
+    near_cols = lax.ppermute(near_cols, "gy", pairs(gy_count, 0))
 
     state = (3, 2, n_lanes, ext_rows + 2 * SUB, LANES)
     last, pooled, base = call(
         inner_kernel,
         (shape(*state), shape(2, ext_rows // PIX, LANES), shape(4 + STEPS, ext_rows, LANES)),
-        7,
+        8,
         scratch=(
             pltpu.VMEM(state, F32),
             pltpu.VMEM(state, F32),
@@ -568,7 +597,7 @@
         ),
         flops=200 * cells,
         size=96 * cells,
-    )(*blocks, cross, near, src, inner_mats)
+    )(*blocks, cross, near, src, inner_mats, base)
 
     edge_state = (3, ext_rows + 2 * SUB, LANES)
     fields, outgoing = call(
@@ -589,7 +618,7 @@
         ),
         flops=100 * cells,
         size=32 * cells,
-    )(last, pooled, base, from_left, from_right, src_edge, place, edge_mats)
+    )(last, pooled, base, cross_cols, near_cols, src_edge, place, edge_mats)
 
     outgoing = outgoing.reshape(owners, capacity, width)
     incoming = lax.all_to_all(outgoing, ("gx", "gy"), split_axis=0, concat_axis=0, tiled=True)

time: 40.2 us -> 32.3 us (0.80)
  blocking collectives: 15.7 us -> 11.7 us
  local copies, waits for them, and re-layouts: 4.02 us -> 0.7 us
  Pallas kernels: 9.08 us -> 8.45 us
    all_to_all x1, blocking collectives: 15.7 us -> 11.7 us  [on_device(): lax.all_to_all(outgoing, ('gx', 'gy'), split_axis=0, concat_axis=0, tiled...]
    unnamed x27 -> x21, local copies, waits for them, and re-layouts: 4.02 us -> 0.7 us
    pallas_call x1, Pallas kernels: 4.73 us -> 2.51 us  [on_device(): call(inner_kernel, (shape(*state), shape(2, ext_rows // PIX, LANES), shap...]
    pallas_call x1, Pallas kernels: 0.19 us -> 1.21 us  [on_device(): call(rows_kernel, (strip, strip), 3, in_space=pltpu.HBM, scratch=(pltpu.V...]
    pallas_call x2 -> x1, Pallas kernels: 1.43 us -> 1.98 us  [on_device(): call(lambda *refs: prep_kernel(capacity, *refs), (packed, packed, shape(4...]
  transfers between devices with their start and end apart: 4 -> 4, of which waited for: 2 -> 1; matrix products, arithmetic and copies ran while one was open for 0% -> 0% of each run, Pallas kernels for 15% -> 14%
where the time goes in v1:
time: 32.3 us; the launch traced here: 32.1 us
  blocking collectives  11.7 us (36%)
  starting transfers between devices  10.2 us (32%)
  Pallas kernels  8.45 us (26%)
  between operations  0.81 us (3%)
  local copies, waits for them, and re-layouts  0.7 us (2%)
    all_to_all x1, blocking collectives, on_device(): lax.all_to_all(outgoing, ('gx', 'gy'), split_axis=0, concat_axis=0, tiled...  11.7 us
    ppermute x1, starting transfers between devices, on_device(): near_cols = lax.ppermute(near_cols, 'gy', pairs(gy_count, 0))  4.46 us
    ppermute x1, starting transfers between devices, on_device(): near = lax.ppermute(near, 'gx', pairs(gx_count, 0))  4.36 us
    pallas_call x1, Pallas kernels, on_device(): call(edge_kernel, (shape(3, 2, rows, cols), shape(owners * capacity, widt...  2.57 us
    pallas_call x1, Pallas kernels, on_device(): call(inner_kernel, (shape(*state), shape(2, ext_rows // PIX, LANES), shap...  2.51 us
    pallas_call x1, Pallas kernels, on_device(): call(lambda *refs: prep_kernel(capacity, *refs), (packed, packed, shape(4...  1.98 us
    pallas_call x1, Pallas kernels, on_device(): call(rows_kernel, (strip, strip), 3, in_space=pltpu.HBM, scratch=(pltpu.V...  1.21 us
    unnamed x21, local copies, waits for them, and re-layouts  0.7 us
  transfers between devices with their start and end apart: 4, of which 1 were waited for; matrix products, arithmetic and copies ran while one was open for 0% of the time, Pallas kernels for 14%

profile of v1, /device:TPU:0, one launch (start us, length us, event | category | flops | bytes accessed | tf_op | source)
XLA Modules:
  0.0 32.1 jit_solution(8925105111731775772)
XLA Ops:
  0.6 0.0 copy-start
  0.6 0.0 copy-start.2
  0.7 0.0 copy-start.1
  0.7 0.0 copy-start.9
  0.7 0.0 copy-start.8
  0.7 0.0 copy-start.5
  0.7 0.0 copy-start.7
  0.7 0.0 copy-start.6
  0.7 1.2 %shard_map.113 = (f32[16,8,256]{2,1,0:T(8,128)S(1)}, f32[16,8,256]{2,1,0:T(8,128)S(1)}) custom-call(f32[3,2,128,256]{3,2,1,0:T(8,128)} %fields.3, f32[2,128,256]{2,1,0:T(8,128)} %eps.3, f32[4,2,128,256]{3,2,1,0:T(8,128)} %fwd.3), custom_call_target="tpu_custom_call" | custom-call | bytes 1048576 | tf_op jit(solution)/shard_map/pallas_call | solution.py:541
  1.9 0.0 copy-start.4
  1.9 0.7 %collective-permute-start = (f32[16,8,256]{2,1,0:T(8,128)S(1)}, f32[16,8,256]{2,1,0:T(8,128)S(1)}, u32[]{:S(2)}, u32[]{:S(2)}) collective-permute-start(f32[16,8,256]{2,1,0:T(8,128)S(1)} %get-tuple-element.17), channel_id=1, source_target_pairs={{4,8},{8,4},{5,9},{9,5},{6,10},{10,6},{7,11},{11,7},{20,24},{24,20... | collective-permute-start | bytes 393224 | tf_op jit(solution)/shard_map/ppermute | solution.py:555
  2.6 4.4 %collective-permute-start.1 = (f32[16,8,256]{2,1,0:T(8,128)S(1)}, f32[16,8,256]{2,1,0:T(8,128)S(1)}, u32[]{:S(2)}, u32[]{:S(2)}) collective-permute-start(f32[16,8,256]{2,1,0:T(8,128)S(1)} %get-tuple-element.18), channel_id=1, source_target_pairs={{0,4},{8,12},{4,0},{12,8},{1,5},{9,13},{5,1},{13,9},{2,6},{10,14},... | collective-permute-start | bytes 393224 | tf_op jit(solution)/shard_map/ppermute | solution.py:556
  7.0 0.0 copy-done
  7.0 0.0 copy-done.2
  7.0 0.0 copy-done.1
  7.0 0.0 copy-done.9
  7.0 0.0 copy-done.8
  7.0 0.0 copy-done.5
  7.0 0.0 copy-done.7
  7.0 0.0 copy-done.6
  7.0 2.0 %shard_map.114 = (f32[160,128]{1,0:T(8,128)S(1)}, f32[160,128]{1,0:T(8,128)S(1)}, f32[8,160,128]{2,1,0:T(8,128)S(1)}, f32[4,2,160,256]{3,2,1,0:T(8,128)S(1)}, f3...) custom-call(f32[3,2,128,256]{3,2,1,0:T(8,128)S(1)} %copy-done.1, f32[2,128,256]{2,1,0:T(8,128)S(1)} %copy-done.2, ...), custom_call_target="tpu_custom_call" | custom-call | flops 188743680 | bytes 2097152 | tf_op jit(solution)/shard_map/pallas_call | solution.py:560
  9.0 0.0 collective-permute-done.cross.cross_rows
  9.0 0.0 collective-permute-done.1.near.near_rows
  9.0 0.2 shard_map.116
  9.2 0.7 %collective-permute-start.2 = (f32[160,128]{1,0:T(8,128)S(1)}, f32[160,128]{1,0:T(8,128)S(1)}, u32[]{:S(2)}, u32[]{:S(2)}) collective-permute-start(f32[160,128]{1,0:T(8,128)S(1)} %get-tuple-element.26), channel_id=1, source_target_pairs={{1,2},{2,1},{5,6},{6,5},{9,10},{10,9},{13,14},{14,13},{17,18},{18,... | collective-permute-start | bytes 245768 | tf_op jit(solution)/shard_map/ppermute | solution.py:584
  9.9 4.5 %collective-permute-start.3 = (f32[160,128]{1,0:T(8,128)S(1)}, f32[160,128]{1,0:T(8,128)S(1)}, u32[]{:S(2)}, u32[]{:S(2)}) collective-permute-start(f32[160,128]{1,0:T(8,128)S(1)} %get-tuple-element.27), channel_id=1, source_target_pairs={{0,1},{2,3},{1,0},{3,2},{4,5},{6,7},{5,4},{7,6},{8,9},{10,11},{9,8... | collective-permute-start | bytes 245768 | tf_op jit(solution)/shard_map/ppermute | solution.py:585
  14.3 0.0 copy-done.4
  14.3 0.0 copy-start.3
  14.3 2.5 %shard_map.115 = (f32[3,2,2,176,128]{4,3,2,1,0:T(8,128)S(1)}, f32[2,80,128]{2,1,0:T(8,128)S(1)}, f32[8,160,128]{2,1,0:T(8,128)S(1)}) custom-call(f32[3,2,128,256]{3,2,1,0:T(8,128)S(1)} %copy-done.1, f32[2,128,256]{2,1,0:T(8,128)S(1)} %copy-done.2, f32[4,2,128,256]{3,2,1,0:T(8,128)S(1)} %copy-done, f32[16,8,256]{2,1,0:T(8,128)S(1)} %collective-permute-done.cross.cross_rows, ...), custom_call_target="tpu_custom_call" | custom-call | flops 6553600 | bytes 3145728 | tf_op jit(solution)/shard_map/pallas_call | solution.py:588
  16.9 0.0 collective-permute-done.2.cross
  16.9 0.3 collective-permute-done.3.near
  17.2 0.0 copy-done.3
  17.2 2.6 %shard_map.117 = (f32[3,2,128,256]{3,2,1,0:T(8,128)}, f32[256,128]{1,0:T(8,128)S(1)}) custom-call(f32[3,2,2,176,128]{4,3,2,1,0:T(8,128)S(1)} %get-tuple-element.21.last, f32[2,80,128]{2,1,0:T(8,128)S(1)} %get-tuple-element.22.pooled_in, f32[8,160,128]{2,1,0:T(8,128)S(1)} %get-tuple-element.23.base, f32[160,128]{1,0:T(8,128)S(1)} %collective-permute-done.2.cross, ...), custom_call_target="tpu_custom_call" | custom-call | flops 3276800 | bytes 1048576 | tf_op jit(solution)/shard_map/pallas_call | solution.py:603
  19.8 11.7 %all_to_all.5 = f32[16,16,128]{2,1,0:T(8,128)S(1)} all-to-all(f32[16,16,128]{2,1,0:T(8,128)S(1)} %bitcast.6), channel_id=1, replica_groups=mesh['parts'=2,'gx'=4,'gy'=4] {'gx','gy'}, dimensions={0} | all-to-all | bytes 262144 | tf_op jit(solution)/shard_map/all_to_all | solution.py:624
  31.5 0.7 %copy.13 = f32[1,16,16,128]{3,2,1,0:T(8,128)} copy(f32[1,16,16,128]{3,2,1,0:T(8,128)S(1)} %bitcast.11) | data formatting | bytes 262144
Async XLA Ops:
  0.6 6.4 %copy-start = (f32[4,2,128,256]{3,2,1,0:T(8,128)S(1)}, f32[4,2,128,256]{3,2,1,0:T(8,128)}, u32[]{:S(2)}) copy-start(f32[4,2,128,256]{3,2,1,0:T(8,128)} %fwd.3) | copy-start | bytes 3145732
  0.6 6.3 %copy-start.2 = (f32[2,128,256]{2,1,0:T(8,128)S(1)}, f32[2,128,256]{2,1,0:T(8,128)}, u32[]{:S(2)}) copy-start(f32[2,128,256]{2,1,0:T(8,128)} %eps.3) | copy-start | bytes 786436
  0.7 6.3 %copy-start.1 = (f32[3,2,128,256]{3,2,1,0:T(8,128)S(1)}, f32[3,2,128,256]{3,2,1,0:T(8,128)}, u32[]{:S(2)}) copy-start(f32[3,2,128,256]{3,2,1,0:T(8,128)} %fields.3) | copy-start | bytes 2359300
  0.7 6.3 %copy-start.9 = (s32[1,1,128,1]{2,3,1,0:T(1,128)S(1)}, s32[1,1,128,1]{2,3,1,0:T(1,128)}, u32[]{:S(2)}) copy-start(s32[1,1,128,1]{2,3,1,0:T(1,128)} %param.17) | copy-start | bytes 1540
  0.7 6.3 %copy-start.8 = (s32[1,1,128]{2,1,0:T(1,128)S(1)}, s32[1,1,128]{2,1,0:T(1,128)}, u32[]{:S(2)}) copy-start(s32[1,1,128]{2,1,0:T(1,128)} %param.16) | copy-start | bytes 1540
  0.7 6.3 %copy-start.5 = (f32[4,64]{1,0:T(4,128)S(1)}, f32[4,64]{1,0:T(4,128)}, u32[]{:S(2)}) copy-start(f32[4,64]{1,0:T(4,128)} %refs_5_.1) | copy-start | bytes 3076
  0.7 6.3 %copy-start.7 = (s32[64]{0:T(128)S(1)}, s32[64]{0:T(128)}, u32[]{:S(2)}) copy-start(s32[64]{0:T(128)} %param.14) | copy-start | bytes 772
  0.7 6.3 %copy-start.6 = (s32[64]{0:T(128)S(1)}, s32[64]{0:T(128)}, u32[]{:S(2)}) copy-start(s32[64]{0:T(128)} %param.13) | copy-start | bytes 772
  1.9 12.4 %copy-start.4 = (bf16[2,128,128]{2,1,0:T(8,128)(2,1)S(1)}, bf16[2,128,128]{2,1,0:T(8,128)(2,1)}, u32[]{:S(2)}) copy-start(bf16[2,128,128]{2,1,0:T(8,128)(2,1)} %constant.4.clone.mats) | copy-start | bytes 196612
  1.9 7.1 %collective-permute-start = (f32[16,8,256]{2,1,0:T(8,128)S(1)}, f32[16,8,256]{2,1,0:T(8,128)S(1)}, u32[]{:S(2)}, u32[]{:S(2)}) collective-permute-start(f32[16,8,256]{2,1,0:T(8,128)S(1)} %get-tuple-element.17), channel_id=1, source_target_pairs={{4,8},{8,4},{5,9},{9,5},{6,10},{10,6},{7,11},{11,7},{20,24},{24,20... | collective-permute-start | bytes 393224 | tf_op jit(solution)/shard_map/ppermute | solution.py:555
  2.6 6.4 %collective-permute-start.1 = (f32[16,8,256]{2,1,0:T(8,128)S(1)}, f32[16,8,256]{2,1,0:T(8,128)S(1)}, u32[]{:S(2)}, u32[]{:S(2)}) collective-permute-start(f32[16,8,256]{2,1,0:T(8,128)S(1)} %get-tuple-element.18), channel_id=1, source_target_pairs={{0,4},{8,12},{4,0},{12,8},{1,5},{9,13},{5,1},{13,9},{2,6},{10,14},... | collective-permute-start | bytes 393224 | tf_op jit(solution)/shard_map/ppermute | solution.py:556
  9.2 7.7 %collective-permute-start.2 = (f32[160,128]{1,0:T(8,128)S(1)}, f32[160,128]{1,0:T(8,128)S(1)}, u32[]{:S(2)}, u32[]{:S(2)}) collective-permute-start(f32[160,128]{1,0:T(8,128)S(1)} %get-tuple-element.26), channel_id=1, source_target_pairs={{1,2},{2,1},{5,6},{6,5},{9,10},{10,9},{13,14},{14,13},{17,18},{18,... | collective-permute-start | bytes 245768 | tf_op jit(solution)/shard_map/ppermute | solution.py:584
  9.9 7.3 %collective-permute-start.3 = (f32[160,128]{1,0:T(8,128)S(1)}, f32[160,128]{1,0:T(8,128)S(1)}, u32[]{:S(2)}, u32[]{:S(2)}) collective-permute-start(f32[160,128]{1,0:T(8,128)S(1)} %get-tuple-element.27), channel_id=1, source_target_pairs={{0,1},{2,3},{1,0},{3,2},{4,5},{6,7},{5,4},{7,6},{8,9},{10,11},{9,8... | collective-permute-start | bytes 245768 | tf_op jit(solution)/shard_map/ppermute | solution.py:585
  14.3 2.8 %copy-start.3 = (bf16[128,512]{1,0:T(8,128)(2,1)S(1)}, bf16[128,512]{1,0:T(8,128)(2,1)}, u32[]{:S(2)}) copy-start(bf16[128,512]{1,0:T(8,128)(2,1)} %constant.5.clone.mats) | copy-start | bytes 393220

commit v2 on v1

--- a/solution.py
+++ b/solution.py
@@ -41,19 +41,29 @@
 
 def pool_matrices():
     inner = np.zeros((2, LANES, LANES), np.float32)
-    for j in range(2 * LANES):
-        if KEEP <= j < 2 * LANES - KEEP:
-            inner[j // LANES, j % LANES, j // PIX] = 1.0
-    edge = np.zeros((LANES, 4 * LANES), np.float32)
+    for j in range(KEEP, 2 * LANES - KEEP):
+        inner[j // LANES, j % LANES, j // PIX] = 1.0
+    return inner.astype(ml_dtypes.bfloat16)
+
+
+def edge_matrices():
+    weights = cone_weights(RADIUS)
+    reach = RADIUS - 1
+    result = np.zeros((RADIUS, LANES, 2, LANES), np.float32)
     for lane in range(LANES):
         layer, at = lane // HALF, lane % HALF
         col = at - OUT if at < SIDE else at - SIDE + 2 * LANES - OUT
-        pixel = col // PIX
-        if 0 <= col < KEEP or 2 * LANES - KEEP <= col < 2 * LANES:
-            edge[lane, 2 * layer * LANES + pixel] = 1.0
-        elif -NEAR <= col < 0 or 2 * LANES <= col < 2 * LANES + NEAR:
-            edge[lane, (2 * layer + 1) * LANES + pixel % LANES] = 1.0
-    return inner.astype(ml_dtypes.bfloat16), edge.astype(ml_dtypes.bfloat16)
+        if not (-NEAR <= col < KEEP or 2 * LANES - KEEP <= col < 2 * LANES + NEAR):
+            continue
+        for row in range(RADIUS):
+            for shift in range(-reach, reach + 1):
+                pixel = col // PIX + shift
+                if 0 <= pixel < LANES:
+                    result[row, lane, layer, pixel] = weights[reach + row, reach + shift]
+    result = result.reshape(RADIUS * LANES, 2 * LANES)
+    high = result.astype(ml_dtypes.bfloat16)
+    low = (result - high.astype(np.float32)).astype(ml_dtypes.bfloat16)
+    return high, low
 
 
 def split2(value):
@@ -321,7 +331,7 @@
     return even + ref[lead + (pl.ds(1, count, stride=PIX), slice(None))]
 
 
-def inner_kernel(fields, eps, fwd, cross, near, src, mats, base_in, last, pooled, base, a, b, e, g):
+def inner_kernel(fields, eps, fwd, cross, near, src, mats, base_in, last, filtered, base, a, b, e, g, pooled):
     rows, cols = fields.shape[2], fields.shape[3]
     n_tiles = (rows + 2 * PAD) // SUB
     n_lanes = cols // LANES
@@ -373,6 +383,9 @@
                 total = term if total is None else total + term
         pooled[layer] = total
 
+    for layer in range(2):
+        filtered[layer] = cone_filter(pooled.at[layer], rows // PIX, PAD // PIX)
+
     for t in range(n_tiles):
         for kind in range(4 + STEPS):
             at = pl.ds(t * SUB, SUB)
@@ -384,13 +397,34 @@
                 )
 
 
+def cone_filter(pooled, out_pix, first):
+    weights = cone_weights(RADIUS)
+    reach = RADIUS - 1
+    lane = lax.broadcasted_iota(jnp.int32, (out_pix, LANES), 1)
+    at = [pooled[pl.ds(first + s, out_pix), :] for s in range(-reach, reach + 1)]
+    sums = [at[reach]] + [at[reach + s] + at[reach - s] for s in range(1, reach + 1)]
+    total = None
+    for shift in range(reach + 1):
+        mixed = None
+        for s in range(reach + 1):
+            weight = float(weights[reach + s, reach + shift])
+            if weight > 0.0:
+                term = weight * sums[s]
+                mixed = term if mixed is None else mixed + term
+        if shift == 0:
+            total = mixed
+        else:
+            total = total + turn(jnp.where(lane < shift, 0.0, mixed), -shift, 1)
+            total = total + turn(jnp.where(lane >= LANES - shift, 0.0, mixed), shift, 1)
+    return total
+
+
 def edge_kernel(
-    last, pooled_in, base, cross, near, src, place, mats, out_fields, out_slots,
-    a, b, c, e, d, g, pooled, merged, sem,
+    filtered, base, cross, near, src, place, high_mat, low_mat, c, out_slots, a, b, e, d, g, pooled
 ):
-    rows, cols = merged.shape[2], merged.shape[3]
-    n_tiles = (rows + 2 * PAD) // SUB
-    n_lanes = cols // LANES
+    ext_rows = base.shape[1]
+    rows = ext_rows - 2 * PAD
+    n_tiles = ext_rows // SUB
     lane, odd = lanes(), is_odd("gy")
     spot = lane & (HALF - 1)
     is_left, is_right = spot < OUT, spot >= HALF - OUT
@@ -426,59 +460,15 @@
         lambda values, key: turn(values[()], HALF, 1),
     )
 
-    for t in range(PAD // SUB, n_tiles - PAD // SUB):
-        at, out_at = pl.ds(SUB + t * SUB, SUB), pl.ds(t * SUB - PAD, SUB)
-        for kind in range(3):
-            edge = c[kind, at, :]
-            for layer in range(2):
-                for k in range(n_lanes):
-                    value = last[kind, layer, k, at, :]
-                    if k == 0:
-                        value = jnp.where(lane < KEEP, turn(edge, -HALF * layer - OUT, 1), value)
-                    if k == n_lanes - 1:
-                        value = jnp.where(
-                            lane >= LANES - KEEP, turn(edge, -HALF * layer - SIDE - OUT, 1), value
-                        )
-                    merged[kind, layer, out_at, lane_tile(k)] = value
-    copy = pltpu.make_async_copy(merged, out_fields, sem)
-    copy.start()
-
-    high, low = split2(row_pairs(g, (), n_tiles * SUB // PIX))
-    edge = dot(high, mats[...]) + dot(low, mats[...])
-    for layer in range(2):
-        pooled[layer, 0] = pooled_in[layer] + edge[:, 2 * layer * LANES : (2 * layer + 1) * LANES]
-        pooled[layer, 1] = edge[:, (2 * layer + 1) * LANES : (2 * layer + 2) * LANES]
-
-    weights = cone_weights(RADIUS)
+    pooled[...] = row_pairs(g, (), ext_rows // PIX)
     reach = RADIUS - 1
     out_pix = rows // PIX
     first = PAD // PIX
-    lane_wide = lax.broadcasted_iota(jnp.int32, (out_pix, LANES), 1)
-    blocks = []
-    for layer in range(2):
-        sums = []
-        for part in range(2):
-            at = [pooled[layer, part, pl.ds(first + s, out_pix), :] for s in range(-reach, reach + 1)]
-            sums.append([at[reach]] + [at[reach + s] + at[reach - s] for s in range(1, reach + 1)])
-        total = None
-        for shift in range(reach + 1):
-            mixed = []
-            for part in range(2):
-                value = None
-                for s in range(reach + 1):
-                    weight = float(weights[reach + s, reach + shift])
-                    if weight > 0.0:
-                        term = weight * sums[part][s]
-                        value = term if value is None else value + term
-                mixed.append(value)
-            if shift == 0:
-                total = mixed[0]
-            else:
-                total = total + turn(jnp.where(lane_wide < shift, mixed[1], mixed[0]), -shift, 1)
-                total = total + turn(
-                    jnp.where(lane_wide >= LANES - shift, mixed[1], mixed[0]), shift, 1
-                )
-        blocks.append(total)
+    at = [pooled[pl.ds(first + s, out_pix), :] for s in range(-reach, reach + 1)]
+    sums = [at[reach]] + [at[reach + s] + at[reach - s] for s in range(1, reach + 1)]
+    high, low = split2(jnp.concatenate(sums, axis=1))
+    edge = dot(high, high_mat[...]) + (dot(low, high_mat[...]) + dot(high, low_mat[...]))
+    blocks = [filtered[l] + edge[:, l * LANES : (l + 1) * LANES] for l in range(2)]
 
     span = TS // PIX
     tile_rows = out_pix // span
@@ -499,6 +489,28 @@
     vals = jnp.stack([new_even, new_odd], axis=1).reshape(tile_rows * 2 * span, LANES)
     high, low = split2(vals)
     out_slots[...] = dot(place[...], high) + dot(place[...], low)
+
+
+def merge_kernel(last, edge_last, out_fields, merged, sem):
+    rows, cols = merged.shape[2], merged.shape[3]
+    n_lanes = cols // LANES
+    lane = lanes()
+    for t in range(rows // SUB):
+        at, out_at = pl.ds(SUB + PAD + t * SUB, SUB), pl.ds(t * SUB, SUB)
+        for kind in range(3):
+            edge = edge_last[kind, at, :]
+            for layer in range(2):
+                for k in range(n_lanes):
+                    value = last[kind, layer, k, at, :]
+                    if k == 0:
+                        value = jnp.where(lane < KEEP, turn(edge, -HALF * layer - OUT, 1), value)
+                    if k == n_lanes - 1:
+                        value = jnp.where(
+                            lane >= LANES - KEEP, turn(edge, -HALF * layer - SIDE - OUT, 1), value
+                        )
+                    merged[kind, layer, out_at, lane_tile(k)] = value
+    copy = pltpu.make_async_copy(merged, out_fields, sem)
+    copy.start()
     copy.wait()
 
 
@@ -535,7 +547,7 @@
     n_lanes = cols // LANES
     cells = rows * cols
     blocks = (adj_fields, inv_eps, fwd_diff)
-    inner_mats, edge_mats = pool_matrices()
+
 
     strip = shape(16, SUB, cols)
     cross, near = call(
@@ -585,40 +597,46 @@
     near_cols = lax.ppermute(near_cols, "gy", pairs(gy_count, 0))
 
     state = (3, 2, n_lanes, ext_rows + 2 * SUB, LANES)
-    last, pooled, base = call(
+    last, filtered, base = call(
         inner_kernel,
-        (shape(*state), shape(2, ext_rows // PIX, LANES), shape(4 + STEPS, ext_rows, LANES)),
+        (shape(*state), shape(2, rows // PIX, LANES), shape(4 + STEPS, ext_rows, LANES)),
         8,
         scratch=(
             pltpu.VMEM(state, F32),
             pltpu.VMEM(state, F32),
             pltpu.VMEM((2, n_lanes, ext_rows, LANES), F32),
             pltpu.VMEM((2, n_lanes, ext_rows, LANES), F32),
+            pltpu.VMEM((2, ext_rows // PIX, LANES), F32),
         ),
         flops=200 * cells,
         size=96 * cells,
-    )(*blocks, cross, near, src, inner_mats, base)
+    )(*blocks, cross, near, src, pool_matrices(), base)
 
     edge_state = (3, ext_rows + 2 * SUB, LANES)
-    fields, outgoing = call(
+    edge_last, outgoing = call(
         edge_kernel,
-        (shape(3, 2, rows, cols), shape(owners * capacity, width)),
+        (shape(*edge_state), shape(owners * capacity, width)),
         8,
-        out_specs=(pl.BlockSpec(memory_space=pl.ANY), vmem()),
         scratch=(
-            pltpu.VMEM(edge_state, F32),
             pltpu.VMEM(edge_state, F32),
             pltpu.VMEM(edge_state, F32),
             pltpu.VMEM((ext_rows, LANES), F32),
             pltpu.VMEM((STEPS, ext_rows, LANES), F32),
             pltpu.VMEM((ext_rows, LANES), F32),
-            pltpu.VMEM((2, 2, ext_rows // PIX, LANES), F32),
-            pltpu.VMEM((3, 2, rows, cols), F32),
-            pltpu.SemaphoreType.DMA,
+            pltpu.VMEM((ext_rows // PIX, LANES), F32),
         ),
         flops=100 * cells,
         size=32 * cells,
-    )(last, pooled, base, cross_cols, near_cols, src_edge, place, edge_mats)
+    )(filtered, base, cross_cols, near_cols, src_edge, place, *edge_matrices())
+    (fields,) = call(
+        merge_kernel,
+        (shape(3, 2, rows, cols),),
+        2,
+        out_specs=(pl.BlockSpec(memory_space=pl.ANY),),
+        scratch=(pltpu.VMEM((3, 2, rows, cols), F32), pltpu.SemaphoreType.DMA),
+        flops=20 * cells,
+        size=48 * cells,
+    )(last, edge_last)
 
     outgoing = outgoing.reshape(owners, capacity, width)
     incoming = lax.all_to_all(outgoing, ("gx", "gy"), split_axis=0, concat_axis=0, tiled=True)

time: 32.3 us -> 32.5 us (level)
  blocking collectives: 11.7 us -> 0 us
  waiting for transfers between devices: 0.32 us -> 6.2 us
  starting transfers between devices: 10.2 us -> 14.5 us
  Pallas kernels: 8.45 us -> 10.1 us
    all_to_all x1 -> x0, blocking collectives: 11.7 us -> none  [on_device(): lax.all_to_all(outgoing, ('gx', 'gy'), split_axis=0, concat_axis=0, tiled...]
    all_to_all x0 -> x1, waiting for transfers between devices: none -> 6.19 us  [on_device(): lax.all_to_all(outgoing, ('gx', 'gy'), split_axis=0, concat_axis=0, tiled...]
    all_to_all x0 -> x1, starting transfers between devices: none -> 4.31 us  [on_device(): lax.all_to_all(outgoing, ('gx', 'gy'), split_axis=0, concat_axis=0, tiled...]
    pallas_call x2 -> x3, Pallas kernels: 5.09 us -> 6.71 us  [the longest x1 3.29 us: on_device(): call(inner_kernel, (shape(*state), shape(2, rows // PIX, LANES), shape(4...]
    unnamed x21 -> x23, local copies, waits for them, and re-layouts: 0.7 us -> 0.7 us
  transfers between devices with their start and end apart: 4 -> 5, of which waited for: 1 -> 1; matrix products, arithmetic and copies ran while one was open for 0% -> 0% of each run, Pallas kernels for 14% -> 20%
where the time goes in v2:
time: 32.5 us; the launch traced here: 32.3 us
  starting transfers between devices  14.5 us (45%)
  Pallas kernels  10.1 us (31%)
  waiting for transfers between devices  6.2 us (19%)
  between operations  0.84 us (3%)
  local copies, waits for them, and re-layouts  0.7 us (2%)
    all_to_all x1, waiting for transfers between devices, on_device(): lax.all_to_all(outgoing, ('gx', 'gy'), split_axis=0, concat_axis=0, tiled...  6.19 us
    ppermute x1, starting transfers between devices, on_device(): near_cols = lax.ppermute(near_cols, 'gy', pairs(gy_count, 0))  4.46 us
    ppermute x1, starting transfers between devices, on_device(): near = lax.ppermute(near, 'gx', pairs(gx_count, 0))  4.36 us
    all_to_all x1, starting transfers between devices, on_device(): lax.all_to_all(outgoing, ('gx', 'gy'), split_axis=0, concat_axis=0, tiled...  4.31 us
    pallas_call x1, Pallas kernels, on_device(): call(inner_kernel, (shape(*state), shape(2, rows // PIX, LANES), shape(4...  3.29 us
    pallas_call x1, Pallas kernels, on_device(): call(edge_kernel, (shape(*edge_state), shape(owners * capacity, width)),...  2.26 us
    pallas_call x1, Pallas kernels, on_device(): call(lambda *refs: prep_kernel(capacity, *refs), (packed, packed, shape(4...  1.98 us
    pallas_call x1, Pallas kernels, on_device(): call(rows_kernel, (strip, strip), 3, in_space=pltpu.HBM, scratch=(pltpu.V...  1.21 us
  transfers between devices with their start and end apart: 5, of which 1 were waited for; matrix products, arithmetic and copies ran while one was open for 0% of the time, Pallas kernels for 20%

profile of v2, /device:TPU:0, one launch (start us, length us, event | category | flops | bytes accessed | tf_op | source)
XLA Modules:
  0.0 32.3 jit_solution(15297655677760029955)
XLA Ops:
  0.6 0.0 copy-start
  0.6 0.0 copy-start.2
  0.7 0.0 copy-start.1
  0.7 0.0 copy-start.10
  0.7 0.0 copy-start.9
  0.7 0.0 copy-start.6
  0.7 0.0 copy-start.8
  0.7 0.0 copy-start.7
  0.7 1.2 %shard_map.122 = (f32[16,8,256]{2,1,0:T(8,128)S(1)}, f32[16,8,256]{2,1,0:T(8,128)S(1)}) custom-call(f32[3,2,128,256]{3,2,1,0:T(8,128)} %fields.3, f32[2,128,256]{2,1,0:T(8,128)} %eps.3, f32[4,2,128,256]{3,2,1,0:T(8,128)} %fwd.3), custom_call_target="tpu_custom_call" | custom-call | bytes 1048576 | tf_op jit(solution)/shard_map/pallas_call | solution.py:553
  1.9 0.0 copy-start.5
  1.9 0.7 %collective-permute-start = (f32[16,8,256]{2,1,0:T(8,128)S(1)}, f32[16,8,256]{2,1,0:T(8,128)S(1)}, u32[]{:S(2)}, u32[]{:S(2)}) collective-permute-start(f32[16,8,256]{2,1,0:T(8,128)S(1)} %get-tuple-element.17), channel_id=1, source_target_pairs={{4,8},{8,4},{5,9},{9,5},{6,10},{10,6},{7,11},{11,7},{20,24},{24,20... | collective-permute-start | bytes 393224 | tf_op jit(solution)/shard_map/ppermute | solution.py:567
  2.6 4.4 %collective-permute-start.1 = (f32[16,8,256]{2,1,0:T(8,128)S(1)}, f32[16,8,256]{2,1,0:T(8,128)S(1)}, u32[]{:S(2)}, u32[]{:S(2)}) collective-permute-start(f32[16,8,256]{2,1,0:T(8,128)S(1)} %get-tuple-element.18), channel_id=1, source_target_pairs={{0,4},{8,12},{4,0},{12,8},{1,5},{9,13},{5,1},{13,9},{2,6},{10,14},... | collective-permute-start | bytes 393224 | tf_op jit(solution)/shard_map/ppermute | solution.py:568
  7.0 0.0 copy-done
  7.0 0.0 copy-done.2
  7.0 0.0 copy-done.1
  7.0 0.0 copy-done.10
  7.0 0.0 copy-done.9
  7.0 0.0 copy-done.6
  7.0 0.0 copy-done.8
  7.0 0.0 copy-done.7
  7.0 2.0 %shard_map.123 = (f32[160,128]{1,0:T(8,128)S(1)}, f32[160,128]{1,0:T(8,128)S(1)}, f32[8,160,128]{2,1,0:T(8,128)S(1)}, f32[4,2,160,256]{3,2,1,0:T(8,128)S(1)}, f3...) custom-call(f32[3,2,128,256]{3,2,1,0:T(8,128)S(1)} %copy-done.1, f32[2,128,256]{2,1,0:T(8,128)S(1)} %copy-done.2, ...), custom_call_target="tpu_custom_call" | custom-call | flops 188743680 | bytes 2097152 | tf_op jit(solution)/shard_map/pallas_call | solution.py:572
  9.0 0.0 collective-permute-done.cross.cross_rows
  9.0 0.0 collective-permute-done.1.near.near_rows
  9.0 0.2 shard_map.125
  9.2 0.7 %collective-permute-start.2 = (f32[160,128]{1,0:T(8,128)S(1)}, f32[160,128]{1,0:T(8,128)S(1)}, u32[]{:S(2)}, u32[]{:S(2)}) collective-permute-start(f32[160,128]{1,0:T(8,128)S(1)} %get-tuple-element.26), channel_id=1, source_target_pairs={{1,2},{2,1},{5,6},{6,5},{9,10},{10,9},{13,14},{14,13},{17,18},{18,... | collective-permute-start | bytes 245768 | tf_op jit(solution)/shard_map/ppermute | solution.py:596
  9.9 4.5 %collective-permute-start.3 = (f32[160,128]{1,0:T(8,128)S(1)}, f32[160,128]{1,0:T(8,128)S(1)}, u32[]{:S(2)}, u32[]{:S(2)}) collective-permute-start(f32[160,128]{1,0:T(8,128)S(1)} %get-tuple-element.27), channel_id=1, source_target_pairs={{0,1},{2,3},{1,0},{3,2},{4,5},{6,7},{5,4},{7,6},{8,9},{10,11},{9,8... | collective-permute-start | bytes 245768 | tf_op jit(solution)/shard_map/ppermute | solution.py:597
  14.3 0.0 copy-done.5
  14.3 0.0 copy-start.3
  14.3 0.0 copy-start.4
  14.4 3.3 %shard_map.124 = (f32[3,2,2,176,128]{4,3,2,1,0:T(8,128)S(1)}, f32[2,64,128]{2,1,0:T(8,128)S(1)}, f32[8,160,128]{2,1,0:T(8,128)S(1)}) custom-call(f32[3,2,128,256]{3,2,1,0:T(8,128)S(1)} %copy-done.1, f32[2,128,256]{2,1,0:T(8,128)S(1)} %copy-done.2, f32[4,2,128,256]{3,2,1,0:T(8,128)S(1)} %copy-done, f32[16,8,256]{2,1,0:T(8,128)S(1)} %collective-permute-done.cross.cross_rows, ...), custom_call_target="tpu_custom_call" | custom-call | flops 6553600 | bytes 3145728 | tf_op jit(solution)/shard_map/pallas_call | solution.py:600
  17.7 0.0 collective-permute-done.2.cross
  17.7 0.0 collective-permute-done.3.near
  17.7 0.0 copy-done.3
  17.7 0.0 copy-done.4
  17.7 2.3 %shard_map.126 = (f32[3,176,128]{2,1,0:T(8,128)S(1)}, f32[256,128]{1,0:T(8,128)}) custom-call(f32[2,64,128]{2,1,0:T(8,128)S(1)} %get-tuple-element.22.filtered, f32[8,160,128]{2,1,0:T(8,128)S(1)} %get-tuple-element.23.base, f32[160,128]{1,0:T(8,128)S(1)} %collective-permute-done.2.cross, f32[160,128]{1,0:T(8,128)S(1)} %collective-permute-done.3.near, ...), custom_call_target="tpu_custom_call" | custom-call | flops 3276800 | bytes 1048576 | tf_op jit(solution)/shard_map/pallas_call | solution.py:616
  20.0 4.3 %all-to-all-start = ((f32[16,16,128]{2,1,0:T(8,128)}), f32[16,16,128]{2,1,0:T(8,128)S(1)}, u32[]{:S(2)}, u32[]{:S(2)}) async-start(f32[16,16,128]{2,1,0:T(8,128)} %bitcast.4), calls=%async_computation | async-start | bytes 262144 | tf_op jit(solution)/shard_map/all_to_all | solution.py:642
  24.3 1.2 %shard_map.127 = f32[3,2,128,256]{3,2,1,0:T(8,128)} custom-call(f32[3,2,2,176,128]{4,3,2,1,0:T(8,128)S(1)} %get-tuple-element.21.last, f32[3,176,128]{2,1,0:T(8,128)S(1)} %get-tuple-element.30.edge_last), custom_call_target="tpu_custom_call" | custom-call | flops 655360 | bytes 1572864 | tf_op jit(solution)/shard_map/pallas_call | solution.py:631
  25.4 6.2 %all-to-all-done = f32[16,16,128]{2,1,0:T(8,128)S(1)} async-done(((f32[16,16,128]{2,1,0:T(8,128)}), f32[16,16,128]{2,1,0:T(8,128)S(1)}, u32[]{:S(2)}, u32[]{:S(2)}) %all-to-all-start) | async-done | bytes 131104 | tf_op jit(solution)/shard_map/all_to_all | solution.py:642
  31.6 0.7 %copy.14 = f32[1,16,16,128]{3,2,1,0:T(8,128)} copy(f32[1,16,16,128]{3,2,1,0:T(8,128)S(1)} %bitcast.10) | data formatting | bytes 262144
Async XLA Ops:
  0.6 6.4 %copy-start = (f32[4,2,128,256]{3,2,1,0:T(8,128)S(1)}, f32[4,2,128,256]{3,2,1,0:T(8,128)}, u32[]{:S(2)}) copy-start(f32[4,2,128,256]{3,2,1,0:T(8,128)} %fwd.3) | copy-start | bytes 3145732
  0.6 6.3 %copy-start.2 = (f32[2,128,256]{2,1,0:T(8,128)S(1)}, f32[2,128,256]{2,1,0:T(8,128)}, u32[]{:S(2)}) copy-start(f32[2,128,256]{2,1,0:T(8,128)} %eps.3) | copy-start | bytes 786436
  0.7 6.3 %copy-start.1 = (f32[3,2,128,256]{3,2,1,0:T(8,128)S(1)}, f32[3,2,128,256]{3,2,1,0:T(8,128)}, u32[]{:S(2)}) copy-start(f32[3,2,128,256]{3,2,1,0:T(8,128)} %fields.3) | copy-start | bytes 2359300
  0.7 6.3 %copy-start.10 = (s32[1,1,128,1]{2,3,1,0:T(1,128)S(1)}, s32[1,1,128,1]{2,3,1,0:T(1,128)}, u32[]{:S(2)}) copy-start(s32[1,1,128,1]{2,3,1,0:T(1,128)} %param.18) | copy-start | bytes 1540
  0.7 6.3 %copy-start.9 = (s32[1,1,128]{2,1,0:T(1,128)S(1)}, s32[1,1,128]{2,1,0:T(1,128)}, u32[]{:S(2)}) copy-start(s32[1,1,128]{2,1,0:T(1,128)} %param.17) | copy-start | bytes 1540
  0.7 6.3 %copy-start.6 = (f32[4,64]{1,0:T(4,128)S(1)}, f32[4,64]{1,0:T(4,128)}, u32[]{:S(2)}) copy-start(f32[4,64]{1,0:T(4,128)} %refs_5_.1) | copy-start | bytes 3076
  0.7 6.3 %copy-start.8 = (s32[64]{0:T(128)S(1)}, s32[64]{0:T(128)}, u32[]{:S(2)}) copy-start(s32[64]{0:T(128)} %param.15) | copy-start | bytes 772
  0.7 6.3 %copy-start.7 = (s32[64]{0:T(128)S(1)}, s32[64]{0:T(128)}, u32[]{:S(2)}) copy-start(s32[64]{0:T(128)} %param.14) | copy-start | bytes 772
  1.9 12.4 %copy-start.5 = (bf16[2,128,128]{2,1,0:T(8,128)(2,1)S(1)}, bf16[2,128,128]{2,1,0:T(8,128)(2,1)}, u32[]{:S(2)}) copy-start(bf16[2,128,128]{2,1,0:T(8,128)(2,1)} %constant.6.clone.mats) | copy-start | bytes 196612
  1.9 7.1 %collective-permute-start = (f32[16,8,256]{2,1,0:T(8,128)S(1)}, f32[16,8,256]{2,1,0:T(8,128)S(1)}, u32[]{:S(2)}, u32[]{:S(2)}) collective-permute-start(f32[16,8,256]{2,1,0:T(8,128)S(1)} %get-tuple-element.17), channel_id=1, source_target_pairs={{4,8},{8,4},{5,9},{9,5},{6,10},{10,6},{7,11},{11,7},{20,24},{24,20... | collective-permute-start | bytes 393224 | tf_op jit(solution)/shard_map/ppermute | solution.py:567
  2.6 6.4 %collective-permute-start.1 = (f32[16,8,256]{2,1,0:T(8,128)S(1)}, f32[16,8,256]{2,1,0:T(8,128)S(1)}, u32[]{:S(2)}, u32[]{:S(2)}) collective-permute-start(f32[16,8,256]{2,1,0:T(8,128)S(1)} %get-tuple-element.18), channel_id=1, source_target_pairs={{0,4},{8,12},{4,0},{12,8},{1,5},{9,13},{5,1},{13,9},{2,6},{10,14},... | collective-permute-start | bytes 393224 | tf_op jit(solution)/shard_map/ppermute | solution.py:568
  9.2 8.4 %collective-permute-start.2 = (f32[160,128]{1,0:T(8,128)S(1)}, f32[160,128]{1,0:T(8,128)S(1)}, u32[]{:S(2)}, u32[]{:S(2)}) collective-permute-start(f32[160,128]{1,0:T(8,128)S(1)} %get-tuple-element.26), channel_id=1, source_target_pairs={{1,2},{2,1},{5,6},{6,5},{9,10},{10,9},{13,14},{14,13},{17,18},{18,... | collective-permute-start | bytes 245768 | tf_op jit(solution)/shard_map/ppermute | solution.py:596
  9.9 7.8 %collective-permute-start.3 = (f32[160,128]{1,0:T(8,128)S(1)}, f32[160,128]{1,0:T(8,128)S(1)}, u32[]{:S(2)}, u32[]{:S(2)}) collective-permute-start(f32[160,128]{1,0:T(8,128)S(1)} %get-tuple-element.27), channel_id=1, source_target_pairs={{0,1},{2,3},{1,0},{3,2},{4,5},{6,7},{5,4},{7,6},{8,9},{10,11},{9,8... | collective-permute-start | bytes 245768 | tf_op jit(solution)/shard_map/ppermute | solution.py:597
  14.3 3.3 %copy-start.3 = (bf16[512,256]{1,0:T(8,128)(2,1)S(1)}, bf16[512,256]{1,0:T(8,128)(2,1)}, u32[]{:S(2)}) copy-start(bf16[512,256]{1,0:T(8,128)(2,1)} %constant.8.clone.low_mat) | copy-start | bytes 786436
  14.3 3.3 %copy-start.4 = (bf16[512,256]{1,0:T(8,128)(2,1)S(1)}, bf16[512,256]{1,0:T(8,128)(2,1)}, u32[]{:S(2)}) copy-start(bf16[512,256]{1,0:T(8,128)(2,1)} %constant.7.clone.high_mat) | copy-start | bytes 786436
  20.0 11.7 %all-to-all-start = ((f32[16,16,128]{2,1,0:T(8,128)}), f32[16,16,128]{2,1,0:T(8,128)S(1)}, u32[]{:S(2)}, u32[]{:S(2)}) async-start(f32[16,16,128]{2,1,0:T(8,128)} %bitcast.4), calls=%async_computation | async-start | bytes 262144 | tf_op jit(solution)/shard_map/all_to_all | solution.py:642

commit v3 on v2

--- a/solution.py
+++ b/solution.py
@@ -46,24 +46,17 @@
     return inner.astype(ml_dtypes.bfloat16)
 
 
-def edge_matrices():
-    weights = cone_weights(RADIUS)
-    reach = RADIUS - 1
-    result = np.zeros((RADIUS, LANES, 2, LANES), np.float32)
-    for lane in range(LANES):
-        layer, at = lane // HALF, lane % HALF
-        col = at - OUT if at < SIDE else at - SIDE + 2 * LANES - OUT
-        if not (-NEAR <= col < KEEP or 2 * LANES - KEEP <= col < 2 * LANES + NEAR):
-            continue
-        for row in range(RADIUS):
-            for shift in range(-reach, reach + 1):
-                pixel = col // PIX + shift
-                if 0 <= pixel < LANES:
-                    result[row, lane, layer, pixel] = weights[reach + row, reach + shift]
-    result = result.reshape(RADIUS * LANES, 2 * LANES)
-    high = result.astype(ml_dtypes.bfloat16)
-    low = (result - high.astype(np.float32)).astype(ml_dtypes.bfloat16)
-    return high, low
+def spread_matrix():
+    span = TS // PIX
+    result = np.zeros((2, LANES, 2, 2, span, span), np.float32)
+    for e in range(span):
+        move = (e % 2) + SIDE * (e % 4 // 2)
+        for layer in range(2):
+            for side in range(2):
+                for f in range(span):
+                    lane = (HALF * layer + OUT + OUT * side + PIX * f + move) % LANES
+                    result[e // 4, lane, side, layer, e, f] = 1.0
+    return result.reshape(2 * LANES, 2 * LANES).astype(ml_dtypes.bfloat16)
 
 
 def split2(value):
@@ -97,6 +90,14 @@
 
 def lane_tile(k):
     return pl.ds(k * LANES, LANES)
+
+
+def spread_rows(ext_rows):
+    return (ext_rows // SUB) | 1
+
+
+def nth(r, n):
+    return pl.ds(r, SUB, stride=n)
 
 
 def is_odd(axis):
@@ -234,12 +235,12 @@
     capacity, fields, eps, fwd, mon_x, mon_y, amp, mask, owner, cross, near, base, src, src_edge, place
 ):
     cols_kernel(fields, eps, fwd, cross, near, base)
-    side_kernel(capacity, mon_x, mon_y, amp, mask, owner, src, src_edge, place)
-
-
-def side_kernel(capacity, mon_x, mon_y, amp, mask, owner, src, src_edge, place):
-    _, _, ext_rows, cols = src.shape
-    rows = ext_rows - 2 * PAD
+    side_kernel(capacity, fields.shape[2], mon_x, mon_y, amp, mask, owner, src, src_edge, place)
+
+
+def side_kernel(capacity, rows, mon_x, mon_y, amp, mask, owner, src, src_edge, place):
+    _, _, long_rows, cols = src.shape
+    n = long_rows // SUB
     channels = mon_x.shape[1]
     row = mon_x[...] - lax.axis_index("gx") * rows + PAD
     col = mon_y[...] - lax.axis_index("gy") * cols
@@ -255,7 +256,8 @@
     one_e = jnp.where(one_e, 1.0, 0.0).astype(BF16)
     one_y = jnp.concatenate([one_y] * 3, axis=1)
     one_e = jnp.concatenate([one_e] * 3, axis=1)
-    one_x = lax.broadcasted_iota(jnp.int32, (ext_rows, channels), 0) == row
+    place_of = lax.broadcasted_iota(jnp.int32, (long_rows, channels), 0)
+    one_x = (place_of >> 3) + n * (place_of & (SUB - 1)) == row
     one_x = jnp.where(one_x, 1.0, 0.0).astype(F32)
     nt = (((1,), (1,)), ((), ()))
     for step in range(STEPS):
@@ -280,50 +282,50 @@
     place[...] = jnp.where(hit, 1.0, 0.0).astype(BF16)
 
 
-def yee(bufs, keys, eps_of, change_of, src_of, grad, coef_x, coef_first, next_col, prev_col, other):
-    n_tiles = (bufs[0].shape[-2] - 2 * SUB) // SUB
+def yee(n, keys, start, state, eps_of, src_of, keep, finish, coef_x, next_col, prev_col, other):
+    coef_first = jnp.where(subs() == 0, coef_above(), COURANT)
+
+    def coef_y(r):
+        return coef_first if r < PAD else COURANT
+
     for step in range(STEPS):
-        old, new = ((0, 1), (1, 0), (0, 1), (1, 2))[step]
-        old, new = bufs[old], bufs[new]
-        low = 0 if step < 2 else 1
-        high = n_tiles if step == 0 else n_tiles - 1
-        for t in range(low, high):
-            at = pl.ds(SUB + t * SUB, SUB)
-            under = pl.ds(SUB + t * SUB + 1, SUB)
-            over = pl.ds(SUB + t * SUB - 1, SUB)
-            coef_y = coef_first if t < PAD // SUB else COURANT
-            e = {key: old[(0,) + key + (at, slice(None))] for key in keys}
+
+        def load(kind, key, r):
+            if step == 0:
+                return start(kind, key, r)
+            return state[(kind,) + key + (pl.ds(r * SUB, SUB), slice(None))]
+
+        e = {key: load(0, key, 0) for key in keys}
+        e_wrap = {key: turn(e[key], -1, 0) for key in keys}
+        hy_end = {
+            key: load(2, key, n - 1) - coef_y(n - 1) * (e_wrap[key] - load(0, key, n - 1))
+            for key in keys
+        }
+        hy_above = {key: turn(hy_end[key], 1, 0) for key in keys}
+        for r in range(n):
+            e_below = {key: load(0, key, r + 1) for key in keys} if r < n - 1 else e_wrap
             e_right = next_col(e)
-            hx, hy = {}, {}
-            for key in keys:
-                hx[key] = old[(1,) + key + (at, slice(None))] + coef_x * (e_right[key] - e[key])
-                below = old[(0,) + key + (under, slice(None))]
-                hy[key] = old[(2,) + key + (at, slice(None))] - coef_y * (below - e[key])
-                new[(1,) + key + (at, slice(None))] = hx[key]
-                new[(2,) + key + (at, slice(None))] = hy[key]
+            hx = {key: load(1, key, r) + coef_x * (e_right[key] - e[key]) for key in keys}
+            if r < n - 1:
+                hy = {key: load(2, key, r) - coef_y(r) * (e_below[key] - e[key]) for key in keys}
+            else:
+                hy = hy_end
             hx_left = prev_col(hx)
             for key in keys:
-                hy_above = new[(2,) + key + (over, slice(None))]
-                curl = (hy[key] - hy_above) - (hx[key] - hx_left[key])
+                curl = (hy[key] - hy_above[key]) - (hx[key] - hx_left[key])
                 curl = curl + COUPLING * (other(e, key) - e[key])
-                value = e[key] - eps_of(key, t) * curl + src_of(step, key, t)
-                new[(0,) + key + (at, slice(None))] = value
-                if 1 <= t < n_tiles - 1:
-                    change = value * change_of(step, key, t)
-                    where = key + (pl.ds(t * SUB, SUB), slice(None))
-                    grad[where] = -change if step == 0 else grad[where] - change
+                new = e[key] - eps_of(key, r) * curl + src_of(step, key, r)
+                keep(step, key, r, new)
+                for kind, value in enumerate((new, hx[key], hy[key])):
+                    if step < STEPS - 1:
+                        state[(kind,) + key + (pl.ds(r * SUB, SUB), slice(None))] = value
+                    else:
+                        finish(kind, key, r, value)
+            e, hy_above = e_below, hy
 
 
 def coef_above():
     return jnp.where((subs() * 0 + lax.axis_index("gx")) > 0, COURANT, 0.0).astype(F32)
-
-
-def clear_rims(buf):
-    size = buf.shape[-2]
-    zero = jnp.zeros(buf.shape[:-2] + (SUB, LANES), F32)
-    lead = (slice(None),) * (len(buf.shape) - 2)
-    buf[lead + (pl.ds(0, SUB), slice(None))] = zero
-    buf[lead + (pl.ds(size - SUB, SUB), slice(None))] = zero
 
 
 def row_pairs(ref, lead, count):
@@ -331,9 +333,12 @@
     return even + ref[lead + (pl.ds(1, count, stride=PIX), slice(None))]
 
 
-def inner_kernel(fields, eps, fwd, cross, near, src, mats, base_in, last, filtered, base, a, b, e, g, pooled):
+def inner_kernel(
+    fields, eps, fwd, cross, near, src, mats, base_in, last, vals, base, first, state, e, kept, g, pooled
+):
     rows, cols = fields.shape[2], fields.shape[3]
-    n_tiles = (rows + 2 * PAD) // SUB
+    ext_rows = rows + 2 * PAD
+    n_tiles, n = ext_rows // SUB, spread_rows(ext_rows)
     n_lanes = cols // LANES
     lane, odd = lanes(), is_odd("gx")
     halo_of = {0: 0, 1: 1, n_tiles - 2: 2, n_tiles - 1: 3}
@@ -343,14 +348,14 @@
             return halo_tile(cross, near, odd, halo_of[t], kind, layer, lane_tile(k))
         return core_tile(fields, eps, fwd, pl.ds(t * SUB - PAD, SUB), kind, layer, lane_tile(k))
 
-    for buf in (a, b, last):
-        clear_rims(buf)
-    for t in range(n_tiles):
+    zero = jnp.zeros((SUB, LANES), F32)
+    for t in range(n):
+        at = pl.ds(t * SUB, SUB)
         for layer in range(2):
             for k in range(n_lanes):
                 for kind in range(3):
-                    a[kind, layer, k, pl.ds(SUB + t * SUB, SUB), :] = load(kind, layer, t, k)
-                e[layer, k, pl.ds(t * SUB, SUB), :] = COURANT * load(3, layer, t, k)
+                    first[kind, layer, k, at, :] = load(kind, layer, t, k) if t < n_tiles else zero
+                e[layer, k, at, :] = COURANT * load(3, layer, t, k) if t < n_tiles else zero
 
     at_end, at_start = lane == LANES - 1, lane == 0
     keys = [(layer, k) for layer in range(2) for k in range(n_lanes)]
@@ -367,14 +372,30 @@
             (l, k): jnp.where(at_start, moved[l, (k - 1) % n_lanes], moved[l, k]) for l, k in keys
         }
 
+    def start(kind, key, r):
+        return first[(kind,) + key + (nth(r, n), slice(None))]
+
+    def keep(step, key, r, value):
+        kept[(step,) + key + (nth(r, n), slice(None))] = value
+
+    def finish(kind, key, r, value):
+        last[(kind,) + key + (nth(r, n), slice(None))] = value
+
     yee(
-        (a, b, last), keys,
-        lambda key, t: e[key + (pl.ds(t * SUB, SUB), slice(None))],
-        lambda step, key, t: load(4 + step, key[0], t, key[1]),
-        lambda step, key, t: src[step, key[0], pl.ds(t * SUB, SUB), lane_tile(key[1])],
-        g, COURANT, coef_above(), next_col, prev_col,
+        n, keys, start, state,
+        lambda key, r: e[key + (nth(r, n), slice(None))],
+        lambda step, key, r: src[step, key[0], pl.ds(r * SUB, SUB), lane_tile(key[1])],
+        keep, finish, COURANT, next_col, prev_col,
         lambda values, key: values[1 - key[0], key[1]],
     )
+    for t in range(1, n_tiles - 1):
+        at = pl.ds(t * SUB, SUB)
+        for layer, k in keys:
+            total = None
+            for step in range(STEPS):
+                term = kept[step, layer, k, at, :] * load(4 + step, layer, t, k)
+                total = term if total is None else total + term
+            g[layer, k, at, :] = -total
     for layer in range(2):
         total = None
         for k in range(n_lanes):
@@ -383,8 +404,7 @@
                 total = term if total is None else total + term
         pooled[layer] = total
 
-    for layer in range(2):
-        filtered[layer] = cone_filter(pooled.at[layer], rows // PIX, PAD // PIX)
+    vals[...] = by_tile([cone_filter(pooled.at[layer], rows // PIX, PAD // PIX) for layer in range(2)])
 
     for t in range(n_tiles):
         for kind in range(4 + STEPS):
@@ -419,59 +439,9 @@
     return total
 
 
-def edge_kernel(
-    filtered, base, cross, near, src, place, high_mat, low_mat, c, out_slots, a, b, e, d, g, pooled
-):
-    ext_rows = base.shape[1]
-    rows = ext_rows - 2 * PAD
-    n_tiles = ext_rows // SUB
-    lane, odd = lanes(), is_odd("gy")
-    spot = lane & (HALF - 1)
-    is_left, is_right = spot < OUT, spot >= HALF - OUT
-
-    for buf in (a, b, c):
-        clear_rims(buf)
-    for t in range(n_tiles):
-        at = pl.ds(t * SUB, SUB)
-        far, close = cross[at, :], near[at, :]
-        high, low = jnp.where(odd, close, far), jnp.where(odd, far, close)
-        for kind, width in enumerate(WIDTHS):
-            if kind >= 4 and t in (0, n_tiles - 1):
-                continue
-            value = jnp.where(is_left, turn(high, OUT - width - FIRST[kind], 1), base[kind, at, :])
-            value = jnp.where(is_right, turn(low, HALF - OUT - FIRST[kind], 1), value)
-            if kind < 3:
-                a[kind, pl.ds(SUB + t * SUB, SUB), :] = value
-            elif kind == 3:
-                e[at, :] = COURANT * value
-            else:
-                d[kind - 4, at, :] = value
-
-    before = (lax.axis_index("gy") + lane * 0) > 0
-    coef_x = jnp.where(before | (spot >= OUT), COURANT, 0.0).astype(F32)
-    yee(
-        (a, b, c), [()],
-        lambda key, t: e[pl.ds(t * SUB, SUB), :],
-        lambda step, key, t: d[step, pl.ds(t * SUB, SUB), :],
-        lambda step, key, t: src[step, pl.ds(t * SUB, SUB), :],
-        g, coef_x, coef_above(),
-        lambda values: {(): turn(values[()], -1, 1)},
-        lambda values: {(): turn(values[()], 1, 1)},
-        lambda values, key: turn(values[()], HALF, 1),
-    )
-
-    pooled[...] = row_pairs(g, (), ext_rows // PIX)
-    reach = RADIUS - 1
-    out_pix = rows // PIX
-    first = PAD // PIX
-    at = [pooled[pl.ds(first + s, out_pix), :] for s in range(-reach, reach + 1)]
-    sums = [at[reach]] + [at[reach + s] + at[reach - s] for s in range(1, reach + 1)]
-    high, low = split2(jnp.concatenate(sums, axis=1))
-    edge = dot(high, high_mat[...]) + (dot(low, high_mat[...]) + dot(high, low_mat[...]))
-    blocks = [filtered[l] + edge[:, l * LANES : (l + 1) * LANES] for l in range(2)]
-
+def by_tile(blocks):
     span = TS // PIX
-    tile_rows = out_pix // span
+    tile_rows = blocks[0].shape[0] // span
     x = jnp.stack([block.reshape(tile_rows, span, LANES) for block in blocks], axis=1)
     x = x.reshape(tile_rows * 2, span, LANES)
     group = lax.broadcasted_iota(jnp.int32, x.shape, 2) // span
@@ -486,8 +456,106 @@
     upper = lax.broadcasted_iota(jnp.int32, even.shape, 2) >= HALF
     new_even = jnp.where(upper, turn(odd, HALF, 2), even)
     new_odd = jnp.where(upper, odd, turn(even, HALF, 2))
-    vals = jnp.stack([new_even, new_odd], axis=1).reshape(tile_rows * 2 * span, LANES)
-    high, low = split2(vals)
+    return jnp.stack([new_even, new_odd], axis=1).reshape(tile_rows * 2 * span, LANES)
+
+
+def merge_spans(rows_of, lane):
+    even = (lane & 1) == 0
+    window = ((lane - OUT) & (HALF - 1)) < SIDE
+    merged = []
+    for e in (0, 4):
+        low = jnp.where(even, rows_of(e), turn(rows_of(e + 1), 1, 1))
+        high = jnp.where(even, turn(rows_of(e + 2), SIDE, 1), turn(rows_of(e + 3), SIDE + 1, 1))
+        merged.append(jnp.where(window, low, high))
+    return jnp.concatenate(merged, axis=1)
+
+
+def edge_kernel(
+    vals_in, base, cross, near, src, place, spread, last, out_slots,
+    first, state, e, kept, g, pooled, pixels, vals,
+):
+    ext_rows = base.shape[1]
+    rows = ext_rows - 2 * PAD
+    n_tiles, n = ext_rows // SUB, spread_rows(ext_rows)
+    lane, odd = lanes(), is_odd("gy")
+    spot = lane & (HALF - 1)
+    is_left, is_right = spot < OUT, spot >= HALF - OUT
+
+    def load(kind, t):
+        at = pl.ds(t * SUB, SUB)
+        far, close = cross[at, :], near[at, :]
+        high, low = jnp.where(odd, close, far), jnp.where(odd, far, close)
+        value = jnp.where(is_left, turn(high, OUT - WIDTHS[kind] - FIRST[kind], 1), base[kind, at, :])
+        return jnp.where(is_right, turn(low, HALF - OUT - FIRST[kind], 1), value)
+
+    zero = jnp.zeros((SUB, LANES), F32)
+    for t in range(n):
+        at = pl.ds(t * SUB, SUB)
+        for kind in range(3):
+            first[kind, at, :] = load(kind, t) if t < n_tiles else zero
+        e[at, :] = COURANT * load(3, t) if t < n_tiles else zero
+
+    before = (lax.axis_index("gy") + lane * 0) > 0
+    coef_x = jnp.where(before | (spot >= OUT), COURANT, 0.0).astype(F32)
+
+    def keep(step, key, r, value):
+        kept[step, nth(r, n), :] = value
+
+    def finish(kind, key, r, value):
+        last[kind, nth(r, n), :] = value
+
+    yee(
+        n, [()],
+        lambda kind, key, r: first[kind, nth(r, n), :],
+        state,
+        lambda key, r: e[nth(r, n), :],
+        lambda step, key, r: src[step, pl.ds(r * SUB, SUB), :],
+        keep, finish, coef_x,
+        lambda values: {(): turn(values[()], -1, 1)},
+        lambda values: {(): turn(values[()], 1, 1)},
+        lambda values, key: turn(values[()], HALF, 1),
+    )
+
+    inside = (spot >= OUT - NEAR) & (spot < OUT + KEEP)
+    inside = inside | ((spot >= HALF - OUT - KEEP) & (spot < HALF - OUT + NEAR))
+    for t in range(1, n_tiles - 1):
+        at = pl.ds(t * SUB, SUB)
+        total = None
+        for step in range(STEPS):
+            term = kept[step, at, :] * load(4 + step, t)
+            total = term if total is None else total + term
+        g[at, :] = jnp.where(inside, -total, 0.0)
+
+    summed = row_pairs(g, (), ext_rows // PIX)
+    pooled[...] = summed + turn(summed, -1, 1)
+    weights = cone_weights(RADIUS)
+    reach = RADIUS - 1
+    out_pix, top = rows // PIX, PAD // PIX
+    at = [pooled[pl.ds(top + s, out_pix), :] for s in range(-reach, reach + 1)]
+    sums = [at[reach]] + [at[reach + s] + at[reach - s] for s in range(1, reach + 1)]
+    total = None
+    for shift in range(reach + 1):
+        mixed = None
+        for s in range(reach + 1):
+            weight = float(weights[reach + s, reach + shift])
+            if weight > 0.0:
+                term = weight * sums[s]
+                mixed = term if mixed is None else mixed + term
+        if shift:
+            mixed = turn(mixed, -PIX * shift, 1) + turn(mixed, PIX * shift, 1)
+        total = mixed if total is None else total + mixed
+    pixels[...] = total
+
+    span = TS // PIX
+    tile_rows, tile_cols = rows // TS, vals.shape[0] // (rows // TS)
+    merged = merge_spans(lambda row: pixels[pl.ds(row, tile_rows, stride=span), :], lane)
+    high, low = split2(merged)
+    edge = dot(high, spread[...]) + dot(low, spread[...])
+    vals[...] = vals_in[...]
+    for side, row in enumerate((0, tile_cols - 1)):
+        spots = pl.ds(row, tile_rows, stride=tile_cols)
+        vals[spots, :] = vals[spots, :] + edge[:, side * LANES : (side + 1) * LANES]
+    high, low = split2(vals[...])
     out_slots[...] = dot(place[...], high) + dot(place[...], low)
 
 
@@ -496,7 +564,7 @@
     n_lanes = cols // LANES
     lane = lanes()
     for t in range(rows // SUB):
-        at, out_at = pl.ds(SUB + PAD + t * SUB, SUB), pl.ds(t * SUB, SUB)
+        at, out_at = pl.ds(PAD + t * SUB, SUB), pl.ds(t * SUB, SUB)
         for kind in range(3):
             edge = edge_last[kind, at, :]
             for layer in range(2):
@@ -514,6 +582,21 @@
     copy.wait()
 
 
+def deliver_kernel(array, out, sems):
+    parts = sems.shape[0]
+    size = array.shape[0] // parts
+    copies = [
+        pltpu.make_async_copy(
+            array.at[pl.ds(i * size, size)], out.at[0, pl.ds(i * size, size)], sems.at[i]
+        )
+        for i in range(parts)
+    ]
+    for copy in copies:
+        copy.start()
+    for copy in copies:
+        copy.wait()
+
+
 def vmem():
     return pl.BlockSpec(memory_space=pltpu.VMEM)
 
@@ -543,7 +626,9 @@
     width = 2 * (TS // PIX) ** 2
     assert width == LANES
     capacity = max(8, 2 * tiles // owners)
+    assert rows == TS * SUB and cols == 2 * TS * SUB
     ext_rows = rows + 2 * PAD
+    long_rows = SUB * spread_rows(ext_rows)
     n_lanes = cols // LANES
     cells = rows * cols
     blocks = (adj_fields, inv_eps, fwd_diff)
@@ -575,8 +660,8 @@
             packed,
             packed,
             shape(4 + STEPS, ext_rows, LANES),
-            shape(STEPS, 2, ext_rows, cols),
-            shape(STEPS, ext_rows, LANES),
+            shape(STEPS, 2, long_rows, cols),
+            shape(STEPS, long_rows, LANES),
             shape(owners * capacity, tiles, dtype=BF16),
         ),
         8,
@@ -596,15 +681,16 @@
     cross_cols = lax.ppermute(cross_cols, "gy", pairs(gy_count, 1))
     near_cols = lax.ppermute(near_cols, "gy", pairs(gy_count, 0))
 
-    state = (3, 2, n_lanes, ext_rows + 2 * SUB, LANES)
-    last, filtered, base = call(
+    state = (3, 2, n_lanes, long_rows, LANES)
+    last, vals, base = call(
         inner_kernel,
-        (shape(*state), shape(2, rows // PIX, LANES), shape(4 + STEPS, ext_rows, LANES)),
+        (shape(*state), shape(tiles, LANES), shape(4 + STEPS, ext_rows, LANES)),
         8,
         scratch=(
             pltpu.VMEM(state, F32),
             pltpu.VMEM(state, F32),
-            pltpu.VMEM((2, n_lanes, ext_rows, LANES), F32),
+            pltpu.VMEM((2, n_lanes, long_rows, LANES), F32),
+            pltpu.VMEM((STEPS, 2, n_lanes, long_rows, LANES), F32),
             pltpu.VMEM((2, n_lanes, ext_rows, LANES), F32),
             pltpu.VMEM((2, ext_rows // PIX, LANES), F32),
         ),
@@ -612,22 +698,24 @@
         size=96 * cells,
     )(*blocks, cross, near, src, pool_matrices(), base)
 
-    edge_state = (3, ext_rows + 2 * SUB, LANES)
+    edge_state = (3, long_rows, LANES)
     edge_last, outgoing = call(
         edge_kernel,
         (shape(*edge_state), shape(owners * capacity, width)),
-        8,
+        7,
         scratch=(
             pltpu.VMEM(edge_state, F32),
             pltpu.VMEM(edge_state, F32),
-            pltpu.VMEM((ext_rows, LANES), F32),
-            pltpu.VMEM((STEPS, ext_rows, LANES), F32),
+            pltpu.VMEM((long_rows, LANES), F32),
+            pltpu.VMEM((STEPS, long_rows, LANES), F32),
             pltpu.VMEM((ext_rows, LANES), F32),
             pltpu.VMEM((ext_rows // PIX, LANES), F32),
+            pltpu.VMEM((rows // PIX, LANES), F32),
+            pltpu.VMEM((tiles, LANES), F32),
         ),
         flops=100 * cells,
         size=32 * cells,
-    )(filtered, base, cross_cols, near_cols, src_edge, place, *edge_matrices())
+    )(vals, base, cross_cols, near_cols, src_edge, place, spread_matrix())
     (fields,) = call(
         merge_kernel,
         (shape(3, 2, rows, cols),),
@@ -640,7 +728,15 @@
 
     outgoing = outgoing.reshape(owners, capacity, width)
     incoming = lax.all_to_all(outgoing, ("gx", "gy"), split_axis=0, concat_axis=0, tiled=True)
-    return fields, incoming[None]
+    (incoming,) = call(
+        deliver_kernel,
+        (shape(1, *incoming.shape),),
+        1,
+        out_specs=(pl.BlockSpec(memory_space=pl.ANY),),
+        scratch=(pltpu.SemaphoreType.DMA((4,)),),
+        size=8 * owners * capacity * width,
+    )(pltpu.with_memory_space_constraint(incoming, pltpu.VMEM))
+    return fields, incoming
 
 
 def solution(mesh):

time: 32.5 us -> 33.4 us (1.028)
  Pallas kernels: 10.1 us -> 11.7 us
  local copies, waits for them, and re-layouts: 0.7 us -> 0.04 us
    pallas_call x1 -> x2, Pallas kernels: 3.29 us -> 4.92 us  [the longest x1 4.24 us: on_device(): call(inner_kernel, (shape(*state), shape(tiles, LANES), shape(4 + STEPS,...]
    unnamed x23 -> x20, local copies, waits for them, and re-layouts: 0.7 us -> 0.04 us
  transfers between devices with their start and end apart: 5 -> 5, of which waited for: 1 -> 1; matrix products, arithmetic and copies ran while one was open for 0% -> 0% of each run, Pallas kernels for 20% -> 22%
where the time goes in v3:
time: 33.4 us; the launch traced here: 33.2 us
  starting transfers between devices  14.4 us (43%)
  Pallas kernels  11.7 us (35%)
  waiting for transfers between devices  6.2 us (19%)
  between operations  0.83 us (2%)
    all_to_all x1, waiting for transfers between devices, on_device(): lax.all_to_all(outgoing, ('gx', 'gy'), split_axis=0, concat_axis=0, tiled...  6.19 us
    ppermute x1, starting transfers between devices, on_device(): near_cols = lax.ppermute(near_cols, 'gy', pairs(gy_count, 0))  4.46 us
    ppermute x1, starting transfers between devices, on_device(): near = lax.ppermute(near, 'gx', pairs(gx_count, 0))  4.36 us
    all_to_all x1, starting transfers between devices, on_device(): lax.all_to_all(outgoing, ('gx', 'gy'), split_axis=0, concat_axis=0, tiled...  4.29 us
    pallas_call x1, Pallas kernels, on_device(): call(inner_kernel, (shape(*state), shape(tiles, LANES), shape(4 + STEPS,...  4.24 us
    pallas_call x1, Pallas kernels, on_device(): call(edge_kernel, (shape(*edge_state), shape(owners * capacity, width)),...  2.21 us
    pallas_call x1, Pallas kernels, on_device(): call(lambda *refs: prep_kernel(capacity, *refs), (packed, packed, shape(4...  2 us
    pallas_call x1, Pallas kernels, on_device(): call(rows_kernel, (strip, strip), 3, in_space=pltpu.HBM, scratch=(pltpu.V...  1.21 us
  transfers between devices with their start and end apart: 5, of which 1 were waited for; matrix products, arithmetic and copies ran while one was open for 0% of the time, Pallas kernels for 22%

profile of v3, /device:TPU:0, one launch (start us, length us, event | category | flops | bytes accessed | tf_op | source)
XLA Modules:
  0.0 33.2 jit_solution(6881725187919956014)
XLA Ops:
  0.6 0.0 copy-start
  0.6 0.0 copy-start.2
  0.7 0.0 copy-start.1
  0.7 0.0 copy-start.9
  0.7 0.0 copy-start.8
  0.7 0.0 copy-start.5
  0.7 0.0 copy-start.7
  0.7 0.0 copy-start.6
  0.7 1.2 %shard_map.113 = (f32[16,8,256]{2,1,0:T(8,128)S(1)}, f32[16,8,256]{2,1,0:T(8,128)S(1)}) custom-call(f32[3,2,128,256]{3,2,1,0:T(8,128)} %fields.3, f32[2,128,256]{2,1,0:T(8,128)} %eps.3, f32[4,2,128,256]{3,2,1,0:T(8,128)} %fwd.3), custom_call_target="tpu_custom_call" | custom-call | bytes 1048576 | tf_op jit(solution)/shard_map/pallas_call | solution.py:638
  1.9 0.0 copy-start.4
  1.9 0.7 %collective-permute-start = (f32[16,8,256]{2,1,0:T(8,128)S(1)}, f32[16,8,256]{2,1,0:T(8,128)S(1)}, u32[]{:S(2)}, u32[]{:S(2)}) collective-permute-start(f32[16,8,256]{2,1,0:T(8,128)S(1)} %get-tuple-element.17), channel_id=1, source_target_pairs={{4,8},{8,4},{5,9},{9,5},{6,10},{10,6},{7,11},{11,7},{20,24},{24,20... | collective-permute-start | bytes 393224 | tf_op jit(solution)/shard_map/ppermute | solution.py:652
  2.6 4.4 %collective-permute-start.1 = (f32[16,8,256]{2,1,0:T(8,128)S(1)}, f32[16,8,256]{2,1,0:T(8,128)S(1)}, u32[]{:S(2)}, u32[]{:S(2)}) collective-permute-start(f32[16,8,256]{2,1,0:T(8,128)S(1)} %get-tuple-element.18), channel_id=1, source_target_pairs={{0,4},{8,12},{4,0},{12,8},{1,5},{9,13},{5,1},{13,9},{2,6},{10,14},... | collective-permute-start | bytes 393224 | tf_op jit(solution)/shard_map/ppermute | solution.py:653
  7.0 0.0 copy-done
  7.0 0.0 copy-done.2
  7.0 0.0 copy-done.1
  7.0 0.0 copy-done.9
  7.0 0.0 copy-done.8
  7.0 0.0 copy-done.5
  7.0 0.0 copy-done.7
  7.0 0.0 copy-done.6
  7.0 2.0 %shard_map.114 = (f32[160,128]{1,0:T(8,128)S(1)}, f32[160,128]{1,0:T(8,128)S(1)}, f32[8,160,128]{2,1,0:T(8,128)S(1)}, f32[4,2,168,256]{3,2,1,0:T(8,128)S(1)}, f3...) custom-call(f32[3,2,128,256]{3,2,1,0:T(8,128)S(1)} %copy-done.1, f32[2,128,256]{2,1,0:T(8,128)S(1)} %copy-done.2, ...), custom_call_target="tpu_custom_call" | custom-call | flops 188743680 | bytes 2097152 | tf_op jit(solution)/shard_map/pallas_call | solution.py:657
  9.0 0.0 collective-permute-done.cross.cross_rows
  9.0 0.0 collective-permute-done.1.near.near_rows
  9.1 0.2 shard_map.116
  9.2 0.7 %collective-permute-start.2 = (f32[160,128]{1,0:T(8,128)S(1)}, f32[160,128]{1,0:T(8,128)S(1)}, u32[]{:S(2)}, u32[]{:S(2)}) collective-permute-start(f32[160,128]{1,0:T(8,128)S(1)} %get-tuple-element.26), channel_id=1, source_target_pairs={{1,2},{2,1},{5,6},{6,5},{9,10},{10,9},{13,14},{14,13},{17,18},{18,... | collective-permute-start | bytes 245768 | tf_op jit(solution)/shard_map/ppermute | solution.py:681
  9.9 4.5 %collective-permute-start.3 = (f32[160,128]{1,0:T(8,128)S(1)}, f32[160,128]{1,0:T(8,128)S(1)}, u32[]{:S(2)}, u32[]{:S(2)}) collective-permute-start(f32[160,128]{1,0:T(8,128)S(1)} %get-tuple-element.27), channel_id=1, source_target_pairs={{0,1},{2,3},{1,0},{3,2},{4,5},{6,7},{5,4},{7,6},{8,9},{10,11},{9,8... | collective-permute-start | bytes 245768 | tf_op jit(solution)/shard_map/ppermute | solution.py:682
  14.4 0.0 copy-done.4
  14.4 0.0 copy-start.3
  14.4 4.2 %shard_map.115 = (f32[3,2,2,168,128]{4,3,2,1,0:T(8,128)S(1)}, f32[128,128]{1,0:T(8,128)S(1)}, f32[8,160,128]{2,1,0:T(8,128)S(1)}) custom-call(f32[3,2,128,256]{3,2,1,0:T(8,128)S(1)} %copy-done.1, f32[2,128,256]{2,1,0:T(8,128)S(1)} %copy-done.2, f32[4,2,128,256]{3,2,1,0:T(8,128)S(1)} %copy-done, f32[16,8,256]{2,1,0:T(8,128)S(1)} %collective-permute-done.cross.cross_rows, ...), custom_call_target="tpu_custom_call" | custom-call | flops 6553600 | bytes 3145728 | tf_op jit(solution)/shard_map/pallas_call | solution.py:685
  18.6 0.0 collective-permute-done.2.cross
  18.6 0.0 collective-permute-done.3.near
  18.6 0.0 copy-done.3
  18.6 2.2 %shard_map.117 = (f32[3,168,128]{2,1,0:T(8,128)S(1)}, f32[256,128]{1,0:T(8,128)}) custom-call(f32[128,128]{1,0:T(8,128)S(1)} %get-tuple-element.22.vals_in, f32[8,160,128]{2,1,0:T(8,128)S(1)} %get-tuple-element.23.base, f32[160,128]{1,0:T(8,128)S(1)} %collective-permute-done.2.cross, f32[160,128]{1,0:T(8,128)S(1)} %collective-permute-done.3.near, ...), custom_call_target="tpu_custom_call" | custom-call | flops 3276800 | bytes 1048576 | tf_op jit(solution)/shard_map/pallas_call | solution.py:702
  20.9 4.3 %all-to-all-start = ((f32[16,16,128]{2,1,0:T(8,128)}), f32[16,16,128]{2,1,0:T(8,128)S(1)}, u32[]{:S(2)}, u32[]{:S(2)}) async-start(f32[16,16,128]{2,1,0:T(8,128)} %bitcast.4), calls=%async_computation | async-start | bytes 262144 | tf_op jit(solution)/shard_map/all_to_all | solution.py:730
  25.2 1.2 %shard_map.118 = f32[3,2,128,256]{3,2,1,0:T(8,128)} custom-call(f32[3,2,2,168,128]{4,3,2,1,0:T(8,128)S(1)} %get-tuple-element.21.last, f32[3,168,128]{2,1,0:T(8,128)S(1)} %get-tuple-element.30.edge_last), custom_call_target="tpu_custom_call" | custom-call | flops 655360 | bytes 1572864 | tf_op jit(solution)/shard_map/pallas_call | solution.py:719
  26.3 6.2 %all-to-all-done.array = f32[16,16,128]{2,1,0:T(8,128)S(1)} async-done(((f32[16,16,128]{2,1,0:T(8,128)}), f32[16,16,128]{2,1,0:T(8,128)S(1)}, u32[]{:S(2)}, u32[]{:S(2)}) %all-to-all-start) | async-done | bytes 131104 | tf_op jit(solution)/shard_map/all_to_all | solution.py:730
  32.5 0.7 %shard_map.119 = f32[1,16,16,128]{3,2,1,0:T(8,128)} custom-call(f32[16,16,128]{2,1,0:T(8,128)S(1)} %all-to-all-done.array), custom_call_target="tpu_custom_call" | custom-call | bytes 262144 | tf_op jit(solution)/shard_map/pallas_call | solution.py:731
Async XLA Ops:
  0.6 6.4 %copy-start = (f32[4,2,128,256]{3,2,1,0:T(8,128)S(1)}, f32[4,2,128,256]{3,2,1,0:T(8,128)}, u32[]{:S(2)}) copy-start(f32[4,2,128,256]{3,2,1,0:T(8,128)} %fwd.3) | copy-start | bytes 3145732
  0.6 6.3 %copy-start.2 = (f32[2,128,256]{2,1,0:T(8,128)S(1)}, f32[2,128,256]{2,1,0:T(8,128)}, u32[]{:S(2)}) copy-start(f32[2,128,256]{2,1,0:T(8,128)} %eps.3) | copy-start | bytes 786436
  0.7 6.3 %copy-start.1 = (f32[3,2,128,256]{3,2,1,0:T(8,128)S(1)}, f32[3,2,128,256]{3,2,1,0:T(8,128)}, u32[]{:S(2)}) copy-start(f32[3,2,128,256]{3,2,1,0:T(8,128)} %fields.3) | copy-start | bytes 2359300
  0.7 6.3 %copy-start.9 = (s32[1,1,128,1]{2,3,1,0:T(1,128)S(1)}, s32[1,1,128,1]{2,3,1,0:T(1,128)}, u32[]{:S(2)}) copy-start(s32[1,1,128,1]{2,3,1,0:T(1,128)} %param.17) | copy-start | bytes 1540
  0.7 6.3 %copy-start.8 = (s32[1,1,128]{2,1,0:T(1,128)S(1)}, s32[1,1,128]{2,1,0:T(1,128)}, u32[]{:S(2)}) copy-start(s32[1,1,128]{2,1,0:T(1,128)} %param.16) | copy-start | bytes 1540
  0.7 6.3 %copy-start.5 = (f32[4,64]{1,0:T(4,128)S(1)}, f32[4,64]{1,0:T(4,128)}, u32[]{:S(2)}) copy-start(f32[4,64]{1,0:T(4,128)} %refs_5_.1) | copy-start | bytes 3076
  0.7 6.3 %copy-start.7 = (s32[64]{0:T(128)S(1)}, s32[64]{0:T(128)}, u32[]{:S(2)}) copy-start(s32[64]{0:T(128)} %param.14) | copy-start | bytes 772
  0.7 6.3 %copy-start.6 = (s32[64]{0:T(128)S(1)}, s32[64]{0:T(128)}, u32[]{:S(2)}) copy-start(s32[64]{0:T(128)} %param.13) | copy-start | bytes 772
  1.9 12.4 %copy-start.4 = (bf16[2,128,128]{2,1,0:T(8,128)(2,1)S(1)}, bf16[2,128,128]{2,1,0:T(8,128)(2,1)}, u32[]{:S(2)}) copy-start(bf16[2,128,128]{2,1,0:T(8,128)(2,1)} %constant.4.clone.mats) | copy-start | bytes 196612
  1.9 7.1 %collective-permute-start = (f32[16,8,256]{2,1,0:T(8,128)S(1)}, f32[16,8,256]{2,1,0:T(8,128)S(1)}, u32[]{:S(2)}, u32[]{:S(2)}) collective-permute-start(f32[16,8,256]{2,1,0:T(8,128)S(1)} %get-tuple-element.17), channel_id=1, source_target_pairs={{4,8},{8,4},{5,9},{9,5},{6,10},{10,6},{7,11},{11,7},{20,24},{24,20... | collective-permute-start | bytes 393224 | tf_op jit(solution)/shard_map/ppermute | solution.py:652
  2.6 6.4 %collective-permute-start.1 = (f32[16,8,256]{2,1,0:T(8,128)S(1)}, f32[16,8,256]{2,1,0:T(8,128)S(1)}, u32[]{:S(2)}, u32[]{:S(2)}) collective-permute-start(f32[16,8,256]{2,1,0:T(8,128)S(1)} %get-tuple-element.18), channel_id=1, source_target_pairs={{0,4},{8,12},{4,0},{12,8},{1,5},{9,13},{5,1},{13,9},{2,6},{10,14},... | collective-permute-start | bytes 393224 | tf_op jit(solution)/shard_map/ppermute | solution.py:653
  9.2 9.4 %collective-permute-start.2 = (f32[160,128]{1,0:T(8,128)S(1)}, f32[160,128]{1,0:T(8,128)S(1)}, u32[]{:S(2)}, u32[]{:S(2)}) collective-permute-start(f32[160,128]{1,0:T(8,128)S(1)} %get-tuple-element.26), channel_id=1, source_target_pairs={{1,2},{2,1},{5,6},{6,5},{9,10},{10,9},{13,14},{14,13},{17,18},{18,... | collective-permute-start | bytes 245768 | tf_op jit(solution)/shard_map/ppermute | solution.py:681
  9.9 8.7 %collective-permute-start.3 = (f32[160,128]{1,0:T(8,128)S(1)}, f32[160,128]{1,0:T(8,128)S(1)}, u32[]{:S(2)}, u32[]{:S(2)}) collective-permute-start(f32[160,128]{1,0:T(8,128)S(1)} %get-tuple-element.27), channel_id=1, source_target_pairs={{0,1},{2,3},{1,0},{3,2},{4,5},{6,7},{5,4},{7,6},{8,9},{10,11},{9,8... | collective-permute-start | bytes 245768 | tf_op jit(solution)/shard_map/ppermute | solution.py:682
  14.4 4.3 %copy-start.3 = (bf16[256,256]{1,0:T(8,128)(2,1)S(1)}, bf16[256,256]{1,0:T(8,128)(2,1)}, u32[]{:S(2)}) copy-start(bf16[256,256]{1,0:T(8,128)(2,1)} %constant.5.clone.spread) | copy-start | bytes 393220
  20.9 11.6 %all-to-all-start = ((f32[16,16,128]{2,1,0:T(8,128)}), f32[16,16,128]{2,1,0:T(8,128)S(1)}, u32[]{:S(2)}, u32[]{:S(2)}) async-start(f32[16,16,128]{2,1,0:T(8,128)} %bitcast.4), calls=%async_computation | async-start | bytes 262144 | tf_op jit(solution)/shard_map/all_to_all | solution.py:730

commit v4 on v2

--- a/solution.py
+++ b/solution.py
@@ -46,24 +46,17 @@
     return inner.astype(ml_dtypes.bfloat16)
 
 
-def edge_matrices():
-    weights = cone_weights(RADIUS)
-    reach = RADIUS - 1
-    result = np.zeros((RADIUS, LANES, 2, LANES), np.float32)
-    for lane in range(LANES):
-        layer, at = lane // HALF, lane % HALF
-        col = at - OUT if at < SIDE else at - SIDE + 2 * LANES - OUT
-        if not (-NEAR <= col < KEEP or 2 * LANES - KEEP <= col < 2 * LANES + NEAR):
-            continue
-        for row in range(RADIUS):
-            for shift in range(-reach, reach + 1):
-                pixel = col // PIX + shift
-                if 0 <= pixel < LANES:
-                    result[row, lane, layer, pixel] = weights[reach + row, reach + shift]
-    result = result.reshape(RADIUS * LANES, 2 * LANES)
-    high = result.astype(ml_dtypes.bfloat16)
-    low = (result - high.astype(np.float32)).astype(ml_dtypes.bfloat16)
-    return high, low
+def spread_matrix():
+    span = TS // PIX
+    result = np.zeros((2, LANES, 2, 2, span, span), np.float32)
+    for e in range(span):
+        move = (e % 2) + SIDE * (e % 4 // 2)
+        for layer in range(2):
+            for side in range(2):
+                for f in range(span):
+                    lane = (HALF * layer + OUT + OUT * side + PIX * f + move) % LANES
+                    result[e // 4, lane, side, layer, e, f] = 1.0
+    return result.reshape(2 * LANES, 2 * LANES).astype(ml_dtypes.bfloat16)
 
 
 def split2(value):
@@ -234,12 +227,11 @@
     capacity, fields, eps, fwd, mon_x, mon_y, amp, mask, owner, cross, near, base, src, src_edge, place
 ):
     cols_kernel(fields, eps, fwd, cross, near, base)
-    side_kernel(capacity, mon_x, mon_y, amp, mask, owner, src, src_edge, place)
-
-
-def side_kernel(capacity, mon_x, mon_y, amp, mask, owner, src, src_edge, place):
+    side_kernel(capacity, fields.shape[2], mon_x, mon_y, amp, mask, owner, src, src_edge, place)
+
+
+def side_kernel(capacity, rows, mon_x, mon_y, amp, mask, owner, src, src_edge, place):
     _, _, ext_rows, cols = src.shape
-    rows = ext_rows - 2 * PAD
     channels = mon_x.shape[1]
     row = mon_x[...] - lax.axis_index("gx") * rows + PAD
     col = mon_y[...] - lax.axis_index("gy") * cols
@@ -331,7 +323,7 @@
     return even + ref[lead + (pl.ds(1, count, stride=PIX), slice(None))]
 
 
-def inner_kernel(fields, eps, fwd, cross, near, src, mats, base_in, last, filtered, base, a, b, e, g, pooled):
+def inner_kernel(fields, eps, fwd, cross, near, src, base_in, last, g, base, a, b, e):
     rows, cols = fields.shape[2], fields.shape[3]
     n_tiles = (rows + 2 * PAD) // SUB
     n_lanes = cols // LANES
@@ -375,17 +367,6 @@
         g, COURANT, coef_above(), next_col, prev_col,
         lambda values, key: values[1 - key[0], key[1]],
     )
-    for layer in range(2):
-        total = None
-        for k in range(n_lanes):
-            for part in split2(row_pairs(g, (layer, k), n_tiles * SUB // PIX)):
-                term = dot(part, mats[k])
-                total = term if total is None else total + term
-        pooled[layer] = total
-
-    for layer in range(2):
-        filtered[layer] = cone_filter(pooled.at[layer], rows // PIX, PAD // PIX)
-
     for t in range(n_tiles):
         for kind in range(4 + STEPS):
             at = pl.ds(t * SUB, SUB)
@@ -395,6 +376,20 @@
                 base[kind, at, :] = edge_tile(
                     lambda kind, layer, k: load(kind, layer, t, k), kind, lane, n_lanes
                 )
+
+
+def inner_tiles_kernel(g, mats, vals, pooled):
+    n_lanes, ext_rows = g.shape[1], g.shape[2]
+    for layer in range(2):
+        total = None
+        for k in range(n_lanes):
+            for part in split2(row_pairs(g, (layer, k), ext_rows // PIX)):
+                term = dot(part, mats[k])
+                total = term if total is None else total + term
+        pooled[layer] = total
+
+    out_pix = ext_rows // PIX - 2 * PAD // PIX
+    vals[...] = by_tile([cone_filter(pooled.at[layer], out_pix, PAD // PIX) for layer in range(2)])
 
 
 def cone_filter(pooled, out_pix, first):
@@ -419,9 +414,38 @@
     return total
 
 
-def edge_kernel(
-    filtered, base, cross, near, src, place, high_mat, low_mat, c, out_slots, a, b, e, d, g, pooled
-):
+def by_tile(blocks):
+    span = TS // PIX
+    tile_rows = blocks[0].shape[0] // span
+    x = jnp.stack([block.reshape(tile_rows, span, LANES) for block in blocks], axis=1)
+    x = x.reshape(tile_rows * 2, span, LANES)
+    group = lax.broadcasted_iota(jnp.int32, x.shape, 2) // span
+    row = lax.broadcasted_iota(jnp.int32, x.shape, 1)
+    for bit in (1, 2, 4):
+        row_on, lane_on = (row & bit) != 0, (group & bit) != 0
+        ahead = turn(turn(x, -bit, 1), bit * span, 2)
+        behind = turn(turn(x, bit, 1), -bit * span, 2)
+        x = jnp.where(row_on == lane_on, x, jnp.where(lane_on, ahead, behind))
+    x = x.reshape(tile_rows, 2, span, LANES)
+    even, odd = x[:, 0], x[:, 1]
+    upper = lax.broadcasted_iota(jnp.int32, even.shape, 2) >= HALF
+    new_even = jnp.where(upper, turn(odd, HALF, 2), even)
+    new_odd = jnp.where(upper, odd, turn(even, HALF, 2))
+    return jnp.stack([new_even, new_odd], axis=1).reshape(tile_rows * 2 * span, LANES)
+
+
+def merge_spans(rows_of, lane):
+    even = (lane & 1) == 0
+    window = ((lane - OUT) & (HALF - 1)) < SIDE
+    merged = []
+    for e in (0, 4):
+        low = jnp.where(even, rows_of(e), turn(rows_of(e + 1), 1, 1))
+        high = jnp.where(even, turn(rows_of(e + 2), SIDE, 1), turn(rows_of(e + 3), SIDE + 1, 1))
+        merged.append(jnp.where(window, low, high))
+    return jnp.concatenate(merged, axis=1)
+
+
+def edge_kernel(base, cross, near, src, c, g, a, b, e, d):
     ext_rows = base.shape[1]
     rows = ext_rows - 2 * PAD
     n_tiles = ext_rows // SUB
@@ -460,34 +484,47 @@
         lambda values, key: turn(values[()], HALF, 1),
     )
 
-    pooled[...] = row_pairs(g, (), ext_rows // PIX)
+    inside = (spot >= OUT - NEAR) & (spot < OUT + KEEP)
+    inside = inside | ((spot >= HALF - OUT - KEEP) & (spot < HALF - OUT + NEAR))
+    for t in range(1, n_tiles - 1):
+        at = pl.ds(t * SUB, SUB)
+        g[at, :] = jnp.where(inside, g[at, :], 0.0)
+
+
+def tiles_kernel(vals_in, g, place, spread, out_slots, pooled, pixels, vals):
+    ext_rows = g.shape[0]
+    rows = ext_rows - 2 * PAD
+    lane = lanes()
+    summed = row_pairs(g, (), ext_rows // PIX)
+    pooled[...] = summed + turn(summed, -1, 1)
+    weights = cone_weights(RADIUS)
     reach = RADIUS - 1
-    out_pix = rows // PIX
-    first = PAD // PIX
-    at = [pooled[pl.ds(first + s, out_pix), :] for s in range(-reach, reach + 1)]
+    out_pix, top = rows // PIX, PAD // PIX
+    at = [pooled[pl.ds(top + s, out_pix), :] for s in range(-reach, reach + 1)]
     sums = [at[reach]] + [at[reach + s] + at[reach - s] for s in range(1, reach + 1)]
-    high, low = split2(jnp.concatenate(sums, axis=1))
-    edge = dot(high, high_mat[...]) + (dot(low, high_mat[...]) + dot(high, low_mat[...]))
-    blocks = [filtered[l] + edge[:, l * LANES : (l + 1) * LANES] for l in range(2)]
+    total = None
+    for shift in range(reach + 1):
+        mixed = None
+        for s in range(reach + 1):
+            weight = float(weights[reach + s, reach + shift])
+            if weight > 0.0:
+                term = weight * sums[s]
+                mixed = term if mixed is None else mixed + term
+        if shift:
+            mixed = turn(mixed, -PIX * shift, 1) + turn(mixed, PIX * shift, 1)
+        total = mixed if total is None else total + mixed
+    pixels[...] = total
 
     span = TS // PIX
-    tile_rows = out_pix // span
-    x = jnp.stack([block.reshape(tile_rows, span, LANES) for block in blocks], axis=1)
-    x = x.reshape(tile_rows * 2, span, LANES)
-    group = lax.broadcasted_iota(jnp.int32, x.shape, 2) // span
-    row = lax.broadcasted_iota(jnp.int32, x.shape, 1)
-    for bit in (1, 2, 4):
-        row_on, lane_on = (row & bit) != 0, (group & bit) != 0
-        ahead = turn(turn(x, -bit, 1), bit * span, 2)
-        behind = turn(turn(x, bit, 1), -bit * span, 2)
-        x = jnp.where(row_on == lane_on, x, jnp.where(lane_on, ahead, behind))
-    x = x.reshape(tile_rows, 2, span, LANES)
-    even, odd = x[:, 0], x[:, 1]
-    upper = lax.broadcasted_iota(jnp.int32, even.shape, 2) >= HALF
-    new_even = jnp.where(upper, turn(odd, HALF, 2), even)
-    new_odd = jnp.where(upper, odd, turn(even, HALF, 2))
-    vals = jnp.stack([new_even, new_odd], axis=1).reshape(tile_rows * 2 * span, LANES)
-    high, low = split2(vals)
+    tile_rows, tile_cols = rows // TS, vals.shape[0] // (rows // TS)
+    merged = merge_spans(lambda row: pixels[pl.ds(row, tile_rows, stride=span), :], lane)
+    high, low = split2(merged)
+    edge = dot(high, spread[...]) + dot(low, spread[...])
+    vals[...] = vals_in[...]
+    for side, row in enumerate((0, tile_cols - 1)):
+        spots = pl.ds(row, tile_rows, stride=tile_cols)
+        vals[spots, :] = vals[spots, :] + edge[:, side * LANES : (side + 1) * LANES]
+    high, low = split2(vals[...])
     out_slots[...] = dot(place[...], high) + dot(place[...], low)
 
 
@@ -543,6 +580,7 @@
     width = 2 * (TS // PIX) ** 2
     assert width == LANES
     capacity = max(8, 2 * tiles // owners)
+    assert rows == TS * SUB and cols == 2 * TS * SUB
     ext_rows = rows + 2 * PAD
     n_lanes = cols // LANES
     cells = rows * cols
@@ -597,37 +635,53 @@
     near_cols = lax.ppermute(near_cols, "gy", pairs(gy_count, 0))
 
     state = (3, 2, n_lanes, ext_rows + 2 * SUB, LANES)
-    last, filtered, base = call(
+    last, g, base = call(
         inner_kernel,
-        (shape(*state), shape(2, rows // PIX, LANES), shape(4 + STEPS, ext_rows, LANES)),
-        8,
+        (shape(*state), shape(2, n_lanes, ext_rows, LANES), shape(4 + STEPS, ext_rows, LANES)),
+        7,
         scratch=(
             pltpu.VMEM(state, F32),
             pltpu.VMEM(state, F32),
             pltpu.VMEM((2, n_lanes, ext_rows, LANES), F32),
-            pltpu.VMEM((2, n_lanes, ext_rows, LANES), F32),
-            pltpu.VMEM((2, ext_rows // PIX, LANES), F32),
         ),
         flops=200 * cells,
         size=96 * cells,
-    )(*blocks, cross, near, src, pool_matrices(), base)
+    )(*blocks, cross, near, src, base)
+    (vals,) = call(
+        inner_tiles_kernel,
+        (shape(tiles, LANES),),
+        2,
+        scratch=(pltpu.VMEM((2, ext_rows // PIX, LANES), F32),),
+        flops=100 * cells,
+        size=32 * cells,
+    )(g, pool_matrices())
 
     edge_state = (3, ext_rows + 2 * SUB, LANES)
-    edge_last, outgoing = call(
+    edge_last, edge_g = call(
         edge_kernel,
-        (shape(*edge_state), shape(owners * capacity, width)),
-        8,
+        (shape(*edge_state), shape(ext_rows, LANES)),
+        4,
         scratch=(
             pltpu.VMEM(edge_state, F32),
             pltpu.VMEM(edge_state, F32),
             pltpu.VMEM((ext_rows, LANES), F32),
             pltpu.VMEM((STEPS, ext_rows, LANES), F32),
-            pltpu.VMEM((ext_rows, LANES), F32),
+        ),
+        flops=50 * cells,
+        size=16 * cells,
+    )(base, cross_cols, near_cols, src_edge)
+    (outgoing,) = call(
+        tiles_kernel,
+        (shape(owners * capacity, width),),
+        4,
+        scratch=(
             pltpu.VMEM((ext_rows // PIX, LANES), F32),
+            pltpu.VMEM((rows // PIX, LANES), F32),
+            pltpu.VMEM((tiles, LANES), F32),
         ),
-        flops=100 * cells,
-        size=32 * cells,
-    )(filtered, base, cross_cols, near_cols, src_edge, place, *edge_matrices())
+        flops=50 * cells,
+        size=16 * cells,
+    )(vals, edge_g, place, spread_matrix())
     (fields,) = call(
         merge_kernel,
         (shape(3, 2, rows, cols),),

time: 32.5 us -> 34.1 us (1.049)
  Pallas kernels: 10.1 us -> 11.6 us
    pallas_call x2 -> x4, Pallas kernels: 5.56 us -> 7.09 us  [the longest x1 4.13 us: on_device(): call(inner_kernel, (shape(*state), shape(2, n_lanes, ext_rows, LANES), sh...]
    unnamed x23 -> x21, local copies, waits for them, and re-layouts: 0.7 us -> 0.7 us
  transfers between devices with their start and end apart: 5 -> 5, of which waited for: 1 -> 1; matrix products, arithmetic and copies ran while one was open for 0% -> 0% of each run, Pallas kernels for 20% -> 24%
where the time goes in v4:
time: 34.1 us; the launch traced here: 33.8 us
  starting transfers between devices  14.5 us (43%)
  Pallas kernels  11.6 us (34%)
  waiting for transfers between devices  6.2 us (18%)
  between operations  0.84 us (2%)
  local copies, waits for them, and re-layouts  0.7 us (2%)
    all_to_all x1, waiting for transfers between devices, on_device(): lax.all_to_all(outgoing, ('gx', 'gy'), split_axis=0, concat_axis=0, tiled...  6.19 us
    ppermute x1, starting transfers between devices, on_device(): near_cols = lax.ppermute(near_cols, 'gy', pairs(gy_count, 0))  4.46 us
    ppermute x1, starting transfers between devices, on_device(): near = lax.ppermute(near, 'gx', pairs(gx_count, 0))  4.36 us
    all_to_all x1, starting transfers between devices, on_device(): lax.all_to_all(outgoing, ('gx', 'gy'), split_axis=0, concat_axis=0, tiled...  4.3 us
    pallas_call x1, Pallas kernels, on_device(): call(inner_kernel, (shape(*state), shape(2, n_lanes, ext_rows, LANES), sh...  4.13 us
    pallas_call x1, Pallas kernels, on_device(): call(lambda *refs: prep_kernel(capacity, *refs), (packed, packed, shape(4...  1.98 us
    pallas_call x1, Pallas kernels, on_device(): call(tiles_kernel, (shape(owners * capacity, width),), 4, scratch=(pltpu....  1.31 us
    pallas_call x1, Pallas kernels, on_device(): call(rows_kernel, (strip, strip), 3, in_space=pltpu.HBM, scratch=(pltpu.V...  1.21 us
  transfers between devices with their start and end apart: 5, of which 1 were waited for; matrix products, arithmetic and copies ran while one was open for 0% of the time, Pallas kernels for 24%

profile of v4, /device:TPU:0, one launch (start us, length us, event | category | flops | bytes accessed | tf_op | source)
XLA Modules:
  0.0 33.8 jit_solution(6464247076455036200)
XLA Ops:
  0.6 0.0 copy-start
  0.6 0.0 copy-start.2
  0.7 0.0 copy-start.1
  0.7 0.0 copy-start.9
  0.7 0.0 copy-start.8
  0.7 0.0 copy-start.5
  0.7 0.0 copy-start.7
  0.7 0.0 copy-start.6
  0.7 1.2 %shard_map.113 = (f32[16,8,256]{2,1,0:T(8,128)S(1)}, f32[16,8,256]{2,1,0:T(8,128)S(1)}) custom-call(f32[3,2,128,256]{3,2,1,0:T(8,128)} %fields.3, f32[2,128,256]{2,1,0:T(8,128)} %eps.3, f32[4,2,128,256]{3,2,1,0:T(8,128)} %fwd.3), custom_call_target="tpu_custom_call" | custom-call | bytes 1048576 | tf_op jit(solution)/shard_map/pallas_call | solution.py:591
  1.9 0.7 %collective-permute-start = (f32[16,8,256]{2,1,0:T(8,128)S(1)}, f32[16,8,256]{2,1,0:T(8,128)S(1)}, u32[]{:S(2)}, u32[]{:S(2)}) collective-permute-start(f32[16,8,256]{2,1,0:T(8,128)S(1)} %get-tuple-element.17), channel_id=1, source_target_pairs={{4,8},{8,4},{5,9},{9,5},{6,10},{10,6},{7,11},{11,7},{20,24},{24,20... | collective-permute-start | bytes 393224 | tf_op jit(solution)/shard_map/ppermute | solution.py:605
  2.6 4.4 %collective-permute-start.1 = (f32[16,8,256]{2,1,0:T(8,128)S(1)}, f32[16,8,256]{2,1,0:T(8,128)S(1)}, u32[]{:S(2)}, u32[]{:S(2)}) collective-permute-start(f32[16,8,256]{2,1,0:T(8,128)S(1)} %get-tuple-element.18), channel_id=1, source_target_pairs={{0,4},{8,12},{4,0},{12,8},{1,5},{9,13},{5,1},{13,9},{2,6},{10,14},... | collective-permute-start | bytes 393224 | tf_op jit(solution)/shard_map/ppermute | solution.py:606
  7.0 0.0 copy-done
  7.0 0.0 copy-done.2
  7.0 0.0 copy-done.1
  7.0 0.0 copy-done.9
  7.0 0.0 copy-done.8
  7.0 0.0 copy-done.5
  7.0 0.0 copy-done.7
  7.0 0.0 copy-done.6
  7.0 2.0 %shard_map.114 = (f32[160,128]{1,0:T(8,128)S(1)}, f32[160,128]{1,0:T(8,128)S(1)}, f32[8,160,128]{2,1,0:T(8,128)S(1)}, f32[4,2,160,256]{3,2,1,0:T(8,128)S(1)}, f3...) custom-call(f32[3,2,128,256]{3,2,1,0:T(8,128)S(1)} %copy-done.1, f32[2,128,256]{2,1,0:T(8,128)S(1)} %copy-done.2, ...), custom_call_target="tpu_custom_call" | custom-call | flops 188743680 | bytes 2097152 | tf_op jit(solution)/shard_map/pallas_call | solution.py:610
  9.0 0.0 collective-permute-done.cross.cross_rows
  9.0 0.0 collective-permute-done.1.near.near_rows
  9.0 0.2 shard_map.116
  9.2 0.7 %collective-permute-start.2 = (f32[160,128]{1,0:T(8,128)S(1)}, f32[160,128]{1,0:T(8,128)S(1)}, u32[]{:S(2)}, u32[]{:S(2)}) collective-permute-start(f32[160,128]{1,0:T(8,128)S(1)} %get-tuple-element.25), channel_id=1, source_target_pairs={{1,2},{2,1},{5,6},{6,5},{9,10},{10,9},{13,14},{14,13},{17,18},{18,... | collective-permute-start | bytes 245768 | tf_op jit(solution)/shard_map/ppermute | solution.py:634
  9.9 4.5 %collective-permute-start.3 = (f32[160,128]{1,0:T(8,128)S(1)}, f32[160,128]{1,0:T(8,128)S(1)}, u32[]{:S(2)}, u32[]{:S(2)}) collective-permute-start(f32[160,128]{1,0:T(8,128)S(1)} %get-tuple-element.26), channel_id=1, source_target_pairs={{0,1},{2,3},{1,0},{3,2},{4,5},{6,7},{5,4},{7,6},{8,9},{10,11},{9,8... | collective-permute-start | bytes 245768 | tf_op jit(solution)/shard_map/ppermute | solution.py:635
  14.3 0.0 copy-start.4
  14.3 4.1 %shard_map.115 = (f32[3,2,2,176,128]{4,3,2,1,0:T(8,128)S(1)}, f32[2,2,160,128]{3,2,1,0:T(8,128)S(1)}, f32[8,160,128]{2,1,0:T(8,128)S(1)}) custom-call(f32[3,2,128,256]{3,2,1,0:T(8,128)S(1)} %copy-done.1, f32[2,128,256]{2,1,0:T(8,128)S(1)} %copy-done.2, f32[4,2,128,256]{3,2,1,0:T(8,128)S(1)} %copy-done, ...), custom_call_target="tpu_custom_call" | custom-call | flops 6553600 | bytes 3145728 | tf_op jit(solution)/shard_map/pallas_call | solution.py:638
  18.5 0.0 copy-start.3
  18.5 0.0 copy-done.4
  18.5 0.7 %shard_map.119.vals_in = f32[128,128]{1,0:T(8,128)S(1)} custom-call(f32[2,2,160,128]{3,2,1,0:T(8,128)S(1)} %get-tuple-element.29.g, bf16[2,128,128]{2,1,0:T(8,128)(2,1)S(1)} %copy-done.4), custom_call_target="tpu_custom_call" | custom-call | flops 3276800 | bytes 1048576 | tf_op jit(solution)/shard_map/pallas_call | solution.py:650
  19.2 0.0 collective-permute-done.2.cross
  19.2 0.0 collective-permute-done.3.near
  19.2 1.0 %shard_map.117 = (f32[3,176,128]{2,1,0:T(8,128)S(1)}, f32[160,128]{1,0:T(8,128)S(1)}) custom-call(f32[8,160,128]{2,1,0:T(8,128)S(1)} %get-tuple-element.22.base, f32[160,128]{1,0:T(8,128)S(1)} %collective-permute-done.2.cross, f32[160,128]{1,0:T(8,128)S(1)} %collective-permute-done.3.near, f32[4,160,128]{2,1,0:T(8,128)S(1)} %get-tuple-element.27.src), custom_call_target="tpu_custom_call" | custom-call | flops 1638400 | bytes 524288 | tf_op jit(solution)/shard_map/pallas_call | solution.py:660
  20.2 0.0 copy-done.3
  20.2 1.3 %shard_map.120 = f32[256,128]{1,0:T(8,128)} custom-call(f32[128,128]{1,0:T(8,128)S(1)} %shard_map.119.vals_in, f32[160,128]{1,0:T(8,128)S(1)} %get-tuple-element.30.g, bf16[256,128]{1,0:T(8,128)(2,1)S(1)} %get-tuple-element.31.place, bf16[256,256]{1,0:T(8,128)(2,1)S(1)} %copy-done.3), custom_call_target="tpu_custom_call" | custom-call | flops 1638400 | bytes 524288 | tf_op jit(solution)/shard_map/pallas_call | solution.py:673
  21.5 4.3 %all-to-all-start = ((f32[16,16,128]{2,1,0:T(8,128)}), f32[16,16,128]{2,1,0:T(8,128)S(1)}, u32[]{:S(2)}, u32[]{:S(2)}) async-start(f32[16,16,128]{2,1,0:T(8,128)} %bitcast.4), calls=%async_computation | async-start | bytes 262144 | tf_op jit(solution)/shard_map/all_to_all | solution.py:696
  25.8 1.2 %shard_map.118 = f32[3,2,128,256]{3,2,1,0:T(8,128)} custom-call(f32[3,2,2,176,128]{4,3,2,1,0:T(8,128)S(1)} %get-tuple-element.21.last, f32[3,176,128]{2,1,0:T(8,128)S(1)} %get-tuple-element.28.edge_last), custom_call_target="tpu_custom_call" | custom-call | flops 655360 | bytes 1572864 | tf_op jit(solution)/shard_map/pallas_call | solution.py:685
  27.0 6.2 %all-to-all-done = f32[16,16,128]{2,1,0:T(8,128)S(1)} async-done(((f32[16,16,128]{2,1,0:T(8,128)}), f32[16,16,128]{2,1,0:T(8,128)S(1)}, u32[]{:S(2)}, u32[]{:S(2)}) %all-to-all-start) | async-done | bytes 131104 | tf_op jit(solution)/shard_map/all_to_all | solution.py:696
  33.1 0.7 %copy.13 = f32[1,16,16,128]{3,2,1,0:T(8,128)} copy(f32[1,16,16,128]{3,2,1,0:T(8,128)S(1)} %bitcast.10) | data formatting | bytes 262144
Async XLA Ops:
  0.6 6.3 %copy-start = (f32[4,2,128,256]{3,2,1,0:T(8,128)S(1)}, f32[4,2,128,256]{3,2,1,0:T(8,128)}, u32[]{:S(2)}) copy-start(f32[4,2,128,256]{3,2,1,0:T(8,128)} %fwd.3) | copy-start | bytes 3145732
  0.6 6.3 %copy-start.2 = (f32[2,128,256]{2,1,0:T(8,128)S(1)}, f32[2,128,256]{2,1,0:T(8,128)}, u32[]{:S(2)}) copy-start(f32[2,128,256]{2,1,0:T(8,128)} %eps.3) | copy-start | bytes 786436
  0.7 6.3 %copy-start.1 = (f32[3,2,128,256]{3,2,1,0:T(8,128)S(1)}, f32[3,2,128,256]{3,2,1,0:T(8,128)}, u32[]{:S(2)}) copy-start(f32[3,2,128,256]{3,2,1,0:T(8,128)} %fields.3) | copy-start | bytes 2359300
  0.7 6.3 %copy-start.9 = (s32[1,1,128,1]{2,3,1,0:T(1,128)S(1)}, s32[1,1,128,1]{2,3,1,0:T(1,128)}, u32[]{:S(2)}) copy-start(s32[1,1,128,1]{2,3,1,0:T(1,128)} %param.17) | copy-start | bytes 1540
  0.7 6.3 %copy-start.8 = (s32[1,1,128]{2,1,0:T(1,128)S(1)}, s32[1,1,128]{2,1,0:T(1,128)}, u32[]{:S(2)}) copy-start(s32[1,1,128]{2,1,0:T(1,128)} %param.16) | copy-start | bytes 1540
  0.7 6.3 %copy-start.5 = (f32[4,64]{1,0:T(4,128)S(1)}, f32[4,64]{1,0:T(4,128)}, u32[]{:S(2)}) copy-start(f32[4,64]{1,0:T(4,128)} %refs_5_.1) | copy-start | bytes 3076
  0.7 6.3 %copy-start.7 = (s32[64]{0:T(128)S(1)}, s32[64]{0:T(128)}, u32[]{:S(2)}) copy-start(s32[64]{0:T(128)} %param.14) | copy-start | bytes 772
  0.7 6.3 %copy-start.6 = (s32[64]{0:T(128)S(1)}, s32[64]{0:T(128)}, u32[]{:S(2)}) copy-start(s32[64]{0:T(128)} %param.13) | copy-start | bytes 772
  1.9 7.1 %collective-permute-start = (f32[16,8,256]{2,1,0:T(8,128)S(1)}, f32[16,8,256]{2,1,0:T(8,128)S(1)}, u32[]{:S(2)}, u32[]{:S(2)}) collective-permute-start(f32[16,8,256]{2,1,0:T(8,128)S(1)} %get-tuple-element.17), channel_id=1, source_target_pairs={{4,8},{8,4},{5,9},{9,5},{6,10},{10,6},{7,11},{11,7},{20,24},{24,20... | collective-permute-start | bytes 393224 | tf_op jit(solution)/shard_map/ppermute | solution.py:605
  2.6 6.4 %collective-permute-start.1 = (f32[16,8,256]{2,1,0:T(8,128)S(1)}, f32[16,8,256]{2,1,0:T(8,128)S(1)}, u32[]{:S(2)}, u32[]{:S(2)}) collective-permute-start(f32[16,8,256]{2,1,0:T(8,128)S(1)} %get-tuple-element.18), channel_id=1, source_target_pairs={{0,4},{8,12},{4,0},{12,8},{1,5},{9,13},{5,1},{13,9},{2,6},{10,14},... | collective-permute-start | bytes 393224 | tf_op jit(solution)/shard_map/ppermute | solution.py:606
  9.2 10.0 %collective-permute-start.2 = (f32[160,128]{1,0:T(8,128)S(1)}, f32[160,128]{1,0:T(8,128)S(1)}, u32[]{:S(2)}, u32[]{:S(2)}) collective-permute-start(f32[160,128]{1,0:T(8,128)S(1)} %get-tuple-element.25), channel_id=1, source_target_pairs={{1,2},{2,1},{5,6},{6,5},{9,10},{10,9},{13,14},{14,13},{17,18},{18,... | collective-permute-start | bytes 245768 | tf_op jit(solution)/shard_map/ppermute | solution.py:634
  9.9 9.3 %collective-permute-start.3 = (f32[160,128]{1,0:T(8,128)S(1)}, f32[160,128]{1,0:T(8,128)S(1)}, u32[]{:S(2)}, u32[]{:S(2)}) collective-permute-start(f32[160,128]{1,0:T(8,128)S(1)} %get-tuple-element.26), channel_id=1, source_target_pairs={{0,1},{2,3},{1,0},{3,2},{4,5},{6,7},{5,4},{7,6},{8,9},{10,11},{9,8... | collective-permute-start | bytes 245768 | tf_op jit(solution)/shard_map/ppermute | solution.py:635
  14.3 4.2 %copy-start.4 = (bf16[2,128,128]{2,1,0:T(8,128)(2,1)S(1)}, bf16[2,128,128]{2,1,0:T(8,128)(2,1)}, u32[]{:S(2)}) copy-start(bf16[2,128,128]{2,1,0:T(8,128)(2,1)} %constant.4.clone.mats) | copy-start | bytes 196612
  18.5 1.7 %copy-start.3 = (bf16[256,256]{1,0:T(8,128)(2,1)S(1)}, bf16[256,256]{1,0:T(8,128)(2,1)}, u32[]{:S(2)}) copy-start(bf16[256,256]{1,0:T(8,128)(2,1)} %constant.5.clone.spread) | copy-start | bytes 393220
  21.5 11.7 %all-to-all-start = ((f32[16,16,128]{2,1,0:T(8,128)}), f32[16,16,128]{2,1,0:T(8,128)S(1)}, u32[]{:S(2)}, u32[]{:S(2)}) async-start(f32[16,16,128]{2,1,0:T(8,128)} %bitcast.4), calls=%async_computation | async-start | bytes 262144 | tf_op jit(solution)/shard_map/all_to_all | solution.py:696

commit v5 on v4

--- a/solution.py
+++ b/solution.py
@@ -192,12 +192,12 @@
         cross[out_at, :] = jnp.where(odd, right, left)
         near[out_at, :] = jnp.where(odd, left, right)
         for kind in range(4 + STEPS):
-            base[kind, out_at, :] = edge_tile(load, kind, lane, n_lanes)
+            base[kind, at, :] = edge_tile(load, kind, lane, n_lanes)
         return carry
 
     lax.fori_loop(0, rows // SUB, tile, 0, unroll=4)
     zero = jnp.zeros((PAD, LANES), F32)
-    for out in (cross, near) + tuple(base.at[kind] for kind in range(4 + STEPS)):
+    for out in (cross, near):
         out[pl.ds(0, PAD), :] = zero
         out[pl.ds(PAD + rows, PAD), :] = zero
 
@@ -224,13 +224,13 @@
 
 
 def prep_kernel(
-    capacity, fields, eps, fwd, mon_x, mon_y, amp, mask, owner, cross, near, base, src, src_edge, place
+    capacity, fields, eps, fwd, mon_x, mon_y, amp, mask, owner, cross, near, base, src, src_edge, place, place_edge
 ):
     cols_kernel(fields, eps, fwd, cross, near, base)
-    side_kernel(capacity, fields.shape[2], mon_x, mon_y, amp, mask, owner, src, src_edge, place)
-
-
-def side_kernel(capacity, rows, mon_x, mon_y, amp, mask, owner, src, src_edge, place):
+    side_kernel(capacity, fields.shape[2], mon_x, mon_y, amp, mask, owner, src, src_edge, place, place_edge)
+
+
+def side_kernel(capacity, rows, mon_x, mon_y, amp, mask, owner, src, src_edge, place, place_edge):
     _, _, ext_rows, cols = src.shape
     channels = mon_x.shape[1]
     row = mon_x[...] - lax.axis_index("gx") * rows + PAD
@@ -269,7 +269,13 @@
     dest = owner[...] * capacity + slot.astype(jnp.int32)
     dest = jnp.where(mask[...] != 0, dest, -1)
     hit = lax.broadcasted_iota(jnp.int32, place.shape, 0) == dest
-    place[...] = jnp.where(hit, 1.0, 0.0).astype(BF16)
+    hit = jnp.where(hit, 1.0, 0.0).astype(BF16)
+    place[...] = hit
+    tile_cols = cols // TS
+    column = lax.broadcasted_iota(jnp.int32, (tiles, 4 * SUB), 1)
+    wanted = (column % SUB) * tile_cols + ((column // SUB) & 1) * (tile_cols - 1)
+    picked = lax.broadcasted_iota(jnp.int32, (tiles, 4 * SUB), 0) == wanted
+    place_edge[...] = dot(hit, jnp.where(picked, 1.0, 0.0).astype(BF16)).astype(BF16)
 
 
 def yee(bufs, keys, eps_of, change_of, src_of, grad, coef_x, coef_first, next_col, prev_col, other):
@@ -323,7 +329,7 @@
     return even + ref[lead + (pl.ds(1, count, stride=PIX), slice(None))]
 
 
-def inner_kernel(fields, eps, fwd, cross, near, src, base_in, last, g, base, a, b, e):
+def inner_kernel(fields, eps, fwd, cross, near, src, last, g_out, base, a, b, c, e, g):
     rows, cols = fields.shape[2], fields.shape[3]
     n_tiles = (rows + 2 * PAD) // SUB
     n_lanes = cols // LANES
@@ -335,7 +341,7 @@
             return halo_tile(cross, near, odd, halo_of[t], kind, layer, lane_tile(k))
         return core_tile(fields, eps, fwd, pl.ds(t * SUB - PAD, SUB), kind, layer, lane_tile(k))
 
-    for buf in (a, b, last):
+    for buf in (a, b, c):
         clear_rims(buf)
     for t in range(n_tiles):
         for layer in range(2):
@@ -360,25 +366,24 @@
         }
 
     yee(
-        (a, b, last), keys,
+        (a, b, c), keys,
         lambda key, t: e[key + (pl.ds(t * SUB, SUB), slice(None))],
         lambda step, key, t: load(4 + step, key[0], t, key[1]),
         lambda step, key, t: src[step, key[0], pl.ds(t * SUB, SUB), lane_tile(key[1])],
         g, COURANT, coef_above(), next_col, prev_col,
         lambda values, key: values[1 - key[0], key[1]],
     )
-    for t in range(n_tiles):
+    last[...] = c[:, :, :, pl.ds(SUB + PAD, rows), :]
+    g_out[...] = g[...]
+    for t, row in halo_of.items():
         for kind in range(4 + STEPS):
-            at = pl.ds(t * SUB, SUB)
-            if t not in halo_of:
-                base[kind, at, :] = base_in[kind, at, :]
-            elif kind < 4 or t not in (0, n_tiles - 1):
-                base[kind, at, :] = edge_tile(
+            if kind < 4 or row in (1, 2):
+                base[kind, pl.ds(row * SUB, SUB), :] = edge_tile(
                     lambda kind, layer, k: load(kind, layer, t, k), kind, lane, n_lanes
                 )
 
 
-def inner_tiles_kernel(g, mats, vals, pooled):
+def inner_tiles_kernel(g, mats, place, slots, pooled):
     n_lanes, ext_rows = g.shape[1], g.shape[2]
     for layer in range(2):
         total = None
@@ -389,7 +394,9 @@
         pooled[layer] = total
 
     out_pix = ext_rows // PIX - 2 * PAD // PIX
-    vals[...] = by_tile([cone_filter(pooled.at[layer], out_pix, PAD // PIX) for layer in range(2)])
+    vals = by_tile([cone_filter(pooled.at[layer], out_pix, PAD // PIX) for layer in range(2)])
+    high, low = split2(vals)
+    slots[...] = dot(place[...], high) + dot(place[...], low)
 
 
 def cone_filter(pooled, out_pix, first):
@@ -434,24 +441,27 @@
     return jnp.stack([new_even, new_odd], axis=1).reshape(tile_rows * 2 * span, LANES)
 
 
-def merge_spans(rows_of, lane):
+def merge_spans(spans, lane):
     even = (lane & 1) == 0
     window = ((lane - OUT) & (HALF - 1)) < SIDE
     merged = []
     for e in (0, 4):
-        low = jnp.where(even, rows_of(e), turn(rows_of(e + 1), 1, 1))
-        high = jnp.where(even, turn(rows_of(e + 2), SIDE, 1), turn(rows_of(e + 3), SIDE + 1, 1))
+        low = jnp.where(even, spans[e], turn(spans[e + 1], 1, 1))
+        high = jnp.where(even, turn(spans[e + 2], SIDE, 1), turn(spans[e + 3], SIDE + 1, 1))
         merged.append(jnp.where(window, low, high))
     return jnp.concatenate(merged, axis=1)
 
 
-def edge_kernel(base, cross, near, src, c, g, a, b, e, d):
-    ext_rows = base.shape[1]
-    rows = ext_rows - 2 * PAD
+def edge_kernel(
+    slots_in, base, base_halo, cross, near, src, place, spread, last, slots, a, b, c, e, d, g
+):
+    rows = base.shape[1]
+    ext_rows = rows + 2 * PAD
     n_tiles = ext_rows // SUB
     lane, odd = lanes(), is_odd("gy")
     spot = lane & (HALF - 1)
     is_left, is_right = spot < OUT, spot >= HALF - OUT
+    halo_of = {0: 0, 1: 1, n_tiles - 2: 2, n_tiles - 1: 3}
 
     for buf in (a, b, c):
         clear_rims(buf)
@@ -462,7 +472,11 @@
         for kind, width in enumerate(WIDTHS):
             if kind >= 4 and t in (0, n_tiles - 1):
                 continue
-            value = jnp.where(is_left, turn(high, OUT - width - FIRST[kind], 1), base[kind, at, :])
+            if t in halo_of:
+                value = base_halo[kind, pl.ds(halo_of[t] * SUB, SUB), :]
+            else:
+                value = base[kind, pl.ds(t * SUB - PAD, SUB), :]
+            value = jnp.where(is_left, turn(high, OUT - width - FIRST[kind], 1), value)
             value = jnp.where(is_right, turn(low, HALF - OUT - FIRST[kind], 1), value)
             if kind < 3:
                 a[kind, pl.ds(SUB + t * SUB, SUB), :] = value
@@ -486,46 +500,35 @@
 
     inside = (spot >= OUT - NEAR) & (spot < OUT + KEEP)
     inside = inside | ((spot >= HALF - OUT - KEEP) & (spot < HALF - OUT + NEAR))
-    for t in range(1, n_tiles - 1):
-        at = pl.ds(t * SUB, SUB)
-        g[at, :] = jnp.where(inside, g[at, :], 0.0)
-
-
-def tiles_kernel(vals_in, g, place, spread, out_slots, pooled, pixels, vals):
-    ext_rows = g.shape[0]
-    rows = ext_rows - 2 * PAD
-    lane = lanes()
-    summed = row_pairs(g, (), ext_rows // PIX)
-    pooled[...] = summed + turn(summed, -1, 1)
+    span, reach = TS // PIX, RADIUS - 1
+    pixel = {}
+    for j in range(-reach, span + reach):
+        value = g[pl.ds(PAD + PIX * j, SUB, stride=TS), :]
+        value = jnp.where(inside, value + g[pl.ds(PAD + PIX * j + 1, SUB, stride=TS), :], 0.0)
+        pixel[j] = value + turn(value, -1, 1)
+
     weights = cone_weights(RADIUS)
-    reach = RADIUS - 1
-    out_pix, top = rows // PIX, PAD // PIX
-    at = [pooled[pl.ds(top + s, out_pix), :] for s in range(-reach, reach + 1)]
-    sums = [at[reach]] + [at[reach + s] + at[reach - s] for s in range(1, reach + 1)]
-    total = None
-    for shift in range(reach + 1):
-        mixed = None
-        for s in range(reach + 1):
-            weight = float(weights[reach + s, reach + shift])
-            if weight > 0.0:
-                term = weight * sums[s]
-                mixed = term if mixed is None else mixed + term
-        if shift:
-            mixed = turn(mixed, -PIX * shift, 1) + turn(mixed, PIX * shift, 1)
-        total = mixed if total is None else total + mixed
-    pixels[...] = total
-
-    span = TS // PIX
-    tile_rows, tile_cols = rows // TS, vals.shape[0] // (rows // TS)
-    merged = merge_spans(lambda row: pixels[pl.ds(row, tile_rows, stride=span), :], lane)
-    high, low = split2(merged)
-    edge = dot(high, spread[...]) + dot(low, spread[...])
-    vals[...] = vals_in[...]
-    for side, row in enumerate((0, tile_cols - 1)):
-        spots = pl.ds(row, tile_rows, stride=tile_cols)
-        vals[spots, :] = vals[spots, :] + edge[:, side * LANES : (side + 1) * LANES]
-    high, low = split2(vals[...])
-    out_slots[...] = dot(place[...], high) + dot(place[...], low)
+    spans = []
+    for row in range(span):
+        sums = [pixel[row]] + [pixel[row + s] + pixel[row - s] for s in range(1, reach + 1)]
+        total = None
+        for shift in range(reach + 1):
+            mixed = None
+            for s in range(reach + 1):
+                weight = float(weights[reach + s, reach + shift])
+                if weight > 0.0:
+                    term = weight * sums[s]
+                    mixed = term if mixed is None else mixed + term
+            if shift:
+                mixed = turn(mixed, -PIX * shift, 1) + turn(mixed, PIX * shift, 1)
+            total = mixed if total is None else total + mixed
+        spans.append(total)
+
+    edge = dot(jnp.concatenate(split2(merge_spans(spans, lane)), axis=0), spread[...])
+    edge = edge[:SUB] + edge[SUB:]
+    edge = jnp.concatenate([edge[:, :LANES], edge[:, LANES:]], axis=0)
+    slots[...] = slots_in[...] + dot(place[...], jnp.concatenate(split2(edge), axis=0))
+    last[...] = c[:, pl.ds(SUB + PAD, rows), :]
 
 
 def merge_kernel(last, edge_last, out_fields, merged, sem):
@@ -533,7 +536,7 @@
     n_lanes = cols // LANES
     lane = lanes()
     for t in range(rows // SUB):
-        at, out_at = pl.ds(SUB + PAD + t * SUB, SUB), pl.ds(t * SUB, SUB)
+        at = pl.ds(t * SUB, SUB)
         for kind in range(3):
             edge = edge_last[kind, at, :]
             for layer in range(2):
@@ -545,7 +548,7 @@
                         value = jnp.where(
                             lane >= LANES - KEEP, turn(edge, -HALF * layer - SIDE - OUT, 1), value
                         )
-                    merged[kind, layer, out_at, lane_tile(k)] = value
+                    merged[kind, layer, at, lane_tile(k)] = value
     copy = pltpu.make_async_copy(merged, out_fields, sem)
     copy.start()
     copy.wait()
@@ -607,15 +610,16 @@
 
     packed = shape(ext_rows, LANES)
     channels = mon_x.shape[0]
-    cross_cols, near_cols, base, src, src_edge, place = call(
+    cross_cols, near_cols, base, src, src_edge, place, place_edge = call(
         lambda *refs: prep_kernel(capacity, *refs),
         (
             packed,
             packed,
-            shape(4 + STEPS, ext_rows, LANES),
+            shape(4 + STEPS, rows, LANES),
             shape(STEPS, 2, ext_rows, cols),
             shape(STEPS, ext_rows, LANES),
             shape(owners * capacity, tiles, dtype=BF16),
+            shape(owners * capacity, 4 * SUB, dtype=BF16),
         ),
         8,
         flops=16 * ext_rows * (cols + LANES) * 3 * channels,
@@ -635,53 +639,49 @@
     near_cols = lax.ppermute(near_cols, "gy", pairs(gy_count, 0))
 
     state = (3, 2, n_lanes, ext_rows + 2 * SUB, LANES)
-    last, g, base = call(
+    last, g, base_halo = call(
         inner_kernel,
-        (shape(*state), shape(2, n_lanes, ext_rows, LANES), shape(4 + STEPS, ext_rows, LANES)),
-        7,
+        (
+            shape(3, 2, n_lanes, rows, LANES),
+            shape(2, n_lanes, ext_rows, LANES),
+            shape(4 + STEPS, 2 * PAD, LANES),
+        ),
+        6,
         scratch=(
             pltpu.VMEM(state, F32),
             pltpu.VMEM(state, F32),
+            pltpu.VMEM(state, F32),
+            pltpu.VMEM((2, n_lanes, ext_rows, LANES), F32),
             pltpu.VMEM((2, n_lanes, ext_rows, LANES), F32),
         ),
         flops=200 * cells,
         size=96 * cells,
-    )(*blocks, cross, near, src, base)
-    (vals,) = call(
+    )(*blocks, cross, near, src)
+    (slots,) = call(
         inner_tiles_kernel,
-        (shape(tiles, LANES),),
-        2,
+        (shape(owners * capacity, width),),
+        3,
         scratch=(pltpu.VMEM((2, ext_rows // PIX, LANES), F32),),
         flops=100 * cells,
         size=32 * cells,
-    )(g, pool_matrices())
+    )(g, pool_matrices(), place)
 
     edge_state = (3, ext_rows + 2 * SUB, LANES)
-    edge_last, edge_g = call(
+    edge_last, outgoing = call(
         edge_kernel,
-        (shape(*edge_state), shape(ext_rows, LANES)),
-        4,
+        (shape(3, rows, LANES), shape(owners * capacity, width)),
+        8,
         scratch=(
+            pltpu.VMEM(edge_state, F32),
             pltpu.VMEM(edge_state, F32),
             pltpu.VMEM(edge_state, F32),
             pltpu.VMEM((ext_rows, LANES), F32),
             pltpu.VMEM((STEPS, ext_rows, LANES), F32),
+            pltpu.VMEM((ext_rows, LANES), F32),
         ),
         flops=50 * cells,
         size=16 * cells,
-    )(base, cross_cols, near_cols, src_edge)
-    (outgoing,) = call(
-        tiles_kernel,
-        (shape(owners * capacity, width),),
-        4,
-        scratch=(
-            pltpu.VMEM((ext_rows // PIX, LANES), F32),
-            pltpu.VMEM((rows // PIX, LANES), F32),
-            pltpu.VMEM((tiles, LANES), F32),
-        ),
-        flops=50 * cells,
-        size=16 * cells,
-    )(vals, edge_g, place, spread_matrix())
+    )(slots, base, base_halo, cross_cols, near_cols, src_edge, place_edge, spread_matrix())
     (fields,) = call(
         merge_kernel,
         (shape(3, 2, rows, cols),),

time: 34.1 us -> 34 us (level)
    pallas_call x4 -> x3, Pallas kernels: 7.09 us -> 7 us  [the longest x1 4.11 us: on_device(): call(inner_kernel, (shape(3, 2, n_lanes, rows, LANES), shape(2, n_lanes,...]
where the time goes in v5:
time: 34 us; the launch traced here: 33.7 us
  starting transfers between devices  14.4 us (42%)
  Pallas kernels  11.5 us (34%)
  waiting for transfers between devices  6.2 us (18%)
  between operations  0.85 us (2%)
  local copies, waits for them, and re-layouts  0.7 us (2%)
    all_to_all x1, waiting for transfers between devices, on_device(): lax.all_to_all(outgoing, ('gx', 'gy'), split_axis=0, concat_axis=0, tiled...  6.19 us
    ppermute x1, starting transfers between devices, on_device(): near_cols = lax.ppermute(near_cols, 'gy', pairs(gy_count, 0))  4.46 us
    ppermute x1, starting transfers between devices, on_device(): near = lax.ppermute(near, 'gx', pairs(gx_count, 0))  4.36 us
    all_to_all x1, starting transfers between devices, on_device(): lax.all_to_all(outgoing, ('gx', 'gy'), split_axis=0, concat_axis=0, tiled...  4.29 us
    pallas_call x1, Pallas kernels, on_device(): call(inner_kernel, (shape(3, 2, n_lanes, rows, LANES), shape(2, n_lanes,...  4.11 us
    pallas_call x1, Pallas kernels, on_device(): call(edge_kernel, (shape(3, rows, LANES), shape(owners * capacity, width)...  2.04 us
    pallas_call x1, Pallas kernels, on_device(): call(lambda *refs: prep_kernel(capacity, *refs), (packed, packed, shape(4...  1.99 us
    pallas_call x1, Pallas kernels, on_device(): call(rows_kernel, (strip, strip), 3, in_space=pltpu.HBM, scratch=(pltpu.V...  1.21 us
  transfers between devices with their start and end apart: 5, of which 1 were waited for; matrix products, arithmetic and copies ran while one was open for 0% of the time, Pallas kernels for 24%

profile of v5, /device:TPU:0, one launch (start us, length us, event | category | flops | bytes accessed | tf_op | source)
XLA Modules:
  0.0 33.7 jit_solution(3277986301845344675)
XLA Ops:
  0.6 0.0 copy-start
  0.6 0.0 copy-start.2
  0.7 0.0 copy-start.1
  0.7 0.0 copy-start.9
  0.7 0.0 copy-start.8
  0.7 0.0 copy-start.5
  0.7 0.0 copy-start.7
  0.7 0.0 copy-start.6
  0.7 1.2 %shard_map.113 = (f32[16,8,256]{2,1,0:T(8,128)S(1)}, f32[16,8,256]{2,1,0:T(8,128)S(1)}) custom-call(f32[3,2,128,256]{3,2,1,0:T(8,128)} %fields.3, f32[2,128,256]{2,1,0:T(8,128)} %eps.3, f32[4,2,128,256]{3,2,1,0:T(8,128)} %fwd.3), custom_call_target="tpu_custom_call" | custom-call | bytes 1048576 | tf_op jit(solution)/shard_map/pallas_call | solution.py:594
  1.9 0.7 %collective-permute-start = (f32[16,8,256]{2,1,0:T(8,128)S(1)}, f32[16,8,256]{2,1,0:T(8,128)S(1)}, u32[]{:S(2)}, u32[]{:S(2)}) collective-permute-start(f32[16,8,256]{2,1,0:T(8,128)S(1)} %get-tuple-element.18), channel_id=1, source_target_pairs={{4,8},{8,4},{5,9},{9,5},{6,10},{10,6},{7,11},{11,7},{20,24},{24,20... | collective-permute-start | bytes 393224 | tf_op jit(solution)/shard_map/ppermute | solution.py:608
  2.6 4.4 %collective-permute-start.1 = (f32[16,8,256]{2,1,0:T(8,128)S(1)}, f32[16,8,256]{2,1,0:T(8,128)S(1)}, u32[]{:S(2)}, u32[]{:S(2)}) collective-permute-start(f32[16,8,256]{2,1,0:T(8,128)S(1)} %get-tuple-element.19), channel_id=1, source_target_pairs={{0,4},{8,12},{4,0},{12,8},{1,5},{9,13},{5,1},{13,9},{2,6},{10,14},... | collective-permute-start | bytes 393224 | tf_op jit(solution)/shard_map/ppermute | solution.py:609
  7.0 0.0 copy-done
  7.0 0.0 copy-done.2
  7.0 0.0 copy-done.1
  7.0 0.0 copy-done.9
  7.0 0.0 copy-done.8
  7.0 0.0 copy-done.5
  7.0 0.0 copy-done.7
  7.0 0.0 copy-done.6
  7.0 2.0 %shard_map.114 = (f32[160,128]{1,0:T(8,128)S(1)}, f32[160,128]{1,0:T(8,128)S(1)}, f32[8,128,128]{2,1,0:T(8,128)S(1)}, f32[4,2,160,256]{3,2,1,0:T(8,128)S(1)}, f3...) custom-call(f32[3,2,128,256]{3,2,1,0:T(8,128)S(1)} %copy-done.1, ...), custom_call_target="tpu_custom_call" | custom-call | flops 188743680 | bytes 2097152 | tf_op jit(solution)/shard_map/pallas_call | solution.py:613
  9.0 0.0 collective-permute-done.cross.cross_rows
  9.0 0.0 collective-permute-done.1.near.near_rows
  9.0 0.2 shard_map.117
  9.2 0.7 %collective-permute-start.2 = (f32[160,128]{1,0:T(8,128)S(1)}, f32[160,128]{1,0:T(8,128)S(1)}, u32[]{:S(2)}, u32[]{:S(2)}) collective-permute-start(f32[160,128]{1,0:T(8,128)S(1)} %get-tuple-element.28), channel_id=1, source_target_pairs={{1,2},{2,1},{5,6},{6,5},{9,10},{10,9},{13,14},{14,13},{17,18},{18,... | collective-permute-start | bytes 245768 | tf_op jit(solution)/shard_map/ppermute | solution.py:638
  9.9 4.5 %collective-permute-start.3 = (f32[160,128]{1,0:T(8,128)S(1)}, f32[160,128]{1,0:T(8,128)S(1)}, u32[]{:S(2)}, u32[]{:S(2)}) collective-permute-start(f32[160,128]{1,0:T(8,128)S(1)} %get-tuple-element.29), channel_id=1, source_target_pairs={{0,1},{2,3},{1,0},{3,2},{4,5},{6,7},{5,4},{7,6},{8,9},{10,11},{9,8... | collective-permute-start | bytes 245768 | tf_op jit(solution)/shard_map/ppermute | solution.py:639
  14.3 0.0 copy-start.4
  14.4 0.0 copy-start.3
  14.4 4.1 %shard_map.115 = (f32[3,2,2,128,128]{4,3,2,1,0:T(8,128)S(1)}, f32[2,2,160,128]{3,2,1,0:T(8,128)S(1)}, f32[8,32,128]{2,1,0:T(8,128)S(1)}) custom-call(f32[3,2,128,256]{3,2,1,0:T(8,128)S(1)} %copy-done.1, f32[2,128,256]{2,1,0:T(8,128)S(1)} %copy-done.2, f32[4,2,128,256]{3,2,1,0:T(8,128)S(1)} %copy-done, ...), custom_call_target="tpu_custom_call" | custom-call | flops 6553600 | bytes 3145728 | tf_op jit(solution)/shard_map/pallas_call | solution.py:642
  18.5 0.0 copy-done.4
  18.5 0.8 %shard_map.116.slots_in = f32[256,128]{1,0:T(8,128)S(1)} custom-call(f32[2,2,160,128]{3,2,1,0:T(8,128)S(1)} %get-tuple-element.22.g, bf16[2,128,128]{2,1,0:T(8,128)(2,1)S(1)} %copy-done.4, bf16[256,128]{1,0:T(8,128)(2,1)S(1)} %get-tuple-element.23.place), custom_call_target="tpu_custom_call" | custom-call | flops 3276800 | bytes 1048576 | tf_op jit(solution)/shard_map/pallas_call | solution.py:660
  19.3 0.0 collective-permute-done.2.cross
  19.3 0.0 collective-permute-done.3.near
  19.4 0.0 copy-done.3
  19.4 2.0 %shard_map.118 = (f32[3,128,128]{2,1,0:T(8,128)S(1)}, f32[256,128]{1,0:T(8,128)}) custom-call(f32[256,128]{1,0:T(8,128)S(1)} %shard_map.116.slots_in, f32[8,128,128]{2,1,0:T(8,128)S(1)} %get-tuple-element.24.base, f32[8,32,128]{2,1,0:T(8,128)S(1)} %get-tuple-element.25.base_halo, f32[160,128]{1,0:T(8,128)S(1)} %collective-permute-done.2.cross, ...), custom_call_target="tpu_custom_call" | custom-call | flops 1638400 | bytes 524288 | tf_op jit(solution)/shard_map/pallas_call | solution.py:670
  21.4 4.3 %all-to-all-start = ((f32[16,16,128]{2,1,0:T(8,128)}), f32[16,16,128]{2,1,0:T(8,128)S(1)}, u32[]{:S(2)}, u32[]{:S(2)}) async-start(f32[16,16,128]{2,1,0:T(8,128)} %bitcast.4), calls=%async_computation | async-start | bytes 262144 | tf_op jit(solution)/shard_map/all_to_all | solution.py:696
  25.7 1.2 %shard_map.119 = f32[3,2,128,256]{3,2,1,0:T(8,128)} custom-call(f32[3,2,2,128,128]{4,3,2,1,0:T(8,128)S(1)} %get-tuple-element.21.last, f32[3,128,128]{2,1,0:T(8,128)S(1)} %get-tuple-element.32.edge_last), custom_call_target="tpu_custom_call" | custom-call | flops 655360 | bytes 1572864 | tf_op jit(solution)/shard_map/pallas_call | solution.py:685
  26.9 6.2 %all-to-all-done = f32[16,16,128]{2,1,0:T(8,128)S(1)} async-done(((f32[16,16,128]{2,1,0:T(8,128)}), f32[16,16,128]{2,1,0:T(8,128)S(1)}, u32[]{:S(2)}, u32[]{:S(2)}) %all-to-all-start) | async-done | bytes 131104 | tf_op jit(solution)/shard_map/all_to_all | solution.py:696
  33.1 0.7 %copy.13 = f32[1,16,16,128]{3,2,1,0:T(8,128)} copy(f32[1,16,16,128]{3,2,1,0:T(8,128)S(1)} %bitcast.10) | data formatting | bytes 262144
Async XLA Ops:
  0.6 6.3 %copy-start = (f32[4,2,128,256]{3,2,1,0:T(8,128)S(1)}, f32[4,2,128,256]{3,2,1,0:T(8,128)}, u32[]{:S(2)}) copy-start(f32[4,2,128,256]{3,2,1,0:T(8,128)} %fwd.3) | copy-start | bytes 3145732
  0.6 6.3 %copy-start.2 = (f32[2,128,256]{2,1,0:T(8,128)S(1)}, f32[2,128,256]{2,1,0:T(8,128)}, u32[]{:S(2)}) copy-start(f32[2,128,256]{2,1,0:T(8,128)} %eps.3) | copy-start | bytes 786436
  0.7 6.3 %copy-start.1 = (f32[3,2,128,256]{3,2,1,0:T(8,128)S(1)}, f32[3,2,128,256]{3,2,1,0:T(8,128)}, u32[]{:S(2)}) copy-start(f32[3,2,128,256]{3,2,1,0:T(8,128)} %fields.3) | copy-start | bytes 2359300
  0.7 6.3 %copy-start.9 = (s32[1,1,128,1]{2,3,1,0:T(1,128)S(1)}, s32[1,1,128,1]{2,3,1,0:T(1,128)}, u32[]{:S(2)}) copy-start(s32[1,1,128,1]{2,3,1,0:T(1,128)} %param.17) | copy-start | bytes 1540
  0.7 6.3 %copy-start.8 = (s32[1,1,128]{2,1,0:T(1,128)S(1)}, s32[1,1,128]{2,1,0:T(1,128)}, u32[]{:S(2)}) copy-start(s32[1,1,128]{2,1,0:T(1,128)} %param.16) | copy-start | bytes 1540
  0.7 6.3 %copy-start.5 = (f32[4,64]{1,0:T(4,128)S(1)}, f32[4,64]{1,0:T(4,128)}, u32[]{:S(2)}) copy-start(f32[4,64]{1,0:T(4,128)} %refs_5_.1) | copy-start | bytes 3076
  0.7 6.3 %copy-start.7 = (s32[64]{0:T(128)S(1)}, s32[64]{0:T(128)}, u32[]{:S(2)}) copy-start(s32[64]{0:T(128)} %param.14) | copy-start | bytes 772
  0.7 6.3 %copy-start.6 = (s32[64]{0:T(128)S(1)}, s32[64]{0:T(128)}, u32[]{:S(2)}) copy-start(s32[64]{0:T(128)} %param.13) | copy-start | bytes 772
  1.9 7.1 %collective-permute-start = (f32[16,8,256]{2,1,0:T(8,128)S(1)}, f32[16,8,256]{2,1,0:T(8,128)S(1)}, u32[]{:S(2)}, u32[]{:S(2)}) collective-permute-start(f32[16,8,256]{2,1,0:T(8,128)S(1)} %get-tuple-element.18), channel_id=1, source_target_pairs={{4,8},{8,4},{5,9},{9,5},{6,10},{10,6},{7,11},{11,7},{20,24},{24,20... | collective-permute-start | bytes 393224 | tf_op jit(solution)/shard_map/ppermute | solution.py:608
  2.6 6.4 %collective-permute-start.1 = (f32[16,8,256]{2,1,0:T(8,128)S(1)}, f32[16,8,256]{2,1,0:T(8,128)S(1)}, u32[]{:S(2)}, u32[]{:S(2)}) collective-permute-start(f32[16,8,256]{2,1,0:T(8,128)S(1)} %get-tuple-element.19), channel_id=1, source_target_pairs={{0,4},{8,12},{4,0},{12,8},{1,5},{9,13},{5,1},{13,9},{2,6},{10,14},... | collective-permute-start | bytes 393224 | tf_op jit(solution)/shard_map/ppermute | solution.py:609
  9.2 10.1 %collective-permute-start.2 = (f32[160,128]{1,0:T(8,128)S(1)}, f32[160,128]{1,0:T(8,128)S(1)}, u32[]{:S(2)}, u32[]{:S(2)}) collective-permute-start(f32[160,128]{1,0:T(8,128)S(1)} %get-tuple-element.28), channel_id=1, source_target_pairs={{1,2},{2,1},{5,6},{6,5},{9,10},{10,9},{13,14},{14,13},{17,18},{18,... | collective-permute-start | bytes 245768 | tf_op jit(solution)/shard_map/ppermute | solution.py:638
  9.9 9.5 %collective-permute-start.3 = (f32[160,128]{1,0:T(8,128)S(1)}, f32[160,128]{1,0:T(8,128)S(1)}, u32[]{:S(2)}, u32[]{:S(2)}) collective-permute-start(f32[160,128]{1,0:T(8,128)S(1)} %get-tuple-element.29), channel_id=1, source_target_pairs={{0,1},{2,3},{1,0},{3,2},{4,5},{6,7},{5,4},{7,6},{8,9},{10,11},{9,8... | collective-permute-start | bytes 245768 | tf_op jit(solution)/shard_map/ppermute | solution.py:639
  14.3 4.1 %copy-start.4 = (bf16[2,128,128]{2,1,0:T(8,128)(2,1)S(1)}, bf16[2,128,128]{2,1,0:T(8,128)(2,1)}, u32[]{:S(2)}) copy-start(bf16[2,128,128]{2,1,0:T(8,128)(2,1)} %constant.4.clone.mats) | copy-start | bytes 196612
  14.4 5.0 %copy-start.3 = (bf16[256,256]{1,0:T(8,128)(2,1)S(1)}, bf16[256,256]{1,0:T(8,128)(2,1)}, u32[]{:S(2)}) copy-start(bf16[256,256]{1,0:T(8,128)(2,1)} %constant.5.clone.spread) | copy-start | bytes 393220
  21.4 11.6 %all-to-all-start = ((f32[16,16,128]{2,1,0:T(8,128)}), f32[16,16,128]{2,1,0:T(8,128)S(1)}, u32[]{:S(2)}, u32[]{:S(2)}) async-start(f32[16,16,128]{2,1,0:T(8,128)} %bitcast.4), calls=%async_computation | async-start | bytes 262144 | tf_op jit(solution)/shard_map/all_to_all | solution.py:696

commit v6 on v5

--- a/solution.py
+++ b/solution.py
@@ -192,7 +192,7 @@
         cross[out_at, :] = jnp.where(odd, right, left)
         near[out_at, :] = jnp.where(odd, left, right)
         for kind in range(4 + STEPS):
-            base[kind, at, :] = edge_tile(load, kind, lane, n_lanes)
+            base[kind, out_at, :] = edge_tile(load, kind, lane, n_lanes)
         return carry
 
     lax.fori_loop(0, rows // SUB, tile, 0, unroll=4)
@@ -329,7 +329,7 @@
     return even + ref[lead + (pl.ds(1, count, stride=PIX), slice(None))]
 
 
-def inner_kernel(fields, eps, fwd, cross, near, src, last, g_out, base, a, b, c, e, g):
+def inner_kernel(fields, eps, fwd, cross, near, src, mats, base_in, place, last, slots, base, a, b, e, g, pooled):
     rows, cols = fields.shape[2], fields.shape[3]
     n_tiles = (rows + 2 * PAD) // SUB
     n_lanes = cols // LANES
@@ -341,7 +341,7 @@
             return halo_tile(cross, near, odd, halo_of[t], kind, layer, lane_tile(k))
         return core_tile(fields, eps, fwd, pl.ds(t * SUB - PAD, SUB), kind, layer, lane_tile(k))
 
-    for buf in (a, b, c):
+    for buf in (a, b, last):
         clear_rims(buf)
     for t in range(n_tiles):
         for layer in range(2):
@@ -366,37 +366,34 @@
         }
 
     yee(
-        (a, b, c), keys,
+        (a, b, last), keys,
         lambda key, t: e[key + (pl.ds(t * SUB, SUB), slice(None))],
         lambda step, key, t: load(4 + step, key[0], t, key[1]),
         lambda step, key, t: src[step, key[0], pl.ds(t * SUB, SUB), lane_tile(key[1])],
         g, COURANT, coef_above(), next_col, prev_col,
         lambda values, key: values[1 - key[0], key[1]],
     )
-    last[...] = c[:, :, :, pl.ds(SUB + PAD, rows), :]
-    g_out[...] = g[...]
-    for t, row in halo_of.items():
-        for kind in range(4 + STEPS):
-            if kind < 4 or row in (1, 2):
-                base[kind, pl.ds(row * SUB, SUB), :] = edge_tile(
-                    lambda kind, layer, k: load(kind, layer, t, k), kind, lane, n_lanes
-                )
-
-
-def inner_tiles_kernel(g, mats, place, slots, pooled):
-    n_lanes, ext_rows = g.shape[1], g.shape[2]
     for layer in range(2):
         total = None
         for k in range(n_lanes):
-            for part in split2(row_pairs(g, (layer, k), ext_rows // PIX)):
+            for part in split2(row_pairs(g, (layer, k), n_tiles * SUB // PIX)):
                 term = dot(part, mats[k])
                 total = term if total is None else total + term
         pooled[layer] = total
 
-    out_pix = ext_rows // PIX - 2 * PAD // PIX
-    vals = by_tile([cone_filter(pooled.at[layer], out_pix, PAD // PIX) for layer in range(2)])
+    vals = by_tile([cone_filter(pooled.at[layer], rows // PIX, PAD // PIX) for layer in range(2)])
     high, low = split2(vals)
     slots[...] = dot(place[...], high) + dot(place[...], low)
+
+    for t in range(n_tiles):
+        for kind in range(4 + STEPS):
+            at = pl.ds(t * SUB, SUB)
+            if t not in halo_of:
+                base[kind, at, :] = base_in[kind, at, :]
+            elif kind < 4 or t not in (0, n_tiles - 1):
+                base[kind, at, :] = edge_tile(
+                    lambda kind, layer, k: load(kind, layer, t, k), kind, lane, n_lanes
+                )
 
 
 def cone_filter(pooled, out_pix, first):
@@ -453,15 +450,14 @@
 
 
 def edge_kernel(
-    slots_in, base, base_halo, cross, near, src, place, spread, last, slots, a, b, c, e, d, g
+    last, slots_in, base, cross, near, src, place, spread, out_fields, slots, a, b, c, e, d, g, merged, sem
 ):
-    rows = base.shape[1]
-    ext_rows = rows + 2 * PAD
+    ext_rows = base.shape[1]
+    rows = ext_rows - 2 * PAD
     n_tiles = ext_rows // SUB
     lane, odd = lanes(), is_odd("gy")
     spot = lane & (HALF - 1)
     is_left, is_right = spot < OUT, spot >= HALF - OUT
-    halo_of = {0: 0, 1: 1, n_tiles - 2: 2, n_tiles - 1: 3}
 
     for buf in (a, b, c):
         clear_rims(buf)
@@ -472,11 +468,7 @@
         for kind, width in enumerate(WIDTHS):
             if kind >= 4 and t in (0, n_tiles - 1):
                 continue
-            if t in halo_of:
-                value = base_halo[kind, pl.ds(halo_of[t] * SUB, SUB), :]
-            else:
-                value = base[kind, pl.ds(t * SUB - PAD, SUB), :]
-            value = jnp.where(is_left, turn(high, OUT - width - FIRST[kind], 1), value)
+            value = jnp.where(is_left, turn(high, OUT - width - FIRST[kind], 1), base[kind, at, :])
             value = jnp.where(is_right, turn(low, HALF - OUT - FIRST[kind], 1), value)
             if kind < 3:
                 a[kind, pl.ds(SUB + t * SUB, SUB), :] = value
@@ -497,6 +489,24 @@
         lambda values: {(): turn(values[()], 1, 1)},
         lambda values, key: turn(values[()], HALF, 1),
     )
+
+    n_lanes = merged.shape[3] // LANES
+    for t in range(rows // SUB):
+        at, out_at = pl.ds(SUB + PAD + t * SUB, SUB), pl.ds(t * SUB, SUB)
+        for kind in range(3):
+            edge = c[kind, at, :]
+            for layer in range(2):
+                for k in range(n_lanes):
+                    value = last[kind, layer, k, at, :]
+                    if k == 0:
+                        value = jnp.where(lane < KEEP, turn(edge, -HALF * layer - OUT, 1), value)
+                    if k == n_lanes - 1:
+                        value = jnp.where(
+                            lane >= LANES - KEEP, turn(edge, -HALF * layer - SIDE - OUT, 1), value
+                        )
+                    merged[kind, layer, out_at, lane_tile(k)] = value
+    copy = pltpu.make_async_copy(merged, out_fields, sem)
+    copy.start()
 
     inside = (spot >= OUT - NEAR) & (spot < OUT + KEEP)
     inside = inside | ((spot >= HALF - OUT - KEEP) & (spot < HALF - OUT + NEAR))
@@ -528,29 +538,6 @@
     edge = edge[:SUB] + edge[SUB:]
     edge = jnp.concatenate([edge[:, :LANES], edge[:, LANES:]], axis=0)
     slots[...] = slots_in[...] + dot(place[...], jnp.concatenate(split2(edge), axis=0))
-    last[...] = c[:, pl.ds(SUB + PAD, rows), :]
-
-
-def merge_kernel(last, edge_last, out_fields, merged, sem):
-    rows, cols = merged.shape[2], merged.shape[3]
-    n_lanes = cols // LANES
-    lane = lanes()
-    for t in range(rows // SUB):
-        at = pl.ds(t * SUB, SUB)
-        for kind in range(3):
-            edge = edge_last[kind, at, :]
-            for layer in range(2):
-                for k in range(n_lanes):
-                    value = last[kind, layer, k, at, :]
-                    if k == 0:
-                        value = jnp.where(lane < KEEP, turn(edge, -HALF * layer - OUT, 1), value)
-                    if k == n_lanes - 1:
-                        value = jnp.where(
-                            lane >= LANES - KEEP, turn(edge, -HALF * layer - SIDE - OUT, 1), value
-                        )
-                    merged[kind, layer, at, lane_tile(k)] = value
-    copy = pltpu.make_async_copy(merged, out_fields, sem)
-    copy.start()
     copy.wait()
 
 
@@ -615,7 +602,7 @@
         (
             packed,
             packed,
-            shape(4 + STEPS, rows, LANES),
+            shape(4 + STEPS, ext_rows, LANES),
             shape(STEPS, 2, ext_rows, cols),
             shape(STEPS, ext_rows, LANES),
             shape(owners * capacity, tiles, dtype=BF16),
@@ -639,38 +626,27 @@
     near_cols = lax.ppermute(near_cols, "gy", pairs(gy_count, 0))
 
     state = (3, 2, n_lanes, ext_rows + 2 * SUB, LANES)
-    last, g, base_halo = call(
+    last, slots, base = call(
         inner_kernel,
-        (
-            shape(3, 2, n_lanes, rows, LANES),
-            shape(2, n_lanes, ext_rows, LANES),
-            shape(4 + STEPS, 2 * PAD, LANES),
-        ),
-        6,
+        (shape(*state), shape(owners * capacity, width), shape(4 + STEPS, ext_rows, LANES)),
+        9,
         scratch=(
-            pltpu.VMEM(state, F32),
             pltpu.VMEM(state, F32),
             pltpu.VMEM(state, F32),
             pltpu.VMEM((2, n_lanes, ext_rows, LANES), F32),
             pltpu.VMEM((2, n_lanes, ext_rows, LANES), F32),
+            pltpu.VMEM((2, ext_rows // PIX, LANES), F32),
         ),
         flops=200 * cells,
         size=96 * cells,
-    )(*blocks, cross, near, src)
-    (slots,) = call(
-        inner_tiles_kernel,
-        (shape(owners * capacity, width),),
-        3,
-        scratch=(pltpu.VMEM((2, ext_rows // PIX, LANES), F32),),
-        flops=100 * cells,
-        size=32 * cells,
-    )(g, pool_matrices(), place)
+    )(*blocks, cross, near, src, pool_matrices(), base, place)
 
     edge_state = (3, ext_rows + 2 * SUB, LANES)
-    edge_last, outgoing = call(
+    fields, outgoing = call(
         edge_kernel,
-        (shape(3, rows, LANES), shape(owners * capacity, width)),
+        (shape(3, 2, rows, cols), shape(owners * capacity, width)),
         8,
+        out_specs=(pl.BlockSpec(memory_space=pl.ANY), vmem()),
         scratch=(
             pltpu.VMEM(edge_state, F32),
             pltpu.VMEM(edge_state, F32),
@@ -678,19 +654,12 @@
             pltpu.VMEM((ext_rows, LANES), F32),
             pltpu.VMEM((STEPS, ext_rows, LANES), F32),
             pltpu.VMEM((ext_rows, LANES), F32),
+            pltpu.VMEM((3, 2, rows, cols), F32),
+            pltpu.SemaphoreType.DMA,
         ),
         flops=50 * cells,
         size=16 * cells,
-    )(slots, base, base_halo, cross_cols, near_cols, src_edge, place_edge, spread_matrix())
-    (fields,) = call(
-        merge_kernel,
-        (shape(3, 2, rows, cols),),
-        2,
-        out_specs=(pl.BlockSpec(memory_space=pl.ANY),),
-        scratch=(pltpu.VMEM((3, 2, rows, cols), F32), pltpu.SemaphoreType.DMA),
-        flops=20 * cells,
-        size=48 * cells,
-    )(last, edge_last)
+    )(last, slots, base, cross_cols, near_cols, src_edge, place_edge, spread_matrix())
 
     outgoing = outgoing.reshape(owners, capacity, width)
     incoming = lax.all_to_all(outgoing, ("gx", "gy"), split_axis=0, concat_axis=0, tiled=True)

time: 34 us -> 32.1 us (0.944)
  blocking collectives: 0 us -> 11.7 us
  waiting for transfers between devices: 6.2 us -> 0.81 us
  starting transfers between devices: 14.4 us -> 10.2 us
  Pallas kernels: 11.5 us -> 7.7 us
    all_to_all x0 -> x1, blocking collectives: none -> 11.7 us  [on_device(): lax.all_to_all(outgoing, ('gx', 'gy'), split_axis=0, concat_axis=0, tiled...]
    all_to_all x1 -> x0, waiting for transfers between devices: 6.19 us -> none  [on_device(): lax.all_to_all(outgoing, ('gx', 'gy'), split_axis=0, concat_axis=0, tiled...]
    all_to_all x1 -> x0, starting transfers between devices: 4.29 us -> none  [on_device(): lax.all_to_all(outgoing, ('gx', 'gy'), split_axis=0, concat_axis=0, tiled...]
    pallas_call x4 -> x2, Pallas kernels: 8.15 us -> 4.33 us  [the longest x1 2.33 us: on_device(): call(edge_kernel, (shape(3, 2, rows, cols), shape(owners * capacity, widt...]
    ppermute x1, waiting for transfers between devices: 0.01 us -> 0.8 us  [on_device(): near_cols = lax.ppermute(near_cols, 'gy', pairs(gy_count, 0))]
  transfers between devices with their start and end apart: 5 -> 4, of which waited for: 1 -> 1; matrix products, arithmetic and copies ran while one was open for 0% -> 0% of each run, Pallas kernels for 24% -> 13%
where the time goes in v6:
time: 32.1 us; the launch traced here: 31.9 us
  blocking collectives  11.7 us (36%)
  starting transfers between devices  10.2 us (32%)
  Pallas kernels  7.7 us (24%)
  between operations  0.82 us (3%)
  waiting for transfers between devices  0.81 us (3%)
  local copies, waits for them, and re-layouts  0.7 us (2%)
    all_to_all x1, blocking collectives, on_device(): lax.all_to_all(outgoing, ('gx', 'gy'), split_axis=0, concat_axis=0, tiled...  11.7 us
    ppermute x1, starting transfers between devices, on_device(): near_cols = lax.ppermute(near_cols, 'gy', pairs(gy_count, 0))  4.46 us
    ppermute x1, starting transfers between devices, on_device(): near = lax.ppermute(near, 'gx', pairs(gx_count, 0))  4.36 us
    pallas_call x1, Pallas kernels, on_device(): call(edge_kernel, (shape(3, 2, rows, cols), shape(owners * capacity, widt...  2.33 us
    pallas_call x1, Pallas kernels, on_device(): call(inner_kernel, (shape(*state), shape(owners * capacity, width), shape...  2 us
    pallas_call x1, Pallas kernels, on_device(): call(lambda *refs: prep_kernel(capacity, *refs), (packed, packed, shape(4...  1.99 us
    pallas_call x1, Pallas kernels, on_device(): call(rows_kernel, (strip, strip), 3, in_space=pltpu.HBM, scratch=(pltpu.V...  1.21 us
    ppermute x1, waiting for transfers between devices, on_device(): near_cols = lax.ppermute(near_cols, 'gy', pairs(gy_count, 0))  0.8 us
  transfers between devices with their start and end apart: 4, of which 1 were waited for; matrix products, arithmetic and copies ran while one was open for 0% of the time, Pallas kernels for 13%

profile of v6, /device:TPU:0, one launch (start us, length us, event | category | flops | bytes accessed | tf_op | source)
XLA Modules:
  0.0 31.9 jit_solution(14356646647918367669)
XLA Ops:
  0.6 0.0 copy-start
  0.6 0.0 copy-start.2
  0.7 0.0 copy-start.1
  0.7 0.0 copy-start.9
  0.7 0.0 copy-start.8
  0.7 0.0 copy-start.5
  0.7 0.0 copy-start.7
  0.7 0.0 copy-start.6
  0.7 1.2 %shard_map.113 = (f32[16,8,256]{2,1,0:T(8,128)S(1)}, f32[16,8,256]{2,1,0:T(8,128)S(1)}) custom-call(f32[3,2,128,256]{3,2,1,0:T(8,128)} %fields.3, f32[2,128,256]{2,1,0:T(8,128)} %eps.3, f32[4,2,128,256]{3,2,1,0:T(8,128)} %fwd.3), custom_call_target="tpu_custom_call" | custom-call | bytes 1048576 | tf_op jit(solution)/shard_map/pallas_call | solution.py:581
  1.9 0.0 copy-start.4
  1.9 0.7 %collective-permute-start = (f32[16,8,256]{2,1,0:T(8,128)S(1)}, f32[16,8,256]{2,1,0:T(8,128)S(1)}, u32[]{:S(2)}, u32[]{:S(2)}) collective-permute-start(f32[16,8,256]{2,1,0:T(8,128)S(1)} %get-tuple-element.18), channel_id=1, source_target_pairs={{4,8},{8,4},{5,9},{9,5},{6,10},{10,6},{7,11},{11,7},{20,24},{24,20... | collective-permute-start | bytes 393224 | tf_op jit(solution)/shard_map/ppermute | solution.py:595
  2.6 4.4 %collective-permute-start.1 = (f32[16,8,256]{2,1,0:T(8,128)S(1)}, f32[16,8,256]{2,1,0:T(8,128)S(1)}, u32[]{:S(2)}, u32[]{:S(2)}) collective-permute-start(f32[16,8,256]{2,1,0:T(8,128)S(1)} %get-tuple-element.19), channel_id=1, source_target_pairs={{0,4},{8,12},{4,0},{12,8},{1,5},{9,13},{5,1},{13,9},{2,6},{10,14},... | collective-permute-start | bytes 393224 | tf_op jit(solution)/shard_map/ppermute | solution.py:596
  7.0 0.0 copy-done
  7.0 0.0 copy-done.2
  7.0 0.0 copy-done.1
  7.0 0.0 copy-done.9
  7.0 0.0 copy-done.8
  7.0 0.0 copy-done.5
  7.0 0.0 copy-done.7
  7.0 0.0 copy-done.6
  7.0 2.0 %shard_map.114 = (f32[160,128]{1,0:T(8,128)S(1)}, f32[160,128]{1,0:T(8,128)S(1)}, f32[8,160,128]{2,1,0:T(8,128)S(1)}, f32[4,2,160,256]{3,2,1,0:T(8,128)S(1)}, f3...) custom-call(f32[3,2,128,256]{3,2,1,0:T(8,128)S(1)} %copy-done.1, ...), custom_call_target="tpu_custom_call" | custom-call | flops 188743680 | bytes 2097152 | tf_op jit(solution)/shard_map/pallas_call | solution.py:600
  9.0 0.0 collective-permute-done.cross.cross_rows
  9.0 0.0 collective-permute-done.1.near.near_rows
  9.1 0.2 shard_map.116
  9.2 0.7 %collective-permute-start.2 = (f32[160,128]{1,0:T(8,128)S(1)}, f32[160,128]{1,0:T(8,128)S(1)}, u32[]{:S(2)}, u32[]{:S(2)}) collective-permute-start(f32[160,128]{1,0:T(8,128)S(1)} %get-tuple-element.28), channel_id=1, source_target_pairs={{1,2},{2,1},{5,6},{6,5},{9,10},{10,9},{13,14},{14,13},{17,18},{18,... | collective-permute-start | bytes 245768 | tf_op jit(solution)/shard_map/ppermute | solution.py:625
  9.9 4.5 %collective-permute-start.3 = (f32[160,128]{1,0:T(8,128)S(1)}, f32[160,128]{1,0:T(8,128)S(1)}, u32[]{:S(2)}, u32[]{:S(2)}) collective-permute-start(f32[160,128]{1,0:T(8,128)S(1)} %get-tuple-element.29), channel_id=1, source_target_pairs={{0,1},{2,3},{1,0},{3,2},{4,5},{6,7},{5,4},{7,6},{8,9},{10,11},{9,8... | collective-permute-start | bytes 245768 | tf_op jit(solution)/shard_map/ppermute | solution.py:626
  14.4 0.0 copy-done.4
  14.4 0.0 copy-start.3
  14.4 2.0 %shard_map.115 = (f32[3,2,2,176,128]{4,3,2,1,0:T(8,128)S(1)}, f32[256,128]{1,0:T(8,128)S(1)}, f32[8,160,128]{2,1,0:T(8,128)S(1)}) custom-call(f32[3,2,128,256]{3,2,1,0:T(8,128)S(1)} %copy-done.1, f32[2,128,256]{2,1,0:T(8,128)S(1)} %copy-done.2, f32[4,2,128,256]{3,2,1,0:T(8,128)S(1)} %copy-done, f32[16,8,256]{2,1,0:T(8,128)S(1)} %collective-permute-done.cross.cross_rows, ...), custom_call_target="tpu_custom_call" | custom-call | flops 6553600 | bytes 3145728 | tf_op jit(solution)/shard_map/pallas_call | solution.py:629
  16.4 0.0 collective-permute-done.2.cross
  16.4 0.8 %collective-permute-done.3.near = f32[160,128]{1,0:T(8,128)S(1)} collective-permute-done((f32[160,128]{1,0:T(8,128)S(1)}, f32[160,128]{1,0:T(8,128)S(1)}, u32[]{:S(2)}, u32[]{:S(2)}) %collective-permute-start.3) | collective-permute-done | bytes 81952 | tf_op jit(solution)/shard_map/ppermute | solution.py:626
  17.2 0.0 copy-done.3
  17.2 2.3 %shard_map.117 = (f32[3,2,128,256]{3,2,1,0:T(8,128)}, f32[256,128]{1,0:T(8,128)S(1)}) custom-call(f32[3,2,2,176,128]{4,3,2,1,0:T(8,128)S(1)} %get-tuple-element.23.last, f32[256,128]{1,0:T(8,128)S(1)} %get-tuple-element.24.slots_in, f32[8,160,128]{2,1,0:T(8,128)S(1)} %get-tuple-element.25.base, f32[160,128]{1,0:T(8,128)S(1)} %collective-permute-done.2.cross, ...), custom_call_target="tpu_custom_call" | custom-call | flops 1638400 | bytes 524288 | tf_op jit(solution)/shard_map/pallas_call | solution.py:645
  19.5 11.7 %all_to_all.5 = f32[16,16,128]{2,1,0:T(8,128)S(1)} all-to-all(f32[16,16,128]{2,1,0:T(8,128)S(1)} %bitcast.6), channel_id=1, replica_groups=mesh['parts'=2,'gx'=4,'gy'=4] {'gx','gy'}, dimensions={0} | all-to-all | bytes 262144 | tf_op jit(solution)/shard_map/all_to_all | solution.py:665
  31.2 0.7 %copy.13 = f32[1,16,16,128]{3,2,1,0:T(8,128)} copy(f32[1,16,16,128]{3,2,1,0:T(8,128)S(1)} %bitcast.11) | data formatting | bytes 262144
Async XLA Ops:
  0.6 6.4 %copy-start = (f32[4,2,128,256]{3,2,1,0:T(8,128)S(1)}, f32[4,2,128,256]{3,2,1,0:T(8,128)}, u32[]{:S(2)}) copy-start(f32[4,2,128,256]{3,2,1,0:T(8,128)} %fwd.3) | copy-start | bytes 3145732
  0.6 6.3 %copy-start.2 = (f32[2,128,256]{2,1,0:T(8,128)S(1)}, f32[2,128,256]{2,1,0:T(8,128)}, u32[]{:S(2)}) copy-start(f32[2,128,256]{2,1,0:T(8,128)} %eps.3) | copy-start | bytes 786436
  0.7 6.3 %copy-start.1 = (f32[3,2,128,256]{3,2,1,0:T(8,128)S(1)}, f32[3,2,128,256]{3,2,1,0:T(8,128)}, u32[]{:S(2)}) copy-start(f32[3,2,128,256]{3,2,1,0:T(8,128)} %fields.3) | copy-start | bytes 2359300
  0.7 6.3 %copy-start.9 = (s32[1,1,128,1]{2,3,1,0:T(1,128)S(1)}, s32[1,1,128,1]{2,3,1,0:T(1,128)}, u32[]{:S(2)}) copy-start(s32[1,1,128,1]{2,3,1,0:T(1,128)} %param.17) | copy-start | bytes 1540
  0.7 6.3 %copy-start.8 = (s32[1,1,128]{2,1,0:T(1,128)S(1)}, s32[1,1,128]{2,1,0:T(1,128)}, u32[]{:S(2)}) copy-start(s32[1,1,128]{2,1,0:T(1,128)} %param.16) | copy-start | bytes 1540
  0.7 6.3 %copy-start.5 = (f32[4,64]{1,0:T(4,128)S(1)}, f32[4,64]{1,0:T(4,128)}, u32[]{:S(2)}) copy-start(f32[4,64]{1,0:T(4,128)} %refs_5_.1) | copy-start | bytes 3076
  0.7 6.3 %copy-start.7 = (s32[64]{0:T(128)S(1)}, s32[64]{0:T(128)}, u32[]{:S(2)}) copy-start(s32[64]{0:T(128)} %param.14) | copy-start | bytes 772
  0.7 6.3 %copy-start.6 = (s32[64]{0:T(128)S(1)}, s32[64]{0:T(128)}, u32[]{:S(2)}) copy-start(s32[64]{0:T(128)} %param.13) | copy-start | bytes 772
  1.9 12.4 %copy-start.4 = (bf16[2,128,128]{2,1,0:T(8,128)(2,1)S(1)}, bf16[2,128,128]{2,1,0:T(8,128)(2,1)}, u32[]{:S(2)}) copy-start(bf16[2,128,128]{2,1,0:T(8,128)(2,1)} %constant.4.clone.mats) | copy-start | bytes 196612
  1.9 7.1 %collective-permute-start = (f32[16,8,256]{2,1,0:T(8,128)S(1)}, f32[16,8,256]{2,1,0:T(8,128)S(1)}, u32[]{:S(2)}, u32[]{:S(2)}) collective-permute-start(f32[16,8,256]{2,1,0:T(8,128)S(1)} %get-tuple-element.18), channel_id=1, source_target_pairs={{4,8},{8,4},{5,9},{9,5},{6,10},{10,6},{7,11},{11,7},{20,24},{24,20... | collective-permute-start | bytes 393224 | tf_op jit(solution)/shard_map/ppermute | solution.py:595
  2.6 6.4 %collective-permute-start.1 = (f32[16,8,256]{2,1,0:T(8,128)S(1)}, f32[16,8,256]{2,1,0:T(8,128)S(1)}, u32[]{:S(2)}, u32[]{:S(2)}) collective-permute-start(f32[16,8,256]{2,1,0:T(8,128)S(1)} %get-tuple-element.19), channel_id=1, source_target_pairs={{0,4},{8,12},{4,0},{12,8},{1,5},{9,13},{5,1},{13,9},{2,6},{10,14},... | collective-permute-start | bytes 393224 | tf_op jit(solution)/shard_map/ppermute | solution.py:596
  9.2 7.2 %collective-permute-start.2 = (f32[160,128]{1,0:T(8,128)S(1)}, f32[160,128]{1,0:T(8,128)S(1)}, u32[]{:S(2)}, u32[]{:S(2)}) collective-permute-start(f32[160,128]{1,0:T(8,128)S(1)} %get-tuple-element.28), channel_id=1, source_target_pairs={{1,2},{2,1},{5,6},{6,5},{9,10},{10,9},{13,14},{14,13},{17,18},{18,... | collective-permute-start | bytes 245768 | tf_op jit(solution)/shard_map/ppermute | solution.py:625
  9.9 7.3 %collective-permute-start.3 = (f32[160,128]{1,0:T(8,128)S(1)}, f32[160,128]{1,0:T(8,128)S(1)}, u32[]{:S(2)}, u32[]{:S(2)}) collective-permute-start(f32[160,128]{1,0:T(8,128)S(1)} %get-tuple-element.29), channel_id=1, source_target_pairs={{0,1},{2,3},{1,0},{3,2},{4,5},{6,7},{5,4},{7,6},{8,9},{10,11},{9,8... | collective-permute-start | bytes 245768 | tf_op jit(solution)/shard_map/ppermute | solution.py:626
  14.4 2.8 %copy-start.3 = (bf16[256,256]{1,0:T(8,128)(2,1)S(1)}, bf16[256,256]{1,0:T(8,128)(2,1)}, u32[]{:S(2)}) copy-start(bf16[256,256]{1,0:T(8,128)(2,1)} %constant.5.clone.spread) | copy-start | bytes 393220

commit v7 on v6

--- a/solution.py
+++ b/solution.py
@@ -44,19 +44,6 @@
     for j in range(KEEP, 2 * LANES - KEEP):
         inner[j // LANES, j % LANES, j // PIX] = 1.0
     return inner.astype(ml_dtypes.bfloat16)
-
-
-def spread_matrix():
-    span = TS // PIX
-    result = np.zeros((2, LANES, 2, 2, span, span), np.float32)
-    for e in range(span):
-        move = (e % 2) + SIDE * (e % 4 // 2)
-        for layer in range(2):
-            for side in range(2):
-                for f in range(span):
-                    lane = (HALF * layer + OUT + OUT * side + PIX * f + move) % LANES
-                    result[e // 4, lane, side, layer, e, f] = 1.0
-    return result.reshape(2 * LANES, 2 * LANES).astype(ml_dtypes.bfloat16)
 
 
 def split2(value):
@@ -278,50 +265,102 @@
     place_edge[...] = dot(hit, jnp.where(picked, 1.0, 0.0).astype(BF16)).astype(BF16)
 
 
-def yee(bufs, keys, eps_of, change_of, src_of, grad, coef_x, coef_first, next_col, prev_col, other):
-    n_tiles = (bufs[0].shape[-2] - 2 * SUB) // SUB
+class Shifts:
+    def __init__(self, next_col, prev_col):
+        self.next_col, self.prev_col = next_col, prev_col
+        self.bottom, self.top = subs() == SUB - 1, subs() == 0
+
+    def up(self, tile):
+        return {key: turn(value, -1, 0) for key, value in tile.items()}
+
+    def down(self, tile):
+        return {key: turn(value, 1, 0) for key, value in tile.items()}
+
+    def below(self, up_here, up_next):
+        return {key: jnp.where(self.bottom, up_next[key], up_here[key]) for key in up_here}
+
+    def above(self, down_here, down_before):
+        return {key: jnp.where(self.top, down_before[key], down_here[key]) for key in down_here}
+
+
+def tile_at(t):
+    return (pl.ds(t * SUB, SUB), slice(None))
+
+
+def first_curl(n_tiles, shifts, load_hx, load_hy, curl):
+    before = None
+    for t in range(n_tiles):
+        hx, hy = load_hx(t), load_hy(t)
+        down = shifts.down(hy)
+        over = shifts.above(down, before if t else down)
+        left = shifts.prev_col(hx)
+        for key in hx:
+            curl[key + tile_at(t)] = (hy[key] - over[key]) - (hx[key] - left[key])
+        before = down
+
+
+def steps(n_tiles, keys, shifts, e, curl, eps_of, src_of, other):
+    no_above = shifts.top & ((lax.axis_index("gx") + subs() * 0) == 0)
     for step in range(STEPS):
-        old, new = ((0, 1), (1, 0), (0, 1), (1, 2))[step]
-        old, new = bufs[old], bufs[new]
-        low = 0 if step < 2 else 1
-        high = n_tiles if step == 0 else n_tiles - 1
+        low, high = (0, n_tiles) if step == 0 else (1, n_tiles - 1)
+
+        def load(t):
+            return {key: e[(step,) + key + tile_at(t)] for key in keys}
+
+        here = load(low)
+        up = shifts.up(here)
+        down_before = shifts.down(load(max(low - 1, 0)))
         for t in range(low, high):
-            at = pl.ds(SUB + t * SUB, SUB)
-            under = pl.ds(SUB + t * SUB + 1, SUB)
-            over = pl.ds(SUB + t * SUB - 1, SUB)
-            coef_y = coef_first if t < PAD // SUB else COURANT
-            e = {key: old[(0,) + key + (at, slice(None))] for key in keys}
-            e_right = next_col(e)
-            hx, hy = {}, {}
+            after = load(min(t + 1, n_tiles - 1))
+            up_next, down = shifts.up(after), shifts.down(here)
+            below, above = shifts.below(up, up_next), shifts.above(down, down_before)
+            right, left = shifts.next_col(here), shifts.prev_col(here)
             for key in keys:
-                hx[key] = old[(1,) + key + (at, slice(None))] + coef_x * (e_right[key] - e[key])
-                below = old[(0,) + key + (under, slice(None))]
-                hy[key] = old[(2,) + key + (at, slice(None))] - coef_y * (below - e[key])
-                new[(1,) + key + (at, slice(None))] = hx[key]
-                new[(2,) + key + (at, slice(None))] = hy[key]
-            hx_left = prev_col(hx)
-            for key in keys:
-                hy_above = new[(2,) + key + (over, slice(None))]
-                curl = (hy[key] - hy_above) - (hx[key] - hx_left[key])
-                curl = curl + COUPLING * (other(e, key) - e[key])
-                value = e[key] - eps_of(key, t) * curl + src_of(step, key, t)
-                new[(0,) + key + (at, slice(None))] = value
-                if 1 <= t < n_tiles - 1:
-                    change = value * change_of(step, key, t)
-                    where = key + (pl.ds(t * SUB, SUB), slice(None))
-                    grad[where] = -change if step == 0 else grad[where] - change
-
-
-def coef_above():
-    return jnp.where((subs() * 0 + lax.axis_index("gx")) > 0, COURANT, 0.0).astype(F32)
-
-
-def clear_rims(buf):
-    size = buf.shape[-2]
-    zero = jnp.zeros(buf.shape[:-2] + (SUB, LANES), F32)
-    lead = (slice(None),) * (len(buf.shape) - 2)
-    buf[lead + (pl.ds(0, SUB), slice(None))] = zero
-    buf[lead + (pl.ds(size - SUB, SUB), slice(None))] = zero
+                center, over = here[key], above[key]
+                if t == PAD // SUB:
+                    over = jnp.where(no_above, center, over)
+                ring = (below[key] + over) + (right[key] + left[key]) - 4.0 * center
+                change = curl[key + tile_at(t)] - COURANT * ring
+                if step < STEPS - 1:
+                    curl[key + tile_at(t)] = change
+                change = change + COUPLING * (other(here, key) - center)
+                e[(step + 1,) + key + tile_at(t)] = (
+                    center - eps_of(key, t) * change + src_of(step, key, t)
+                )
+            here, up, down_before = after, up_next, down
+
+
+def gradient(keys, t, e, change_of):
+    result = {}
+    for key in keys:
+        total = None
+        for step in range(STEPS):
+            term = e[(step + 1,) + key + tile_at(t)] * change_of(step, key, t)
+            total = term if total is None else total + term
+        result[key] = -total
+    return result
+
+
+def last_fields(tiles, keys, shifts, e, load_hx, load_hy, store):
+    def total(t):
+        result = {}
+        for key in keys:
+            parts = [e[(step,) + key + tile_at(t)] for step in range(STEPS)]
+            result[key] = (parts[0] + parts[1]) + (parts[2] + parts[3])
+        return result
+
+    here = total(tiles[0])
+    up = shifts.up(here)
+    for t in tiles:
+        after = total(t + 1)
+        up_next = shifts.up(after)
+        below, right = shifts.below(up, up_next), shifts.next_col(here)
+        hx, hy = load_hx(t), load_hy(t)
+        for key in keys:
+            store(0, key, t, e[(STEPS,) + key + tile_at(t)])
+            store(1, key, t, hx[key] + COURANT * (right[key] - here[key]))
+            store(2, key, t, hy[key] - COURANT * (below[key] - here[key]))
+        here, up = after, up_next
 
 
 def row_pairs(ref, lead, count):
@@ -329,29 +368,25 @@
     return even + ref[lead + (pl.ds(1, count, stride=PIX), slice(None))]
 
 
-def inner_kernel(fields, eps, fwd, cross, near, src, mats, base_in, place, last, slots, base, a, b, e, g, pooled):
+def inner_kernel(
+    fields, eps, fwd, cross, near, src, mats, base_in, place, last, slots, base, e, curl, eps_c, g, pooled
+):
     rows, cols = fields.shape[2], fields.shape[3]
     n_tiles = (rows + 2 * PAD) // SUB
     n_lanes = cols // LANES
     lane, odd = lanes(), is_odd("gx")
     halo_of = {0: 0, 1: 1, n_tiles - 2: 2, n_tiles - 1: 3}
+    keys = [(layer, k) for layer in range(2) for k in range(n_lanes)]
 
     def load(kind, layer, t, k):
         if t in halo_of:
             return halo_tile(cross, near, odd, halo_of[t], kind, layer, lane_tile(k))
         return core_tile(fields, eps, fwd, pl.ds(t * SUB - PAD, SUB), kind, layer, lane_tile(k))
 
-    for buf in (a, b, last):
-        clear_rims(buf)
-    for t in range(n_tiles):
-        for layer in range(2):
-            for k in range(n_lanes):
-                for kind in range(3):
-                    a[kind, layer, k, pl.ds(SUB + t * SUB, SUB), :] = load(kind, layer, t, k)
-                e[layer, k, pl.ds(t * SUB, SUB), :] = COURANT * load(3, layer, t, k)
+    def load_all(kind, t):
+        return {key: load(kind, key[0], t, key[1]) for key in keys}
 
     at_end, at_start = lane == LANES - 1, lane == 0
-    keys = [(layer, k) for layer in range(2) for k in range(n_lanes)]
 
     def next_col(values):
         moved = {key: turn(value, -1, 1) for key, value in values.items()}
@@ -365,13 +400,29 @@
             (l, k): jnp.where(at_start, moved[l, (k - 1) % n_lanes], moved[l, k]) for l, k in keys
         }
 
-    yee(
-        (a, b, last), keys,
-        lambda key, t: e[key + (pl.ds(t * SUB, SUB), slice(None))],
-        lambda step, key, t: load(4 + step, key[0], t, key[1]),
+    shifts = Shifts(next_col, prev_col)
+    for t in range(n_tiles):
+        for key in keys:
+            e[(0,) + key + tile_at(t)] = load(0, key[0], t, key[1])
+            eps_c[key + tile_at(t)] = COURANT * load(3, key[0], t, key[1])
+    first_curl(n_tiles, shifts, lambda t: load_all(1, t), lambda t: load_all(2, t), curl)
+    steps(
+        n_tiles, keys, shifts, e, curl,
+        lambda key, t: eps_c[key + tile_at(t)],
         lambda step, key, t: src[step, key[0], pl.ds(t * SUB, SUB), lane_tile(key[1])],
-        g, COURANT, coef_above(), next_col, prev_col,
         lambda values, key: values[1 - key[0], key[1]],
+    )
+    for t in range(1, n_tiles - 1):
+        values = gradient(keys, t, e, lambda step, key, t: load(4 + step, key[0], t, key[1]))
+        for key in keys:
+            g[key + tile_at(t)] = values[key]
+
+    def store(kind, key, t, value):
+        last[(kind,) + key + (pl.ds(t * SUB - PAD, SUB), slice(None))] = value
+
+    last_fields(
+        range(PAD // SUB, n_tiles - PAD // SUB), keys, shifts, e,
+        lambda t: load_all(1, t), lambda t: load_all(2, t), store,
     )
     for layer in range(2):
         total = None
@@ -446,11 +497,19 @@
         low = jnp.where(even, spans[e], turn(spans[e + 1], 1, 1))
         high = jnp.where(even, turn(spans[e + 2], SIDE, 1), turn(spans[e + 3], SIDE + 1, 1))
         merged.append(jnp.where(window, low, high))
-    return jnp.concatenate(merged, axis=1)
+    span = TS // PIX
+    row, pixel = lane // span % span, lane % span
+    start = (lane & HALF) + OUT + PIX * pixel + (row & 1) + SIDE * ((row >> 1) & 1)
+    result = []
+    for side in range(2):
+        index = (start + OUT * side) & (LANES - 1)
+        low, high = (jnp.take_along_axis(value, index, axis=1) for value in merged)
+        result.append(jnp.where(row < span // 2, low, high))
+    return result
 
 
 def edge_kernel(
-    last, slots_in, base, cross, near, src, place, spread, out_fields, slots, a, b, c, e, d, g, merged, sem
+    last, slots_in, base, cross, near, src, place, out_fields, slots, e, first, curl, eps_c, d, g, merged, sem
 ):
     ext_rows = base.shape[1]
     rows = ext_rows - 2 * PAD
@@ -459,8 +518,6 @@
     spot = lane & (HALF - 1)
     is_left, is_right = spot < OUT, spot >= HALF - OUT
 
-    for buf in (a, b, c):
-        clear_rims(buf)
     for t in range(n_tiles):
         at = pl.ds(t * SUB, SUB)
         far, close = cross[at, :], near[at, :]
@@ -470,51 +527,67 @@
                 continue
             value = jnp.where(is_left, turn(high, OUT - width - FIRST[kind], 1), base[kind, at, :])
             value = jnp.where(is_right, turn(low, HALF - OUT - FIRST[kind], 1), value)
-            if kind < 3:
-                a[kind, pl.ds(SUB + t * SUB, SUB), :] = value
+            if kind == 0:
+                e[0, at, :] = value
+            elif kind < 3:
+                first[kind - 1, at, :] = value
             elif kind == 3:
-                e[at, :] = COURANT * value
+                eps_c[at, :] = COURANT * value
             else:
                 d[kind - 4, at, :] = value
 
-    before = (lax.axis_index("gy") + lane * 0) > 0
-    coef_x = jnp.where(before | (spot >= OUT), COURANT, 0.0).astype(F32)
-    yee(
-        (a, b, c), [()],
-        lambda key, t: e[pl.ds(t * SUB, SUB), :],
-        lambda step, key, t: d[step, pl.ds(t * SUB, SUB), :],
-        lambda step, key, t: src[step, pl.ds(t * SUB, SUB), :],
-        g, coef_x, coef_above(),
+    no_left = (spot == OUT) & ((lax.axis_index("gy") + lane * 0) == 0)
+    shifts = Shifts(
         lambda values: {(): turn(values[()], -1, 1)},
         lambda values: {(): turn(values[()], 1, 1)},
+    )
+
+    def load_hx(t):
+        return {(): first[0, pl.ds(t * SUB, SUB), :]}
+
+    def load_hy(t):
+        return {(): first[1, pl.ds(t * SUB, SUB), :]}
+
+    first_curl(n_tiles, shifts, load_hx, load_hy, curl)
+    shifts.prev_col = lambda values: {(): jnp.where(no_left, values[()], turn(values[()], 1, 1))}
+    steps(
+        n_tiles, [()], shifts, e, curl,
+        lambda key, t: eps_c[pl.ds(t * SUB, SUB), :],
+        lambda step, key, t: src[step, pl.ds(t * SUB, SUB), :],
         lambda values, key: turn(values[()], HALF, 1),
     )
+    inside = (spot >= OUT - NEAR) & (spot < OUT + KEEP)
+    inside = inside | ((spot >= HALF - OUT - KEEP) & (spot < HALF - OUT + NEAR))
+    for t in range(1, n_tiles - 1):
+        value = gradient([()], t, e, lambda step, key, t: d[step, pl.ds(t * SUB, SUB), :])[()]
+        g[pl.ds(t * SUB, SUB), :] = jnp.where(inside, value, 0.0)
 
     n_lanes = merged.shape[3] // LANES
-    for t in range(rows // SUB):
-        at, out_at = pl.ds(SUB + PAD + t * SUB, SUB), pl.ds(t * SUB, SUB)
-        for kind in range(3):
-            edge = c[kind, at, :]
-            for layer in range(2):
-                for k in range(n_lanes):
-                    value = last[kind, layer, k, at, :]
-                    if k == 0:
-                        value = jnp.where(lane < KEEP, turn(edge, -HALF * layer - OUT, 1), value)
-                    if k == n_lanes - 1:
-                        value = jnp.where(
-                            lane >= LANES - KEEP, turn(edge, -HALF * layer - SIDE - OUT, 1), value
-                        )
-                    merged[kind, layer, out_at, lane_tile(k)] = value
+
+    def store(kind, key, t, edge):
+        at = pl.ds(t * SUB - PAD, SUB)
+        for layer in range(2):
+            for k in range(n_lanes):
+                value = last[kind, layer, k, at, :]
+                if k == 0:
+                    value = jnp.where(lane < KEEP, turn(edge, -HALF * layer - OUT, 1), value)
+                if k == n_lanes - 1:
+                    value = jnp.where(
+                        lane >= LANES - KEEP, turn(edge, -HALF * layer - SIDE - OUT, 1), value
+                    )
+                merged[kind, layer, at, lane_tile(k)] = value
+
+    last_fields(
+        range(PAD // SUB, n_tiles - PAD // SUB), [()], shifts, e, load_hx, load_hy, store
+    )
     copy = pltpu.make_async_copy(merged, out_fields, sem)
     copy.start()
 
-    inside = (spot >= OUT - NEAR) & (spot < OUT + KEEP)
-    inside = inside | ((spot >= HALF - OUT - KEEP) & (spot < HALF - OUT + NEAR))
     span, reach = TS // PIX, RADIUS - 1
     pixel = {}
     for j in range(-reach, span + reach):
         value = g[pl.ds(PAD + PIX * j, SUB, stride=TS), :]
-        value = jnp.where(inside, value + g[pl.ds(PAD + PIX * j + 1, SUB, stride=TS), :], 0.0)
+        value = value + g[pl.ds(PAD + PIX * j + 1, SUB, stride=TS), :]
         pixel[j] = value + turn(value, -1, 1)
 
     weights = cone_weights(RADIUS)
@@ -534,9 +607,7 @@
             total = mixed if total is None else total + mixed
         spans.append(total)
 
-    edge = dot(jnp.concatenate(split2(merge_spans(spans, lane)), axis=0), spread[...])
-    edge = edge[:SUB] + edge[SUB:]
-    edge = jnp.concatenate([edge[:, :LANES], edge[:, LANES:]], axis=0)
+    edge = jnp.concatenate(merge_spans(spans, lane), axis=0)
     slots[...] = slots_in[...] + dot(place[...], jnp.concatenate(split2(edge), axis=0))
     copy.wait()
 
@@ -625,41 +696,45 @@
     cross_cols = lax.ppermute(cross_cols, "gy", pairs(gy_count, 1))
     near_cols = lax.ppermute(near_cols, "gy", pairs(gy_count, 0))
 
-    state = (3, 2, n_lanes, ext_rows + 2 * SUB, LANES)
+    plane = (2, n_lanes, ext_rows, LANES)
     last, slots, base = call(
         inner_kernel,
-        (shape(*state), shape(owners * capacity, width), shape(4 + STEPS, ext_rows, LANES)),
+        (
+            shape(3, 2, n_lanes, rows, LANES),
+            shape(owners * capacity, width),
+            shape(4 + STEPS, ext_rows, LANES),
+        ),
         9,
         scratch=(
-            pltpu.VMEM(state, F32),
-            pltpu.VMEM(state, F32),
-            pltpu.VMEM((2, n_lanes, ext_rows, LANES), F32),
-            pltpu.VMEM((2, n_lanes, ext_rows, LANES), F32),
+            pltpu.VMEM((1 + STEPS,) + plane, F32),
+            pltpu.VMEM(plane, F32),
+            pltpu.VMEM(plane, F32),
+            pltpu.VMEM(plane, F32),
             pltpu.VMEM((2, ext_rows // PIX, LANES), F32),
         ),
         flops=200 * cells,
         size=96 * cells,
     )(*blocks, cross, near, src, pool_matrices(), base, place)
 
-    edge_state = (3, ext_rows + 2 * SUB, LANES)
+    plane = (ext_rows, LANES)
     fields, outgoing = call(
         edge_kernel,
         (shape(3, 2, rows, cols), shape(owners * capacity, width)),
-        8,
+        7,
         out_specs=(pl.BlockSpec(memory_space=pl.ANY), vmem()),
         scratch=(
-            pltpu.VMEM(edge_state, F32),
-            pltpu.VMEM(edge_state, F32),
-            pltpu.VMEM(edge_state, F32),
-            pltpu.VMEM((ext_rows, LANES), F32),
-            pltpu.VMEM((STEPS, ext_rows, LANES), F32),
-            pltpu.VMEM((ext_rows, LANES), F32),
+            pltpu.VMEM((1 + STEPS,) + plane, F32),
+            pltpu.VMEM((2,) + plane, F32),
+            pltpu.VMEM(plane, F32),
+            pltpu.VMEM(plane, F32),
+            pltpu.VMEM((STEPS,) + plane, F32),
+            pltpu.VMEM(plane, F32),
             pltpu.VMEM((3, 2, rows, cols), F32),
             pltpu.SemaphoreType.DMA,
         ),
         flops=50 * cells,
         size=16 * cells,
-    )(last, slots, base, cross_cols, near_cols, src_edge, place_edge, spread_matrix())
+    )(last, slots, base, cross_cols, near_cols, src_edge, place_edge)
 
     outgoing = outgoing.reshape(owners, capacity, width)
     incoming = lax.all_to_all(outgoing, ("gx", "gy"), split_axis=0, concat_axis=0, tiled=True)

time: 32.1 us -> 32.5 us (1.012)
  Pallas kernels: 7.7 us -> 8.16 us
    pallas_call x1, Pallas kernels: 2.33 us -> 2.75 us  [on_device(): call(edge_kernel, (shape(3, 2, rows, cols), shape(owners * capacity, widt...]
    unnamed x21 -> x19, local copies, waits for them, and re-layouts: 0.7 us -> 0.7 us
  transfers between devices with their start and end apart: 4 -> 4, of which waited for: 1 -> 1; matrix products, arithmetic and copies ran while one was open for 0% -> 0% of each run, Pallas kernels for 13% -> 12%
where the time goes in v7:
time: 32.5 us; the launch traced here: 32.3 us
  blocking collectives  11.7 us (36%)
  starting transfers between devices  10.2 us (31%)
  Pallas kernels  8.16 us (25%)
  between operations  0.82 us (3%)
  waiting for transfers between devices  0.78 us (2%)
  local copies, waits for them, and re-layouts  0.7 us (2%)
    all_to_all x1, blocking collectives, on_device(): lax.all_to_all(outgoing, ('gx', 'gy'), split_axis=0, concat_axis=0, tiled...  11.7 us
    ppermute x1, starting transfers between devices, on_device(): near_cols = lax.ppermute(near_cols, 'gy', pairs(gy_count, 0))  4.46 us
    ppermute x1, starting transfers between devices, on_device(): near = lax.ppermute(near, 'gx', pairs(gx_count, 0))  4.36 us
    pallas_call x1, Pallas kernels, on_device(): call(edge_kernel, (shape(3, 2, rows, cols), shape(owners * capacity, widt...  2.75 us
    pallas_call x1, Pallas kernels, on_device(): call(inner_kernel, (shape(3, 2, n_lanes, rows, LANES), shape(owners * cap...  2.03 us
    pallas_call x1, Pallas kernels, on_device(): call(lambda *refs: prep_kernel(capacity, *refs), (packed, packed, shape(4...  1.99 us
    pallas_call x1, Pallas kernels, on_device(): call(rows_kernel, (strip, strip), 3, in_space=pltpu.HBM, scratch=(pltpu.V...  1.21 us
    ppermute x1, waiting for transfers between devices, on_device(): near_cols = lax.ppermute(near_cols, 'gy', pairs(gy_count, 0))  0.78 us
  transfers between devices with their start and end apart: 4, of which 1 were waited for; matrix products, arithmetic and copies ran while one was open for 0% of the time, Pallas kernels for 12%

profile of v7, /device:TPU:0, one launch (start us, length us, event | category | flops | bytes accessed | tf_op | source)
XLA Modules:
  0.0 32.3 jit_solution(15031275890765796562)
XLA Ops:
  0.6 0.0 copy-start
  0.6 0.0 copy-start.2
  0.7 0.0 copy-start.1
  0.7 0.0 copy-start.8
  0.7 0.0 copy-start.7
  0.7 0.0 copy-start.4
  0.7 0.0 copy-start.6
  0.7 0.0 copy-start.5
  0.7 1.2 %shard_map.104 = (f32[16,8,256]{2,1,0:T(8,128)S(1)}, f32[16,8,256]{2,1,0:T(8,128)S(1)}) custom-call(f32[3,2,128,256]{3,2,1,0:T(8,128)} %fields.3, f32[2,128,256]{2,1,0:T(8,128)} %eps.3, f32[4,2,128,256]{3,2,1,0:T(8,128)} %fwd.3), custom_call_target="tpu_custom_call" | custom-call | bytes 1048576 | tf_op jit(solution)/shard_map/pallas_call | solution.py:652
  1.9 0.0 copy-start.3
  1.9 0.7 %collective-permute-start = (f32[16,8,256]{2,1,0:T(8,128)S(1)}, f32[16,8,256]{2,1,0:T(8,128)S(1)}, u32[]{:S(2)}, u32[]{:S(2)}) collective-permute-start(f32[16,8,256]{2,1,0:T(8,128)S(1)} %get-tuple-element.18), channel_id=1, source_target_pairs={{4,8},{8,4},{5,9},{9,5},{6,10},{10,6},{7,11},{11,7},{20,24},{24,20... | collective-permute-start | bytes 393224 | tf_op jit(solution)/shard_map/ppermute | solution.py:666
  2.6 4.4 %collective-permute-start.1 = (f32[16,8,256]{2,1,0:T(8,128)S(1)}, f32[16,8,256]{2,1,0:T(8,128)S(1)}, u32[]{:S(2)}, u32[]{:S(2)}) collective-permute-start(f32[16,8,256]{2,1,0:T(8,128)S(1)} %get-tuple-element.19), channel_id=1, source_target_pairs={{0,4},{8,12},{4,0},{12,8},{1,5},{9,13},{5,1},{13,9},{2,6},{10,14},... | collective-permute-start | bytes 393224 | tf_op jit(solution)/shard_map/ppermute | solution.py:667
  7.0 0.0 copy-done
  7.0 0.0 copy-done.2
  7.0 0.0 copy-done.1
  7.0 0.0 copy-done.8
  7.0 0.0 copy-done.7
  7.0 0.0 copy-done.4
  7.0 0.0 copy-done.6
  7.0 0.0 copy-done.5
  7.0 2.0 %shard_map.105 = (f32[160,128]{1,0:T(8,128)S(1)}, f32[160,128]{1,0:T(8,128)S(1)}, f32[8,160,128]{2,1,0:T(8,128)S(1)}, f32[4,2,160,256]{3,2,1,0:T(8,128)S(1)}, f3...) custom-call(f32[3,2,128,256]{3,2,1,0:T(8,128)S(1)} %copy-done.1, ...), custom_call_target="tpu_custom_call" | custom-call | flops 188743680 | bytes 2097152 | tf_op jit(solution)/shard_map/pallas_call | solution.py:671
  9.0 0.0 collective-permute-done.cross.cross_rows
  9.0 0.0 collective-permute-done.1.near.near_rows
  9.1 0.2 shard_map.107
  9.2 0.7 %collective-permute-start.2 = (f32[160,128]{1,0:T(8,128)S(1)}, f32[160,128]{1,0:T(8,128)S(1)}, u32[]{:S(2)}, u32[]{:S(2)}) collective-permute-start(f32[160,128]{1,0:T(8,128)S(1)} %get-tuple-element.28), channel_id=1, source_target_pairs={{1,2},{2,1},{5,6},{6,5},{9,10},{10,9},{13,14},{14,13},{17,18},{18,... | collective-permute-start | bytes 245768 | tf_op jit(solution)/shard_map/ppermute | solution.py:696
  9.9 4.5 %collective-permute-start.3 = (f32[160,128]{1,0:T(8,128)S(1)}, f32[160,128]{1,0:T(8,128)S(1)}, u32[]{:S(2)}, u32[]{:S(2)}) collective-permute-start(f32[160,128]{1,0:T(8,128)S(1)} %get-tuple-element.29), channel_id=1, source_target_pairs={{0,1},{2,3},{1,0},{3,2},{4,5},{6,7},{5,4},{7,6},{8,9},{10,11},{9,8... | collective-permute-start | bytes 245768 | tf_op jit(solution)/shard_map/ppermute | solution.py:697
  14.4 0.0 copy-done.3
  14.4 2.0 %shard_map.106 = (f32[3,2,2,128,128]{4,3,2,1,0:T(8,128)S(1)}, f32[256,128]{1,0:T(8,128)S(1)}, f32[8,160,128]{2,1,0:T(8,128)S(1)}) custom-call(f32[3,2,128,256]{3,2,1,0:T(8,128)S(1)} %copy-done.1, f32[2,128,256]{2,1,0:T(8,128)S(1)} %copy-done.2, f32[4,2,128,256]{3,2,1,0:T(8,128)S(1)} %copy-done, f32[16,8,256]{2,1,0:T(8,128)S(1)} %collective-permute-done.cross.cross_rows, ...), custom_call_target="tpu_custom_call" | custom-call | flops 6553600 | bytes 3145728 | tf_op jit(solution)/shard_map/pallas_call | solution.py:700
  16.4 0.0 collective-permute-done.2.cross
  16.4 0.8 %collective-permute-done.3.near = f32[160,128]{1,0:T(8,128)S(1)} collective-permute-done((f32[160,128]{1,0:T(8,128)S(1)}, f32[160,128]{1,0:T(8,128)S(1)}, u32[]{:S(2)}, u32[]{:S(2)}) %collective-permute-start.3) | collective-permute-done | bytes 81952 | tf_op jit(solution)/shard_map/ppermute | solution.py:697
  17.2 2.7 %shard_map.108 = (f32[3,2,128,256]{3,2,1,0:T(8,128)}, f32[256,128]{1,0:T(8,128)S(1)}) custom-call(f32[3,2,2,128,128]{4,3,2,1,0:T(8,128)S(1)} %get-tuple-element.23.last, f32[256,128]{1,0:T(8,128)S(1)} %get-tuple-element.24.slots_in, f32[8,160,128]{2,1,0:T(8,128)S(1)} %get-tuple-element.25.base, f32[160,128]{1,0:T(8,128)S(1)} %collective-permute-done.2.cross, ...), custom_call_target="tpu_custom_call" | custom-call | flops 1638400 | bytes 524288 | tf_op jit(solution)/shard_map/pallas_call | solution.py:720
  19.9 11.7 %all_to_all.5 = f32[16,16,128]{2,1,0:T(8,128)S(1)} all-to-all(f32[16,16,128]{2,1,0:T(8,128)S(1)} %bitcast.6), channel_id=1, replica_groups=mesh['parts'=2,'gx'=4,'gy'=4] {'gx','gy'}, dimensions={0} | all-to-all | bytes 262144 | tf_op jit(solution)/shard_map/all_to_all | solution.py:740
  31.7 0.7 %copy.12 = f32[1,16,16,128]{3,2,1,0:T(8,128)} copy(f32[1,16,16,128]{3,2,1,0:T(8,128)S(1)} %bitcast.11) | data formatting | bytes 262144
Async XLA Ops:
  0.6 6.4 %copy-start = (f32[4,2,128,256]{3,2,1,0:T(8,128)S(1)}, f32[4,2,128,256]{3,2,1,0:T(8,128)}, u32[]{:S(2)}) copy-start(f32[4,2,128,256]{3,2,1,0:T(8,128)} %fwd.3) | copy-start | bytes 3145732
  0.6 6.3 %copy-start.2 = (f32[2,128,256]{2,1,0:T(8,128)S(1)}, f32[2,128,256]{2,1,0:T(8,128)}, u32[]{:S(2)}) copy-start(f32[2,128,256]{2,1,0:T(8,128)} %eps.3) | copy-start | bytes 786436
  0.7 6.3 %copy-start.1 = (f32[3,2,128,256]{3,2,1,0:T(8,128)S(1)}, f32[3,2,128,256]{3,2,1,0:T(8,128)}, u32[]{:S(2)}) copy-start(f32[3,2,128,256]{3,2,1,0:T(8,128)} %fields.3) | copy-start | bytes 2359300
  0.7 6.3 %copy-start.8 = (s32[1,1,128,1]{2,3,1,0:T(1,128)S(1)}, s32[1,1,128,1]{2,3,1,0:T(1,128)}, u32[]{:S(2)}) copy-start(s32[1,1,128,1]{2,3,1,0:T(1,128)} %param.16) | copy-start | bytes 1540
  0.7 6.3 %copy-start.7 = (s32[1,1,128]{2,1,0:T(1,128)S(1)}, s32[1,1,128]{2,1,0:T(1,128)}, u32[]{:S(2)}) copy-start(s32[1,1,128]{2,1,0:T(1,128)} %param.15) | copy-start | bytes 1540
  0.7 6.3 %copy-start.4 = (f32[4,64]{1,0:T(4,128)S(1)}, f32[4,64]{1,0:T(4,128)}, u32[]{:S(2)}) copy-start(f32[4,64]{1,0:T(4,128)} %refs_5_.1) | copy-start | bytes 3076
  0.7 6.3 %copy-start.6 = (s32[64]{0:T(128)S(1)}, s32[64]{0:T(128)}, u32[]{:S(2)}) copy-start(s32[64]{0:T(128)} %param.13) | copy-start | bytes 772
  0.7 6.3 %copy-start.5 = (s32[64]{0:T(128)S(1)}, s32[64]{0:T(128)}, u32[]{:S(2)}) copy-start(s32[64]{0:T(128)} %param.12) | copy-start | bytes 772
  1.9 12.4 %copy-start.3 = (bf16[2,128,128]{2,1,0:T(8,128)(2,1)S(1)}, bf16[2,128,128]{2,1,0:T(8,128)(2,1)}, u32[]{:S(2)}) copy-start(bf16[2,128,128]{2,1,0:T(8,128)(2,1)} %constant.2.clone.mats) | copy-start | bytes 196612
  1.9 7.1 %collective-permute-start = (f32[16,8,256]{2,1,0:T(8,128)S(1)}, f32[16,8,256]{2,1,0:T(8,128)S(1)}, u32[]{:S(2)}, u32[]{:S(2)}) collective-permute-start(f32[16,8,256]{2,1,0:T(8,128)S(1)} %get-tuple-element.18), channel_id=1, source_target_pairs={{4,8},{8,4},{5,9},{9,5},{6,10},{10,6},{7,11},{11,7},{20,24},{24,20... | collective-permute-start | bytes 393224 | tf_op jit(solution)/shard_map/ppermute | solution.py:666
  2.6 6.4 %collective-permute-start.1 = (f32[16,8,256]{2,1,0:T(8,128)S(1)}, f32[16,8,256]{2,1,0:T(8,128)S(1)}, u32[]{:S(2)}, u32[]{:S(2)}) collective-permute-start(f32[16,8,256]{2,1,0:T(8,128)S(1)} %get-tuple-element.19), channel_id=1, source_target_pairs={{0,4},{8,12},{4,0},{12,8},{1,5},{9,13},{5,1},{13,9},{2,6},{10,14},... | collective-permute-start | bytes 393224 | tf_op jit(solution)/shard_map/ppermute | solution.py:667
  9.2 7.2 %collective-permute-start.2 = (f32[160,128]{1,0:T(8,128)S(1)}, f32[160,128]{1,0:T(8,128)S(1)}, u32[]{:S(2)}, u32[]{:S(2)}) collective-permute-start(f32[160,128]{1,0:T(8,128)S(1)} %get-tuple-element.28), channel_id=1, source_target_pairs={{1,2},{2,1},{5,6},{6,5},{9,10},{10,9},{13,14},{14,13},{17,18},{18,... | collective-permute-start | bytes 245768 | tf_op jit(solution)/shard_map/ppermute | solution.py:696
  9.9 7.3 %collective-permute-start.3 = (f32[160,128]{1,0:T(8,128)S(1)}, f32[160,128]{1,0:T(8,128)S(1)}, u32[]{:S(2)}, u32[]{:S(2)}) collective-permute-start(f32[160,128]{1,0:T(8,128)S(1)} %get-tuple-element.29), channel_id=1, source_target_pairs={{0,1},{2,3},{1,0},{3,2},{4,5},{6,7},{5,4},{7,6},{8,9},{10,11},{9,8... | collective-permute-start | bytes 245768 | tf_op jit(solution)/shard_map/ppermute | solution.py:697

commit v8 on v7

--- a/solution.py
+++ b/solution.py
@@ -509,7 +509,7 @@
 
 
 def edge_kernel(
-    last, slots_in, base, cross, near, src, place, out_fields, slots, e, first, curl, eps_c, d, g, merged, sem
+    base, cross, near, src, out, g_out, e, first, curl, eps_c, d, g, result
 ):
     ext_rows = base.shape[1]
     rows = ext_rows - 2 * PAD
@@ -562,27 +562,18 @@
         value = gradient([()], t, e, lambda step, key, t: d[step, pl.ds(t * SUB, SUB), :])[()]
         g[pl.ds(t * SUB, SUB), :] = jnp.where(inside, value, 0.0)
 
-    n_lanes = merged.shape[3] // LANES
-
-    def store(kind, key, t, edge):
-        at = pl.ds(t * SUB - PAD, SUB)
-        for layer in range(2):
-            for k in range(n_lanes):
-                value = last[kind, layer, k, at, :]
-                if k == 0:
-                    value = jnp.where(lane < KEEP, turn(edge, -HALF * layer - OUT, 1), value)
-                if k == n_lanes - 1:
-                    value = jnp.where(
-                        lane >= LANES - KEEP, turn(edge, -HALF * layer - SIDE - OUT, 1), value
-                    )
-                merged[kind, layer, at, lane_tile(k)] = value
+    def store(kind, key, t, value):
+        result[kind, pl.ds(t * SUB - PAD, SUB), :] = value
 
     last_fields(
         range(PAD // SUB, n_tiles - PAD // SUB), [()], shifts, e, load_hx, load_hy, store
     )
-    copy = pltpu.make_async_copy(merged, out_fields, sem)
-    copy.start()
-
+    g_out[...] = g[...]
+    out[...] = result[...]
+
+
+def tiles_kernel(g, slots_in, place, slots):
+    lane = lanes()
     span, reach = TS // PIX, RADIUS - 1
     pixel = {}
     for j in range(-reach, span + reach):
@@ -609,6 +600,28 @@
 
     edge = jnp.concatenate(merge_spans(spans, lane), axis=0)
     slots[...] = slots_in[...] + dot(place[...], jnp.concatenate(split2(edge), axis=0))
+
+
+def merge_kernel(last, edge_last, out_fields, merged, sem):
+    rows, cols = merged.shape[2], merged.shape[3]
+    n_lanes = cols // LANES
+    lane = lanes()
+    for t in range(rows // SUB):
+        at = pl.ds(t * SUB, SUB)
+        for kind in range(3):
+            edge = edge_last[kind, at, :]
+            for layer in range(2):
+                for k in range(n_lanes):
+                    value = last[kind, layer, k, at, :]
+                    if k == 0:
+                        value = jnp.where(lane < KEEP, turn(edge, -HALF * layer - OUT, 1), value)
+                    if k == n_lanes - 1:
+                        value = jnp.where(
+                            lane >= LANES - KEEP, turn(edge, -HALF * layer - SIDE - OUT, 1), value
+                        )
+                    merged[kind, layer, at, lane_tile(k)] = value
+    copy = pltpu.make_async_copy(merged, out_fields, sem)
+    copy.start()
     copy.wait()
 
 
@@ -717,11 +730,10 @@
     )(*blocks, cross, near, src, pool_matrices(), base, place)
 
     plane = (ext_rows, LANES)
-    fields, outgoing = call(
+    edge_last, edge_g = call(
         edge_kernel,
-        (shape(3, 2, rows, cols), shape(owners * capacity, width)),
-        7,
-        out_specs=(pl.BlockSpec(memory_space=pl.ANY), vmem()),
+        (shape(3, rows, LANES), shape(*plane)),
+        4,
         scratch=(
             pltpu.VMEM((1 + STEPS,) + plane, F32),
             pltpu.VMEM((2,) + plane, F32),
@@ -729,12 +741,23 @@
             pltpu.VMEM(plane, F32),
             pltpu.VMEM((STEPS,) + plane, F32),
             pltpu.VMEM(plane, F32),
-            pltpu.VMEM((3, 2, rows, cols), F32),
-            pltpu.SemaphoreType.DMA,
+            pltpu.VMEM((3, rows, LANES), F32),
         ),
         flops=50 * cells,
         size=16 * cells,
-    )(last, slots, base, cross_cols, near_cols, src_edge, place_edge)
+    )(base, cross_cols, near_cols, src_edge)
+    (outgoing,) = call(
+        tiles_kernel, (shape(owners * capacity, width),), 3, flops=20 * cells, size=4 * cells
+    )(edge_g, slots, place_edge)
+    (fields,) = call(
+        merge_kernel,
+        (shape(3, 2, rows, cols),),
+        2,
+        out_specs=(pl.BlockSpec(memory_space=pl.ANY),),
+        scratch=(pltpu.VMEM((3, 2, rows, cols), F32), pltpu.SemaphoreType.DMA),
+        flops=20 * cells,
+        size=48 * cells,
+    )(last, edge_last)
 
     outgoing = outgoing.reshape(owners, capacity, width)
     incoming = lax.all_to_all(outgoing, ("gx", "gy"), split_axis=0, concat_axis=0, tiled=True)

time: 32.5 us -> 32 us (0.985)
  blocking collectives: 11.7 us -> 0 us
  waiting for transfers between devices: 0.78 us -> 6.95 us
  starting transfers between devices: 10.2 us -> 14.7 us
  Pallas kernels: 8.16 us -> 8.57 us
    all_to_all x1 -> x0, blocking collectives: 11.7 us -> none  [on_device(): lax.all_to_all(outgoing, ('gx', 'gy'), split_axis=0, concat_axis=0, tiled...]
    all_to_all x0 -> x1, waiting for transfers between devices: none -> 6.19 us  [on_device(): lax.all_to_all(outgoing, ('gx', 'gy'), split_axis=0, concat_axis=0, tiled...]
    all_to_all x0 -> x1, starting transfers between devices: none -> 4.54 us  [on_device(): lax.all_to_all(outgoing, ('gx', 'gy'), split_axis=0, concat_axis=0, tiled...]
    pallas_call x1 -> x3, Pallas kernels: 2.75 us -> 3.14 us  [the longest x1 1.16 us: on_device(): call(merge_kernel, (shape(3, 2, rows, cols),), 2, out_specs=(pl.BlockSpec...]
  transfers between devices with their start and end apart: 4 -> 5, of which waited for: 1 -> 2; matrix products, arithmetic and copies ran while one was open for 0% -> 0% of each run, Pallas kernels for 12% -> 16%
where the time goes in v8:
time: 32 us; the launch traced here: 31.7 us
  starting transfers between devices  14.7 us (46%)
  Pallas kernels  8.57 us (27%)
  waiting for transfers between devices  6.95 us (22%)
  between operations  0.83 us (3%)
  local copies, waits for them, and re-layouts  0.7 us (2%)
    all_to_all x1, waiting for transfers between devices, on_device(): lax.all_to_all(outgoing, ('gx', 'gy'), split_axis=0, concat_axis=0, tiled...  6.19 us
    all_to_all x1, starting transfers between devices, on_device(): lax.all_to_all(outgoing, ('gx', 'gy'), split_axis=0, concat_axis=0, tiled...  4.54 us
    ppermute x1, starting transfers between devices, on_device(): near_cols = lax.ppermute(near_cols, 'gy', pairs(gy_count, 0))  4.46 us
    ppermute x1, starting transfers between devices, on_device(): near = lax.ppermute(near, 'gx', pairs(gx_count, 0))  4.36 us
    pallas_call x1, Pallas kernels, on_device(): call(inner_kernel, (shape(3, 2, n_lanes, rows, LANES), shape(owners * cap...  2.06 us
    pallas_call x1, Pallas kernels, on_device(): call(lambda *refs: prep_kernel(capacity, *refs), (packed, packed, shape(4...  1.99 us
    pallas_call x1, Pallas kernels, on_device(): call(rows_kernel, (strip, strip), 3, in_space=pltpu.HBM, scratch=(pltpu.V...  1.21 us
    pallas_call x1, Pallas kernels, on_device(): call(merge_kernel, (shape(3, 2, rows, cols),), 2, out_specs=(pl.BlockSpec...  1.16 us
  transfers between devices with their start and end apart: 5, of which 2 were waited for; matrix products, arithmetic and copies ran while one was open for 0% of the time, Pallas kernels for 16%

profile of v8, /device:TPU:0, one launch (start us, length us, event | category | flops | bytes accessed | tf_op | source)
XLA Modules:
  0.0 31.7 jit_solution(9459611647030143976)
XLA Ops:
  0.6 0.0 copy-start
  0.6 0.0 copy-start.2
  0.7 0.0 copy-start.1
  0.7 0.0 copy-start.8
  0.7 0.0 copy-start.7
  0.7 0.0 copy-start.4
  0.7 0.0 copy-start.6
  0.7 0.0 copy-start.5
  0.7 1.2 %shard_map.104 = (f32[16,8,256]{2,1,0:T(8,128)S(1)}, f32[16,8,256]{2,1,0:T(8,128)S(1)}) custom-call(f32[3,2,128,256]{3,2,1,0:T(8,128)} %fields.3, f32[2,128,256]{2,1,0:T(8,128)} %eps.3, f32[4,2,128,256]{3,2,1,0:T(8,128)} %fwd.3), custom_call_target="tpu_custom_call" | custom-call | bytes 1048576 | tf_op jit(solution)/shard_map/pallas_call | solution.py:665
  1.9 0.0 copy-start.3
  1.9 0.7 %collective-permute-start = (f32[16,8,256]{2,1,0:T(8,128)S(1)}, f32[16,8,256]{2,1,0:T(8,128)S(1)}, u32[]{:S(2)}, u32[]{:S(2)}) collective-permute-start(f32[16,8,256]{2,1,0:T(8,128)S(1)} %get-tuple-element.18), channel_id=1, source_target_pairs={{4,8},{8,4},{5,9},{9,5},{6,10},{10,6},{7,11},{11,7},{20,24},{24,20... | collective-permute-start | bytes 393224 | tf_op jit(solution)/shard_map/ppermute | solution.py:679
  2.6 4.4 %collective-permute-start.1 = (f32[16,8,256]{2,1,0:T(8,128)S(1)}, f32[16,8,256]{2,1,0:T(8,128)S(1)}, u32[]{:S(2)}, u32[]{:S(2)}) collective-permute-start(f32[16,8,256]{2,1,0:T(8,128)S(1)} %get-tuple-element.19), channel_id=1, source_target_pairs={{0,4},{8,12},{4,0},{12,8},{1,5},{9,13},{5,1},{13,9},{2,6},{10,14},... | collective-permute-start | bytes 393224 | tf_op jit(solution)/shard_map/ppermute | solution.py:680
  7.0 0.0 copy-done
  7.0 0.0 copy-done.2
  7.0 0.0 copy-done.1
  7.0 0.0 copy-done.8
  7.0 0.0 copy-done.7
  7.0 0.0 copy-done.4
  7.0 0.0 copy-done.6
  7.0 0.0 copy-done.5
  7.0 2.0 %shard_map.105 = (f32[160,128]{1,0:T(8,128)S(1)}, f32[160,128]{1,0:T(8,128)S(1)}, f32[8,160,128]{2,1,0:T(8,128)S(1)}, f32[4,2,160,256]{3,2,1,0:T(8,128)S(1)}, f3...) custom-call(f32[3,2,128,256]{3,2,1,0:T(8,128)S(1)} %copy-done.1, ...), custom_call_target="tpu_custom_call" | custom-call | flops 188743680 | bytes 2097152 | tf_op jit(solution)/shard_map/pallas_call | solution.py:684
  9.0 0.0 collective-permute-done.cross.cross_rows
  9.0 0.0 collective-permute-done.1.near.near_rows
  9.1 0.2 shard_map.107
  9.2 0.7 %collective-permute-start.2 = (f32[160,128]{1,0:T(8,128)S(1)}, f32[160,128]{1,0:T(8,128)S(1)}, u32[]{:S(2)}, u32[]{:S(2)}) collective-permute-start(f32[160,128]{1,0:T(8,128)S(1)} %get-tuple-element.27), channel_id=1, source_target_pairs={{1,2},{2,1},{5,6},{6,5},{9,10},{10,9},{13,14},{14,13},{17,18},{18,... | collective-permute-start | bytes 245768 | tf_op jit(solution)/shard_map/ppermute | solution.py:709
  9.9 4.5 %collective-permute-start.3 = (f32[160,128]{1,0:T(8,128)S(1)}, f32[160,128]{1,0:T(8,128)S(1)}, u32[]{:S(2)}, u32[]{:S(2)}) collective-permute-start(f32[160,128]{1,0:T(8,128)S(1)} %get-tuple-element.28), channel_id=1, source_target_pairs={{0,1},{2,3},{1,0},{3,2},{4,5},{6,7},{5,4},{7,6},{8,9},{10,11},{9,8... | collective-permute-start | bytes 245768 | tf_op jit(solution)/shard_map/ppermute | solution.py:710
  14.4 0.0 copy-done.3
  14.4 2.1 %shard_map.106 = (f32[3,2,2,128,128]{4,3,2,1,0:T(8,128)S(1)}, f32[256,128]{1,0:T(8,128)S(1)}, f32[8,160,128]{2,1,0:T(8,128)S(1)}) custom-call(f32[3,2,128,256]{3,2,1,0:T(8,128)S(1)} %copy-done.1, f32[2,128,256]{2,1,0:T(8,128)S(1)} %copy-done.2, f32[4,2,128,256]{3,2,1,0:T(8,128)S(1)} %copy-done, f32[16,8,256]{2,1,0:T(8,128)S(1)} %collective-permute-done.cross.cross_rows, ...), custom_call_target="tpu_custom_call" | custom-call | flops 6553600 | bytes 3145728 | tf_op jit(solution)/shard_map/pallas_call | solution.py:713
  16.4 0.0 collective-permute-done.2.cross
  16.4 0.8 %collective-permute-done.3.near = f32[160,128]{1,0:T(8,128)S(1)} collective-permute-done((f32[160,128]{1,0:T(8,128)S(1)}, f32[160,128]{1,0:T(8,128)S(1)}, u32[]{:S(2)}, u32[]{:S(2)}) %collective-permute-start.3) | collective-permute-done | bytes 81952 | tf_op jit(solution)/shard_map/ppermute | solution.py:710
  17.2 0.8 %shard_map.108 = (f32[3,128,128]{2,1,0:T(8,128)S(1)}, f32[160,128]{1,0:T(8,128)S(1)}) custom-call(f32[8,160,128]{2,1,0:T(8,128)S(1)} %get-tuple-element.24.base, f32[160,128]{1,0:T(8,128)S(1)} %collective-permute-done.2.cross, f32[160,128]{1,0:T(8,128)S(1)} %collective-permute-done.3.near, f32[4,160,128]{2,1,0:T(8,128)S(1)} %get-tuple-element.29.src), custom_call_target="tpu_custom_call" | custom-call | flops 1638400 | bytes 524288 | tf_op jit(solution)/shard_map/pallas_call | solution.py:733
  18.0 1.1 %shard_map.110 = f32[256,128]{1,0:T(8,128)} custom-call(f32[160,128]{1,0:T(8,128)S(1)} %get-tuple-element.31.g, f32[256,128]{1,0:T(8,128)S(1)} %get-tuple-element.32.slots_in, bf16[256,32]{1,0:T(8,128)(2,1)S(1)} %get-tuple-element.33.place), custom_call_target="tpu_custom_call" | custom-call | flops 655360 | bytes 131072 | tf_op jit(solution)/shard_map/pallas_call | solution.py:749
  19.2 4.5 %all-to-all-start = ((f32[16,16,128]{2,1,0:T(8,128)}), f32[16,16,128]{2,1,0:T(8,128)S(1)}, u32[]{:S(2)}, u32[]{:S(2)}) async-start(f32[16,16,128]{2,1,0:T(8,128)} %bitcast.4), calls=%async_computation | async-start | bytes 262144 | tf_op jit(solution)/shard_map/all_to_all | solution.py:763
  23.7 1.2 %shard_map.109 = f32[3,2,128,256]{3,2,1,0:T(8,128)} custom-call(f32[3,2,2,128,128]{4,3,2,1,0:T(8,128)S(1)} %get-tuple-element.23.last, f32[3,128,128]{2,1,0:T(8,128)S(1)} %get-tuple-element.30.edge_last), custom_call_target="tpu_custom_call" | custom-call | flops 655360 | bytes 1572864 | tf_op jit(solution)/shard_map/pallas_call | solution.py:752
  24.9 6.2 %all-to-all-done = f32[16,16,128]{2,1,0:T(8,128)S(1)} async-done(((f32[16,16,128]{2,1,0:T(8,128)}), f32[16,16,128]{2,1,0:T(8,128)S(1)}, u32[]{:S(2)}, u32[]{:S(2)}) %all-to-all-start) | async-done | bytes 131104 | tf_op jit(solution)/shard_map/all_to_all | solution.py:763
  31.1 0.7 %copy.12 = f32[1,16,16,128]{3,2,1,0:T(8,128)} copy(f32[1,16,16,128]{3,2,1,0:T(8,128)S(1)} %bitcast.10) | data formatting | bytes 262144
Async XLA Ops:
  0.6 6.4 %copy-start = (f32[4,2,128,256]{3,2,1,0:T(8,128)S(1)}, f32[4,2,128,256]{3,2,1,0:T(8,128)}, u32[]{:S(2)}) copy-start(f32[4,2,128,256]{3,2,1,0:T(8,128)} %fwd.3) | copy-start | bytes 3145732
  0.6 6.3 %copy-start.2 = (f32[2,128,256]{2,1,0:T(8,128)S(1)}, f32[2,128,256]{2,1,0:T(8,128)}, u32[]{:S(2)}) copy-start(f32[2,128,256]{2,1,0:T(8,128)} %eps.3) | copy-start | bytes 786436
  0.7 6.3 %copy-start.1 = (f32[3,2,128,256]{3,2,1,0:T(8,128)S(1)}, f32[3,2,128,256]{3,2,1,0:T(8,128)}, u32[]{:S(2)}) copy-start(f32[3,2,128,256]{3,2,1,0:T(8,128)} %fields.3) | copy-start | bytes 2359300
  0.7 6.3 %copy-start.8 = (s32[1,1,128,1]{2,3,1,0:T(1,128)S(1)}, s32[1,1,128,1]{2,3,1,0:T(1,128)}, u32[]{:S(2)}) copy-start(s32[1,1,128,1]{2,3,1,0:T(1,128)} %param.16) | copy-start | bytes 1540
  0.7 6.3 %copy-start.7 = (s32[1,1,128]{2,1,0:T(1,128)S(1)}, s32[1,1,128]{2,1,0:T(1,128)}, u32[]{:S(2)}) copy-start(s32[1,1,128]{2,1,0:T(1,128)} %param.15) | copy-start | bytes 1540
  0.7 6.3 %copy-start.4 = (f32[4,64]{1,0:T(4,128)S(1)}, f32[4,64]{1,0:T(4,128)}, u32[]{:S(2)}) copy-start(f32[4,64]{1,0:T(4,128)} %refs_5_.1) | copy-start | bytes 3076
  0.7 6.3 %copy-start.6 = (s32[64]{0:T(128)S(1)}, s32[64]{0:T(128)}, u32[]{:S(2)}) copy-start(s32[64]{0:T(128)} %param.13) | copy-start | bytes 772
  0.7 6.3 %copy-start.5 = (s32[64]{0:T(128)S(1)}, s32[64]{0:T(128)}, u32[]{:S(2)}) copy-start(s32[64]{0:T(128)} %param.12) | copy-start | bytes 772
  1.9 12.4 %copy-start.3 = (bf16[2,128,128]{2,1,0:T(8,128)(2,1)S(1)}, bf16[2,128,128]{2,1,0:T(8,128)(2,1)}, u32[]{:S(2)}) copy-start(bf16[2,128,128]{2,1,0:T(8,128)(2,1)} %constant.2.clone.mats) | copy-start | bytes 196612
  1.9 7.1 %collective-permute-start = (f32[16,8,256]{2,1,0:T(8,128)S(1)}, f32[16,8,256]{2,1,0:T(8,128)S(1)}, u32[]{:S(2)}, u32[]{:S(2)}) collective-permute-start(f32[16,8,256]{2,1,0:T(8,128)S(1)} %get-tuple-element.18), channel_id=1, source_target_pairs={{4,8},{8,4},{5,9},{9,5},{6,10},{10,6},{7,11},{11,7},{20,24},{24,20... | collective-permute-start | bytes 393224 | tf_op jit(solution)/shard_map/ppermute | solution.py:679
  2.6 6.4 %collective-permute-start.1 = (f32[16,8,256]{2,1,0:T(8,128)S(1)}, f32[16,8,256]{2,1,0:T(8,128)S(1)}, u32[]{:S(2)}, u32[]{:S(2)}) collective-permute-start(f32[16,8,256]{2,1,0:T(8,128)S(1)} %get-tuple-element.19), channel_id=1, source_target_pairs={{0,4},{8,12},{4,0},{12,8},{1,5},{9,13},{5,1},{13,9},{2,6},{10,14},... | collective-permute-start | bytes 393224 | tf_op jit(solution)/shard_map/ppermute | solution.py:680
  9.2 7.2 %collective-permute-start.2 = (f32[160,128]{1,0:T(8,128)S(1)}, f32[160,128]{1,0:T(8,128)S(1)}, u32[]{:S(2)}, u32[]{:S(2)}) collective-permute-start(f32[160,128]{1,0:T(8,128)S(1)} %get-tuple-element.27), channel_id=1, source_target_pairs={{1,2},{2,1},{5,6},{6,5},{9,10},{10,9},{13,14},{14,13},{17,18},{18,... | collective-permute-start | bytes 245768 | tf_op jit(solution)/shard_map/ppermute | solution.py:709
  9.9 7.3 %collective-permute-start.3 = (f32[160,128]{1,0:T(8,128)S(1)}, f32[160,128]{1,0:T(8,128)S(1)}, u32[]{:S(2)}, u32[]{:S(2)}) collective-permute-start(f32[160,128]{1,0:T(8,128)S(1)} %get-tuple-element.28), channel_id=1, source_target_pairs={{0,1},{2,3},{1,0},{3,2},{4,5},{6,7},{5,4},{7,6},{8,9},{10,11},{9,8... | collective-permute-start | bytes 245768 | tf_op jit(solution)/shard_map/ppermute | solution.py:710
  19.2 11.9 %all-to-all-start = ((f32[16,16,128]{2,1,0:T(8,128)}), f32[16,16,128]{2,1,0:T(8,128)S(1)}, u32[]{:S(2)}, u32[]{:S(2)}) async-start(f32[16,16,128]{2,1,0:T(8,128)} %bitcast.4), calls=%async_computation | async-start | bytes 262144 | tf_op jit(solution)/shard_map/all_to_all | solution.py:763

commit v9 on v8

--- a/solution.py
+++ b/solution.py
@@ -489,25 +489,6 @@
     return jnp.stack([new_even, new_odd], axis=1).reshape(tile_rows * 2 * span, LANES)
 
 
-def merge_spans(spans, lane):
-    even = (lane & 1) == 0
-    window = ((lane - OUT) & (HALF - 1)) < SIDE
-    merged = []
-    for e in (0, 4):
-        low = jnp.where(even, spans[e], turn(spans[e + 1], 1, 1))
-        high = jnp.where(even, turn(spans[e + 2], SIDE, 1), turn(spans[e + 3], SIDE + 1, 1))
-        merged.append(jnp.where(window, low, high))
-    span = TS // PIX
-    row, pixel = lane // span % span, lane % span
-    start = (lane & HALF) + OUT + PIX * pixel + (row & 1) + SIDE * ((row >> 1) & 1)
-    result = []
-    for side in range(2):
-        index = (start + OUT * side) & (LANES - 1)
-        low, high = (jnp.take_along_axis(value, index, axis=1) for value in merged)
-        result.append(jnp.where(row < span // 2, low, high))
-    return result
-
-
 def edge_kernel(
     base, cross, near, src, out, g_out, e, first, curl, eps_c, d, g, result
 ):
@@ -572,19 +553,19 @@
     out[...] = result[...]
 
 
-def tiles_kernel(g, slots_in, place, slots):
+def edge_filter_kernel(g, merged):
     lane = lanes()
     span, reach = TS // PIX, RADIUS - 1
     pixel = {}
     for j in range(-reach, span + reach):
         value = g[pl.ds(PAD + PIX * j, SUB, stride=TS), :]
-        value = value + g[pl.ds(PAD + PIX * j + 1, SUB, stride=TS), :]
-        pixel[j] = value + turn(value, -1, 1)
+        pixel[j] = value + g[pl.ds(PAD + PIX * j + 1, SUB, stride=TS), :]
 
     weights = cone_weights(RADIUS)
     spans = []
     for row in range(span):
         sums = [pixel[row]] + [pixel[row + s] + pixel[row - s] for s in range(1, reach + 1)]
+        move = (row & 1) + SIDE * ((row >> 1) & 1)
         total = None
         for shift in range(reach + 1):
             mixed = None
@@ -593,13 +574,29 @@
                 if weight > 0.0:
                     term = weight * sums[s]
                     mixed = term if mixed is None else mixed + term
-            if shift:
-                mixed = turn(mixed, -PIX * shift, 1) + turn(mixed, PIX * shift, 1)
-            total = mixed if total is None else total + mixed
+            for place in {PIX * shift, -PIX * shift}:
+                term = turn(mixed, move + place, 1) + turn(mixed, move + place - 1, 1)
+                total = term if total is None else total + term
         spans.append(total)
-
-    edge = jnp.concatenate(merge_spans(spans, lane), axis=0)
-    slots[...] = slots_in[...] + dot(place[...], jnp.concatenate(split2(edge), axis=0))
+    even = (lane & 1) == 0
+    window = ((lane - OUT) & (HALF - 1)) < SIDE
+    for n in range(2):
+        a, b, c, d = spans[4 * n : 4 * n + 4]
+        merged[n] = jnp.where(window, jnp.where(even, a, b), jnp.where(even, c, d))
+
+
+def edge_slots_kernel(merged, slots_in, place, slots):
+    lane = lanes()
+    span = TS // PIX
+    row, pixel = lane // span % span, lane % span
+    start = (lane & HALF) + OUT + PIX * pixel + (row & 1) + SIDE * ((row >> 1) & 1)
+    edge = []
+    for side in range(2):
+        index = (start + OUT * side) & (LANES - 1)
+        low, high = (jnp.take_along_axis(merged[n], index, axis=1) for n in range(2))
+        edge.append(jnp.where(row < span // 2, low, high))
+    parts = split2(jnp.concatenate(edge, axis=0))
+    slots[...] = slots_in[...] + dot(place[...], jnp.concatenate(parts, axis=0))
 
 
 def merge_kernel(last, edge_last, out_fields, merged, sem):
@@ -746,9 +743,12 @@
         flops=50 * cells,
         size=16 * cells,
     )(base, cross_cols, near_cols, src_edge)
+    (merged,) = call(
+        edge_filter_kernel, (shape(2, SUB, LANES),), 1, flops=20 * cells, size=4 * cells
+    )(edge_g)
     (outgoing,) = call(
-        tiles_kernel, (shape(owners * capacity, width),), 3, flops=20 * cells, size=4 * cells
-    )(edge_g, slots, place_edge)
+        edge_slots_kernel, (shape(owners * capacity, width),), 3, flops=20 * cells, size=4 * cells
+    )(merged, slots, place_edge)
     (fields,) = call(
         merge_kernel,
         (shape(3, 2, rows, cols),),

time: 32 us -> 32 us (level)
    pallas_call x1 -> x2, Pallas kernels: 1.14 us -> 1.08 us  [the longest x1 0.89 us: on_device(): call(edge_slots_kernel, (shape(owners * capacity, width),), 3, flops=20 *...]
where the time goes in v9:
time: 32 us; the launch traced here: 31.7 us
  starting transfers between devices  14.7 us (46%)
  Pallas kernels  8.51 us (27%)
  waiting for transfers between devices  6.95 us (22%)
  between operations  0.84 us (3%)
  local copies, waits for them, and re-layouts  0.7 us (2%)
    all_to_all x1, waiting for transfers between devices, on_device(): lax.all_to_all(outgoing, ('gx', 'gy'), split_axis=0, concat_axis=0, tiled...  6.19 us
    all_to_all x1, starting transfers between devices, on_device(): lax.all_to_all(outgoing, ('gx', 'gy'), split_axis=0, concat_axis=0, tiled...  4.55 us
    ppermute x1, starting transfers between devices, on_device(): near_cols = lax.ppermute(near_cols, 'gy', pairs(gy_count, 0))  4.46 us
    ppermute x1, starting transfers between devices, on_device(): near = lax.ppermute(near, 'gx', pairs(gx_count, 0))  4.36 us
    pallas_call x1, Pallas kernels, on_device(): call(inner_kernel, (shape(3, 2, n_lanes, rows, LANES), shape(owners * cap...  2.06 us
    pallas_call x1, Pallas kernels, on_device(): call(lambda *refs: prep_kernel(capacity, *refs), (packed, packed, shape(4...  1.99 us
    pallas_call x1, Pallas kernels, on_device(): call(rows_kernel, (strip, strip), 3, in_space=pltpu.HBM, scratch=(pltpu.V...  1.21 us
    pallas_call x1, Pallas kernels, on_device(): call(merge_kernel, (shape(3, 2, rows, cols),), 2, out_specs=(pl.BlockSpec...  1.16 us
  transfers between devices with their start and end apart: 5, of which 2 were waited for; matrix products, arithmetic and copies ran while one was open for 0% of the time, Pallas kernels for 16%

profile of v9, /device:TPU:0, one launch (start us, length us, event | category | flops | bytes accessed | tf_op | source)
XLA Modules:
  0.0 31.7 jit_solution(14271584408745762273)
XLA Ops:
  0.6 0.0 copy-start
  0.6 0.0 copy-start.2
  0.7 0.0 copy-start.1
  0.7 0.0 copy-start.8
  0.7 0.0 copy-start.7
  0.7 0.0 copy-start.4
  0.7 0.0 copy-start.6
  0.7 0.0 copy-start.5
  0.7 1.2 %shard_map.104 = (f32[16,8,256]{2,1,0:T(8,128)S(1)}, f32[16,8,256]{2,1,0:T(8,128)S(1)}) custom-call(f32[3,2,128,256]{3,2,1,0:T(8,128)} %fields.3, f32[2,128,256]{2,1,0:T(8,128)} %eps.3, f32[4,2,128,256]{3,2,1,0:T(8,128)} %fwd.3), custom_call_target="tpu_custom_call" | custom-call | bytes 1048576 | tf_op jit(solution)/shard_map/pallas_call | solution.py:662
  1.9 0.0 copy-start.3
  1.9 0.7 %collective-permute-start = (f32[16,8,256]{2,1,0:T(8,128)S(1)}, f32[16,8,256]{2,1,0:T(8,128)S(1)}, u32[]{:S(2)}, u32[]{:S(2)}) collective-permute-start(f32[16,8,256]{2,1,0:T(8,128)S(1)} %get-tuple-element.18), channel_id=1, source_target_pairs={{4,8},{8,4},{5,9},{9,5},{6,10},{10,6},{7,11},{11,7},{20,24},{24,20... | collective-permute-start | bytes 393224 | tf_op jit(solution)/shard_map/ppermute | solution.py:676
  2.6 4.4 %collective-permute-start.1 = (f32[16,8,256]{2,1,0:T(8,128)S(1)}, f32[16,8,256]{2,1,0:T(8,128)S(1)}, u32[]{:S(2)}, u32[]{:S(2)}) collective-permute-start(f32[16,8,256]{2,1,0:T(8,128)S(1)} %get-tuple-element.19), channel_id=1, source_target_pairs={{0,4},{8,12},{4,0},{12,8},{1,5},{9,13},{5,1},{13,9},{2,6},{10,14},... | collective-permute-start | bytes 393224 | tf_op jit(solution)/shard_map/ppermute | solution.py:677
  7.0 0.0 copy-done
  7.0 0.0 copy-done.2
  7.0 0.0 copy-done.1
  7.0 0.0 copy-done.8
  7.0 0.0 copy-done.7
  7.0 0.0 copy-done.4
  7.0 0.0 copy-done.6
  7.0 0.0 copy-done.5
  7.0 2.0 %shard_map.105 = (f32[160,128]{1,0:T(8,128)S(1)}, f32[160,128]{1,0:T(8,128)S(1)}, f32[8,160,128]{2,1,0:T(8,128)S(1)}, f32[4,2,160,256]{3,2,1,0:T(8,128)S(1)}, f3...) custom-call(f32[3,2,128,256]{3,2,1,0:T(8,128)S(1)} %copy-done.1, ...), custom_call_target="tpu_custom_call" | custom-call | flops 188743680 | bytes 2097152 | tf_op jit(solution)/shard_map/pallas_call | solution.py:681
  9.0 0.0 collective-permute-done.cross.cross_rows
  9.0 0.0 collective-permute-done.1.near.near_rows
  9.1 0.2 shard_map.107
  9.2 0.7 %collective-permute-start.2 = (f32[160,128]{1,0:T(8,128)S(1)}, f32[160,128]{1,0:T(8,128)S(1)}, u32[]{:S(2)}, u32[]{:S(2)}) collective-permute-start(f32[160,128]{1,0:T(8,128)S(1)} %get-tuple-element.27), channel_id=1, source_target_pairs={{1,2},{2,1},{5,6},{6,5},{9,10},{10,9},{13,14},{14,13},{17,18},{18,... | collective-permute-start | bytes 245768 | tf_op jit(solution)/shard_map/ppermute | solution.py:706
  9.9 4.5 %collective-permute-start.3 = (f32[160,128]{1,0:T(8,128)S(1)}, f32[160,128]{1,0:T(8,128)S(1)}, u32[]{:S(2)}, u32[]{:S(2)}) collective-permute-start(f32[160,128]{1,0:T(8,128)S(1)} %get-tuple-element.28), channel_id=1, source_target_pairs={{0,1},{2,3},{1,0},{3,2},{4,5},{6,7},{5,4},{7,6},{8,9},{10,11},{9,8... | collective-permute-start | bytes 245768 | tf_op jit(solution)/shard_map/ppermute | solution.py:707
  14.4 0.0 copy-done.3
  14.4 2.1 %shard_map.106 = (f32[3,2,2,128,128]{4,3,2,1,0:T(8,128)S(1)}, f32[256,128]{1,0:T(8,128)S(1)}, f32[8,160,128]{2,1,0:T(8,128)S(1)}) custom-call(f32[3,2,128,256]{3,2,1,0:T(8,128)S(1)} %copy-done.1, f32[2,128,256]{2,1,0:T(8,128)S(1)} %copy-done.2, f32[4,2,128,256]{3,2,1,0:T(8,128)S(1)} %copy-done, f32[16,8,256]{2,1,0:T(8,128)S(1)} %collective-permute-done.cross.cross_rows, ...), custom_call_target="tpu_custom_call" | custom-call | flops 6553600 | bytes 3145728 | tf_op jit(solution)/shard_map/pallas_call | solution.py:710
  16.4 0.0 collective-permute-done.2.cross
  16.4 0.8 %collective-permute-done.3.near = f32[160,128]{1,0:T(8,128)S(1)} collective-permute-done((f32[160,128]{1,0:T(8,128)S(1)}, f32[160,128]{1,0:T(8,128)S(1)}, u32[]{:S(2)}, u32[]{:S(2)}) %collective-permute-start.3) | collective-permute-done | bytes 81952 | tf_op jit(solution)/shard_map/ppermute | solution.py:707
  17.2 0.8 %shard_map.108 = (f32[3,128,128]{2,1,0:T(8,128)S(1)}, f32[160,128]{1,0:T(8,128)S(1)}) custom-call(f32[8,160,128]{2,1,0:T(8,128)S(1)} %get-tuple-element.24.base, f32[160,128]{1,0:T(8,128)S(1)} %collective-permute-done.2.cross, f32[160,128]{1,0:T(8,128)S(1)} %collective-permute-done.3.near, f32[4,160,128]{2,1,0:T(8,128)S(1)} %get-tuple-element.29.src), custom_call_target="tpu_custom_call" | custom-call | flops 1638400 | bytes 524288 | tf_op jit(solution)/shard_map/pallas_call | solution.py:730
  18.0 0.2 shard_map.110.merged
  18.2 0.9 %shard_map.111 = f32[256,128]{1,0:T(8,128)} custom-call(f32[2,8,128]{2,1,0:T(8,128)S(1)} %shard_map.110.merged, f32[256,128]{1,0:T(8,128)S(1)} %get-tuple-element.32.slots_in, bf16[256,32]{1,0:T(8,128)(2,1)S(1)} %get-tuple-element.33.place), custom_call_target="tpu_custom_call" | custom-call | flops 655360 | bytes 131072 | tf_op jit(solution)/shard_map/pallas_call | solution.py:749
  19.1 4.5 %all-to-all-start = ((f32[16,16,128]{2,1,0:T(8,128)}), f32[16,16,128]{2,1,0:T(8,128)S(1)}, u32[]{:S(2)}, u32[]{:S(2)}) async-start(f32[16,16,128]{2,1,0:T(8,128)} %bitcast.4), calls=%async_computation | async-start | bytes 262144 | tf_op jit(solution)/shard_map/all_to_all | solution.py:763
  23.7 1.2 %shard_map.109 = f32[3,2,128,256]{3,2,1,0:T(8,128)} custom-call(f32[3,2,2,128,128]{4,3,2,1,0:T(8,128)S(1)} %get-tuple-element.23.last, f32[3,128,128]{2,1,0:T(8,128)S(1)} %get-tuple-element.30.edge_last), custom_call_target="tpu_custom_call" | custom-call | flops 655360 | bytes 1572864 | tf_op jit(solution)/shard_map/pallas_call | solution.py:752
  24.9 6.2 %all-to-all-done = f32[16,16,128]{2,1,0:T(8,128)S(1)} async-done(((f32[16,16,128]{2,1,0:T(8,128)}), f32[16,16,128]{2,1,0:T(8,128)S(1)}, u32[]{:S(2)}, u32[]{:S(2)}) %all-to-all-start) | async-done | bytes 131104 | tf_op jit(solution)/shard_map/all_to_all | solution.py:763
  31.0 0.7 %copy.12 = f32[1,16,16,128]{3,2,1,0:T(8,128)} copy(f32[1,16,16,128]{3,2,1,0:T(8,128)S(1)} %bitcast.10) | data formatting | bytes 262144
Async XLA Ops:
  0.6 6.4 %copy-start = (f32[4,2,128,256]{3,2,1,0:T(8,128)S(1)}, f32[4,2,128,256]{3,2,1,0:T(8,128)}, u32[]{:S(2)}) copy-start(f32[4,2,128,256]{3,2,1,0:T(8,128)} %fwd.3) | copy-start | bytes 3145732
  0.6 6.3 %copy-start.2 = (f32[2,128,256]{2,1,0:T(8,128)S(1)}, f32[2,128,256]{2,1,0:T(8,128)}, u32[]{:S(2)}) copy-start(f32[2,128,256]{2,1,0:T(8,128)} %eps.3) | copy-start | bytes 786436
  0.7 6.3 %copy-start.1 = (f32[3,2,128,256]{3,2,1,0:T(8,128)S(1)}, f32[3,2,128,256]{3,2,1,0:T(8,128)}, u32[]{:S(2)}) copy-start(f32[3,2,128,256]{3,2,1,0:T(8,128)} %fields.3) | copy-start | bytes 2359300
  0.7 6.3 %copy-start.8 = (s32[1,1,128,1]{2,3,1,0:T(1,128)S(1)}, s32[1,1,128,1]{2,3,1,0:T(1,128)}, u32[]{:S(2)}) copy-start(s32[1,1,128,1]{2,3,1,0:T(1,128)} %param.16) | copy-start | bytes 1540
  0.7 6.3 %copy-start.7 = (s32[1,1,128]{2,1,0:T(1,128)S(1)}, s32[1,1,128]{2,1,0:T(1,128)}, u32[]{:S(2)}) copy-start(s32[1,1,128]{2,1,0:T(1,128)} %param.15) | copy-start | bytes 1540
  0.7 6.3 %copy-start.4 = (f32[4,64]{1,0:T(4,128)S(1)}, f32[4,64]{1,0:T(4,128)}, u32[]{:S(2)}) copy-start(f32[4,64]{1,0:T(4,128)} %refs_5_.1) | copy-start | bytes 3076
  0.7 6.3 %copy-start.6 = (s32[64]{0:T(128)S(1)}, s32[64]{0:T(128)}, u32[]{:S(2)}) copy-start(s32[64]{0:T(128)} %param.13) | copy-start | bytes 772
  0.7 6.3 %copy-start.5 = (s32[64]{0:T(128)S(1)}, s32[64]{0:T(128)}, u32[]{:S(2)}) copy-start(s32[64]{0:T(128)} %param.12) | copy-start | bytes 772
  1.9 12.4 %copy-start.3 = (bf16[2,128,128]{2,1,0:T(8,128)(2,1)S(1)}, bf16[2,128,128]{2,1,0:T(8,128)(2,1)}, u32[]{:S(2)}) copy-start(bf16[2,128,128]{2,1,0:T(8,128)(2,1)} %constant.2.clone.mats) | copy-start | bytes 196612
  1.9 7.1 %collective-permute-start = (f32[16,8,256]{2,1,0:T(8,128)S(1)}, f32[16,8,256]{2,1,0:T(8,128)S(1)}, u32[]{:S(2)}, u32[]{:S(2)}) collective-permute-start(f32[16,8,256]{2,1,0:T(8,128)S(1)} %get-tuple-element.18), channel_id=1, source_target_pairs={{4,8},{8,4},{5,9},{9,5},{6,10},{10,6},{7,11},{11,7},{20,24},{24,20... | collective-permute-start | bytes 393224 | tf_op jit(solution)/shard_map/ppermute | solution.py:676
  2.6 6.4 %collective-permute-start.1 = (f32[16,8,256]{2,1,0:T(8,128)S(1)}, f32[16,8,256]{2,1,0:T(8,128)S(1)}, u32[]{:S(2)}, u32[]{:S(2)}) collective-permute-start(f32[16,8,256]{2,1,0:T(8,128)S(1)} %get-tuple-element.19), channel_id=1, source_target_pairs={{0,4},{8,12},{4,0},{12,8},{1,5},{9,13},{5,1},{13,9},{2,6},{10,14},... | collective-permute-start | bytes 393224 | tf_op jit(solution)/shard_map/ppermute | solution.py:677
  9.2 7.2 %collective-permute-start.2 = (f32[160,128]{1,0:T(8,128)S(1)}, f32[160,128]{1,0:T(8,128)S(1)}, u32[]{:S(2)}, u32[]{:S(2)}) collective-permute-start(f32[160,128]{1,0:T(8,128)S(1)} %get-tuple-element.27), channel_id=1, source_target_pairs={{1,2},{2,1},{5,6},{6,5},{9,10},{10,9},{13,14},{14,13},{17,18},{18,... | collective-permute-start | bytes 245768 | tf_op jit(solution)/shard_map/ppermute | solution.py:706
  9.9 7.3 %collective-permute-start.3 = (f32[160,128]{1,0:T(8,128)S(1)}, f32[160,128]{1,0:T(8,128)S(1)}, u32[]{:S(2)}, u32[]{:S(2)}) collective-permute-start(f32[160,128]{1,0:T(8,128)S(1)} %get-tuple-element.28), channel_id=1, source_target_pairs={{0,1},{2,3},{1,0},{3,2},{4,5},{6,7},{5,4},{7,6},{8,9},{10,11},{9,8... | collective-permute-start | bytes 245768 | tf_op jit(solution)/shard_map/ppermute | solution.py:707
  19.1 11.9 %all-to-all-start = ((f32[16,16,128]{2,1,0:T(8,128)}), f32[16,16,128]{2,1,0:T(8,128)S(1)}, u32[]{:S(2)}, u32[]{:S(2)}) async-start(f32[16,16,128]{2,1,0:T(8,128)} %bitcast.4), calls=%async_computation | async-start | bytes 262144 | tf_op jit(solution)/shard_map/all_to_all | solution.py:763

commit v10 on v9

--- a/solution.py
+++ b/solution.py
@@ -747,7 +747,7 @@
         edge_filter_kernel, (shape(2, SUB, LANES),), 1, flops=20 * cells, size=4 * cells
     )(edge_g)
     (outgoing,) = call(
-        edge_slots_kernel, (shape(owners * capacity, width),), 3, flops=20 * cells, size=4 * cells
+        edge_slots_kernel, (pltpu.VMEM((owners * capacity, width), F32),), 3, flops=20 * cells, size=4 * cells
     )(merged, slots, place_edge)
     (fields,) = call(
         merge_kernel,

time: 32 us -> 32 us (level)
  no operation moved by 1% of the time
where the time goes in v10:
time: 32 us; the launch traced here: 31.7 us
  starting transfers between devices  14.7 us (46%)
  Pallas kernels  8.51 us (27%)
  waiting for transfers between devices  6.95 us (22%)
  between operations  0.84 us (3%)
  local copies, waits for them, and re-layouts  0.7 us (2%)
    all_to_all x1, waiting for transfers between devices, on_device(): lax.all_to_all(outgoing, ('gx', 'gy'), split_axis=0, concat_axis=0, tiled...  6.19 us
    all_to_all x1, starting transfers between devices, on_device(): lax.all_to_all(outgoing, ('gx', 'gy'), split_axis=0, concat_axis=0, tiled...  4.55 us
    ppermute x1, starting transfers between devices, on_device(): near_cols = lax.ppermute(near_cols, 'gy', pairs(gy_count, 0))  4.46 us
    ppermute x1, starting transfers between devices, on_device(): near = lax.ppermute(near, 'gx', pairs(gx_count, 0))  4.36 us
    pallas_call x1, Pallas kernels, on_device(): call(inner_kernel, (shape(3, 2, n_lanes, rows, LANES), shape(owners * cap...  2.06 us
    pallas_call x1, Pallas kernels, on_device(): call(lambda *refs: prep_kernel(capacity, *refs), (packed, packed, shape(4...  1.99 us
    pallas_call x1, Pallas kernels, on_device(): call(rows_kernel, (strip, strip), 3, in_space=pltpu.HBM, scratch=(pltpu.V...  1.21 us
    pallas_call x1, Pallas kernels, on_device(): call(merge_kernel, (shape(3, 2, rows, cols),), 2, out_specs=(pl.BlockSpec...  1.16 us
  transfers between devices with their start and end apart: 5, of which 2 were waited for; matrix products, arithmetic and copies ran while one was open for 0% of the time, Pallas kernels for 16%

profile of v10, /device:TPU:0, one launch (start us, length us, event | category | flops | bytes accessed | tf_op | source)
XLA Modules:
  0.0 31.7 jit_solution(14271584408745762273)
XLA Ops:
  0.6 0.0 copy-start
  0.6 0.0 copy-start.2
  0.7 0.0 copy-start.1
  0.7 0.0 copy-start.8
  0.7 0.0 copy-start.7
  0.7 0.0 copy-start.4
  0.7 0.0 copy-start.6
  0.7 0.0 copy-start.5
  0.7 1.2 %shard_map.104 = (f32[16,8,256]{2,1,0:T(8,128)S(1)}, f32[16,8,256]{2,1,0:T(8,128)S(1)}) custom-call(f32[3,2,128,256]{3,2,1,0:T(8,128)} %fields.3, f32[2,128,256]{2,1,0:T(8,128)} %eps.3, f32[4,2,128,256]{3,2,1,0:T(8,128)} %fwd.3), custom_call_target="tpu_custom_call" | custom-call | bytes 1048576 | tf_op jit(solution)/shard_map/pallas_call | solution.py:662
  1.9 0.0 copy-start.3
  1.9 0.7 %collective-permute-start = (f32[16,8,256]{2,1,0:T(8,128)S(1)}, f32[16,8,256]{2,1,0:T(8,128)S(1)}, u32[]{:S(2)}, u32[]{:S(2)}) collective-permute-start(f32[16,8,256]{2,1,0:T(8,128)S(1)} %get-tuple-element.18), channel_id=1, source_target_pairs={{4,8},{8,4},{5,9},{9,5},{6,10},{10,6},{7,11},{11,7},{20,24},{24,20... | collective-permute-start | bytes 393224 | tf_op jit(solution)/shard_map/ppermute | solution.py:676
  2.6 4.4 %collective-permute-start.1 = (f32[16,8,256]{2,1,0:T(8,128)S(1)}, f32[16,8,256]{2,1,0:T(8,128)S(1)}, u32[]{:S(2)}, u32[]{:S(2)}) collective-permute-start(f32[16,8,256]{2,1,0:T(8,128)S(1)} %get-tuple-element.19), channel_id=1, source_target_pairs={{0,4},{8,12},{4,0},{12,8},{1,5},{9,13},{5,1},{13,9},{2,6},{10,14},... | collective-permute-start | bytes 393224 | tf_op jit(solution)/shard_map/ppermute | solution.py:677
  7.0 0.0 copy-done
  7.0 0.0 copy-done.2
  7.0 0.0 copy-done.1
  7.0 0.0 copy-done.8
  7.0 0.0 copy-done.7
  7.0 0.0 copy-done.4
  7.0 0.0 copy-done.6
  7.0 0.0 copy-done.5
  7.0 2.0 %shard_map.105 = (f32[160,128]{1,0:T(8,128)S(1)}, f32[160,128]{1,0:T(8,128)S(1)}, f32[8,160,128]{2,1,0:T(8,128)S(1)}, f32[4,2,160,256]{3,2,1,0:T(8,128)S(1)}, f3...) custom-call(f32[3,2,128,256]{3,2,1,0:T(8,128)S(1)} %copy-done.1, ...), custom_call_target="tpu_custom_call" | custom-call | flops 188743680 | bytes 2097152 | tf_op jit(solution)/shard_map/pallas_call | solution.py:681
  9.0 0.0 collective-permute-done.cross.cross_rows
  9.0 0.0 collective-permute-done.1.near.near_rows
  9.1 0.2 shard_map.107
  9.2 0.7 %collective-permute-start.2 = (f32[160,128]{1,0:T(8,128)S(1)}, f32[160,128]{1,0:T(8,128)S(1)}, u32[]{:S(2)}, u32[]{:S(2)}) collective-permute-start(f32[160,128]{1,0:T(8,128)S(1)} %get-tuple-element.27), channel_id=1, source_target_pairs={{1,2},{2,1},{5,6},{6,5},{9,10},{10,9},{13,14},{14,13},{17,18},{18,... | collective-permute-start | bytes 245768 | tf_op jit(solution)/shard_map/ppermute | solution.py:706
  9.9 4.5 %collective-permute-start.3 = (f32[160,128]{1,0:T(8,128)S(1)}, f32[160,128]{1,0:T(8,128)S(1)}, u32[]{:S(2)}, u32[]{:S(2)}) collective-permute-start(f32[160,128]{1,0:T(8,128)S(1)} %get-tuple-element.28), channel_id=1, source_target_pairs={{0,1},{2,3},{1,0},{3,2},{4,5},{6,7},{5,4},{7,6},{8,9},{10,11},{9,8... | collective-permute-start | bytes 245768 | tf_op jit(solution)/shard_map/ppermute | solution.py:707
  14.4 0.0 copy-done.3
  14.4 2.1 %shard_map.106 = (f32[3,2,2,128,128]{4,3,2,1,0:T(8,128)S(1)}, f32[256,128]{1,0:T(8,128)S(1)}, f32[8,160,128]{2,1,0:T(8,128)S(1)}) custom-call(f32[3,2,128,256]{3,2,1,0:T(8,128)S(1)} %copy-done.1, f32[2,128,256]{2,1,0:T(8,128)S(1)} %copy-done.2, f32[4,2,128,256]{3,2,1,0:T(8,128)S(1)} %copy-done, f32[16,8,256]{2,1,0:T(8,128)S(1)} %collective-permute-done.cross.cross_rows, ...), custom_call_target="tpu_custom_call" | custom-call | flops 6553600 | bytes 3145728 | tf_op jit(solution)/shard_map/pallas_call | solution.py:710
  16.4 0.0 collective-permute-done.2.cross
  16.4 0.8 %collective-permute-done.3.near = f32[160,128]{1,0:T(8,128)S(1)} collective-permute-done((f32[160,128]{1,0:T(8,128)S(1)}, f32[160,128]{1,0:T(8,128)S(1)}, u32[]{:S(2)}, u32[]{:S(2)}) %collective-permute-start.3) | collective-permute-done | bytes 81952 | tf_op jit(solution)/shard_map/ppermute | solution.py:707
  17.2 0.8 %shard_map.108 = (f32[3,128,128]{2,1,0:T(8,128)S(1)}, f32[160,128]{1,0:T(8,128)S(1)}) custom-call(f32[8,160,128]{2,1,0:T(8,128)S(1)} %get-tuple-element.24.base, f32[160,128]{1,0:T(8,128)S(1)} %collective-permute-done.2.cross, f32[160,128]{1,0:T(8,128)S(1)} %collective-permute-done.3.near, f32[4,160,128]{2,1,0:T(8,128)S(1)} %get-tuple-element.29.src), custom_call_target="tpu_custom_call" | custom-call | flops 1638400 | bytes 524288 | tf_op jit(solution)/shard_map/pallas_call | solution.py:730
  18.0 0.2 shard_map.110.merged
  18.2 0.9 %shard_map.111 = f32[256,128]{1,0:T(8,128)} custom-call(f32[2,8,128]{2,1,0:T(8,128)S(1)} %shard_map.110.merged, f32[256,128]{1,0:T(8,128)S(1)} %get-tuple-element.32.slots_in, bf16[256,32]{1,0:T(8,128)(2,1)S(1)} %get-tuple-element.33.place), custom_call_target="tpu_custom_call" | custom-call | flops 655360 | bytes 131072 | tf_op jit(solution)/shard_map/pallas_call | solution.py:749
  19.1 4.5 %all-to-all-start = ((f32[16,16,128]{2,1,0:T(8,128)}), f32[16,16,128]{2,1,0:T(8,128)S(1)}, u32[]{:S(2)}, u32[]{:S(2)}) async-start(f32[16,16,128]{2,1,0:T(8,128)} %bitcast.4), calls=%async_computation | async-start | bytes 262144 | tf_op jit(solution)/shard_map/all_to_all | solution.py:763
  23.7 1.2 %shard_map.109 = f32[3,2,128,256]{3,2,1,0:T(8,128)} custom-call(f32[3,2,2,128,128]{4,3,2,1,0:T(8,128)S(1)} %get-tuple-element.23.last, f32[3,128,128]{2,1,0:T(8,128)S(1)} %get-tuple-element.30.edge_last), custom_call_target="tpu_custom_call" | custom-call | flops 655360 | bytes 1572864 | tf_op jit(solution)/shard_map/pallas_call | solution.py:752
  24.9 6.2 %all-to-all-done = f32[16,16,128]{2,1,0:T(8,128)S(1)} async-done(((f32[16,16,128]{2,1,0:T(8,128)}), f32[16,16,128]{2,1,0:T(8,128)S(1)}, u32[]{:S(2)}, u32[]{:S(2)}) %all-to-all-start) | async-done | bytes 131104 | tf_op jit(solution)/shard_map/all_to_all | solution.py:763
  31.0 0.7 %copy.12 = f32[1,16,16,128]{3,2,1,0:T(8,128)} copy(f32[1,16,16,128]{3,2,1,0:T(8,128)S(1)} %bitcast.10) | data formatting | bytes 262144
Async XLA Ops:
  0.6 6.4 %copy-start = (f32[4,2,128,256]{3,2,1,0:T(8,128)S(1)}, f32[4,2,128,256]{3,2,1,0:T(8,128)}, u32[]{:S(2)}) copy-start(f32[4,2,128,256]{3,2,1,0:T(8,128)} %fwd.3) | copy-start | bytes 3145732
  0.6 6.3 %copy-start.2 = (f32[2,128,256]{2,1,0:T(8,128)S(1)}, f32[2,128,256]{2,1,0:T(8,128)}, u32[]{:S(2)}) copy-start(f32[2,128,256]{2,1,0:T(8,128)} %eps.3) | copy-start | bytes 786436
  0.7 6.3 %copy-start.1 = (f32[3,2,128,256]{3,2,1,0:T(8,128)S(1)}, f32[3,2,128,256]{3,2,1,0:T(8,128)}, u32[]{:S(2)}) copy-start(f32[3,2,128,256]{3,2,1,0:T(8,128)} %fields.3) | copy-start | bytes 2359300
  0.7 6.3 %copy-start.8 = (s32[1,1,128,1]{2,3,1,0:T(1,128)S(1)}, s32[1,1,128,1]{2,3,1,0:T(1,128)}, u32[]{:S(2)}) copy-start(s32[1,1,128,1]{2,3,1,0:T(1,128)} %param.16) | copy-start | bytes 1540
  0.7 6.3 %copy-start.7 = (s32[1,1,128]{2,1,0:T(1,128)S(1)}, s32[1,1,128]{2,1,0:T(1,128)}, u32[]{:S(2)}) copy-start(s32[1,1,128]{2,1,0:T(1,128)} %param.15) | copy-start | bytes 1540
  0.7 6.3 %copy-start.4 = (f32[4,64]{1,0:T(4,128)S(1)}, f32[4,64]{1,0:T(4,128)}, u32[]{:S(2)}) copy-start(f32[4,64]{1,0:T(4,128)} %refs_5_.1) | copy-start | bytes 3076
  0.7 6.3 %copy-start.6 = (s32[64]{0:T(128)S(1)}, s32[64]{0:T(128)}, u32[]{:S(2)}) copy-start(s32[64]{0:T(128)} %param.13) | copy-start | bytes 772
  0.7 6.3 %copy-start.5 = (s32[64]{0:T(128)S(1)}, s32[64]{0:T(128)}, u32[]{:S(2)}) copy-start(s32[64]{0:T(128)} %param.12) | copy-start | bytes 772
  1.9 12.4 %copy-start.3 = (bf16[2,128,128]{2,1,0:T(8,128)(2,1)S(1)}, bf16[2,128,128]{2,1,0:T(8,128)(2,1)}, u32[]{:S(2)}) copy-start(bf16[2,128,128]{2,1,0:T(8,128)(2,1)} %constant.2.clone.mats) | copy-start | bytes 196612
  1.9 7.1 %collective-permute-start = (f32[16,8,256]{2,1,0:T(8,128)S(1)}, f32[16,8,256]{2,1,0:T(8,128)S(1)}, u32[]{:S(2)}, u32[]{:S(2)}) collective-permute-start(f32[16,8,256]{2,1,0:T(8,128)S(1)} %get-tuple-element.18), channel_id=1, source_target_pairs={{4,8},{8,4},{5,9},{9,5},{6,10},{10,6},{7,11},{11,7},{20,24},{24,20... | collective-permute-start | bytes 393224 | tf_op jit(solution)/shard_map/ppermute | solution.py:676
  2.6 6.4 %collective-permute-start.1 = (f32[16,8,256]{2,1,0:T(8,128)S(1)}, f32[16,8,256]{2,1,0:T(8,128)S(1)}, u32[]{:S(2)}, u32[]{:S(2)}) collective-permute-start(f32[16,8,256]{2,1,0:T(8,128)S(1)} %get-tuple-element.19), channel_id=1, source_target_pairs={{0,4},{8,12},{4,0},{12,8},{1,5},{9,13},{5,1},{13,9},{2,6},{10,14},... | collective-permute-start | bytes 393224 | tf_op jit(solution)/shard_map/ppermute | solution.py:677
  9.2 7.2 %collective-permute-start.2 = (f32[160,128]{1,0:T(8,128)S(1)}, f32[160,128]{1,0:T(8,128)S(1)}, u32[]{:S(2)}, u32[]{:S(2)}) collective-permute-start(f32[160,128]{1,0:T(8,128)S(1)} %get-tuple-element.27), channel_id=1, source_target_pairs={{1,2},{2,1},{5,6},{6,5},{9,10},{10,9},{13,14},{14,13},{17,18},{18,... | collective-permute-start | bytes 245768 | tf_op jit(solution)/shard_map/ppermute | solution.py:706
  9.9 7.3 %collective-permute-start.3 = (f32[160,128]{1,0:T(8,128)S(1)}, f32[160,128]{1,0:T(8,128)S(1)}, u32[]{:S(2)}, u32[]{:S(2)}) collective-permute-start(f32[160,128]{1,0:T(8,128)S(1)} %get-tuple-element.28), channel_id=1, source_target_pairs={{0,1},{2,3},{1,0},{3,2},{4,5},{6,7},{5,4},{7,6},{8,9},{10,11},{9,8... | collective-permute-start | bytes 245768 | tf_op jit(solution)/shard_map/ppermute | solution.py:707
  19.1 11.9 %all-to-all-start = ((f32[16,16,128]{2,1,0:T(8,128)}), f32[16,16,128]{2,1,0:T(8,128)S(1)}, u32[]{:S(2)}, u32[]{:S(2)}) async-start(f32[16,16,128]{2,1,0:T(8,128)} %bitcast.4), calls=%async_computation | async-start | bytes 262144 | tf_op jit(solution)/shard_map/all_to_all | solution.py:763

commit v11 on v10

--- a/solution.py
+++ b/solution.py
@@ -357,9 +357,11 @@
         below, right = shifts.below(up, up_next), shifts.next_col(here)
         hx, hy = load_hx(t), load_hy(t)
         for key in keys:
-            store(0, key, t, e[(STEPS,) + key + tile_at(t)])
-            store(1, key, t, hx[key] + COURANT * (right[key] - here[key]))
-            store(2, key, t, hy[key] - COURANT * (below[key] - here[key]))
+            store(
+                key, t, e[(STEPS,) + key + tile_at(t)],
+                hx[key] + COURANT * (right[key] - here[key]),
+                hy[key] - COURANT * (below[key] - here[key]),
+            )
         here, up = after, up_next
 
 
@@ -417,8 +419,9 @@
         for key in keys:
             g[key + tile_at(t)] = values[key]
 
-    def store(kind, key, t, value):
-        last[(kind,) + key + (pl.ds(t * SUB - PAD, SUB), slice(None))] = value
+    def store(key, t, *values):
+        for kind, value in enumerate(values):
+            last[(kind,) + key + (pl.ds(t * SUB - PAD, SUB), slice(None))] = value
 
     last_fields(
         range(PAD // SUB, n_tiles - PAD // SUB), keys, shifts, e,
@@ -490,7 +493,7 @@
 
 
 def edge_kernel(
-    base, cross, near, src, out, g_out, e, first, curl, eps_c, d, g, result
+    last, slots_in, base, cross, near, src, place, fields, slots, e, first, curl, eps_c, d, g, merged
 ):
     ext_rows = base.shape[1]
     rows = ext_rows - 2 * PAD
@@ -543,17 +546,33 @@
         value = gradient([()], t, e, lambda step, key, t: d[step, pl.ds(t * SUB, SUB), :])[()]
         g[pl.ds(t * SUB, SUB), :] = jnp.where(inside, value, 0.0)
 
-    def store(kind, key, t, value):
-        result[kind, pl.ds(t * SUB - PAD, SUB), :] = value
-
+    n_lanes = fields.shape[3] // LANES
+
+    def store(key, t, *edges):
+        at = pl.ds(t * SUB - PAD, SUB)
+        result = {}
+        for kind, edge in enumerate(edges):
+            for layer in range(2):
+                for k in range(n_lanes):
+                    value = last[kind, layer, k, at, :]
+                    if k == 0:
+                        value = jnp.where(lane < KEEP, turn(edge, -HALF * layer - OUT, 1), value)
+                    if k == n_lanes - 1:
+                        value = jnp.where(
+                            lane >= LANES - KEEP, turn(edge, -HALF * layer - SIDE - OUT, 1), value
+                        )
+                    result[kind, layer, k] = value
+        for (kind, layer, k), value in result.items():
+            fields[kind, layer, at, lane_tile(k)] = value
+
+    edge_filter(g, merged)
+    edge_slots(merged, slots_in, place, slots)
     last_fields(
         range(PAD // SUB, n_tiles - PAD // SUB), [()], shifts, e, load_hx, load_hy, store
     )
-    g_out[...] = g[...]
-    out[...] = result[...]
-
-
-def edge_filter_kernel(g, merged):
+
+
+def edge_filter(g, merged):
     lane = lanes()
     span, reach = TS // PIX, RADIUS - 1
     pixel = {}
@@ -585,7 +604,7 @@
         merged[n] = jnp.where(window, jnp.where(even, a, b), jnp.where(even, c, d))
 
 
-def edge_slots_kernel(merged, slots_in, place, slots):
+def edge_slots(merged, slots_in, place, slots):
     lane = lanes()
     span = TS // PIX
     row, pixel = lane // span % span, lane % span
@@ -599,27 +618,15 @@
     slots[...] = slots_in[...] + dot(place[...], jnp.concatenate(parts, axis=0))
 
 
-def merge_kernel(last, edge_last, out_fields, merged, sem):
-    rows, cols = merged.shape[2], merged.shape[3]
-    n_lanes = cols // LANES
-    lane = lanes()
-    for t in range(rows // SUB):
-        at = pl.ds(t * SUB, SUB)
-        for kind in range(3):
-            edge = edge_last[kind, at, :]
-            for layer in range(2):
-                for k in range(n_lanes):
-                    value = last[kind, layer, k, at, :]
-                    if k == 0:
-                        value = jnp.where(lane < KEEP, turn(edge, -HALF * layer - OUT, 1), value)
-                    if k == n_lanes - 1:
-                        value = jnp.where(
-                            lane >= LANES - KEEP, turn(edge, -HALF * layer - SIDE - OUT, 1), value
-                        )
-                    merged[kind, layer, at, lane_tile(k)] = value
-    copy = pltpu.make_async_copy(merged, out_fields, sem)
-    copy.start()
-    copy.wait()
+def deliver_kernel(fields, slots, out_fields, out_slots, sems):
+    copies = [
+        pltpu.make_async_copy(fields.at[kind], out_fields.at[kind], sems.at[kind]) for kind in range(3)
+    ]
+    copies.append(pltpu.make_async_copy(slots, out_slots.at[0], sems.at[3]))
+    for copy in copies:
+        copy.start()
+    for copy in copies:
+        copy.wait()
 
 
 def vmem():
@@ -727,10 +734,10 @@
     )(*blocks, cross, near, src, pool_matrices(), base, place)
 
     plane = (ext_rows, LANES)
-    edge_last, edge_g = call(
+    fields, outgoing = call(
         edge_kernel,
-        (shape(3, rows, LANES), shape(*plane)),
-        4,
+        (pltpu.VMEM((3, 2, rows, cols), F32), pltpu.VMEM((owners * capacity, width), F32)),
+        7,
         scratch=(
             pltpu.VMEM((1 + STEPS,) + plane, F32),
             pltpu.VMEM((2,) + plane, F32),
@@ -738,30 +745,23 @@
             pltpu.VMEM(plane, F32),
             pltpu.VMEM((STEPS,) + plane, F32),
             pltpu.VMEM(plane, F32),
-            pltpu.VMEM((3, rows, LANES), F32),
+            pltpu.VMEM((2, SUB, LANES), F32),
         ),
         flops=50 * cells,
         size=16 * cells,
-    )(base, cross_cols, near_cols, src_edge)
-    (merged,) = call(
-        edge_filter_kernel, (shape(2, SUB, LANES),), 1, flops=20 * cells, size=4 * cells
-    )(edge_g)
-    (outgoing,) = call(
-        edge_slots_kernel, (pltpu.VMEM((owners * capacity, width), F32),), 3, flops=20 * cells, size=4 * cells
-    )(merged, slots, place_edge)
-    (fields,) = call(
-        merge_kernel,
-        (shape(3, 2, rows, cols),),
-        2,
-        out_specs=(pl.BlockSpec(memory_space=pl.ANY),),
-        scratch=(pltpu.VMEM((3, 2, rows, cols), F32), pltpu.SemaphoreType.DMA),
-        flops=20 * cells,
-        size=48 * cells,
-    )(last, edge_last)
+    )(last, slots, base, cross_cols, near_cols, src_edge, place_edge)
 
     outgoing = outgoing.reshape(owners, capacity, width)
     incoming = lax.all_to_all(outgoing, ("gx", "gy"), split_axis=0, concat_axis=0, tiled=True)
-    return fields, incoming[None]
+    anywhere = pl.BlockSpec(memory_space=pl.ANY)
+    return call(
+        deliver_kernel,
+        (shape(*fields.shape), shape(1, *incoming.shape)),
+        2,
+        out_specs=(anywhere, anywhere),
+        scratch=(pltpu.SemaphoreType.DMA((4,)),),
+        size=16 * cells,
+    )(fields, pltpu.with_memory_space_constraint(incoming, pltpu.VMEM))
 
 
 def solution(mesh):

time: 32 us -> 32.1 us (level)
  blocking collectives: 0 us -> 11.7 us
  waiting for transfers between devices: 6.95 us -> 0.78 us
  starting transfers between devices: 14.7 us -> 10.2 us
  local copies, waits for them, and re-layouts: 0.7 us -> 0.04 us
    all_to_all x0 -> x1, blocking collectives: none -> 11.7 us  [on_device(): lax.all_to_all(outgoing, ('gx', 'gy'), split_axis=0, concat_axis=0, tiled...]
    all_to_all x1 -> x0, waiting for transfers between devices: 6.19 us -> none  [on_device(): lax.all_to_all(outgoing, ('gx', 'gy'), split_axis=0, concat_axis=0, tiled...]
    all_to_all x1 -> x0, starting transfers between devices: 4.55 us -> none  [on_device(): lax.all_to_all(outgoing, ('gx', 'gy'), split_axis=0, concat_axis=0, tiled...]
    unnamed x19 -> x18, local copies, waits for them, and re-layouts: 0.7 us -> 0.04 us
    pallas_call x4 -> x2, Pallas kernels: 3.08 us -> 3.02 us  [the longest x1 2.07 us: on_device(): call(edge_kernel, (pltpu.VMEM((3, 2, rows, cols), F32), pltpu.VMEM((owner...]
  transfers between devices with their start and end apart: 5 -> 4, of which waited for: 2 -> 1; matrix products, arithmetic and copies ran while one was open for 0% -> 0% of each run, Pallas kernels for 16% -> 13%
where the time goes in v11:
time: 32.1 us; the launch traced here: 31.9 us
  blocking collectives  11.7 us (36%)
  starting transfers between devices  10.2 us (32%)
  Pallas kernels  8.43 us (26%)
  between operations  0.82 us (3%)
  waiting for transfers between devices  0.78 us (2%)
    all_to_all x1, blocking collectives, on_device(): lax.all_to_all(outgoing, ('gx', 'gy'), split_axis=0, concat_axis=0, tiled...  11.7 us
    ppermute x1, starting transfers between devices, on_device(): near_cols = lax.ppermute(near_cols, 'gy', pairs(gy_count, 0))  4.46 us
    ppermute x1, starting transfers between devices, on_device(): near = lax.ppermute(near, 'gx', pairs(gx_count, 0))  4.36 us
    pallas_call x1, Pallas kernels, on_device(): call(edge_kernel, (pltpu.VMEM((3, 2, rows, cols), F32), pltpu.VMEM((owner...  2.07 us
    pallas_call x1, Pallas kernels, on_device(): call(inner_kernel, (shape(3, 2, n_lanes, rows, LANES), shape(owners * cap...  2.04 us
    pallas_call x1, Pallas kernels, on_device(): call(lambda *refs: prep_kernel(capacity, *refs), (packed, packed, shape(4...  1.99 us
    pallas_call x1, Pallas kernels, on_device(): call(rows_kernel, (strip, strip), 3, in_space=pltpu.HBM, scratch=(pltpu.V...  1.21 us
    pallas_call x1, Pallas kernels, on_device(): call(deliver_kernel, (shape(*fields.shape), shape(1, *incoming.shape)), 2...  0.95 us
  transfers between devices with their start and end apart: 4, of which 1 were waited for; matrix products, arithmetic and copies ran while one was open for 0% of the time, Pallas kernels for 13%

profile of v11, /device:TPU:0, one launch (start us, length us, event | category | flops | bytes accessed | tf_op | source)
XLA Modules:
  0.0 31.9 jit_solution(1762610605558983952)
XLA Ops:
  0.6 0.0 copy-start
  0.6 0.0 copy-start.2
  0.7 0.0 copy-start.1
  0.7 0.0 copy-start.8
  0.7 0.0 copy-start.7
  0.7 0.0 copy-start.4
  0.7 0.0 copy-start.6
  0.7 0.0 copy-start.5
  0.7 1.2 %shard_map.104 = (f32[16,8,256]{2,1,0:T(8,128)S(1)}, f32[16,8,256]{2,1,0:T(8,128)S(1)}) custom-call(f32[3,2,128,256]{3,2,1,0:T(8,128)} %fields.3, f32[2,128,256]{2,1,0:T(8,128)} %eps.3, f32[4,2,128,256]{3,2,1,0:T(8,128)} %fwd.3), custom_call_target="tpu_custom_call" | custom-call | bytes 1048576 | tf_op jit(solution)/shard_map/pallas_call | solution.py:669
  1.9 0.0 copy-start.3
  1.9 0.7 %collective-permute-start = (f32[16,8,256]{2,1,0:T(8,128)S(1)}, f32[16,8,256]{2,1,0:T(8,128)S(1)}, u32[]{:S(2)}, u32[]{:S(2)}) collective-permute-start(f32[16,8,256]{2,1,0:T(8,128)S(1)} %get-tuple-element.18), channel_id=1, source_target_pairs={{4,8},{8,4},{5,9},{9,5},{6,10},{10,6},{7,11},{11,7},{20,24},{24,20... | collective-permute-start | bytes 393224 | tf_op jit(solution)/shard_map/ppermute | solution.py:683
  2.6 4.4 %collective-permute-start.1 = (f32[16,8,256]{2,1,0:T(8,128)S(1)}, f32[16,8,256]{2,1,0:T(8,128)S(1)}, u32[]{:S(2)}, u32[]{:S(2)}) collective-permute-start(f32[16,8,256]{2,1,0:T(8,128)S(1)} %get-tuple-element.19), channel_id=1, source_target_pairs={{0,4},{8,12},{4,0},{12,8},{1,5},{9,13},{5,1},{13,9},{2,6},{10,14},... | collective-permute-start | bytes 393224 | tf_op jit(solution)/shard_map/ppermute | solution.py:684
  7.0 0.0 copy-done
  7.0 0.0 copy-done.2
  7.0 0.0 copy-done.1
  7.0 0.0 copy-done.8
  7.0 0.0 copy-done.7
  7.0 0.0 copy-done.4
  7.0 0.0 copy-done.6
  7.0 0.0 copy-done.5
  7.0 2.0 %shard_map.105 = (f32[160,128]{1,0:T(8,128)S(1)}, f32[160,128]{1,0:T(8,128)S(1)}, f32[8,160,128]{2,1,0:T(8,128)S(1)}, f32[4,2,160,256]{3,2,1,0:T(8,128)S(1)}, f3...) custom-call(f32[3,2,128,256]{3,2,1,0:T(8,128)S(1)} %copy-done.1, ...), custom_call_target="tpu_custom_call" | custom-call | flops 188743680 | bytes 2097152 | tf_op jit(solution)/shard_map/pallas_call | solution.py:688
  9.0 0.0 collective-permute-done.cross.cross_rows
  9.0 0.0 collective-permute-done.1.near.near_rows
  9.1 0.2 shard_map.107
  9.2 0.7 %collective-permute-start.2 = (f32[160,128]{1,0:T(8,128)S(1)}, f32[160,128]{1,0:T(8,128)S(1)}, u32[]{:S(2)}, u32[]{:S(2)}) collective-permute-start(f32[160,128]{1,0:T(8,128)S(1)} %get-tuple-element.28), channel_id=1, source_target_pairs={{1,2},{2,1},{5,6},{6,5},{9,10},{10,9},{13,14},{14,13},{17,18},{18,... | collective-permute-start | bytes 245768 | tf_op jit(solution)/shard_map/ppermute | solution.py:713
  9.9 4.5 %collective-permute-start.3 = (f32[160,128]{1,0:T(8,128)S(1)}, f32[160,128]{1,0:T(8,128)S(1)}, u32[]{:S(2)}, u32[]{:S(2)}) collective-permute-start(f32[160,128]{1,0:T(8,128)S(1)} %get-tuple-element.29), channel_id=1, source_target_pairs={{0,1},{2,3},{1,0},{3,2},{4,5},{6,7},{5,4},{7,6},{8,9},{10,11},{9,8... | collective-permute-start | bytes 245768 | tf_op jit(solution)/shard_map/ppermute | solution.py:714
  14.4 0.0 copy-done.3
  14.4 2.0 %shard_map.106 = (f32[3,2,2,128,128]{4,3,2,1,0:T(8,128)S(1)}, f32[256,128]{1,0:T(8,128)S(1)}, f32[8,160,128]{2,1,0:T(8,128)S(1)}) custom-call(f32[3,2,128,256]{3,2,1,0:T(8,128)S(1)} %copy-done.1, f32[2,128,256]{2,1,0:T(8,128)S(1)} %copy-done.2, f32[4,2,128,256]{3,2,1,0:T(8,128)S(1)} %copy-done, f32[16,8,256]{2,1,0:T(8,128)S(1)} %collective-permute-done.cross.cross_rows, ...), custom_call_target="tpu_custom_call" | custom-call | flops 6553600 | bytes 3145728 | tf_op jit(solution)/shard_map/pallas_call | solution.py:717
  16.4 0.0 collective-permute-done.2.cross
  16.4 0.8 %collective-permute-done.3.near = f32[160,128]{1,0:T(8,128)S(1)} collective-permute-done((f32[160,128]{1,0:T(8,128)S(1)}, f32[160,128]{1,0:T(8,128)S(1)}, u32[]{:S(2)}, u32[]{:S(2)}) %collective-permute-start.3) | collective-permute-done | bytes 81952 | tf_op jit(solution)/shard_map/ppermute | solution.py:714
  17.2 2.1 %shard_map.108 = (f32[3,2,128,256]{3,2,1,0:T(8,128)S(1)}, f32[256,128]{1,0:T(8,128)S(1)}) custom-call(f32[3,2,2,128,128]{4,3,2,1,0:T(8,128)S(1)} %get-tuple-element.23.last, f32[256,128]{1,0:T(8,128)S(1)} %get-tuple-element.24.slots_in, f32[8,160,128]{2,1,0:T(8,128)S(1)} %get-tuple-element.25.base, f32[160,128]{1,0:T(8,128)S(1)} %collective-permute-done.2.cross, ...), custom_call_target="tpu_custom_call" | custom-call | flops 1638400 | bytes 524288 | tf_op jit(solution)/shard_map/pallas_call | solution.py:737
  19.3 11.7 %all_to_all.5.slots = f32[16,16,128]{2,1,0:T(8,128)S(1)} all-to-all(f32[16,16,128]{2,1,0:T(8,128)S(1)} %bitcast.5), channel_id=1, replica_groups=mesh['parts'=2,'gx'=4,'gy'=4] {'gx','gy'}, dimensions={0} | all-to-all | bytes 262144 | tf_op jit(solution)/shard_map/all_to_all | solution.py:755
  31.0 0.9 %shard_map.109 = (f32[3,2,128,256]{3,2,1,0:T(8,128)}, f32[1,16,16,128]{3,2,1,0:T(8,128)}) custom-call(f32[3,2,128,256]{3,2,1,0:T(8,128)S(1)} %get-tuple-element.32.fields, f32[16,16,128]{2,1,0:T(8,128)S(1)} %all_to_all.5.slots), custom_call_target="tpu_custom_call" | custom-call | bytes 524288 | tf_op jit(solution)/shard_map/pallas_call | solution.py:757
Async XLA Ops:
  0.6 6.4 %copy-start = (f32[4,2,128,256]{3,2,1,0:T(8,128)S(1)}, f32[4,2,128,256]{3,2,1,0:T(8,128)}, u32[]{:S(2)}) copy-start(f32[4,2,128,256]{3,2,1,0:T(8,128)} %fwd.3) | copy-start | bytes 3145732
  0.6 6.3 %copy-start.2 = (f32[2,128,256]{2,1,0:T(8,128)S(1)}, f32[2,128,256]{2,1,0:T(8,128)}, u32[]{:S(2)}) copy-start(f32[2,128,256]{2,1,0:T(8,128)} %eps.3) | copy-start | bytes 786436
  0.7 6.3 %copy-start.1 = (f32[3,2,128,256]{3,2,1,0:T(8,128)S(1)}, f32[3,2,128,256]{3,2,1,0:T(8,128)}, u32[]{:S(2)}) copy-start(f32[3,2,128,256]{3,2,1,0:T(8,128)} %fields.3) | copy-start | bytes 2359300
  0.7 6.3 %copy-start.8 = (s32[1,1,128,1]{2,3,1,0:T(1,128)S(1)}, s32[1,1,128,1]{2,3,1,0:T(1,128)}, u32[]{:S(2)}) copy-start(s32[1,1,128,1]{2,3,1,0:T(1,128)} %param.16) | copy-start | bytes 1540
  0.7 6.3 %copy-start.7 = (s32[1,1,128]{2,1,0:T(1,128)S(1)}, s32[1,1,128]{2,1,0:T(1,128)}, u32[]{:S(2)}) copy-start(s32[1,1,128]{2,1,0:T(1,128)} %param.15) | copy-start | bytes 1540
  0.7 6.3 %copy-start.4 = (f32[4,64]{1,0:T(4,128)S(1)}, f32[4,64]{1,0:T(4,128)}, u32[]{:S(2)}) copy-start(f32[4,64]{1,0:T(4,128)} %refs_5_.1) | copy-start | bytes 3076
  0.7 6.3 %copy-start.6 = (s32[64]{0:T(128)S(1)}, s32[64]{0:T(128)}, u32[]{:S(2)}) copy-start(s32[64]{0:T(128)} %param.13) | copy-start | bytes 772
  0.7 6.3 %copy-start.5 = (s32[64]{0:T(128)S(1)}, s32[64]{0:T(128)}, u32[]{:S(2)}) copy-start(s32[64]{0:T(128)} %param.12) | copy-start | bytes 772
  1.9 12.4 %copy-start.3 = (bf16[2,128,128]{2,1,0:T(8,128)(2,1)S(1)}, bf16[2,128,128]{2,1,0:T(8,128)(2,1)}, u32[]{:S(2)}) copy-start(bf16[2,128,128]{2,1,0:T(8,128)(2,1)} %constant.2.clone.mats) | copy-start | bytes 196612
  1.9 7.1 %collective-permute-start = (f32[16,8,256]{2,1,0:T(8,128)S(1)}, f32[16,8,256]{2,1,0:T(8,128)S(1)}, u32[]{:S(2)}, u32[]{:S(2)}) collective-permute-start(f32[16,8,256]{2,1,0:T(8,128)S(1)} %get-tuple-element.18), channel_id=1, source_target_pairs={{4,8},{8,4},{5,9},{9,5},{6,10},{10,6},{7,11},{11,7},{20,24},{24,20... | collective-permute-start | bytes 393224 | tf_op jit(solution)/shard_map/ppermute | solution.py:683
  2.6 6.4 %collective-permute-start.1 = (f32[16,8,256]{2,1,0:T(8,128)S(1)}, f32[16,8,256]{2,1,0:T(8,128)S(1)}, u32[]{:S(2)}, u32[]{:S(2)}) collective-permute-start(f32[16,8,256]{2,1,0:T(8,128)S(1)} %get-tuple-element.19), channel_id=1, source_target_pairs={{0,4},{8,12},{4,0},{12,8},{1,5},{9,13},{5,1},{13,9},{2,6},{10,14},... | collective-permute-start | bytes 393224 | tf_op jit(solution)/shard_map/ppermute | solution.py:684
  9.2 7.2 %collective-permute-start.2 = (f32[160,128]{1,0:T(8,128)S(1)}, f32[160,128]{1,0:T(8,128)S(1)}, u32[]{:S(2)}, u32[]{:S(2)}) collective-permute-start(f32[160,128]{1,0:T(8,128)S(1)} %get-tuple-element.28), channel_id=1, source_target_pairs={{1,2},{2,1},{5,6},{6,5},{9,10},{10,9},{13,14},{14,13},{17,18},{18,... | collective-permute-start | bytes 245768 | tf_op jit(solution)/shard_map/ppermute | solution.py:713
  9.9 7.3 %collective-permute-start.3 = (f32[160,128]{1,0:T(8,128)S(1)}, f32[160,128]{1,0:T(8,128)S(1)}, u32[]{:S(2)}, u32[]{:S(2)}) collective-permute-start(f32[160,128]{1,0:T(8,128)S(1)} %get-tuple-element.29), channel_id=1, source_target_pairs={{0,1},{2,3},{1,0},{3,2},{4,5},{6,7},{5,4},{7,6},{8,9},{10,11},{9,8... | collective-permute-start | bytes 245768 | tf_op jit(solution)/shard_map/ppermute | solution.py:714

commit v12 on v11

--- a/solution.py
+++ b/solution.py
@@ -492,25 +492,46 @@
     return jnp.stack([new_even, new_odd], axis=1).reshape(tile_rows * 2 * span, LANES)
 
 
+def from_partner(is_cross, lane):
+    next_one = (lax.axis_index("gy") + (0 if is_cross else 1)) & 1
+    spot = lane & (HALF - 1)
+    start = next_one * (HALF - OUT)
+    mine = (spot >= start) & (spot < start + OUT)
+    shifts = []
+    for kind, width in enumerate(WIDTHS):
+        left, right = (OUT - width - FIRST[kind]) % LANES, (HALF - OUT - FIRST[kind]) % LANES
+        shifts.append(left + next_one * (right - left))
+    return mine, shifts
+
+
+def edge_cross_kernel(base, cross, result):
+    n_tiles = base.shape[1] // SUB
+    mine, shifts = from_partner(True, lanes())
+    for t in range(n_tiles):
+        at = pl.ds(t * SUB, SUB)
+        kinds = range(4 if t in (0, n_tiles - 1) else 4 + STEPS)
+        values = [
+            jnp.where(mine, pltpu.roll(cross[at, :], shifts[kind], 1), base[kind, at, :])
+            for kind in kinds
+        ]
+        for kind in kinds:
+            result[kind, at, :] = values[kind]
+
+
 def edge_kernel(
-    last, slots_in, base, cross, near, src, place, fields, slots, e, first, curl, eps_c, d, g, merged
+    slots_in, base, near, src, place, edge_last, slots, e, first, curl, eps_c, d, g, merged
 ):
     ext_rows = base.shape[1]
     rows = ext_rows - 2 * PAD
     n_tiles = ext_rows // SUB
-    lane, odd = lanes(), is_odd("gy")
+    lane = lanes()
     spot = lane & (HALF - 1)
-    is_left, is_right = spot < OUT, spot >= HALF - OUT
+    mine, moves = from_partner(False, lane)
 
     for t in range(n_tiles):
         at = pl.ds(t * SUB, SUB)
-        far, close = cross[at, :], near[at, :]
-        high, low = jnp.where(odd, close, far), jnp.where(odd, far, close)
-        for kind, width in enumerate(WIDTHS):
-            if kind >= 4 and t in (0, n_tiles - 1):
-                continue
-            value = jnp.where(is_left, turn(high, OUT - width - FIRST[kind], 1), base[kind, at, :])
-            value = jnp.where(is_right, turn(low, HALF - OUT - FIRST[kind], 1), value)
+        for kind in range(4 if t in (0, n_tiles - 1) else 4 + STEPS):
+            value = jnp.where(mine, pltpu.roll(near[at, :], moves[kind], 1), base[kind, at, :])
             if kind == 0:
                 e[0, at, :] = value
             elif kind < 3:
@@ -546,24 +567,9 @@
         value = gradient([()], t, e, lambda step, key, t: d[step, pl.ds(t * SUB, SUB), :])[()]
         g[pl.ds(t * SUB, SUB), :] = jnp.where(inside, value, 0.0)
 
-    n_lanes = fields.shape[3] // LANES
-
-    def store(key, t, *edges):
-        at = pl.ds(t * SUB - PAD, SUB)
-        result = {}
-        for kind, edge in enumerate(edges):
-            for layer in range(2):
-                for k in range(n_lanes):
-                    value = last[kind, layer, k, at, :]
-                    if k == 0:
-                        value = jnp.where(lane < KEEP, turn(edge, -HALF * layer - OUT, 1), value)
-                    if k == n_lanes - 1:
-                        value = jnp.where(
-                            lane >= LANES - KEEP, turn(edge, -HALF * layer - SIDE - OUT, 1), value
-                        )
-                    result[kind, layer, k] = value
-        for (kind, layer, k), value in result.items():
-            fields[kind, layer, at, lane_tile(k)] = value
+    def store(key, t, *values):
+        for kind, value in enumerate(values):
+            edge_last[kind, pl.ds(t * SUB - PAD, SUB), :] = value
 
     edge_filter(g, merged)
     edge_slots(merged, slots_in, place, slots)
@@ -618,13 +624,28 @@
     slots[...] = slots_in[...] + dot(place[...], jnp.concatenate(parts, axis=0))
 
 
-def deliver_kernel(fields, slots, out_fields, out_slots, sems):
-    copies = [
-        pltpu.make_async_copy(fields.at[kind], out_fields.at[kind], sems.at[kind]) for kind in range(3)
-    ]
-    copies.append(pltpu.make_async_copy(slots, out_slots.at[0], sems.at[3]))
-    for copy in copies:
-        copy.start()
+def deliver_kernel(last, edge_last, slots, out_fields, out_slots, merged, sems):
+    rows, cols = merged.shape[2], merged.shape[3]
+    n_lanes = cols // LANES
+    lane = lanes()
+    copies = [pltpu.make_async_copy(slots, out_slots.at[0], sems.at[3])]
+    copies[0].start()
+    for kind in range(3):
+        for t in range(rows // SUB):
+            at = pl.ds(t * SUB, SUB)
+            edge = edge_last[kind, at, :]
+            for layer in range(2):
+                for k in range(n_lanes):
+                    value = last[kind, layer, k, at, :]
+                    if k == 0:
+                        value = jnp.where(lane < KEEP, turn(edge, -HALF * layer - OUT, 1), value)
+                    if k == n_lanes - 1:
+                        value = jnp.where(
+                            lane >= LANES - KEEP, turn(edge, -HALF * layer - SIDE - OUT, 1), value
+                        )
+                    merged[kind, layer, at, lane_tile(k)] = value
+        copies.append(pltpu.make_async_copy(merged.at[kind], out_fields.at[kind], sems.at[kind]))
+        copies[-1].start()
     for copy in copies:
         copy.wait()
 
@@ -734,10 +755,13 @@
     )(*blocks, cross, near, src, pool_matrices(), base, place)
 
     plane = (ext_rows, LANES)
-    fields, outgoing = call(
+    (base,) = call(
+        edge_cross_kernel, (shape(4 + STEPS, *plane),), 2, flops=10 * cells, size=8 * cells
+    )(base, cross_cols)
+    edge_last, outgoing = call(
         edge_kernel,
-        (pltpu.VMEM((3, 2, rows, cols), F32), pltpu.VMEM((owners * capacity, width), F32)),
-        7,
+        (shape(3, rows, LANES), pltpu.VMEM((owners * capacity, width), F32)),
+        5,
         scratch=(
             pltpu.VMEM((1 + STEPS,) + plane, F32),
             pltpu.VMEM((2,) + plane, F32),
@@ -749,19 +773,20 @@
         ),
         flops=50 * cells,
         size=16 * cells,
-    )(last, slots, base, cross_cols, near_cols, src_edge, place_edge)
+    )(slots, base, near_cols, src_edge, place_edge)
 
     outgoing = outgoing.reshape(owners, capacity, width)
     incoming = lax.all_to_all(outgoing, ("gx", "gy"), split_axis=0, concat_axis=0, tiled=True)
     anywhere = pl.BlockSpec(memory_space=pl.ANY)
     return call(
         deliver_kernel,
-        (shape(*fields.shape), shape(1, *incoming.shape)),
-        2,
+        (shape(3, 2, rows, cols), shape(1, *incoming.shape)),
+        3,
         out_specs=(anywhere, anywhere),
-        scratch=(pltpu.SemaphoreType.DMA((4,)),),
-        size=16 * cells,
-    )(fields, pltpu.with_memory_space_constraint(incoming, pltpu.VMEM))
+        scratch=(pltpu.VMEM((3, 2, rows, cols), F32), pltpu.SemaphoreType.DMA((4,))),
+        flops=20 * cells,
+        size=48 * cells,
+    )(last, edge_last, pltpu.with_memory_space_constraint(incoming, pltpu.VMEM))
 
 
 def solution(mesh):

time: 32.1 us -> 31.2 us (0.972)
  Pallas kernels: 8.43 us -> 7.76 us
    pallas_call x2 -> x3, Pallas kernels: 3.02 us -> 2.35 us  [the longest x1 1.07 us: on_device(): call(edge_kernel, (shape(3, rows, LANES), pltpu.VMEM((owners * capacity,...]
  transfers between devices with their start and end apart: 4 -> 4, of which waited for: 1 -> 1; matrix products, arithmetic and copies ran while one was open for 0% -> 0% of each run, Pallas kernels for 13% -> 14%
where the time goes in v12:
time: 31.2 us; the launch traced here: 31 us
  blocking collectives  11.7 us (38%)
  starting transfers between devices  10.2 us (33%)
  Pallas kernels  7.76 us (25%)
  between operations  0.82 us (3%)
  waiting for transfers between devices  0.53 us (2%)
    all_to_all x1, blocking collectives, on_device(): lax.all_to_all(outgoing, ('gx', 'gy'), split_axis=0, concat_axis=0, tiled...  11.7 us
    ppermute x1, starting transfers between devices, on_device(): near_cols = lax.ppermute(near_cols, 'gy', pairs(gy_count, 0))  4.46 us
    ppermute x1, starting transfers between devices, on_device(): near = lax.ppermute(near, 'gx', pairs(gx_count, 0))  4.36 us
    pallas_call x1, Pallas kernels, on_device(): call(inner_kernel, (shape(3, 2, n_lanes, rows, LANES), shape(owners * cap...  2.04 us
    pallas_call x1, Pallas kernels, on_device(): call(lambda *refs: prep_kernel(capacity, *refs), (packed, packed, shape(4...  1.99 us
    pallas_call x1, Pallas kernels, on_device(): call(rows_kernel, (strip, strip), 3, in_space=pltpu.HBM, scratch=(pltpu.V...  1.21 us
    pallas_call x1, Pallas kernels, on_device(): call(edge_kernel, (shape(3, rows, LANES), pltpu.VMEM((owners * capacity,...  1.07 us
    pallas_call x1, Pallas kernels, on_device(): call(deliver_kernel, (shape(3, 2, rows, cols), shape(1, *incoming.shape))...  1.04 us
  transfers between devices with their start and end apart: 4, of which 1 were waited for; matrix products, arithmetic and copies ran while one was open for 0% of the time, Pallas kernels for 14%

profile of v12, /device:TPU:0, one launch (start us, length us, event | category | flops | bytes accessed | tf_op | source)
XLA Modules:
  0.0 31.0 jit_solution(16499038566299009529)
XLA Ops:
  0.6 0.0 copy-start
  0.6 0.0 copy-start.2
  0.7 0.0 copy-start.1
  0.7 0.0 copy-start.8
  0.7 0.0 copy-start.7
  0.7 0.0 copy-start.4
  0.7 0.0 copy-start.6
  0.7 0.0 copy-start.5
  0.7 1.2 %shard_map.104 = (f32[16,8,256]{2,1,0:T(8,128)S(1)}, f32[16,8,256]{2,1,0:T(8,128)S(1)}) custom-call(f32[3,2,128,256]{3,2,1,0:T(8,128)} %fields.3, f32[2,128,256]{2,1,0:T(8,128)} %eps.3, f32[4,2,128,256]{3,2,1,0:T(8,128)} %fwd.3), custom_call_target="tpu_custom_call" | custom-call | bytes 1048576 | tf_op jit(solution)/shard_map/pallas_call | solution.py:690
  1.9 0.0 copy-start.3
  1.9 0.7 %collective-permute-start = (f32[16,8,256]{2,1,0:T(8,128)S(1)}, f32[16,8,256]{2,1,0:T(8,128)S(1)}, u32[]{:S(2)}, u32[]{:S(2)}) collective-permute-start(f32[16,8,256]{2,1,0:T(8,128)S(1)} %get-tuple-element.18), channel_id=1, source_target_pairs={{4,8},{8,4},{5,9},{9,5},{6,10},{10,6},{7,11},{11,7},{20,24},{24,20... | collective-permute-start | bytes 393224 | tf_op jit(solution)/shard_map/ppermute | solution.py:704
  2.6 4.4 %collective-permute-start.1 = (f32[16,8,256]{2,1,0:T(8,128)S(1)}, f32[16,8,256]{2,1,0:T(8,128)S(1)}, u32[]{:S(2)}, u32[]{:S(2)}) collective-permute-start(f32[16,8,256]{2,1,0:T(8,128)S(1)} %get-tuple-element.19), channel_id=1, source_target_pairs={{0,4},{8,12},{4,0},{12,8},{1,5},{9,13},{5,1},{13,9},{2,6},{10,14},... | collective-permute-start | bytes 393224 | tf_op jit(solution)/shard_map/ppermute | solution.py:705
  7.0 0.0 copy-done
  7.0 0.0 copy-done.2
  7.0 0.0 copy-done.1
  7.0 0.0 copy-done.8
  7.0 0.0 copy-done.7
  7.0 0.0 copy-done.4
  7.0 0.0 copy-done.6
  7.0 0.0 copy-done.5
  7.0 2.0 %shard_map.105 = (f32[160,128]{1,0:T(8,128)S(1)}, f32[160,128]{1,0:T(8,128)S(1)}, f32[8,160,128]{2,1,0:T(8,128)S(1)}, f32[4,2,160,256]{3,2,1,0:T(8,128)S(1)}, f3...) custom-call(f32[3,2,128,256]{3,2,1,0:T(8,128)S(1)} %copy-done.1, ...), custom_call_target="tpu_custom_call" | custom-call | flops 188743680 | bytes 2097152 | tf_op jit(solution)/shard_map/pallas_call | solution.py:709
  9.0 0.0 collective-permute-done.cross.cross_rows
  9.0 0.0 collective-permute-done.1.near.near_rows
  9.1 0.2 shard_map.107
  9.2 0.7 %collective-permute-start.2 = (f32[160,128]{1,0:T(8,128)S(1)}, f32[160,128]{1,0:T(8,128)S(1)}, u32[]{:S(2)}, u32[]{:S(2)}) collective-permute-start(f32[160,128]{1,0:T(8,128)S(1)} %get-tuple-element.28), channel_id=1, source_target_pairs={{1,2},{2,1},{5,6},{6,5},{9,10},{10,9},{13,14},{14,13},{17,18},{18,... | collective-permute-start | bytes 245768 | tf_op jit(solution)/shard_map/ppermute | solution.py:734
  9.9 4.5 %collective-permute-start.3 = (f32[160,128]{1,0:T(8,128)S(1)}, f32[160,128]{1,0:T(8,128)S(1)}, u32[]{:S(2)}, u32[]{:S(2)}) collective-permute-start(f32[160,128]{1,0:T(8,128)S(1)} %get-tuple-element.29), channel_id=1, source_target_pairs={{0,1},{2,3},{1,0},{3,2},{4,5},{6,7},{5,4},{7,6},{8,9},{10,11},{9,8... | collective-permute-start | bytes 245768 | tf_op jit(solution)/shard_map/ppermute | solution.py:735
  14.4 0.0 copy-done.3
  14.4 2.0 %shard_map.106 = (f32[3,2,2,128,128]{4,3,2,1,0:T(8,128)S(1)}, f32[256,128]{1,0:T(8,128)S(1)}, f32[8,160,128]{2,1,0:T(8,128)S(1)}) custom-call(f32[3,2,128,256]{3,2,1,0:T(8,128)S(1)} %copy-done.1, f32[2,128,256]{2,1,0:T(8,128)S(1)} %copy-done.2, f32[4,2,128,256]{3,2,1,0:T(8,128)S(1)} %copy-done, f32[16,8,256]{2,1,0:T(8,128)S(1)} %collective-permute-done.cross.cross_rows, ...), custom_call_target="tpu_custom_call" | custom-call | flops 6553600 | bytes 3145728 | tf_op jit(solution)/shard_map/pallas_call | solution.py:738
  16.4 0.0 collective-permute-done.2.cross
  16.4 0.2 shard_map.108.base
  16.7 0.5 %collective-permute-done.3.near = f32[160,128]{1,0:T(8,128)S(1)} collective-permute-done((f32[160,128]{1,0:T(8,128)S(1)}, f32[160,128]{1,0:T(8,128)S(1)}, u32[]{:S(2)}, u32[]{:S(2)}) %collective-permute-start.3) | collective-permute-done | bytes 81952 | tf_op jit(solution)/shard_map/ppermute | solution.py:735
  17.2 1.1 %shard_map.109 = (f32[3,128,128]{2,1,0:T(8,128)S(1)}, f32[256,128]{1,0:T(8,128)S(1)}) custom-call(f32[256,128]{1,0:T(8,128)S(1)} %get-tuple-element.24.slots_in, f32[8,160,128]{2,1,0:T(8,128)S(1)} %shard_map.108.base, f32[160,128]{1,0:T(8,128)S(1)} %collective-permute-done.3.near, f32[4,160,128]{2,1,0:T(8,128)S(1)} %get-tuple-element.30.src, ...), custom_call_target="tpu_custom_call" | custom-call | flops 1638400 | bytes 524288 | tf_op jit(solution)/shard_map/pallas_call | solution.py:761
  18.3 11.7 %all_to_all.5.slots = f32[16,16,128]{2,1,0:T(8,128)S(1)} all-to-all(f32[16,16,128]{2,1,0:T(8,128)S(1)} %bitcast.5), channel_id=1, replica_groups=mesh['parts'=2,'gx'=4,'gy'=4] {'gx','gy'}, dimensions={0} | all-to-all | bytes 262144 | tf_op jit(solution)/shard_map/all_to_all | solution.py:779
  30.0 1.0 %shard_map.110 = (f32[3,2,128,256]{3,2,1,0:T(8,128)}, f32[1,16,16,128]{3,2,1,0:T(8,128)}) custom-call(f32[3,2,2,128,128]{4,3,2,1,0:T(8,128)S(1)} %get-tuple-element.23.last, f32[3,128,128]{2,1,0:T(8,128)S(1)} %get-tuple-element.32.edge_last, f32[16,16,128]{2,1,0:T(8,128)S(1)} %all_to_all.5.slots), custom_call_target="tpu_custom_call" | custom-call | flops 655360 | bytes 1572864 | tf_op jit(solution)/shard_map/pallas_call | solution.py:781
Async XLA Ops:
  0.6 6.4 %copy-start = (f32[4,2,128,256]{3,2,1,0:T(8,128)S(1)}, f32[4,2,128,256]{3,2,1,0:T(8,128)}, u32[]{:S(2)}) copy-start(f32[4,2,128,256]{3,2,1,0:T(8,128)} %fwd.3) | copy-start | bytes 3145732
  0.6 6.3 %copy-start.2 = (f32[2,128,256]{2,1,0:T(8,128)S(1)}, f32[2,128,256]{2,1,0:T(8,128)}, u32[]{:S(2)}) copy-start(f32[2,128,256]{2,1,0:T(8,128)} %eps.3) | copy-start | bytes 786436
  0.7 6.3 %copy-start.1 = (f32[3,2,128,256]{3,2,1,0:T(8,128)S(1)}, f32[3,2,128,256]{3,2,1,0:T(8,128)}, u32[]{:S(2)}) copy-start(f32[3,2,128,256]{3,2,1,0:T(8,128)} %fields.3) | copy-start | bytes 2359300
  0.7 6.3 %copy-start.8 = (s32[1,1,128,1]{2,3,1,0:T(1,128)S(1)}, s32[1,1,128,1]{2,3,1,0:T(1,128)}, u32[]{:S(2)}) copy-start(s32[1,1,128,1]{2,3,1,0:T(1,128)} %param.16) | copy-start | bytes 1540
  0.7 6.3 %copy-start.7 = (s32[1,1,128]{2,1,0:T(1,128)S(1)}, s32[1,1,128]{2,1,0:T(1,128)}, u32[]{:S(2)}) copy-start(s32[1,1,128]{2,1,0:T(1,128)} %param.15) | copy-start | bytes 1540
  0.7 6.3 %copy-start.4 = (f32[4,64]{1,0:T(4,128)S(1)}, f32[4,64]{1,0:T(4,128)}, u32[]{:S(2)}) copy-start(f32[4,64]{1,0:T(4,128)} %refs_5_.1) | copy-start | bytes 3076
  0.7 6.3 %copy-start.6 = (s32[64]{0:T(128)S(1)}, s32[64]{0:T(128)}, u32[]{:S(2)}) copy-start(s32[64]{0:T(128)} %param.13) | copy-start | bytes 772
  0.7 6.3 %copy-start.5 = (s32[64]{0:T(128)S(1)}, s32[64]{0:T(128)}, u32[]{:S(2)}) copy-start(s32[64]{0:T(128)} %param.12) | copy-start | bytes 772
  1.9 12.4 %copy-start.3 = (bf16[2,128,128]{2,1,0:T(8,128)(2,1)S(1)}, bf16[2,128,128]{2,1,0:T(8,128)(2,1)}, u32[]{:S(2)}) copy-start(bf16[2,128,128]{2,1,0:T(8,128)(2,1)} %constant.2.clone.mats) | copy-start | bytes 196612
  1.9 7.1 %collective-permute-start = (f32[16,8,256]{2,1,0:T(8,128)S(1)}, f32[16,8,256]{2,1,0:T(8,128)S(1)}, u32[]{:S(2)}, u32[]{:S(2)}) collective-permute-start(f32[16,8,256]{2,1,0:T(8,128)S(1)} %get-tuple-element.18), channel_id=1, source_target_pairs={{4,8},{8,4},{5,9},{9,5},{6,10},{10,6},{7,11},{11,7},{20,24},{24,20... | collective-permute-start | bytes 393224 | tf_op jit(solution)/shard_map/ppermute | solution.py:704
  2.6 6.4 %collective-permute-start.1 = (f32[16,8,256]{2,1,0:T(8,128)S(1)}, f32[16,8,256]{2,1,0:T(8,128)S(1)}, u32[]{:S(2)}, u32[]{:S(2)}) collective-permute-start(f32[16,8,256]{2,1,0:T(8,128)S(1)} %get-tuple-element.19), channel_id=1, source_target_pairs={{0,4},{8,12},{4,0},{12,8},{1,5},{9,13},{5,1},{13,9},{2,6},{10,14},... | collective-permute-start | bytes 393224 | tf_op jit(solution)/shard_map/ppermute | solution.py:705
  9.2 7.2 %collective-permute-start.2 = (f32[160,128]{1,0:T(8,128)S(1)}, f32[160,128]{1,0:T(8,128)S(1)}, u32[]{:S(2)}, u32[]{:S(2)}) collective-permute-start(f32[160,128]{1,0:T(8,128)S(1)} %get-tuple-element.28), channel_id=1, source_target_pairs={{1,2},{2,1},{5,6},{6,5},{9,10},{10,9},{13,14},{14,13},{17,18},{18,... | collective-permute-start | bytes 245768 | tf_op jit(solution)/shard_map/ppermute | solution.py:734
  9.9 7.3 %collective-permute-start.3 = (f32[160,128]{1,0:T(8,128)S(1)}, f32[160,128]{1,0:T(8,128)S(1)}, u32[]{:S(2)}, u32[]{:S(2)}) collective-permute-start(f32[160,128]{1,0:T(8,128)S(1)} %get-tuple-element.29), channel_id=1, source_target_pairs={{0,1},{2,3},{1,0},{3,2},{4,5},{6,7},{5,4},{7,6},{8,9},{10,11},{9,8... | collective-permute-start | bytes 245768 | tf_op jit(solution)/shard_map/ppermute | solution.py:735

commit v13 on v12

--- a/solution.py
+++ b/solution.py
@@ -83,38 +83,47 @@
     return ((subs() * 0 + lax.axis_index(axis)) & 1) == 1
 
 
-def rows_kernel(fields, eps, fwd, cross, near, hold, hold_fwd, sems):
+def rows_kernel(fields, eps, fwd, cross, near, hold, sems):
     rows, cols = fields.shape[2], fields.shape[3]
-    copies = []
-    for n, at in enumerate((0, rows - PAD)):
-        at_fwd = 0 if n == 0 else rows - SUB
+    sub = subs()
+    odd = lax.axis_index("gx") & 1
+    parts = []
+    for n, (out, at_end) in enumerate(((cross, odd), (near, 1 - odd))):
+        at = pl.ds(pl.multiple_of(at_end * (rows - SUB), SUB), SUB)
+        rest = pl.ds(pl.multiple_of(SUB + at_end * (rows - 3 * SUB), SUB), SUB)
         pairs = (
-            (fields.at[:, :, pl.ds(at, PAD), :], hold.at[n, pl.ds(0, 3)]),
-            (eps.at[:, pl.ds(at, PAD), :], hold.at[n, 3]),
-            (fwd.at[:, :, pl.ds(at_fwd, SUB), :], hold_fwd.at[n]),
+            (fields.at[:, :, rest, :], hold.at[n, pl.ds(0, 3)]),
+            (eps.at[:, rest, :], hold.at[n, 3]),
+            (fwd.at[:, :, at, :], out.at[pl.ds(4, STEPS)]),
+            (fields.at[:, :, at, :], out.at[pl.ds(0, 3)]),
+            (eps.at[:, at, :], out.at[3]),
         )
-        for m, (src, dst) in enumerate(pairs):
-            copies.append(pltpu.make_async_copy(src, dst, sems.at[3 * n + m]))
-    for copy in copies:
-        copy.start()
-    for copy in copies:
-        copy.wait()
-    odd, sub = is_odd("gx"), subs()
-    for kind in range(4):
-        for layer in range(2):
-            plane = 2 * kind + layer
-            for k in range(cols // LANES):
-                at = lane_tile(k)
-                low = hold[0, kind, layer, pl.ds(0, SUB), at]
-                high = hold[1, kind, layer, pl.ds(SUB, SUB), at]
-                cross[plane, :, at] = jnp.where(odd, high, low)
-                near[plane, :, at] = jnp.where(odd, low, high)
-                rest_low = turn(hold[0, kind, layer, pl.ds(SUB, SUB), at], -LEFT_OVER, 0)
-                rest_high = turn(hold[1, kind, layer, pl.ds(0, SUB), at], LEFT_OVER, 0)
-                low = jnp.where(sub >= NEAR, rest_low, hold_fwd[0, kind, layer, :, at])
-                high = jnp.where(sub < SUB - NEAR, rest_high, hold_fwd[1, kind, layer, :, at])
-                cross[8 + plane, :, at] = jnp.where(odd, high, low)
-                near[8 + plane, :, at] = jnp.where(odd, low, high)
+        copies = [
+            pltpu.make_async_copy(src, dst, sems.at[len(pairs) * n + m])
+            for m, (src, dst) in enumerate(pairs)
+        ]
+        parts.append((n, out, at_end, copies))
+    for group in (slice(0, 3), slice(3, 5)):
+        for part in parts:
+            for copy in part[3][group]:
+                copy.start()
+    for n, out, at_end, copies in parts:
+        for copy in copies[:3]:
+            copy.wait()
+        low = (1 - at_end) * NEAR
+        rest = (sub >= low) & (sub < low + LEFT_OVER)
+        shift = NEAR + at_end * (LEFT_OVER - NEAR)
+        for kind in range(4):
+            for layer in range(2):
+                values = []
+                for k in range(cols // LANES):
+                    moved = pltpu.roll(hold[n, kind, layer, :, lane_tile(k)], shift, 0)
+                    values.append(jnp.where(rest, moved, out[4 + kind, layer, :, lane_tile(k)]))
+                for k, value in enumerate(values):
+                    out[4 + kind, layer, :, lane_tile(k)] = value
+    for part in parts:
+        for copy in part[3][3:]:
+            copy.wait()
 
 
 def halo_tile(cross, near, odd, tile, kind, layer, at):
@@ -122,8 +131,8 @@
     outer = tile in (0, 3)
     if outer and kind >= 4:
         return None
-    plane = 2 * kind + layer + (8 if outer else 0)
-    a, b = near[plane, :, at], cross[plane, :, at]
+    plane = kind + (4 if outer else 0)
+    a, b = near[plane, layer, :, at], cross[plane, layer, :, at]
     value = jnp.where(odd, a, b) if is_above else jnp.where(odd, b, a)
     if outer:
         value = turn(value, -LEFT_OVER if is_above else LEFT_OVER, 0)
@@ -190,7 +199,7 @@
 
 
 def corners_kernel(cross_in, near_in, cross_rows, near_rows, cross, near):
-    rows, cols = cross.shape[0] - 2 * PAD, cross_rows.shape[2]
+    rows, cols = cross.shape[0] - 2 * PAD, cross_rows.shape[3]
     lane, odd, odd_col = lanes(), is_odd("gx"), is_odd("gy")
     core = pl.ds(PAD, rows)
     cross[core, :] = cross_in[core, :]
@@ -628,13 +637,13 @@
     rows, cols = merged.shape[2], merged.shape[3]
     n_lanes = cols // LANES
     lane = lanes()
-    copies = [pltpu.make_async_copy(slots, out_slots.at[0], sems.at[3])]
+    copies = [pltpu.make_async_copy(slots, out_slots.at[0], sems.at[6])]
     copies[0].start()
     for kind in range(3):
-        for t in range(rows // SUB):
-            at = pl.ds(t * SUB, SUB)
-            edge = edge_last[kind, at, :]
-            for layer in range(2):
+        for layer in range(2):
+            for t in range(rows // SUB):
+                at = pl.ds(t * SUB, SUB)
+                edge = edge_last[kind, at, :]
                 for k in range(n_lanes):
                     value = last[kind, layer, k, at, :]
                     if k == 0:
@@ -644,8 +653,12 @@
                             lane >= LANES - KEEP, turn(edge, -HALF * layer - SIDE - OUT, 1), value
                         )
                     merged[kind, layer, at, lane_tile(k)] = value
-        copies.append(pltpu.make_async_copy(merged.at[kind], out_fields.at[kind], sems.at[kind]))
-        copies[-1].start()
+            copies.append(
+                pltpu.make_async_copy(
+                    merged.at[kind, layer], out_fields.at[kind, layer], sems.at[2 * kind + layer]
+                )
+            )
+            copies[-1].start()
     for copy in copies:
         copy.wait()
 
@@ -686,13 +699,12 @@
     blocks = (adj_fields, inv_eps, fwd_diff)
 
 
-    strip = shape(16, SUB, cols)
+    strip = shape(4 + STEPS, 2, SUB, cols)
     cross, near = call(
         rows_kernel, (strip, strip), 3, in_space=pltpu.HBM,
         scratch=(
-            pltpu.VMEM((2, 4, 2, PAD, cols), F32),
-            pltpu.VMEM((2, STEPS, 2, SUB, cols), F32),
-            pltpu.SemaphoreType.DMA((6,)),
+            pltpu.VMEM((2, 4, 2, SUB, cols), F32),
+            pltpu.SemaphoreType.DMA((10,)),
         ),
         size=2**20,
     )(*(pltpu.with_memory_space_constraint(block, pltpu.HBM) for block in blocks))
@@ -783,7 +795,7 @@
         (shape(3, 2, rows, cols), shape(1, *incoming.shape)),
         3,
         out_specs=(anywhere, anywhere),
-        scratch=(pltpu.VMEM((3, 2, rows, cols), F32), pltpu.SemaphoreType.DMA((4,))),
+        scratch=(pltpu.VMEM((3, 2, rows, cols), F32), pltpu.SemaphoreType.DMA((7,))),
         flops=20 * cells,
         size=48 * cells,
     )(last, edge_last, pltpu.with_memory_space_constraint(incoming, pltpu.VMEM))

time: 31.2 us -> 31.2 us (level)
  no operation moved by 1% of the time
where the time goes in v13:
time: 31.2 us; the launch traced here: 31 us
  blocking collectives  11.7 us (38%)
  starting transfers between devices  10.2 us (33%)
  Pallas kernels  7.72 us (25%)
  between operations  0.82 us (3%)
  waiting for transfers between devices  0.53 us (2%)
    all_to_all x1, blocking collectives, on_device(): lax.all_to_all(outgoing, ('gx', 'gy'), split_axis=0, concat_axis=0, tiled...  11.7 us
    ppermute x1, starting transfers between devices, on_device(): near_cols = lax.ppermute(near_cols, 'gy', pairs(gy_count, 0))  4.46 us
    ppermute x1, starting transfers between devices, on_device(): near = lax.ppermute(near, 'gx', pairs(gx_count, 0))  4.36 us
    pallas_call x1, Pallas kernels, on_device(): call(inner_kernel, (shape(3, 2, n_lanes, rows, LANES), shape(owners * cap...  2.04 us
    pallas_call x1, Pallas kernels, on_device(): call(lambda *refs: prep_kernel(capacity, *refs), (packed, packed, shape(4...  1.99 us
    pallas_call x1, Pallas kernels, on_device(): call(rows_kernel, (strip, strip), 3, in_space=pltpu.HBM, scratch=(pltpu.V...  1.18 us
    pallas_call x1, Pallas kernels, on_device(): call(edge_kernel, (shape(3, rows, LANES), pltpu.VMEM((owners * capacity,...  1.07 us
    pallas_call x1, Pallas kernels, on_device(): call(deliver_kernel, (shape(3, 2, rows, cols), shape(1, *incoming.shape))...  1.03 us
  transfers between devices with their start and end apart: 4, of which 1 were waited for; matrix products, arithmetic and copies ran while one was open for 0% of the time, Pallas kernels for 14%

profile of v13, /device:TPU:0, one launch (start us, length us, event | category | flops | bytes accessed | tf_op | source)
XLA Modules:
  0.0 31.0 jit_solution(11865473526789967981)
XLA Ops:
  0.6 0.0 copy-start
  0.6 0.0 copy-start.2
  0.7 0.0 copy-start.1
  0.7 0.0 copy-start.8
  0.7 0.0 copy-start.7
  0.7 0.0 copy-start.4
  0.7 0.0 copy-start.6
  0.7 0.0 copy-start.5
  0.7 1.2 %shard_map.104 = (f32[8,2,8,256]{3,2,1,0:T(8,128)S(1)}, f32[8,2,8,256]{3,2,1,0:T(8,128)S(1)}) custom-call(f32[3,2,128,256]{3,2,1,0:T(8,128)} %fields.3, f32[2,128,256]{2,1,0:T(8,128)} %eps.3, f32[4,2,128,256]{3,2,1,0:T(8,128)} %fwd.3), custom_call_target="tpu_custom_call" | custom-call | bytes 1048576 | tf_op jit(solution)/shard_map/pallas_call | solution.py:703
  1.9 0.0 copy-start.3
  1.9 0.7 %collective-permute-start = (f32[8,2,8,256]{3,2,1,0:T(8,128)S(1)}, f32[8,2,8,256]{3,2,1,0:T(8,128)S(1)}, u32[]{:S(2)}, u32[]{:S(2)}) collective-permute-start(f32[8,2,8,256]{3,2,1,0:T(8,128)S(1)} %get-tuple-element.18), channel_id=1, source_target_pairs={{4,8},{8,4},{5,9},{9,5},{6,10},{10,6},{7,11},{11,7},{20,24},{24,20... | collective-permute-start | bytes 393224 | tf_op jit(solution)/shard_map/ppermute | solution.py:716
  2.6 4.4 %collective-permute-start.1 = (f32[8,2,8,256]{3,2,1,0:T(8,128)S(1)}, f32[8,2,8,256]{3,2,1,0:T(8,128)S(1)}, u32[]{:S(2)}, u32[]{:S(2)}) collective-permute-start(f32[8,2,8,256]{3,2,1,0:T(8,128)S(1)} %get-tuple-element.19), channel_id=1, source_target_pairs={{0,4},{8,12},{4,0},{12,8},{1,5},{9,13},{5,1},{13,9},{2,6},{10,14},... | collective-permute-start | bytes 393224 | tf_op jit(solution)/shard_map/ppermute | solution.py:717
  7.0 0.0 copy-done
  7.0 0.0 copy-done.2
  7.0 0.0 copy-done.1
  7.0 0.0 copy-done.8
  7.0 0.0 copy-done.7
  7.0 0.0 copy-done.4
  7.0 0.0 copy-done.6
  7.0 0.0 copy-done.5
  7.0 2.0 %shard_map.105 = (f32[160,128]{1,0:T(8,128)S(1)}, f32[160,128]{1,0:T(8,128)S(1)}, f32[8,160,128]{2,1,0:T(8,128)S(1)}, f32[4,2,160,256]{3,2,1,0:T(8,128)S(1)}, f3...) custom-call(f32[3,2,128,256]{3,2,1,0:T(8,128)S(1)} %copy-done.1, ...), custom_call_target="tpu_custom_call" | custom-call | flops 188743680 | bytes 2097152 | tf_op jit(solution)/shard_map/pallas_call | solution.py:721
  9.0 0.0 collective-permute-done.cross.cross_rows
  9.0 0.0 collective-permute-done.1.near.near_rows
  9.0 0.2 shard_map.107
  9.2 0.7 %collective-permute-start.2 = (f32[160,128]{1,0:T(8,128)S(1)}, f32[160,128]{1,0:T(8,128)S(1)}, u32[]{:S(2)}, u32[]{:S(2)}) collective-permute-start(f32[160,128]{1,0:T(8,128)S(1)} %get-tuple-element.28), channel_id=1, source_target_pairs={{1,2},{2,1},{5,6},{6,5},{9,10},{10,9},{13,14},{14,13},{17,18},{18,... | collective-permute-start | bytes 245768 | tf_op jit(solution)/shard_map/ppermute | solution.py:746
  9.9 4.5 %collective-permute-start.3 = (f32[160,128]{1,0:T(8,128)S(1)}, f32[160,128]{1,0:T(8,128)S(1)}, u32[]{:S(2)}, u32[]{:S(2)}) collective-permute-start(f32[160,128]{1,0:T(8,128)S(1)} %get-tuple-element.29), channel_id=1, source_target_pairs={{0,1},{2,3},{1,0},{3,2},{4,5},{6,7},{5,4},{7,6},{8,9},{10,11},{9,8... | collective-permute-start | bytes 245768 | tf_op jit(solution)/shard_map/ppermute | solution.py:747
  14.3 0.0 copy-done.3
  14.3 2.0 %shard_map.106 = (f32[3,2,2,128,128]{4,3,2,1,0:T(8,128)S(1)}, f32[256,128]{1,0:T(8,128)S(1)}, f32[8,160,128]{2,1,0:T(8,128)S(1)}) custom-call(f32[3,2,128,256]{3,2,1,0:T(8,128)S(1)} %copy-done.1, f32[2,128,256]{2,1,0:T(8,128)S(1)} %copy-done.2, f32[4,2,128,256]{3,2,1,0:T(8,128)S(1)} %copy-done, f32[8,2,8,256]{3,2,1,0:T(8,128)S(1)} %collective-permute-done.cross.cross_rows, ...), custom_call_target="tpu_custom_call" | custom-call | flops 6553600 | bytes 3145728 | tf_op jit(solution)/shard_map/pallas_call | solution.py:750
  16.4 0.0 collective-permute-done.2.cross
  16.4 0.2 shard_map.108.base
  16.6 0.5 %collective-permute-done.3.near = f32[160,128]{1,0:T(8,128)S(1)} collective-permute-done((f32[160,128]{1,0:T(8,128)S(1)}, f32[160,128]{1,0:T(8,128)S(1)}, u32[]{:S(2)}, u32[]{:S(2)}) %collective-permute-start.3) | collective-permute-done | bytes 81952 | tf_op jit(solution)/shard_map/ppermute | solution.py:747
  17.2 1.1 %shard_map.109 = (f32[3,128,128]{2,1,0:T(8,128)S(1)}, f32[256,128]{1,0:T(8,128)S(1)}) custom-call(f32[256,128]{1,0:T(8,128)S(1)} %get-tuple-element.24.slots_in, f32[8,160,128]{2,1,0:T(8,128)S(1)} %shard_map.108.base, f32[160,128]{1,0:T(8,128)S(1)} %collective-permute-done.3.near, f32[4,160,128]{2,1,0:T(8,128)S(1)} %get-tuple-element.30.src, ...), custom_call_target="tpu_custom_call" | custom-call | flops 1638400 | bytes 524288 | tf_op jit(solution)/shard_map/pallas_call | solution.py:773
  18.2 11.7 %all_to_all.5.slots = f32[16,16,128]{2,1,0:T(8,128)S(1)} all-to-all(f32[16,16,128]{2,1,0:T(8,128)S(1)} %bitcast.5), channel_id=1, replica_groups=mesh['parts'=2,'gx'=4,'gy'=4] {'gx','gy'}, dimensions={0} | all-to-all | bytes 262144 | tf_op jit(solution)/shard_map/all_to_all | solution.py:791
  29.9 1.0 %shard_map.110 = (f32[3,2,128,256]{3,2,1,0:T(8,128)}, f32[1,16,16,128]{3,2,1,0:T(8,128)}) custom-call(f32[3,2,2,128,128]{4,3,2,1,0:T(8,128)S(1)} %get-tuple-element.23.last, f32[3,128,128]{2,1,0:T(8,128)S(1)} %get-tuple-element.32.edge_last, f32[16,16,128]{2,1,0:T(8,128)S(1)} %all_to_all.5.slots), custom_call_target="tpu_custom_call" | custom-call | flops 655360 | bytes 1572864 | tf_op jit(solution)/shard_map/pallas_call | solution.py:793
Async XLA Ops:
  0.6 6.3 %copy-start = (f32[4,2,128,256]{3,2,1,0:T(8,128)S(1)}, f32[4,2,128,256]{3,2,1,0:T(8,128)}, u32[]{:S(2)}) copy-start(f32[4,2,128,256]{3,2,1,0:T(8,128)} %fwd.3) | copy-start | bytes 3145732
  0.6 6.3 %copy-start.2 = (f32[2,128,256]{2,1,0:T(8,128)S(1)}, f32[2,128,256]{2,1,0:T(8,128)}, u32[]{:S(2)}) copy-start(f32[2,128,256]{2,1,0:T(8,128)} %eps.3) | copy-start | bytes 786436
  0.7 6.3 %copy-start.1 = (f32[3,2,128,256]{3,2,1,0:T(8,128)S(1)}, f32[3,2,128,256]{3,2,1,0:T(8,128)}, u32[]{:S(2)}) copy-start(f32[3,2,128,256]{3,2,1,0:T(8,128)} %fields.3) | copy-start | bytes 2359300
  0.7 6.3 %copy-start.8 = (s32[1,1,128,1]{2,3,1,0:T(1,128)S(1)}, s32[1,1,128,1]{2,3,1,0:T(1,128)}, u32[]{:S(2)}) copy-start(s32[1,1,128,1]{2,3,1,0:T(1,128)} %param.16) | copy-start | bytes 1540
  0.7 6.3 %copy-start.7 = (s32[1,1,128]{2,1,0:T(1,128)S(1)}, s32[1,1,128]{2,1,0:T(1,128)}, u32[]{:S(2)}) copy-start(s32[1,1,128]{2,1,0:T(1,128)} %param.15) | copy-start | bytes 1540
  0.7 6.3 %copy-start.4 = (f32[4,64]{1,0:T(4,128)S(1)}, f32[4,64]{1,0:T(4,128)}, u32[]{:S(2)}) copy-start(f32[4,64]{1,0:T(4,128)} %refs_5_.1) | copy-start | bytes 3076
  0.7 6.3 %copy-start.6 = (s32[64]{0:T(128)S(1)}, s32[64]{0:T(128)}, u32[]{:S(2)}) copy-start(s32[64]{0:T(128)} %param.13) | copy-start | bytes 772
  0.7 6.3 %copy-start.5 = (s32[64]{0:T(128)S(1)}, s32[64]{0:T(128)}, u32[]{:S(2)}) copy-start(s32[64]{0:T(128)} %param.12) | copy-start | bytes 772
  1.9 12.4 %copy-start.3 = (bf16[2,128,128]{2,1,0:T(8,128)(2,1)S(1)}, bf16[2,128,128]{2,1,0:T(8,128)(2,1)}, u32[]{:S(2)}) copy-start(bf16[2,128,128]{2,1,0:T(8,128)(2,1)} %constant.2.clone.mats) | copy-start | bytes 196612
  1.9 7.1 %collective-permute-start = (f32[8,2,8,256]{3,2,1,0:T(8,128)S(1)}, f32[8,2,8,256]{3,2,1,0:T(8,128)S(1)}, u32[]{:S(2)}, u32[]{:S(2)}) collective-permute-start(f32[8,2,8,256]{3,2,1,0:T(8,128)S(1)} %get-tuple-element.18), channel_id=1, source_target_pairs={{4,8},{8,4},{5,9},{9,5},{6,10},{10,6},{7,11},{11,7},{20,24},{24,20... | collective-permute-start | bytes 393224 | tf_op jit(solution)/shard_map/ppermute | solution.py:716
  2.6 6.4 %collective-permute-start.1 = (f32[8,2,8,256]{3,2,1,0:T(8,128)S(1)}, f32[8,2,8,256]{3,2,1,0:T(8,128)S(1)}, u32[]{:S(2)}, u32[]{:S(2)}) collective-permute-start(f32[8,2,8,256]{3,2,1,0:T(8,128)S(1)} %get-tuple-element.19), channel_id=1, source_target_pairs={{0,4},{8,12},{4,0},{12,8},{1,5},{9,13},{5,1},{13,9},{2,6},{10,14},... | collective-permute-start | bytes 393224 | tf_op jit(solution)/shard_map/ppermute | solution.py:717
  9.2 7.2 %collective-permute-start.2 = (f32[160,128]{1,0:T(8,128)S(1)}, f32[160,128]{1,0:T(8,128)S(1)}, u32[]{:S(2)}, u32[]{:S(2)}) collective-permute-start(f32[160,128]{1,0:T(8,128)S(1)} %get-tuple-element.28), channel_id=1, source_target_pairs={{1,2},{2,1},{5,6},{6,5},{9,10},{10,9},{13,14},{14,13},{17,18},{18,... | collective-permute-start | bytes 245768 | tf_op jit(solution)/shard_map/ppermute | solution.py:746
  9.9 7.3 %collective-permute-start.3 = (f32[160,128]{1,0:T(8,128)S(1)}, f32[160,128]{1,0:T(8,128)S(1)}, u32[]{:S(2)}, u32[]{:S(2)}) collective-permute-start(f32[160,128]{1,0:T(8,128)S(1)} %get-tuple-element.29), channel_id=1, source_target_pairs={{0,1},{2,3},{1,0},{3,2},{4,5},{6,7},{5,4},{7,6},{8,9},{10,11},{9,8... | collective-permute-start | bytes 245768 | tf_op jit(solution)/shard_map/ppermute | solution.py:747

commit v14 on v13

--- a/solution.py
+++ b/solution.py
@@ -296,6 +296,10 @@
     return (pl.ds(t * SUB, SUB), slice(None))
 
 
+def e_at(t, shift=0):
+    return (pl.ds(SUB + t * SUB + shift, SUB), slice(None))
+
+
 def first_curl(n_tiles, shifts, load_hx, load_hy, curl):
     before = None
     for t in range(n_tiles):
@@ -313,16 +317,10 @@
     for step in range(STEPS):
         low, high = (0, n_tiles) if step == 0 else (1, n_tiles - 1)
 
-        def load(t):
-            return {key: e[(step,) + key + tile_at(t)] for key in keys}
-
-        here = load(low)
-        up = shifts.up(here)
-        down_before = shifts.down(load(max(low - 1, 0)))
         for t in range(low, high):
-            after = load(min(t + 1, n_tiles - 1))
-            up_next, down = shifts.up(after), shifts.down(here)
-            below, above = shifts.below(up, up_next), shifts.above(down, down_before)
+            here = {key: e[(step,) + key + e_at(t)] for key in keys}
+            below = {key: e[(step,) + key + e_at(t, 1)] for key in keys}
+            above = {key: e[(step,) + key + e_at(t, -1)] for key in keys}
             right, left = shifts.next_col(here), shifts.prev_col(here)
             for key in keys:
                 center, over = here[key], above[key]
@@ -333,10 +331,9 @@
                 if step < STEPS - 1:
                     curl[key + tile_at(t)] = change
                 change = change + COUPLING * (other(here, key) - center)
-                e[(step + 1,) + key + tile_at(t)] = (
+                e[(step + 1,) + key + e_at(t)] = (
                     center - eps_of(key, t) * change + src_of(step, key, t)
                 )
-            here, up, down_before = after, up_next, down
 
 
 def gradient(keys, t, e, change_of):
@@ -344,7 +341,7 @@
     for key in keys:
         total = None
         for step in range(STEPS):
-            term = e[(step + 1,) + key + tile_at(t)] * change_of(step, key, t)
+            term = e[(step + 1,) + key + e_at(t)] * change_of(step, key, t)
             total = term if total is None else total + term
         result[key] = -total
     return result
@@ -354,7 +351,7 @@
     def total(t):
         result = {}
         for key in keys:
-            parts = [e[(step,) + key + tile_at(t)] for step in range(STEPS)]
+            parts = [e[(step,) + key + e_at(t)] for step in range(STEPS)]
             result[key] = (parts[0] + parts[1]) + (parts[2] + parts[3])
         return result
 
@@ -367,7 +364,7 @@
         hx, hy = load_hx(t), load_hy(t)
         for key in keys:
             store(
-                key, t, e[(STEPS,) + key + tile_at(t)],
+                key, t, e[(STEPS,) + key + e_at(t)],
                 hx[key] + COURANT * (right[key] - here[key]),
                 hy[key] - COURANT * (below[key] - here[key]),
             )
@@ -412,9 +409,12 @@
         }
 
     shifts = Shifts(next_col, prev_col)
+    for key in keys:
+        for t in (-1, n_tiles):
+            e[(0,) + key + e_at(t)] = jnp.zeros((SUB, LANES), F32)
     for t in range(n_tiles):
         for key in keys:
-            e[(0,) + key + tile_at(t)] = load(0, key[0], t, key[1])
+            e[(0,) + key + e_at(t)] = load(0, key[0], t, key[1])
             eps_c[key + tile_at(t)] = COURANT * load(3, key[0], t, key[1])
     first_curl(n_tiles, shifts, lambda t: load_all(1, t), lambda t: load_all(2, t), curl)
     steps(
@@ -536,13 +536,15 @@
     lane = lanes()
     spot = lane & (HALF - 1)
     mine, moves = from_partner(False, lane)
+    for t in (-1, n_tiles):
+        e[(0,) + e_at(t)] = jnp.zeros((SUB, LANES), F32)
 
     for t in range(n_tiles):
         at = pl.ds(t * SUB, SUB)
         for kind in range(4 if t in (0, n_tiles - 1) else 4 + STEPS):
             value = jnp.where(mine, pltpu.roll(near[at, :], moves[kind], 1), base[kind, at, :])
             if kind == 0:
-                e[0, at, :] = value
+                e[(0,) + e_at(t)] = value
             elif kind < 3:
                 first[kind - 1, at, :] = value
             elif kind == 3:
@@ -756,7 +758,7 @@
         ),
         9,
         scratch=(
-            pltpu.VMEM((1 + STEPS,) + plane, F32),
+            pltpu.VMEM((1 + STEPS, 2, n_lanes, ext_rows + 2 * SUB, LANES), F32),
             pltpu.VMEM(plane, F32),
             pltpu.VMEM(plane, F32),
             pltpu.VMEM(plane, F32),
@@ -775,7 +777,7 @@
         (shape(3, rows, LANES), pltpu.VMEM((owners * capacity, width), F32)),
         5,
         scratch=(
-            pltpu.VMEM((1 + STEPS,) + plane, F32),
+            pltpu.VMEM((1 + STEPS, ext_rows + 2 * SUB, LANES), F32),
             pltpu.VMEM((2,) + plane, F32),
             pltpu.VMEM(plane, F32),
             pltpu.VMEM(plane, F32),

time: 31.2 us -> 31.2 us (level)
  no operation moved by 1% of the time
where the time goes in v14:
time: 31.2 us; the launch traced here: 31 us
  blocking collectives  11.7 us (38%)
  starting transfers between devices  10.2 us (33%)
  Pallas kernels  7.67 us (25%)
  between operations  0.82 us (3%)
  waiting for transfers between devices  0.61 us (2%)
    all_to_all x1, blocking collectives, on_device(): lax.all_to_all(outgoing, ('gx', 'gy'), split_axis=0, concat_axis=0, tiled...  11.7 us
    ppermute x1, starting transfers between devices, on_device(): near_cols = lax.ppermute(near_cols, 'gy', pairs(gy_count, 0))  4.46 us
    ppermute x1, starting transfers between devices, on_device(): near = lax.ppermute(near, 'gx', pairs(gx_count, 0))  4.36 us
    pallas_call x1, Pallas kernels, on_device(): call(lambda *refs: prep_kernel(capacity, *refs), (packed, packed, shape(4...  1.99 us
    pallas_call x1, Pallas kernels, on_device(): call(inner_kernel, (shape(3, 2, n_lanes, rows, LANES), shape(owners * cap...  1.97 us
    pallas_call x1, Pallas kernels, on_device(): call(rows_kernel, (strip, strip), 3, in_space=pltpu.HBM, scratch=(pltpu.V...  1.18 us
    pallas_call x1, Pallas kernels, on_device(): call(edge_kernel, (shape(3, rows, LANES), pltpu.VMEM((owners * capacity,...  1.1 us
    pallas_call x1, Pallas kernels, on_device(): call(deliver_kernel, (shape(3, 2, rows, cols), shape(1, *incoming.shape))...  1.03 us
  transfers between devices with their start and end apart: 4, of which 1 were waited for; matrix products, arithmetic and copies ran while one was open for 0% of the time, Pallas kernels for 14%

profile of v14, /device:TPU:0, one launch (start us, length us, event | category | flops | bytes accessed | tf_op | source)
XLA Modules:
  0.0 31.0 jit_solution(765980986481213954)
XLA Ops:
  0.6 0.0 copy-start
  0.6 0.0 copy-start.2
  0.7 0.0 copy-start.1
  0.7 0.0 copy-start.8
  0.7 0.0 copy-start.7
  0.7 0.0 copy-start.4
  0.7 0.0 copy-start.6
  0.7 0.0 copy-start.5
  0.7 1.2 %shard_map.104 = (f32[8,2,8,256]{3,2,1,0:T(8,128)S(1)}, f32[8,2,8,256]{3,2,1,0:T(8,128)S(1)}) custom-call(f32[3,2,128,256]{3,2,1,0:T(8,128)} %fields.3, f32[2,128,256]{2,1,0:T(8,128)} %eps.3, f32[4,2,128,256]{3,2,1,0:T(8,128)} %fwd.3), custom_call_target="tpu_custom_call" | custom-call | bytes 1048576 | tf_op jit(solution)/shard_map/pallas_call | solution.py:705
  1.9 0.0 copy-start.3
  1.9 0.7 %collective-permute-start = (f32[8,2,8,256]{3,2,1,0:T(8,128)S(1)}, f32[8,2,8,256]{3,2,1,0:T(8,128)S(1)}, u32[]{:S(2)}, u32[]{:S(2)}) collective-permute-start(f32[8,2,8,256]{3,2,1,0:T(8,128)S(1)} %get-tuple-element.18), channel_id=1, source_target_pairs={{4,8},{8,4},{5,9},{9,5},{6,10},{10,6},{7,11},{11,7},{20,24},{24,20... | collective-permute-start | bytes 393224 | tf_op jit(solution)/shard_map/ppermute | solution.py:718
  2.6 4.4 %collective-permute-start.1 = (f32[8,2,8,256]{3,2,1,0:T(8,128)S(1)}, f32[8,2,8,256]{3,2,1,0:T(8,128)S(1)}, u32[]{:S(2)}, u32[]{:S(2)}) collective-permute-start(f32[8,2,8,256]{3,2,1,0:T(8,128)S(1)} %get-tuple-element.19), channel_id=1, source_target_pairs={{0,4},{8,12},{4,0},{12,8},{1,5},{9,13},{5,1},{13,9},{2,6},{10,14},... | collective-permute-start | bytes 393224 | tf_op jit(solution)/shard_map/ppermute | solution.py:719
  7.0 0.0 copy-done
  7.0 0.0 copy-done.2
  7.0 0.0 copy-done.1
  7.0 0.0 copy-done.8
  7.0 0.0 copy-done.7
  7.0 0.0 copy-done.4
  7.0 0.0 copy-done.6
  7.0 0.0 copy-done.5
  7.0 2.0 %shard_map.105 = (f32[160,128]{1,0:T(8,128)S(1)}, f32[160,128]{1,0:T(8,128)S(1)}, f32[8,160,128]{2,1,0:T(8,128)S(1)}, f32[4,2,160,256]{3,2,1,0:T(8,128)S(1)}, f3...) custom-call(f32[3,2,128,256]{3,2,1,0:T(8,128)S(1)} %copy-done.1, ...), custom_call_target="tpu_custom_call" | custom-call | flops 188743680 | bytes 2097152 | tf_op jit(solution)/shard_map/pallas_call | solution.py:723
  9.0 0.0 collective-permute-done.cross.cross_rows
  9.0 0.0 collective-permute-done.1.near.near_rows
  9.0 0.2 shard_map.107
  9.2 0.7 %collective-permute-start.2 = (f32[160,128]{1,0:T(8,128)S(1)}, f32[160,128]{1,0:T(8,128)S(1)}, u32[]{:S(2)}, u32[]{:S(2)}) collective-permute-start(f32[160,128]{1,0:T(8,128)S(1)} %get-tuple-element.28), channel_id=1, source_target_pairs={{1,2},{2,1},{5,6},{6,5},{9,10},{10,9},{13,14},{14,13},{17,18},{18,... | collective-permute-start | bytes 245768 | tf_op jit(solution)/shard_map/ppermute | solution.py:748
  9.9 4.5 %collective-permute-start.3 = (f32[160,128]{1,0:T(8,128)S(1)}, f32[160,128]{1,0:T(8,128)S(1)}, u32[]{:S(2)}, u32[]{:S(2)}) collective-permute-start(f32[160,128]{1,0:T(8,128)S(1)} %get-tuple-element.29), channel_id=1, source_target_pairs={{0,1},{2,3},{1,0},{3,2},{4,5},{6,7},{5,4},{7,6},{8,9},{10,11},{9,8... | collective-permute-start | bytes 245768 | tf_op jit(solution)/shard_map/ppermute | solution.py:749
  14.3 0.0 copy-done.3
  14.3 2.0 %shard_map.106 = (f32[3,2,2,128,128]{4,3,2,1,0:T(8,128)S(1)}, f32[256,128]{1,0:T(8,128)S(1)}, f32[8,160,128]{2,1,0:T(8,128)S(1)}) custom-call(f32[3,2,128,256]{3,2,1,0:T(8,128)S(1)} %copy-done.1, f32[2,128,256]{2,1,0:T(8,128)S(1)} %copy-done.2, f32[4,2,128,256]{3,2,1,0:T(8,128)S(1)} %copy-done, f32[8,2,8,256]{3,2,1,0:T(8,128)S(1)} %collective-permute-done.cross.cross_rows, ...), custom_call_target="tpu_custom_call" | custom-call | flops 6553600 | bytes 3145728 | tf_op jit(solution)/shard_map/pallas_call | solution.py:752
  16.3 0.0 collective-permute-done.2.cross
  16.3 0.2 shard_map.108.base
  16.6 0.6 %collective-permute-done.3.near = f32[160,128]{1,0:T(8,128)S(1)} collective-permute-done((f32[160,128]{1,0:T(8,128)S(1)}, f32[160,128]{1,0:T(8,128)S(1)}, u32[]{:S(2)}, u32[]{:S(2)}) %collective-permute-start.3) | collective-permute-done | bytes 81952 | tf_op jit(solution)/shard_map/ppermute | solution.py:749
  17.2 1.1 %shard_map.109 = (f32[3,128,128]{2,1,0:T(8,128)S(1)}, f32[256,128]{1,0:T(8,128)S(1)}) custom-call(f32[256,128]{1,0:T(8,128)S(1)} %get-tuple-element.24.slots_in, f32[8,160,128]{2,1,0:T(8,128)S(1)} %shard_map.108.base, f32[160,128]{1,0:T(8,128)S(1)} %collective-permute-done.3.near, f32[4,160,128]{2,1,0:T(8,128)S(1)} %get-tuple-element.30.src, ...), custom_call_target="tpu_custom_call" | custom-call | flops 1638400 | bytes 524288 | tf_op jit(solution)/shard_map/pallas_call | solution.py:775
  18.3 11.7 %all_to_all.5.slots = f32[16,16,128]{2,1,0:T(8,128)S(1)} all-to-all(f32[16,16,128]{2,1,0:T(8,128)S(1)} %bitcast.5), channel_id=1, replica_groups=mesh['parts'=2,'gx'=4,'gy'=4] {'gx','gy'}, dimensions={0} | all-to-all | bytes 262144 | tf_op jit(solution)/shard_map/all_to_all | solution.py:793
  30.0 1.0 %shard_map.110 = (f32[3,2,128,256]{3,2,1,0:T(8,128)}, f32[1,16,16,128]{3,2,1,0:T(8,128)}) custom-call(f32[3,2,2,128,128]{4,3,2,1,0:T(8,128)S(1)} %get-tuple-element.23.last, f32[3,128,128]{2,1,0:T(8,128)S(1)} %get-tuple-element.32.edge_last, f32[16,16,128]{2,1,0:T(8,128)S(1)} %all_to_all.5.slots), custom_call_target="tpu_custom_call" | custom-call | flops 655360 | bytes 1572864 | tf_op jit(solution)/shard_map/pallas_call | solution.py:795
Async XLA Ops:
  0.6 6.3 %copy-start = (f32[4,2,128,256]{3,2,1,0:T(8,128)S(1)}, f32[4,2,128,256]{3,2,1,0:T(8,128)}, u32[]{:S(2)}) copy-start(f32[4,2,128,256]{3,2,1,0:T(8,128)} %fwd.3) | copy-start | bytes 3145732
  0.6 6.3 %copy-start.2 = (f32[2,128,256]{2,1,0:T(8,128)S(1)}, f32[2,128,256]{2,1,0:T(8,128)}, u32[]{:S(2)}) copy-start(f32[2,128,256]{2,1,0:T(8,128)} %eps.3) | copy-start | bytes 786436
  0.7 6.3 %copy-start.1 = (f32[3,2,128,256]{3,2,1,0:T(8,128)S(1)}, f32[3,2,128,256]{3,2,1,0:T(8,128)}, u32[]{:S(2)}) copy-start(f32[3,2,128,256]{3,2,1,0:T(8,128)} %fields.3) | copy-start | bytes 2359300
  0.7 6.3 %copy-start.8 = (s32[1,1,128,1]{2,3,1,0:T(1,128)S(1)}, s32[1,1,128,1]{2,3,1,0:T(1,128)}, u32[]{:S(2)}) copy-start(s32[1,1,128,1]{2,3,1,0:T(1,128)} %param.16) | copy-start | bytes 1540
  0.7 6.3 %copy-start.7 = (s32[1,1,128]{2,1,0:T(1,128)S(1)}, s32[1,1,128]{2,1,0:T(1,128)}, u32[]{:S(2)}) copy-start(s32[1,1,128]{2,1,0:T(1,128)} %param.15) | copy-start | bytes 1540
  0.7 6.3 %copy-start.4 = (f32[4,64]{1,0:T(4,128)S(1)}, f32[4,64]{1,0:T(4,128)}, u32[]{:S(2)}) copy-start(f32[4,64]{1,0:T(4,128)} %refs_5_.1) | copy-start | bytes 3076
  0.7 6.3 %copy-start.6 = (s32[64]{0:T(128)S(1)}, s32[64]{0:T(128)}, u32[]{:S(2)}) copy-start(s32[64]{0:T(128)} %param.13) | copy-start | bytes 772
  0.7 6.3 %copy-start.5 = (s32[64]{0:T(128)S(1)}, s32[64]{0:T(128)}, u32[]{:S(2)}) copy-start(s32[64]{0:T(128)} %param.12) | copy-start | bytes 772
  1.9 12.4 %copy-start.3 = (bf16[2,128,128]{2,1,0:T(8,128)(2,1)S(1)}, bf16[2,128,128]{2,1,0:T(8,128)(2,1)}, u32[]{:S(2)}) copy-start(bf16[2,128,128]{2,1,0:T(8,128)(2,1)} %constant.2.clone.mats) | copy-start | bytes 196612
  1.9 7.1 %collective-permute-start = (f32[8,2,8,256]{3,2,1,0:T(8,128)S(1)}, f32[8,2,8,256]{3,2,1,0:T(8,128)S(1)}, u32[]{:S(2)}, u32[]{:S(2)}) collective-permute-start(f32[8,2,8,256]{3,2,1,0:T(8,128)S(1)} %get-tuple-element.18), channel_id=1, source_target_pairs={{4,8},{8,4},{5,9},{9,5},{6,10},{10,6},{7,11},{11,7},{20,24},{24,20... | collective-permute-start | bytes 393224 | tf_op jit(solution)/shard_map/ppermute | solution.py:718
  2.6 6.4 %collective-permute-start.1 = (f32[8,2,8,256]{3,2,1,0:T(8,128)S(1)}, f32[8,2,8,256]{3,2,1,0:T(8,128)S(1)}, u32[]{:S(2)}, u32[]{:S(2)}) collective-permute-start(f32[8,2,8,256]{3,2,1,0:T(8,128)S(1)} %get-tuple-element.19), channel_id=1, source_target_pairs={{0,4},{8,12},{4,0},{12,8},{1,5},{9,13},{5,1},{13,9},{2,6},{10,14},... | collective-permute-start | bytes 393224 | tf_op jit(solution)/shard_map/ppermute | solution.py:719
  9.2 7.1 %collective-permute-start.2 = (f32[160,128]{1,0:T(8,128)S(1)}, f32[160,128]{1,0:T(8,128)S(1)}, u32[]{:S(2)}, u32[]{:S(2)}) collective-permute-start(f32[160,128]{1,0:T(8,128)S(1)} %get-tuple-element.28), channel_id=1, source_target_pairs={{1,2},{2,1},{5,6},{6,5},{9,10},{10,9},{13,14},{14,13},{17,18},{18,... | collective-permute-start | bytes 245768 | tf_op jit(solution)/shard_map/ppermute | solution.py:748
  9.9 7.3 %collective-permute-start.3 = (f32[160,128]{1,0:T(8,128)S(1)}, f32[160,128]{1,0:T(8,128)S(1)}, u32[]{:S(2)}, u32[]{:S(2)}) collective-permute-start(f32[160,128]{1,0:T(8,128)S(1)} %get-tuple-element.29), channel_id=1, source_target_pairs={{0,1},{2,3},{1,0},{3,2},{4,5},{6,7},{5,4},{7,6},{8,9},{10,11},{9,8... | collective-permute-start | bytes 245768 | tf_op jit(solution)/shard_map/ppermute | solution.py:749

commit v15 on v13

--- a/solution.py
+++ b/solution.py
@@ -192,29 +192,39 @@
         return carry
 
     lax.fori_loop(0, rows // SUB, tile, 0, unroll=4)
-    zero = jnp.zeros((PAD, LANES), F32)
+    zero = jnp.zeros((SUB, LANES), F32)
     for out in (cross, near):
-        out[pl.ds(0, PAD), :] = zero
-        out[pl.ds(PAD + rows, PAD), :] = zero
+        for at in (0, SUB, PAD + rows):
+            out[pl.ds(at, SUB), :] = zero
+
+
+def packed_at(t, n_tiles):
+    return pl.ds((t if t < n_tiles - 1 else 0) * SUB, SUB)
 
 
 def corners_kernel(cross_in, near_in, cross_rows, near_rows, cross, near):
-    rows, cols = cross.shape[0] - 2 * PAD, cross_rows.shape[3]
+    rows, cols = cross.shape[0] - 3 * SUB, cross_rows.shape[3]
     lane, odd, odd_col = lanes(), is_odd("gx"), is_odd("gy")
+    is_first = subs() >= SUB - LEFT_OVER
     core = pl.ds(PAD, rows)
     cross[core, :] = cross_in[core, :]
     near[core, :] = near_in[core, :]
-    for tile in range(4):
-        at = pl.ds(tile * SUB if tile < 2 else PAD + rows + (tile - 2) * SUB, SUB)
-        left, right = (
-            pack_tile(
-                lambda kind, layer: halo_tile(
-                    cross_rows, near_rows, odd, tile, kind, layer, pl.ds(lo, LANES)
-                ),
-                lane, is_right,
-            )
-            for lo, is_right in ((0, False), (cols - LANES, True))
-        )
+    for base, tiles in ((0, (0, 3)), (SUB, (1,)), (PAD + rows, (2,))):
+        at = pl.ds(base, SUB)
+        packs = []
+        for lo, is_right in ((0, False), (cols - LANES, True)):
+
+            def load(kind, layer):
+                values = [
+                    halo_tile(cross_rows, near_rows, odd, tile, kind, layer, pl.ds(lo, LANES))
+                    for tile in tiles
+                ]
+                if len(values) == 1 or values[0] is None:
+                    return values[0]
+                return jnp.where(is_first, values[0], values[1])
+
+            packs.append(pack_tile(load, lane, is_right))
+        left, right = packs
         cross[at, :] = jnp.where(odd_col, right, left)
         near[at, :] = jnp.where(odd_col, left, right)
 
@@ -518,9 +528,10 @@
     mine, shifts = from_partner(True, lanes())
     for t in range(n_tiles):
         at = pl.ds(t * SUB, SUB)
+        strip = cross[packed_at(t, n_tiles), :]
         kinds = range(4 if t in (0, n_tiles - 1) else 4 + STEPS)
         values = [
-            jnp.where(mine, pltpu.roll(cross[at, :], shifts[kind], 1), base[kind, at, :])
+            jnp.where(mine, pltpu.roll(strip, shifts[kind], 1), base[kind, at, :])
             for kind in kinds
         ]
         for kind in kinds:
@@ -539,8 +550,9 @@
 
     for t in range(n_tiles):
         at = pl.ds(t * SUB, SUB)
+        strip = near[packed_at(t, n_tiles), :]
         for kind in range(4 if t in (0, n_tiles - 1) else 4 + STEPS):
-            value = jnp.where(mine, pltpu.roll(near[at, :], moves[kind], 1), base[kind, at, :])
+            value = jnp.where(mine, pltpu.roll(strip, moves[kind], 1), base[kind, at, :])
             if kind == 0:
                 e[0, at, :] = value
             elif kind < 3:
@@ -716,7 +728,7 @@
     cross = lax.ppermute(cross, "gx", pairs(gx_count, 1))
     near = lax.ppermute(near, "gx", pairs(gx_count, 0))
 
-    packed = shape(ext_rows, LANES)
+    packed = shape(ext_rows - SUB, LANES)
     channels = mon_x.shape[0]
     cross_cols, near_cols, base, src, src_edge, place, place_edge = call(
         lambda *refs: prep_kernel(capacity, *refs),

time: 31.2 us -> 31.1 us (level)
  no operation moved by 1% of the time
where the time goes in v15:
time: 31.1 us; the launch traced here: 30.9 us
  blocking collectives  11.7 us (38%)
  starting transfers between devices  10.2 us (33%)
  Pallas kernels  7.72 us (25%)
  between operations  0.82 us (3%)
  waiting for transfers between devices  0.44 us (1%)
    all_to_all x1, blocking collectives, on_device(): lax.all_to_all(outgoing, ('gx', 'gy'), split_axis=0, concat_axis=0, tiled...  11.7 us
    ppermute x1, starting transfers between devices, on_device(): near_cols = lax.ppermute(near_cols, 'gy', pairs(gy_count, 0))  4.46 us
    ppermute x1, starting transfers between devices, on_device(): near = lax.ppermute(near, 'gx', pairs(gx_count, 0))  4.36 us
    pallas_call x1, Pallas kernels, on_device(): call(inner_kernel, (shape(3, 2, n_lanes, rows, LANES), shape(owners * cap...  2.04 us
    pallas_call x1, Pallas kernels, on_device(): call(lambda *refs: prep_kernel(capacity, *refs), (packed, packed, shape(4...  1.99 us
    pallas_call x1, Pallas kernels, on_device(): call(rows_kernel, (strip, strip), 3, in_space=pltpu.HBM, scratch=(pltpu.V...  1.18 us
    pallas_call x1, Pallas kernels, on_device(): call(edge_kernel, (shape(3, rows, LANES), pltpu.VMEM((owners * capacity,...  1.08 us
    pallas_call x1, Pallas kernels, on_device(): call(deliver_kernel, (shape(3, 2, rows, cols), shape(1, *incoming.shape))...  1.03 us
  transfers between devices with their start and end apart: 4, of which 1 were waited for; matrix products, arithmetic and copies ran while one was open for 0% of the time, Pallas kernels for 14%

profile of v15, /device:TPU:0, one launch (start us, length us, event | category | flops | bytes accessed | tf_op | source)
XLA Modules:
  0.0 30.9 jit_solution(16182870610526379308)
XLA Ops:
  0.6 0.0 copy-start
  0.6 0.0 copy-start.2
  0.7 0.0 copy-start.1
  0.7 0.0 copy-start.8
  0.7 0.0 copy-start.7
  0.7 0.0 copy-start.4
  0.7 0.0 copy-start.6
  0.7 0.0 copy-start.5
  0.7 1.2 %shard_map.104 = (f32[8,2,8,256]{3,2,1,0:T(8,128)S(1)}, f32[8,2,8,256]{3,2,1,0:T(8,128)S(1)}) custom-call(f32[3,2,128,256]{3,2,1,0:T(8,128)} %fields.3, f32[2,128,256]{2,1,0:T(8,128)} %eps.3, f32[4,2,128,256]{3,2,1,0:T(8,128)} %fwd.3), custom_call_target="tpu_custom_call" | custom-call | bytes 1048576 | tf_op jit(solution)/shard_map/pallas_call | solution.py:715
  1.9 0.0 copy-start.3
  1.9 0.7 %collective-permute-start = (f32[8,2,8,256]{3,2,1,0:T(8,128)S(1)}, f32[8,2,8,256]{3,2,1,0:T(8,128)S(1)}, u32[]{:S(2)}, u32[]{:S(2)}) collective-permute-start(f32[8,2,8,256]{3,2,1,0:T(8,128)S(1)} %get-tuple-element.18), channel_id=1, source_target_pairs={{4,8},{8,4},{5,9},{9,5},{6,10},{10,6},{7,11},{11,7},{20,24},{24,20... | collective-permute-start | bytes 393224 | tf_op jit(solution)/shard_map/ppermute | solution.py:728
  2.6 4.4 %collective-permute-start.1 = (f32[8,2,8,256]{3,2,1,0:T(8,128)S(1)}, f32[8,2,8,256]{3,2,1,0:T(8,128)S(1)}, u32[]{:S(2)}, u32[]{:S(2)}) collective-permute-start(f32[8,2,8,256]{3,2,1,0:T(8,128)S(1)} %get-tuple-element.19), channel_id=1, source_target_pairs={{0,4},{8,12},{4,0},{12,8},{1,5},{9,13},{5,1},{13,9},{2,6},{10,14},... | collective-permute-start | bytes 393224 | tf_op jit(solution)/shard_map/ppermute | solution.py:729
  7.0 0.0 copy-done
  7.0 0.0 copy-done.2
  7.0 0.0 copy-done.1
  7.0 0.0 copy-done.8
  7.0 0.0 copy-done.7
  7.0 0.0 copy-done.4
  7.0 0.0 copy-done.6
  7.0 0.0 copy-done.5
  7.0 2.0 %shard_map.105 = (f32[152,128]{1,0:T(8,128)S(1)}, f32[152,128]{1,0:T(8,128)S(1)}, f32[8,160,128]{2,1,0:T(8,128)S(1)}, f32[4,2,160,256]{3,2,1,0:T(8,128)S(1)}, f3...) custom-call(f32[3,2,128,256]{3,2,1,0:T(8,128)S(1)} %copy-done.1, ...), custom_call_target="tpu_custom_call" | custom-call | flops 188743680 | bytes 2097152 | tf_op jit(solution)/shard_map/pallas_call | solution.py:733
  9.0 0.0 collective-permute-done.cross.cross_rows
  9.0 0.0 collective-permute-done.1.near.near_rows
  9.0 0.2 shard_map.107
  9.2 0.7 %collective-permute-start.2 = (f32[152,128]{1,0:T(8,128)S(1)}, f32[152,128]{1,0:T(8,128)S(1)}, u32[]{:S(2)}, u32[]{:S(2)}) collective-permute-start(f32[152,128]{1,0:T(8,128)S(1)} %get-tuple-element.28), channel_id=1, source_target_pairs={{1,2},{2,1},{5,6},{6,5},{9,10},{10,9},{13,14},{14,13},{17,18},{18,... | collective-permute-start | bytes 233480 | tf_op jit(solution)/shard_map/ppermute | solution.py:758
  9.9 4.5 %collective-permute-start.3 = (f32[152,128]{1,0:T(8,128)S(1)}, f32[152,128]{1,0:T(8,128)S(1)}, u32[]{:S(2)}, u32[]{:S(2)}) collective-permute-start(f32[152,128]{1,0:T(8,128)S(1)} %get-tuple-element.29), channel_id=1, source_target_pairs={{0,1},{2,3},{1,0},{3,2},{4,5},{6,7},{5,4},{7,6},{8,9},{10,11},{9,8... | collective-permute-start | bytes 233480 | tf_op jit(solution)/shard_map/ppermute | solution.py:759
  14.3 0.0 copy-done.3
  14.3 2.0 %shard_map.106 = (f32[3,2,2,128,128]{4,3,2,1,0:T(8,128)S(1)}, f32[256,128]{1,0:T(8,128)S(1)}, f32[8,160,128]{2,1,0:T(8,128)S(1)}) custom-call(f32[3,2,128,256]{3,2,1,0:T(8,128)S(1)} %copy-done.1, f32[2,128,256]{2,1,0:T(8,128)S(1)} %copy-done.2, f32[4,2,128,256]{3,2,1,0:T(8,128)S(1)} %copy-done, f32[8,2,8,256]{3,2,1,0:T(8,128)S(1)} %collective-permute-done.cross.cross_rows, ...), custom_call_target="tpu_custom_call" | custom-call | flops 6553600 | bytes 3145728 | tf_op jit(solution)/shard_map/pallas_call | solution.py:762
  16.4 0.0 collective-permute-done.2.cross
  16.4 0.2 shard_map.108.base
  16.6 0.4 %collective-permute-done.3.near = f32[152,128]{1,0:T(8,128)S(1)} collective-permute-done((f32[152,128]{1,0:T(8,128)S(1)}, f32[152,128]{1,0:T(8,128)S(1)}, u32[]{:S(2)}, u32[]{:S(2)}) %collective-permute-start.3) | collective-permute-done | bytes 77856 | tf_op jit(solution)/shard_map/ppermute | solution.py:759
  17.1 1.1 %shard_map.109 = (f32[3,128,128]{2,1,0:T(8,128)S(1)}, f32[256,128]{1,0:T(8,128)S(1)}) custom-call(f32[256,128]{1,0:T(8,128)S(1)} %get-tuple-element.24.slots_in, f32[8,160,128]{2,1,0:T(8,128)S(1)} %shard_map.108.base, f32[152,128]{1,0:T(8,128)S(1)} %collective-permute-done.3.near, f32[4,160,128]{2,1,0:T(8,128)S(1)} %get-tuple-element.30.src, ...), custom_call_target="tpu_custom_call" | custom-call | flops 1638400 | bytes 524288 | tf_op jit(solution)/shard_map/pallas_call | solution.py:785
  18.1 11.7 %all_to_all.5.slots = f32[16,16,128]{2,1,0:T(8,128)S(1)} all-to-all(f32[16,16,128]{2,1,0:T(8,128)S(1)} %bitcast.5), channel_id=1, replica_groups=mesh['parts'=2,'gx'=4,'gy'=4] {'gx','gy'}, dimensions={0} | all-to-all | bytes 262144 | tf_op jit(solution)/shard_map/all_to_all | solution.py:803
  29.9 1.0 %shard_map.110 = (f32[3,2,128,256]{3,2,1,0:T(8,128)}, f32[1,16,16,128]{3,2,1,0:T(8,128)}) custom-call(f32[3,2,2,128,128]{4,3,2,1,0:T(8,128)S(1)} %get-tuple-element.23.last, f32[3,128,128]{2,1,0:T(8,128)S(1)} %get-tuple-element.32.edge_last, f32[16,16,128]{2,1,0:T(8,128)S(1)} %all_to_all.5.slots), custom_call_target="tpu_custom_call" | custom-call | flops 655360 | bytes 1572864 | tf_op jit(solution)/shard_map/pallas_call | solution.py:805
Async XLA Ops:
  0.6 6.3 %copy-start = (f32[4,2,128,256]{3,2,1,0:T(8,128)S(1)}, f32[4,2,128,256]{3,2,1,0:T(8,128)}, u32[]{:S(2)}) copy-start(f32[4,2,128,256]{3,2,1,0:T(8,128)} %fwd.3) | copy-start | bytes 3145732
  0.6 6.3 %copy-start.2 = (f32[2,128,256]{2,1,0:T(8,128)S(1)}, f32[2,128,256]{2,1,0:T(8,128)}, u32[]{:S(2)}) copy-start(f32[2,128,256]{2,1,0:T(8,128)} %eps.3) | copy-start | bytes 786436
  0.7 6.3 %copy-start.1 = (f32[3,2,128,256]{3,2,1,0:T(8,128)S(1)}, f32[3,2,128,256]{3,2,1,0:T(8,128)}, u32[]{:S(2)}) copy-start(f32[3,2,128,256]{3,2,1,0:T(8,128)} %fields.3) | copy-start | bytes 2359300
  0.7 6.3 %copy-start.8 = (s32[1,1,128,1]{2,3,1,0:T(1,128)S(1)}, s32[1,1,128,1]{2,3,1,0:T(1,128)}, u32[]{:S(2)}) copy-start(s32[1,1,128,1]{2,3,1,0:T(1,128)} %param.16) | copy-start | bytes 1540
  0.7 6.3 %copy-start.7 = (s32[1,1,128]{2,1,0:T(1,128)S(1)}, s32[1,1,128]{2,1,0:T(1,128)}, u32[]{:S(2)}) copy-start(s32[1,1,128]{2,1,0:T(1,128)} %param.15) | copy-start | bytes 1540
  0.7 6.3 %copy-start.4 = (f32[4,64]{1,0:T(4,128)S(1)}, f32[4,64]{1,0:T(4,128)}, u32[]{:S(2)}) copy-start(f32[4,64]{1,0:T(4,128)} %refs_5_.1) | copy-start | bytes 3076
  0.7 6.3 %copy-start.6 = (s32[64]{0:T(128)S(1)}, s32[64]{0:T(128)}, u32[]{:S(2)}) copy-start(s32[64]{0:T(128)} %param.13) | copy-start | bytes 772
  0.7 6.3 %copy-start.5 = (s32[64]{0:T(128)S(1)}, s32[64]{0:T(128)}, u32[]{:S(2)}) copy-start(s32[64]{0:T(128)} %param.12) | copy-start | bytes 772
  1.9 12.4 %copy-start.3 = (bf16[2,128,128]{2,1,0:T(8,128)(2,1)S(1)}, bf16[2,128,128]{2,1,0:T(8,128)(2,1)}, u32[]{:S(2)}) copy-start(bf16[2,128,128]{2,1,0:T(8,128)(2,1)} %constant.2.clone.mats) | copy-start | bytes 196612
  1.9 7.1 %collective-permute-start = (f32[8,2,8,256]{3,2,1,0:T(8,128)S(1)}, f32[8,2,8,256]{3,2,1,0:T(8,128)S(1)}, u32[]{:S(2)}, u32[]{:S(2)}) collective-permute-start(f32[8,2,8,256]{3,2,1,0:T(8,128)S(1)} %get-tuple-element.18), channel_id=1, source_target_pairs={{4,8},{8,4},{5,9},{9,5},{6,10},{10,6},{7,11},{11,7},{20,24},{24,20... | collective-permute-start | bytes 393224 | tf_op jit(solution)/shard_map/ppermute | solution.py:728
  2.6 6.4 %collective-permute-start.1 = (f32[8,2,8,256]{3,2,1,0:T(8,128)S(1)}, f32[8,2,8,256]{3,2,1,0:T(8,128)S(1)}, u32[]{:S(2)}, u32[]{:S(2)}) collective-permute-start(f32[8,2,8,256]{3,2,1,0:T(8,128)S(1)} %get-tuple-element.19), channel_id=1, source_target_pairs={{0,4},{8,12},{4,0},{12,8},{1,5},{9,13},{5,1},{13,9},{2,6},{10,14},... | collective-permute-start | bytes 393224 | tf_op jit(solution)/shard_map/ppermute | solution.py:729
  9.2 7.2 %collective-permute-start.2 = (f32[152,128]{1,0:T(8,128)S(1)}, f32[152,128]{1,0:T(8,128)S(1)}, u32[]{:S(2)}, u32[]{:S(2)}) collective-permute-start(f32[152,128]{1,0:T(8,128)S(1)} %get-tuple-element.28), channel_id=1, source_target_pairs={{1,2},{2,1},{5,6},{6,5},{9,10},{10,9},{13,14},{14,13},{17,18},{18,... | collective-permute-start | bytes 233480 | tf_op jit(solution)/shard_map/ppermute | solution.py:758
  9.9 7.2 %collective-permute-start.3 = (f32[152,128]{1,0:T(8,128)S(1)}, f32[152,128]{1,0:T(8,128)S(1)}, u32[]{:S(2)}, u32[]{:S(2)}) collective-permute-start(f32[152,128]{1,0:T(8,128)S(1)} %get-tuple-element.29), channel_id=1, source_target_pairs={{0,1},{2,3},{1,0},{3,2},{4,5},{6,7},{5,4},{7,6},{8,9},{10,11},{9,8... | collective-permute-start | bytes 233480 | tf_op jit(solution)/shard_map/ppermute | solution.py:759

commit v16 on v15

--- a/solution.py
+++ b/solution.py
@@ -592,11 +592,11 @@
         for kind, value in enumerate(values):
             edge_last[kind, pl.ds(t * SUB - PAD, SUB), :] = value
 
+    last_fields(
+        range(PAD // SUB, n_tiles - PAD // SUB), [()], shifts, e, load_hx, load_hy, store
+    )
     edge_filter(g, merged)
     edge_slots(merged, slots_in, place, slots)
-    last_fields(
-        range(PAD // SUB, n_tiles - PAD // SUB), [()], shifts, e, load_hx, load_hy, store
-    )
 
 
 def edge_filter(g, merged):

time: 31.1 us -> 31.1 us (level)
  no operation moved by 1% of the time
where the time goes in v16:
time: 31.1 us; the launch traced here: 30.9 us
  blocking collectives  11.7 us (38%)
  starting transfers between devices  10.2 us (33%)
  Pallas kernels  7.72 us (25%)
  between operations  0.82 us (3%)
  waiting for transfers between devices  0.44 us (1%)
    all_to_all x1, blocking collectives, on_device(): lax.all_to_all(outgoing, ('gx', 'gy'), split_axis=0, concat_axis=0, tiled...  11.7 us
    ppermute x1, starting transfers between devices, on_device(): near_cols = lax.ppermute(near_cols, 'gy', pairs(gy_count, 0))  4.46 us
    ppermute x1, starting transfers between devices, on_device(): near = lax.ppermute(near, 'gx', pairs(gx_count, 0))  4.36 us
    pallas_call x1, Pallas kernels, on_device(): call(inner_kernel, (shape(3, 2, n_lanes, rows, LANES), shape(owners * cap...  2.04 us
    pallas_call x1, Pallas kernels, on_device(): call(lambda *refs: prep_kernel(capacity, *refs), (packed, packed, shape(4...  1.99 us
    pallas_call x1, Pallas kernels, on_device(): call(rows_kernel, (strip, strip), 3, in_space=pltpu.HBM, scratch=(pltpu.V...  1.18 us
    pallas_call x1, Pallas kernels, on_device(): call(edge_kernel, (shape(3, rows, LANES), pltpu.VMEM((owners * capacity,...  1.08 us
    pallas_call x1, Pallas kernels, on_device(): call(deliver_kernel, (shape(3, 2, rows, cols), shape(1, *incoming.shape))...  1.03 us
  transfers between devices with their start and end apart: 4, of which 1 were waited for; matrix products, arithmetic and copies ran while one was open for 0% of the time, Pallas kernels for 14%

profile of v16, /device:TPU:0, one launch (start us, length us, event | category | flops | bytes accessed | tf_op | source)
XLA Modules:
  0.0 30.9 jit_solution(16182870610526379308)
XLA Ops:
  0.6 0.0 copy-start
  0.6 0.0 copy-start.2
  0.7 0.0 copy-start.1
  0.7 0.0 copy-start.8
  0.7 0.0 copy-start.7
  0.7 0.0 copy-start.4
  0.7 0.0 copy-start.6
  0.7 0.0 copy-start.5
  0.7 1.2 %shard_map.104 = (f32[8,2,8,256]{3,2,1,0:T(8,128)S(1)}, f32[8,2,8,256]{3,2,1,0:T(8,128)S(1)}) custom-call(f32[3,2,128,256]{3,2,1,0:T(8,128)} %fields.3, f32[2,128,256]{2,1,0:T(8,128)} %eps.3, f32[4,2,128,256]{3,2,1,0:T(8,128)} %fwd.3), custom_call_target="tpu_custom_call" | custom-call | bytes 1048576 | tf_op jit(solution)/shard_map/pallas_call | solution.py:715
  1.9 0.0 copy-start.3
  1.9 0.7 %collective-permute-start = (f32[8,2,8,256]{3,2,1,0:T(8,128)S(1)}, f32[8,2,8,256]{3,2,1,0:T(8,128)S(1)}, u32[]{:S(2)}, u32[]{:S(2)}) collective-permute-start(f32[8,2,8,256]{3,2,1,0:T(8,128)S(1)} %get-tuple-element.18), channel_id=1, source_target_pairs={{4,8},{8,4},{5,9},{9,5},{6,10},{10,6},{7,11},{11,7},{20,24},{24,20... | collective-permute-start | bytes 393224 | tf_op jit(solution)/shard_map/ppermute | solution.py:728
  2.6 4.4 %collective-permute-start.1 = (f32[8,2,8,256]{3,2,1,0:T(8,128)S(1)}, f32[8,2,8,256]{3,2,1,0:T(8,128)S(1)}, u32[]{:S(2)}, u32[]{:S(2)}) collective-permute-start(f32[8,2,8,256]{3,2,1,0:T(8,128)S(1)} %get-tuple-element.19), channel_id=1, source_target_pairs={{0,4},{8,12},{4,0},{12,8},{1,5},{9,13},{5,1},{13,9},{2,6},{10,14},... | collective-permute-start | bytes 393224 | tf_op jit(solution)/shard_map/ppermute | solution.py:729
  7.0 0.0 copy-done
  7.0 0.0 copy-done.2
  7.0 0.0 copy-done.1
  7.0 0.0 copy-done.8
  7.0 0.0 copy-done.7
  7.0 0.0 copy-done.4
  7.0 0.0 copy-done.6
  7.0 0.0 copy-done.5
  7.0 2.0 %shard_map.105 = (f32[152,128]{1,0:T(8,128)S(1)}, f32[152,128]{1,0:T(8,128)S(1)}, f32[8,160,128]{2,1,0:T(8,128)S(1)}, f32[4,2,160,256]{3,2,1,0:T(8,128)S(1)}, f3...) custom-call(f32[3,2,128,256]{3,2,1,0:T(8,128)S(1)} %copy-done.1, ...), custom_call_target="tpu_custom_call" | custom-call | flops 188743680 | bytes 2097152 | tf_op jit(solution)/shard_map/pallas_call | solution.py:733
  9.0 0.0 collective-permute-done.cross.cross_rows
  9.0 0.0 collective-permute-done.1.near.near_rows
  9.0 0.2 shard_map.107
  9.2 0.7 %collective-permute-start.2 = (f32[152,128]{1,0:T(8,128)S(1)}, f32[152,128]{1,0:T(8,128)S(1)}, u32[]{:S(2)}, u32[]{:S(2)}) collective-permute-start(f32[152,128]{1,0:T(8,128)S(1)} %get-tuple-element.28), channel_id=1, source_target_pairs={{1,2},{2,1},{5,6},{6,5},{9,10},{10,9},{13,14},{14,13},{17,18},{18,... | collective-permute-start | bytes 233480 | tf_op jit(solution)/shard_map/ppermute | solution.py:758
  9.9 4.5 %collective-permute-start.3 = (f32[152,128]{1,0:T(8,128)S(1)}, f32[152,128]{1,0:T(8,128)S(1)}, u32[]{:S(2)}, u32[]{:S(2)}) collective-permute-start(f32[152,128]{1,0:T(8,128)S(1)} %get-tuple-element.29), channel_id=1, source_target_pairs={{0,1},{2,3},{1,0},{3,2},{4,5},{6,7},{5,4},{7,6},{8,9},{10,11},{9,8... | collective-permute-start | bytes 233480 | tf_op jit(solution)/shard_map/ppermute | solution.py:759
  14.3 0.0 copy-done.3
  14.3 2.0 %shard_map.106 = (f32[3,2,2,128,128]{4,3,2,1,0:T(8,128)S(1)}, f32[256,128]{1,0:T(8,128)S(1)}, f32[8,160,128]{2,1,0:T(8,128)S(1)}) custom-call(f32[3,2,128,256]{3,2,1,0:T(8,128)S(1)} %copy-done.1, f32[2,128,256]{2,1,0:T(8,128)S(1)} %copy-done.2, f32[4,2,128,256]{3,2,1,0:T(8,128)S(1)} %copy-done, f32[8,2,8,256]{3,2,1,0:T(8,128)S(1)} %collective-permute-done.cross.cross_rows, ...), custom_call_target="tpu_custom_call" | custom-call | flops 6553600 | bytes 3145728 | tf_op jit(solution)/shard_map/pallas_call | solution.py:762
  16.4 0.0 collective-permute-done.2.cross
  16.4 0.2 shard_map.108.base
  16.6 0.4 %collective-permute-done.3.near = f32[152,128]{1,0:T(8,128)S(1)} collective-permute-done((f32[152,128]{1,0:T(8,128)S(1)}, f32[152,128]{1,0:T(8,128)S(1)}, u32[]{:S(2)}, u32[]{:S(2)}) %collective-permute-start.3) | collective-permute-done | bytes 77856 | tf_op jit(solution)/shard_map/ppermute | solution.py:759
  17.1 1.1 %shard_map.109 = (f32[3,128,128]{2,1,0:T(8,128)S(1)}, f32[256,128]{1,0:T(8,128)S(1)}) custom-call(f32[256,128]{1,0:T(8,128)S(1)} %get-tuple-element.24.slots_in, f32[8,160,128]{2,1,0:T(8,128)S(1)} %shard_map.108.base, f32[152,128]{1,0:T(8,128)S(1)} %collective-permute-done.3.near, f32[4,160,128]{2,1,0:T(8,128)S(1)} %get-tuple-element.30.src, ...), custom_call_target="tpu_custom_call" | custom-call | flops 1638400 | bytes 524288 | tf_op jit(solution)/shard_map/pallas_call | solution.py:785
  18.1 11.7 %all_to_all.5.slots = f32[16,16,128]{2,1,0:T(8,128)S(1)} all-to-all(f32[16,16,128]{2,1,0:T(8,128)S(1)} %bitcast.5), channel_id=1, replica_groups=mesh['parts'=2,'gx'=4,'gy'=4] {'gx','gy'}, dimensions={0} | all-to-all | bytes 262144 | tf_op jit(solution)/shard_map/all_to_all | solution.py:803
  29.9 1.0 %shard_map.110 = (f32[3,2,128,256]{3,2,1,0:T(8,128)}, f32[1,16,16,128]{3,2,1,0:T(8,128)}) custom-call(f32[3,2,2,128,128]{4,3,2,1,0:T(8,128)S(1)} %get-tuple-element.23.last, f32[3,128,128]{2,1,0:T(8,128)S(1)} %get-tuple-element.32.edge_last, f32[16,16,128]{2,1,0:T(8,128)S(1)} %all_to_all.5.slots), custom_call_target="tpu_custom_call" | custom-call | flops 655360 | bytes 1572864 | tf_op jit(solution)/shard_map/pallas_call | solution.py:805
Async XLA Ops:
  0.6 6.3 %copy-start = (f32[4,2,128,256]{3,2,1,0:T(8,128)S(1)}, f32[4,2,128,256]{3,2,1,0:T(8,128)}, u32[]{:S(2)}) copy-start(f32[4,2,128,256]{3,2,1,0:T(8,128)} %fwd.3) | copy-start | bytes 3145732
  0.6 6.3 %copy-start.2 = (f32[2,128,256]{2,1,0:T(8,128)S(1)}, f32[2,128,256]{2,1,0:T(8,128)}, u32[]{:S(2)}) copy-start(f32[2,128,256]{2,1,0:T(8,128)} %eps.3) | copy-start | bytes 786436
  0.7 6.3 %copy-start.1 = (f32[3,2,128,256]{3,2,1,0:T(8,128)S(1)}, f32[3,2,128,256]{3,2,1,0:T(8,128)}, u32[]{:S(2)}) copy-start(f32[3,2,128,256]{3,2,1,0:T(8,128)} %fields.3) | copy-start | bytes 2359300
  0.7 6.3 %copy-start.8 = (s32[1,1,128,1]{2,3,1,0:T(1,128)S(1)}, s32[1,1,128,1]{2,3,1,0:T(1,128)}, u32[]{:S(2)}) copy-start(s32[1,1,128,1]{2,3,1,0:T(1,128)} %param.16) | copy-start | bytes 1540
  0.7 6.3 %copy-start.7 = (s32[1,1,128]{2,1,0:T(1,128)S(1)}, s32[1,1,128]{2,1,0:T(1,128)}, u32[]{:S(2)}) copy-start(s32[1,1,128]{2,1,0:T(1,128)} %param.15) | copy-start | bytes 1540
  0.7 6.3 %copy-start.4 = (f32[4,64]{1,0:T(4,128)S(1)}, f32[4,64]{1,0:T(4,128)}, u32[]{:S(2)}) copy-start(f32[4,64]{1,0:T(4,128)} %refs_5_.1) | copy-start | bytes 3076
  0.7 6.3 %copy-start.6 = (s32[64]{0:T(128)S(1)}, s32[64]{0:T(128)}, u32[]{:S(2)}) copy-start(s32[64]{0:T(128)} %param.13) | copy-start | bytes 772
  0.7 6.3 %copy-start.5 = (s32[64]{0:T(128)S(1)}, s32[64]{0:T(128)}, u32[]{:S(2)}) copy-start(s32[64]{0:T(128)} %param.12) | copy-start | bytes 772
  1.9 12.4 %copy-start.3 = (bf16[2,128,128]{2,1,0:T(8,128)(2,1)S(1)}, bf16[2,128,128]{2,1,0:T(8,128)(2,1)}, u32[]{:S(2)}) copy-start(bf16[2,128,128]{2,1,0:T(8,128)(2,1)} %constant.2.clone.mats) | copy-start | bytes 196612
  1.9 7.1 %collective-permute-start = (f32[8,2,8,256]{3,2,1,0:T(8,128)S(1)}, f32[8,2,8,256]{3,2,1,0:T(8,128)S(1)}, u32[]{:S(2)}, u32[]{:S(2)}) collective-permute-start(f32[8,2,8,256]{3,2,1,0:T(8,128)S(1)} %get-tuple-element.18), channel_id=1, source_target_pairs={{4,8},{8,4},{5,9},{9,5},{6,10},{10,6},{7,11},{11,7},{20,24},{24,20... | collective-permute-start | bytes 393224 | tf_op jit(solution)/shard_map/ppermute | solution.py:728
  2.6 6.4 %collective-permute-start.1 = (f32[8,2,8,256]{3,2,1,0:T(8,128)S(1)}, f32[8,2,8,256]{3,2,1,0:T(8,128)S(1)}, u32[]{:S(2)}, u32[]{:S(2)}) collective-permute-start(f32[8,2,8,256]{3,2,1,0:T(8,128)S(1)} %get-tuple-element.19), channel_id=1, source_target_pairs={{0,4},{8,12},{4,0},{12,8},{1,5},{9,13},{5,1},{13,9},{2,6},{10,14},... | collective-permute-start | bytes 393224 | tf_op jit(solution)/shard_map/ppermute | solution.py:729
  9.2 7.2 %collective-permute-start.2 = (f32[152,128]{1,0:T(8,128)S(1)}, f32[152,128]{1,0:T(8,128)S(1)}, u32[]{:S(2)}, u32[]{:S(2)}) collective-permute-start(f32[152,128]{1,0:T(8,128)S(1)} %get-tuple-element.28), channel_id=1, source_target_pairs={{1,2},{2,1},{5,6},{6,5},{9,10},{10,9},{13,14},{14,13},{17,18},{18,... | collective-permute-start | bytes 233480 | tf_op jit(solution)/shard_map/ppermute | solution.py:758
  9.9 7.2 %collective-permute-start.3 = (f32[152,128]{1,0:T(8,128)S(1)}, f32[152,128]{1,0:T(8,128)S(1)}, u32[]{:S(2)}, u32[]{:S(2)}) collective-permute-start(f32[152,128]{1,0:T(8,128)S(1)} %get-tuple-element.29), channel_id=1, source_target_pairs={{0,1},{2,3},{1,0},{3,2},{4,5},{6,7},{5,4},{7,6},{8,9},{10,11},{9,8... | collective-permute-start | bytes 233480 | tf_op jit(solution)/shard_map/ppermute | solution.py:759

commit v17 on v15

--- a/solution.py
+++ b/solution.py
@@ -525,7 +525,7 @@
 
 def edge_cross_kernel(base, cross, result):
     n_tiles = base.shape[1] // SUB
-    mine, shifts = from_partner(True, lanes())
+    mine, shifts = from_partner(False, lanes())
     for t in range(n_tiles):
         at = pl.ds(t * SUB, SUB)
         strip = cross[packed_at(t, n_tiles), :]
@@ -546,7 +546,7 @@
     n_tiles = ext_rows // SUB
     lane = lanes()
     spot = lane & (HALF - 1)
-    mine, moves = from_partner(False, lane)
+    mine, moves = from_partner(True, lane)
 
     for t in range(n_tiles):
         at = pl.ds(t * SUB, SUB)
@@ -755,8 +755,8 @@
     cross_cols, near_cols = call(
         corners_kernel, (packed, packed), 4, flops=cells, size=8 * ext_rows * LANES
     )(cross_cols, near_cols, cross, near)
+    near_cols = lax.ppermute(near_cols, "gy", pairs(gy_count, 0))
     cross_cols = lax.ppermute(cross_cols, "gy", pairs(gy_count, 1))
-    near_cols = lax.ppermute(near_cols, "gy", pairs(gy_count, 0))
 
     plane = (2, n_lanes, ext_rows, LANES)
     last, slots, base = call(
@@ -781,7 +781,7 @@
     plane = (ext_rows, LANES)
     (base,) = call(
         edge_cross_kernel, (shape(4 + STEPS, *plane),), 2, flops=10 * cells, size=8 * cells
-    )(base, cross_cols)
+    )(base, near_cols)
     edge_last, outgoing = call(
         edge_kernel,
         (shape(3, rows, LANES), pltpu.VMEM((owners * capacity, width), F32)),
@@ -797,7 +797,7 @@
         ),
         flops=50 * cells,
         size=16 * cells,
-    )(slots, base, near_cols, src_edge, place_edge)
+    )(slots, base, cross_cols, src_edge, place_edge)
 
     outgoing = outgoing.reshape(owners, capacity, width)
     incoming = lax.all_to_all(outgoing, ("gx", "gy"), split_axis=0, concat_axis=0, tiled=True)

time: 31.1 us -> 32.1 us (1.032)
  blocking collectives: 11.7 us -> 15.5 us
  starting transfers between devices: 10.2 us -> 7.32 us
    all_to_all x1, blocking collectives: 11.7 us -> 15.5 us  [on_device(): lax.all_to_all(outgoing, ('gx', 'gy'), split_axis=0, concat_axis=0, tiled...]
    ppermute x1, starting transfers between devices: 4.46 us -> 1.64 us  [on_device(): near_cols = lax.ppermute(near_cols, 'gy', pairs(gy_count, 0))]
  transfers between devices with their start and end apart: 4 -> 4, of which waited for: 1 -> 1; matrix products, arithmetic and copies ran while one was open for 0% -> 0% of each run, Pallas kernels for 14% -> 13%
where the time goes in v17:
time: 32.1 us; the launch traced here: 31.9 us
  blocking collectives  15.5 us (48%)
  Pallas kernels  7.73 us (24%)
  starting transfers between devices  7.32 us (23%)
  between operations  0.83 us (3%)
  waiting for transfers between devices  0.47 us (1%)
    all_to_all x1, blocking collectives, on_device(): lax.all_to_all(outgoing, ('gx', 'gy'), split_axis=0, concat_axis=0, tiled...  15.5 us
    ppermute x1, starting transfers between devices, on_device(): near = lax.ppermute(near, 'gx', pairs(gx_count, 0))  4.36 us
    pallas_call x1, Pallas kernels, on_device(): call(inner_kernel, (shape(3, 2, n_lanes, rows, LANES), shape(owners * cap...  2.05 us
    pallas_call x1, Pallas kernels, on_device(): call(lambda *refs: prep_kernel(capacity, *refs), (packed, packed, shape(4...  1.99 us
    ppermute x1, starting transfers between devices, on_device(): near_cols = lax.ppermute(near_cols, 'gy', pairs(gy_count, 0))  1.64 us
    pallas_call x1, Pallas kernels, on_device(): call(rows_kernel, (strip, strip), 3, in_space=pltpu.HBM, scratch=(pltpu.V...  1.18 us
    pallas_call x1, Pallas kernels, on_device(): call(edge_kernel, (shape(3, rows, LANES), pltpu.VMEM((owners * capacity,...  1.09 us
    pallas_call x1, Pallas kernels, on_device(): call(deliver_kernel, (shape(3, 2, rows, cols), shape(1, *incoming.shape))...  1.03 us
  transfers between devices with their start and end apart: 4, of which 1 were waited for; matrix products, arithmetic and copies ran while one was open for 0% of the time, Pallas kernels for 13%

profile of v17, /device:TPU:0, one launch (start us, length us, event | category | flops | bytes accessed | tf_op | source)
XLA Modules:
  0.0 31.9 jit_solution(5136528167641556867)
XLA Ops:
  0.6 0.0 copy-start
  0.6 0.0 copy-start.2
  0.7 0.0 copy-start.1
  0.7 0.0 copy-start.8
  0.7 0.0 copy-start.7
  0.7 0.0 copy-start.4
  0.7 0.0 copy-start.6
  0.7 0.0 copy-start.5
  0.7 1.2 %shard_map.104 = (f32[8,2,8,256]{3,2,1,0:T(8,128)S(1)}, f32[8,2,8,256]{3,2,1,0:T(8,128)S(1)}) custom-call(f32[3,2,128,256]{3,2,1,0:T(8,128)} %fields.3, f32[2,128,256]{2,1,0:T(8,128)} %eps.3, f32[4,2,128,256]{3,2,1,0:T(8,128)} %fwd.3), custom_call_target="tpu_custom_call" | custom-call | bytes 1048576 | tf_op jit(solution)/shard_map/pallas_call | solution.py:715
  1.9 0.0 copy-start.3
  1.9 0.7 %collective-permute-start = (f32[8,2,8,256]{3,2,1,0:T(8,128)S(1)}, f32[8,2,8,256]{3,2,1,0:T(8,128)S(1)}, u32[]{:S(2)}, u32[]{:S(2)}) collective-permute-start(f32[8,2,8,256]{3,2,1,0:T(8,128)S(1)} %get-tuple-element.18), channel_id=1, source_target_pairs={{4,8},{8,4},{5,9},{9,5},{6,10},{10,6},{7,11},{11,7},{20,24},{24,20... | collective-permute-start | bytes 393224 | tf_op jit(solution)/shard_map/ppermute | solution.py:728
  2.6 4.4 %collective-permute-start.1 = (f32[8,2,8,256]{3,2,1,0:T(8,128)S(1)}, f32[8,2,8,256]{3,2,1,0:T(8,128)S(1)}, u32[]{:S(2)}, u32[]{:S(2)}) collective-permute-start(f32[8,2,8,256]{3,2,1,0:T(8,128)S(1)} %get-tuple-element.19), channel_id=1, source_target_pairs={{0,4},{8,12},{4,0},{12,8},{1,5},{9,13},{5,1},{13,9},{2,6},{10,14},... | collective-permute-start | bytes 393224 | tf_op jit(solution)/shard_map/ppermute | solution.py:729
  7.0 0.0 copy-done
  7.0 0.0 copy-done.2
  7.0 0.0 copy-done.1
  7.0 0.0 copy-done.8
  7.0 0.0 copy-done.7
  7.0 0.0 copy-done.4
  7.0 0.0 copy-done.6
  7.0 0.0 copy-done.5
  7.0 2.0 %shard_map.105 = (f32[152,128]{1,0:T(8,128)S(1)}, f32[152,128]{1,0:T(8,128)S(1)}, f32[8,160,128]{2,1,0:T(8,128)S(1)}, f32[4,2,160,256]{3,2,1,0:T(8,128)S(1)}, f3...) custom-call(f32[3,2,128,256]{3,2,1,0:T(8,128)S(1)} %copy-done.1, ...), custom_call_target="tpu_custom_call" | custom-call | flops 188743680 | bytes 2097152 | tf_op jit(solution)/shard_map/pallas_call | solution.py:733
  9.0 0.0 collective-permute-done.cross.cross_rows
  9.0 0.0 collective-permute-done.1.near.near_rows
  9.0 0.2 shard_map.107
  9.2 1.6 %collective-permute-start.2 = (f32[152,128]{1,0:T(8,128)S(1)}, f32[152,128]{1,0:T(8,128)S(1)}, u32[]{:S(2)}, u32[]{:S(2)}) collective-permute-start(f32[152,128]{1,0:T(8,128)S(1)} %get-tuple-element.28), channel_id=1, source_target_pairs={{0,1},{2,3},{1,0},{3,2},{4,5},{6,7},{5,4},{7,6},{8,9},{10,11},{9,8... | collective-permute-start | bytes 233480 | tf_op jit(solution)/shard_map/ppermute | solution.py:758
  10.8 0.7 %collective-permute-start.3 = (f32[152,128]{1,0:T(8,128)S(1)}, f32[152,128]{1,0:T(8,128)S(1)}, u32[]{:S(2)}, u32[]{:S(2)}) collective-permute-start(f32[152,128]{1,0:T(8,128)S(1)} %get-tuple-element.29), channel_id=1, source_target_pairs={{1,2},{2,1},{5,6},{6,5},{9,10},{10,9},{13,14},{14,13},{17,18},{18,... | collective-permute-start | bytes 233480 | tf_op jit(solution)/shard_map/ppermute | solution.py:759
  11.5 0.0 copy-done.3
  11.5 2.0 %shard_map.106 = (f32[3,2,2,128,128]{4,3,2,1,0:T(8,128)S(1)}, f32[256,128]{1,0:T(8,128)S(1)}, f32[8,160,128]{2,1,0:T(8,128)S(1)}) custom-call(f32[3,2,128,256]{3,2,1,0:T(8,128)S(1)} %copy-done.1, f32[2,128,256]{2,1,0:T(8,128)S(1)} %copy-done.2, f32[4,2,128,256]{3,2,1,0:T(8,128)S(1)} %copy-done, f32[8,2,8,256]{3,2,1,0:T(8,128)S(1)} %collective-permute-done.cross.cross_rows, ...), custom_call_target="tpu_custom_call" | custom-call | flops 6553600 | bytes 3145728 | tf_op jit(solution)/shard_map/pallas_call | solution.py:762
  13.6 0.5 %collective-permute-done.2.cross = f32[152,128]{1,0:T(8,128)S(1)} collective-permute-done((f32[152,128]{1,0:T(8,128)S(1)}, f32[152,128]{1,0:T(8,128)S(1)}, u32[]{:S(2)}, u32[]{:S(2)}) %collective-permute-start.2) | collective-permute-done | bytes 77856 | tf_op jit(solution)/shard_map/ppermute | solution.py:758
  14.0 0.2 shard_map.108.base
  14.3 0.0 collective-permute-done.3.near
  14.3 1.1 %shard_map.109 = (f32[3,128,128]{2,1,0:T(8,128)S(1)}, f32[256,128]{1,0:T(8,128)S(1)}) custom-call(f32[256,128]{1,0:T(8,128)S(1)} %get-tuple-element.24.slots_in, f32[8,160,128]{2,1,0:T(8,128)S(1)} %shard_map.108.base, f32[152,128]{1,0:T(8,128)S(1)} %collective-permute-done.3.near, f32[4,160,128]{2,1,0:T(8,128)S(1)} %get-tuple-element.30.src, ...), custom_call_target="tpu_custom_call" | custom-call | flops 1638400 | bytes 524288 | tf_op jit(solution)/shard_map/pallas_call | solution.py:785
  15.4 15.5 %all_to_all.5.slots = f32[16,16,128]{2,1,0:T(8,128)S(1)} all-to-all(f32[16,16,128]{2,1,0:T(8,128)S(1)} %bitcast.5), channel_id=1, replica_groups=mesh['parts'=2,'gx'=4,'gy'=4] {'gx','gy'}, dimensions={0} | all-to-all | bytes 262144 | tf_op jit(solution)/shard_map/all_to_all | solution.py:803
  30.9 1.0 %shard_map.110 = (f32[3,2,128,256]{3,2,1,0:T(8,128)}, f32[1,16,16,128]{3,2,1,0:T(8,128)}) custom-call(f32[3,2,2,128,128]{4,3,2,1,0:T(8,128)S(1)} %get-tuple-element.23.last, f32[3,128,128]{2,1,0:T(8,128)S(1)} %get-tuple-element.32.edge_last, f32[16,16,128]{2,1,0:T(8,128)S(1)} %all_to_all.5.slots), custom_call_target="tpu_custom_call" | custom-call | flops 655360 | bytes 1572864 | tf_op jit(solution)/shard_map/pallas_call | solution.py:805
Async XLA Ops:
  0.6 6.3 %copy-start = (f32[4,2,128,256]{3,2,1,0:T(8,128)S(1)}, f32[4,2,128,256]{3,2,1,0:T(8,128)}, u32[]{:S(2)}) copy-start(f32[4,2,128,256]{3,2,1,0:T(8,128)} %fwd.3) | copy-start | bytes 3145732
  0.6 6.3 %copy-start.2 = (f32[2,128,256]{2,1,0:T(8,128)S(1)}, f32[2,128,256]{2,1,0:T(8,128)}, u32[]{:S(2)}) copy-start(f32[2,128,256]{2,1,0:T(8,128)} %eps.3) | copy-start | bytes 786436
  0.7 6.3 %copy-start.1 = (f32[3,2,128,256]{3,2,1,0:T(8,128)S(1)}, f32[3,2,128,256]{3,2,1,0:T(8,128)}, u32[]{:S(2)}) copy-start(f32[3,2,128,256]{3,2,1,0:T(8,128)} %fields.3) | copy-start | bytes 2359300
  0.7 6.3 %copy-start.8 = (s32[1,1,128,1]{2,3,1,0:T(1,128)S(1)}, s32[1,1,128,1]{2,3,1,0:T(1,128)}, u32[]{:S(2)}) copy-start(s32[1,1,128,1]{2,3,1,0:T(1,128)} %param.16) | copy-start | bytes 1540
  0.7 6.3 %copy-start.7 = (s32[1,1,128]{2,1,0:T(1,128)S(1)}, s32[1,1,128]{2,1,0:T(1,128)}, u32[]{:S(2)}) copy-start(s32[1,1,128]{2,1,0:T(1,128)} %param.15) | copy-start | bytes 1540
  0.7 6.3 %copy-start.4 = (f32[4,64]{1,0:T(4,128)S(1)}, f32[4,64]{1,0:T(4,128)}, u32[]{:S(2)}) copy-start(f32[4,64]{1,0:T(4,128)} %refs_5_.1) | copy-start | bytes 3076
  0.7 6.3 %copy-start.6 = (s32[64]{0:T(128)S(1)}, s32[64]{0:T(128)}, u32[]{:S(2)}) copy-start(s32[64]{0:T(128)} %param.13) | copy-start | bytes 772
  0.7 6.3 %copy-start.5 = (s32[64]{0:T(128)S(1)}, s32[64]{0:T(128)}, u32[]{:S(2)}) copy-start(s32[64]{0:T(128)} %param.12) | copy-start | bytes 772
  1.9 9.6 %copy-start.3 = (bf16[2,128,128]{2,1,0:T(8,128)(2,1)S(1)}, bf16[2,128,128]{2,1,0:T(8,128)(2,1)}, u32[]{:S(2)}) copy-start(bf16[2,128,128]{2,1,0:T(8,128)(2,1)} %constant.2.clone.mats) | copy-start | bytes 196612
  1.9 7.1 %collective-permute-start = (f32[8,2,8,256]{3,2,1,0:T(8,128)S(1)}, f32[8,2,8,256]{3,2,1,0:T(8,128)S(1)}, u32[]{:S(2)}, u32[]{:S(2)}) collective-permute-start(f32[8,2,8,256]{3,2,1,0:T(8,128)S(1)} %get-tuple-element.18), channel_id=1, source_target_pairs={{4,8},{8,4},{5,9},{9,5},{6,10},{10,6},{7,11},{11,7},{20,24},{24,20... | collective-permute-start | bytes 393224 | tf_op jit(solution)/shard_map/ppermute | solution.py:728
  2.6 6.4 %collective-permute-start.1 = (f32[8,2,8,256]{3,2,1,0:T(8,128)S(1)}, f32[8,2,8,256]{3,2,1,0:T(8,128)S(1)}, u32[]{:S(2)}, u32[]{:S(2)}) collective-permute-start(f32[8,2,8,256]{3,2,1,0:T(8,128)S(1)} %get-tuple-element.19), channel_id=1, source_target_pairs={{0,4},{8,12},{4,0},{12,8},{1,5},{9,13},{5,1},{13,9},{2,6},{10,14},... | collective-permute-start | bytes 393224 | tf_op jit(solution)/shard_map/ppermute | solution.py:729
  9.2 4.8 %collective-permute-start.2 = (f32[152,128]{1,0:T(8,128)S(1)}, f32[152,128]{1,0:T(8,128)S(1)}, u32[]{:S(2)}, u32[]{:S(2)}) collective-permute-start(f32[152,128]{1,0:T(8,128)S(1)} %get-tuple-element.28), channel_id=1, source_target_pairs={{0,1},{2,3},{1,0},{3,2},{4,5},{6,7},{5,4},{7,6},{8,9},{10,11},{9,8... | collective-permute-start | bytes 233480 | tf_op jit(solution)/shard_map/ppermute | solution.py:758
  10.8 3.4 %collective-permute-start.3 = (f32[152,128]{1,0:T(8,128)S(1)}, f32[152,128]{1,0:T(8,128)S(1)}, u32[]{:S(2)}, u32[]{:S(2)}) collective-permute-start(f32[152,128]{1,0:T(8,128)S(1)} %get-tuple-element.29), channel_id=1, source_target_pairs={{1,2},{2,1},{5,6},{6,5},{9,10},{10,9},{13,14},{14,13},{17,18},{18,... | collective-permute-start | bytes 233480 | tf_op jit(solution)/shard_map/ppermute | solution.py:759
